TPU v7x, 32 devices: a whole 2x2x4 slice. The times are simulated.
32 devices in a mesh: dp: 16 (over z, x, core), tensor: 2 (over y).
Axes of the slice: x: 2, y: 2, z: 4, core: 2. Of those that a mesh axis runs over, the one named last changes fastest.
Arguments:
- tokens: bfloat16 [16384, 1024], P(('dp', 'tensor')), may hold values from -6 to 6
- lengths: int32 [16, 4], P('dp'), may hold values from 1 to 512, 1024 in all within a row
- norm_gain: float32 [1024], replicated, may hold values from 0.5 to 1.5
- zx_weight: bfloat16 [1024, 2, 2048], P('dp', None, 'tensor'), may hold values from -0.1875 to 0.1875
- bc_weight: bfloat16 [1024, 256], P('dp'), may hold values from -0.1875 to 0.1875
- dt_weight: bfloat16 [1024, 32], P('dp', 'tensor'), may hold values from -0.1875 to 0.1875
- conv_inner: float32 [4, 2048], P(None, 'tensor'), may hold values from -3 to 3
- bias_inner: float32 [2048], P('tensor'), may hold values from -3 to 3
- conv_shared: float32 [4, 256], replicated, may hold values from -3 to 3
- bias_shared: float32 [256], replicated, may hold values from -3 to 3
- step_bias: float32 [32], P('tensor'), may hold values from -6.9 to -2.3
- log_rate: float32 [32], P('tensor'), may hold values from 0 to 2.77
- skip_gain: float32 [32], P('tensor'), may hold values from 0.5 to 1.5
- gate_gain: float32 [2048], P('tensor'), may hold values from 0.5 to 1.5
- out_weight: bfloat16 [1024, 2048], P('dp', 'tensor'), may hold values from -0.125 to 0.125
- cotangent: bfloat16 [16384, 1024], P(('dp', 'tensor')), may hold values from -6 to 6
Outputs:
- block_out: bfloat16 [16384, 1024], P(('dp', 'tensor'))
- grad_tokens: bfloat16 [16384, 1024], P(('dp', 'tensor'))
- grad_norm_gain: float32 [1024], replicated
- grad_zx_weight: float32 [1024, 2, 2048], P('dp', None, 'tensor')
- grad_bc_weight: float32 [1024, 256], P('dp')
- grad_dt_weight: float32 [1024, 32], P('dp', 'tensor')
- grad_conv_inner: float32 [4, 2048], P(None, 'tensor')
- grad_bias_inner: float32 [2048], P('tensor')
- grad_conv_shared: float32 [4, 256], replicated
- grad_bias_shared: float32 [256], replicated
- grad_step_bias: float32 [32], P('tensor')
- grad_log_rate: float32 [32], P('tensor')
- grad_skip_gain: float32 [32], P('tensor')
- grad_gate_gain: float32 [2048], P('tensor')
- grad_out_weight: float32 [1024, 2048], P('dp', 'tensor')
Inputs may be any that keep to these rules, and one draw needn't show every extreme that they name: `lengths`: each row lists the 4 sequences packed in order into the 1024 rows of one index of dp; a row sums to 1024 and its longest entry is 512.
All inputs are finite; a program needn't handle non-finite values.
Results may differ from a plain program's by a relative error of at most 0.014.
Values may be sent and summed in bfloat16 or wider, within the bound.
No kernel may reach another device: no remote copies, remote signals or barrier semaphores. Data moves between devices by JAX's collectives and lax.ppermute only.
A program may use at most 192 MiB of HBM per device.

v0:
```python
from functools import partial

import jax
import jax.numpy as jnp
from jax import lax
from jax.experimental import pallas as pl
from jax.experimental.pallas import tpu as pltpu
from jax.sharding import PartitionSpec as P

EPSILON = 1e-05
SPAN = 256
LANES = 128
TAIL = 8
TAPS = 4
MASKED = -1e30
f32 = jnp.float32
bf16 = jnp.bfloat16
LIMIT = 60 * 1024 * 1024


def mm(left, right, dims):
    return lax.dot_general(left, right, ((dims[0], dims[1]), ((), ())), preferred_element_type=f32)


NN = ((1,), (0,))
NT = ((1,), (1,))
TN = ((0,), (0,))


def halves(value, axis):
    high = value.astype(bf16)
    low = (value - high.astype(f32)).astype(bf16)
    return jnp.concatenate([high, low], axis=axis)


def sigmoid(value):
    return 1.0 / (1.0 + jnp.exp(-value))


def softplus(value):
    return jnp.maximum(value, 0.0) + jnp.log1p(jnp.exp(-jnp.abs(value)))


def segment_at(ends, position):
    total = jnp.zeros(position.shape, jnp.int32)
    for end in ends:
        total = total + (position >= end).astype(jnp.int32)
    return total


def sequence_ends(lengths_ref):
    ends, total = [], 0
    for i in range(lengths_ref.shape[1]):
        total = total + lengths_ref[0, i]
        ends.append(total)
    return ends


def step_parts(step_raw, rate, ends, base):
    rows = step_raw.shape[0]
    step = softplus(step_raw)
    row = lax.broadcasted_iota(jnp.int32, (rows, rows), 0)
    col = lax.broadcasted_iota(jnp.int32, (rows, rows), 1)
    lower = (row >= col).astype(f32).astype(bf16)
    split = mm(lower, halves(step * rate, 1), NN)
    running = split[:, :LANES] + split[:, LANES:]
    position = base + lax.broadcasted_iota(jnp.int32, (rows, 1), 0)
    segment = segment_at(ends, position)
    before = segment_at(ends, jnp.full((1, 1), base - 1, jnp.int32))
    last = segment_at(ends, jnp.full((1, 1), base + rows - 1, jnp.int32))
    carried = ((segment == before) & (position >= rows)).astype(f32)
    matched = (segment == last).astype(f32)
    entry = jnp.exp(running) * carried
    leave = jnp.exp(running[rows - 1 :, :] - running) * matched
    return step, running, entry, leave, lower, segment, row, col


def same_rows(ends, base, rows):
    across = segment_at(ends, base + lax.broadcasted_iota(jnp.int32, (1, rows), 1))
    down = segment_at(ends, base + lax.broadcasted_iota(jnp.int32, (rows, 1), 0))
    return down == across


def forward_kernel(
    lengths_ref, normed_ref, weight_ref, conv_inner_ref, bias_inner_ref,
    conv_shared_ref, bias_shared_ref, step_bias_ref, rate_ref, skip_ref, spread_ref,
    ssm_ref, inner_ref, pre_inner_ref, shared_ref, pre_shared_ref, step_ref, entering_ref,
    inner_tail, shared_tail, state,
):
    block = pl.program_id(0)
    rows = normed_ref.shape[0]
    channels = conv_inner_ref.shape[1]
    base = block * rows
    ends = sequence_ends(lengths_ref)

    @pl.when(block == 0)
    def _():
        inner_tail[0:TAIL, :] = jnp.zeros((TAIL, channels), f32)
        shared_tail[0:TAIL, :] = jnp.zeros((TAIL, shared_tail.shape[1]), f32)
        state[...] = jnp.zeros_like(state)

    @pl.when(block > 0)
    def _():
        inner_tail[0:TAIL, :] = inner_tail[rows : rows + TAIL, :]
        shared_tail[0:TAIL, :] = shared_tail[rows : rows + TAIL, :]

    normed = normed_ref[...]
    small = mm(normed, weight_ref[:, channels:], NN)
    width = conv_shared_ref.shape[1]
    shared_proj = small[:, :width]
    shared_tail[TAIL : TAIL + rows, :] = shared_proj
    shared_ref[...] = shared_proj
    step_raw = small[:, width:] + step_bias_ref[...]
    step_ref[...] = step_raw
    inner_proj = mm(normed, weight_ref[:, :channels], NN)
    inner_tail[TAIL : TAIL + rows, :] = inner_proj
    inner_ref[...] = inner_proj

    step, running, entry, leave, lower, segment, row, col = step_parts(
        step_raw, rate_ref[...], ends, base
    )
    position = base + lax.broadcasted_iota(jnp.int32, (rows, 1), 0)
    keeps = [
        ((segment_at(ends, position - k) == segment) & (position >= k)).astype(f32)
        for k in range(1, TAPS)
    ]

    def conv(tail, taps_ref, bias_ref, lo, hi):
        total = bias_ref[:, lo:hi] + taps_ref[TAPS - 1 : TAPS, lo:hi] * tail[TAIL : TAIL + rows, lo:hi]
        for k in range(1, TAPS):
            shifted = tail[TAIL - k : TAIL - k + rows, lo:hi]
            total = total + taps_ref[TAPS - 1 - k : TAPS - k, lo:hi] * (shifted * keeps[k - 1])
        return total

    pre_shared = conv(shared_tail, conv_shared_ref, bias_shared_ref, 0, width)
    pre_shared_ref[...] = pre_shared
    shared = pre_shared * sigmoid(pre_shared)
    in_map = shared[:, : width // 2].astype(bf16)
    out_map = shared[:, width // 2 :].astype(bf16)
    scores = mm(out_map, in_map, NT)
    allowed = jnp.where((row >= col) & same_rows(ends, base, rows), 0.0, MASKED)
    running_t = jnp.transpose(running)
    step2, entry2, leave2 = halves(step, 1), halves(entry, 1), halves(leave, 1)
    lane = lax.broadcasted_iota(jnp.int32, (rows, LANES), 1)
    for pair in range(channels // LANES):
        lo, hi = pair * LANES, (pair + 1) * LANES
        pre = conv(inner_tail, conv_inner_ref, bias_inner_ref, lo, hi)
        pre_inner_ref[:, lo:hi] = pre
        head_in = pre * sigmoid(pre)
        spread = spread_ref[:, lo:hi]
        scaled = head_in * mm(step2, spread, NN)
        scaled_low = scaled.astype(bf16)
        entry_wide = mm(entry2, spread, NN)
        leave_wide = mm(leave2, spread, NN)
        held = state[:, lo:hi]
        entering_ref[0, :, lo:hi] = held
        carried_out = mm(out_map, held.astype(bf16), NN) * entry_wide
        parts = []
        for side in range(2):
            head = 2 * pair + side
            gap = running[:, head : head + 1] - running_t[head : head + 1, :]
            mixed = (scores * jnp.exp(gap + allowed)).astype(bf16)
            parts.append(mm(mixed, scaled_low, NN))
        intra = jnp.where(lane < LANES // 2, parts[0], parts[1])
        ssm_ref[:, lo:hi] = carried_out + intra + skip_ref[:, lo:hi] * head_in
        added = mm(in_map, (scaled * leave_wide).astype(bf16), TN)
        state[:, lo:hi] = held * entry_wide[rows - 1 :, :] + added


def full(shape):
    return pl.BlockSpec(shape, lambda *_: (0,) * len(shape))


def mixer_forward(
    lengths, normed, weight, conv_inner, bias_inner, conv_shared, bias_shared,
    step_bias, rate, skip, spread, span,
):
    rows, model = normed.shape
    channels = conv_inner.shape[1]
    width = conv_shared.shape[1]
    blocks = rows // span
    by_row = lambda cols: pl.BlockSpec((span, cols), lambda i: (i, 0))
    shape = lambda cols: jax.ShapeDtypeStruct((rows, cols), f32)
    states = width // 2
    return pl.pallas_call(
        forward_kernel,
        grid=(blocks,),
        in_specs=[
            pl.BlockSpec(memory_space=pltpu.SMEM),
            by_row(model),
            full(weight.shape),
            full(conv_inner.shape),
            full(bias_inner.shape),
            full(conv_shared.shape),
            full(bias_shared.shape),
            full(step_bias.shape),
            full(rate.shape),
            full(skip.shape),
            full(spread.shape),
        ],
        out_specs=[
            by_row(channels), by_row(channels), by_row(channels), by_row(width), by_row(width),
            by_row(LANES), pl.BlockSpec((1, states, channels), lambda i: (i, 0, 0)),
        ],
        out_shape=[
            shape(channels), shape(channels), shape(channels), shape(width), shape(width),
            shape(LANES), jax.ShapeDtypeStruct((blocks, states, channels), f32),
        ],
        scratch_shapes=[
            pltpu.VMEM((TAIL + span, channels), f32),
            pltpu.VMEM((TAIL + span, width), f32),
            pltpu.VMEM((states, channels), f32),
        ],
        compiler_params=pltpu.CompilerParams(
            dimension_semantics=("arbitrary",), vmem_limit_bytes=LIMIT
        ),
        name="mixer_forward",
    )(
        lengths, normed, weight, conv_inner, bias_inner, conv_shared, bias_shared,
        step_bias, rate, skip, spread,
    )


def backward_kernel(
    first_block, total_rows, lengths_ref, upstream_ref, ssm_ref, inner_ref, pre_inner_ref, shared_ref, pre_shared_ref,
    step_ref, entering_ref, conv_inner_ref, conv_shared_ref, rate_ref, skip_ref, spread_ref,
    sums_in_ref, inner_in_ref, shared_in_ref, adjoint_in_ref,
    grads_ref, sums_ref, inner_out_ref, shared_out_ref, adjoint, inner_head, shared_head,
):
    turn = pl.program_id(0)
    block = first_block + pl.num_programs(0) - 1 - turn
    rows, channels = upstream_ref.shape
    width = conv_shared_ref.shape[1]
    base = block * rows
    ends = sequence_ends(lengths_ref)

    @pl.when(turn == 0)
    def _():
        inner_head[rows : rows + TAIL, :] = inner_in_ref[...]
        shared_head[rows : rows + TAIL, :] = shared_in_ref[...]
        adjoint[...] = adjoint_in_ref[...]
        sums_ref[...] = sums_in_ref[...]

    @pl.when(turn > 0)
    def _():
        inner_head[rows : rows + TAIL, :] = inner_head[0:TAIL, :]
        shared_head[rows : rows + TAIL, :] = shared_head[0:TAIL, :]

    step_raw = step_ref[...]
    rate = rate_ref[...]
    step, running, entry, leave, lower, segment, row, col = step_parts(step_raw, rate, ends, base)
    position = base + lax.broadcasted_iota(jnp.int32, (rows, 1), 0)
    keeps = [
        ((segment_at(ends, position + k) == segment) & (position + k < total_rows)).astype(f32)
        for k in range(1, TAPS)
    ]
    pre_shared = pre_shared_ref[...]
    shared_gate = sigmoid(pre_shared)
    shared = pre_shared * shared_gate
    half = width // 2
    in_map = shared[:, :half].astype(bf16)
    out_map = shared[:, half:].astype(bf16)
    scores_t = mm(in_map, out_map, NT)
    allowed_t = jnp.where((col >= row) & same_rows(ends, base, rows), 0.0, MASKED)
    running_t = jnp.transpose(running)
    step2, entry2, leave2 = halves(step, 1), halves(entry, 1), halves(leave, 1)
    lane = lax.broadcasted_iota(jnp.int32, (rows, LANES), 1)
    first_half = lane < LANES // 2
    grad_scores_t = jnp.zeros((rows, rows), f32)
    grad_in = jnp.zeros((rows, half), f32)
    grad_out = jnp.zeros((rows, half), f32)
    by_head = jnp.zeros((rows, LANES), f32)
    step_terms = jnp.zeros((rows, LANES), f32)
    leaving = jnp.zeros((TAIL, LANES), f32)
    for pair in range(channels // LANES):
        lo, hi = pair * LANES, (pair + 1) * LANES
        spread = spread_ref[:, lo:hi]
        step_wide = mm(step2, spread, NN)
        entry_wide = mm(entry2, spread, NN)
        leave_wide = mm(leave2, spread, NN)
        pre = pre_inner_ref[:, lo:hi]
        gate = sigmoid(pre)
        head_in = pre * gate
        skip = skip_ref[:, lo:hi]
        upstream = upstream_ref[:, lo:hi]
        upstream_low = upstream.astype(bf16)
        upstream_back = upstream_low.astype(f32)
        scaled = head_in * step_wide
        scaled_low = scaled.astype(bf16)
        scaled_back = scaled_low.astype(f32)
        held = entering_ref[0, :, lo:hi]
        held_low = held.astype(bf16)
        ahead = adjoint[:, lo:hi]
        ahead_low = ahead.astype(bf16)
        entry_up = (upstream_back * entry_wide).astype(bf16)
        grad_out = grad_out + mm(entry_up, held_low, NT)
        grad_in = grad_in + mm((scaled * leave_wide).astype(bf16), ahead_low, NT)
        grad_scaled = mm(in_map, ahead_low, NN) * leave_wide
        through = entry_wide[rows - 1 :, :]
        tail_terms = jnp.sum(scaled_back * grad_scaled, axis=0, keepdims=True) + through * jnp.sum(
            ahead * held, axis=0, keepdims=True
        )
        adjoint[:, lo:hi] = ahead * through + mm(out_map, entry_up, TN)
        parts = []
        for side in range(2):
            head = 2 * pair + side
            gap = running_t[head : head + 1, :] - running[:, head : head + 1]
            decay = jnp.exp(gap + allowed_t)
            mixed = (scores_t * decay).astype(bf16)
            parts.append(mm(mixed, upstream_low, NN))
            mine = first_half if side == 0 else jnp.logical_not(first_half)
            chosen = jnp.where(mine, scaled_back, 0.0).astype(bf16)
            grad_scores_t = grad_scores_t + mm(chosen, upstream_low, NT) * decay
        grad_scaled = grad_scaled + jnp.where(first_half, parts[0], parts[1])
        spread_one = spread[:LANES, :]
        spread_both = jnp.concatenate([spread_one, spread_one], axis=1)
        balance = upstream_back * (ssm_ref[:, lo:hi] - skip * head_in) - scaled_back * grad_scaled
        by_head = by_head + mm(halves(balance, 1), spread_both, NT)
        step_terms = step_terms + mm(halves(head_in * grad_scaled, 1), spread_both, NT)
        skip_terms = jnp.sum(upstream * head_in, axis=0, keepdims=True)
        edge = jnp.concatenate([tail_terms, skip_terms, jnp.zeros((TAIL - 2, LANES), f32)], axis=0)
        leaving = leaving + mm(halves(edge, 1), spread_both, NT)
        grad_pre = (grad_scaled * step_wide + skip * upstream) * (gate * (1.0 + pre * (1.0 - gate)))
        inner_head[0:rows, lo:hi] = grad_pre
        inner_proj = inner_ref[:, lo:hi]
        grad_proj = conv_inner_ref[TAPS - 1 : TAPS, lo:hi] * grad_pre
        sums = [None] * TAPS
        sums[TAPS - 1] = jnp.sum(grad_pre * inner_proj, axis=0, keepdims=True)
        for k in range(1, TAPS):
            moved = inner_head[k : k + rows, lo:hi] * keeps[k - 1]
            grad_proj = grad_proj + conv_inner_ref[TAPS - 1 - k : TAPS - k, lo:hi] * moved
            sums[TAPS - 1 - k] = jnp.sum(moved * inner_proj, axis=0, keepdims=True)
        grads_ref[:, lo:hi] = grad_proj.astype(bf16)
        sums.append(jnp.sum(grad_pre, axis=0, keepdims=True))
        sums.append(jnp.zeros((TAIL - len(sums), LANES), f32))
        sums_ref[:, lo:hi] += jnp.concatenate(sums, axis=0)
    grad_scores_low = grad_scores_t.astype(bf16)
    grad_out = grad_out + mm(grad_scores_low, in_map, TN)
    grad_in = grad_in + mm(grad_scores_low, out_map, NN)
    grad_shared = jnp.concatenate([grad_in, grad_out], axis=1)
    grad_pre = grad_shared * (shared_gate * (1.0 + pre_shared * (1.0 - shared_gate)))
    shared_head[0:rows, :] = grad_pre
    shared_proj = shared_ref[...]
    grad_proj = conv_shared_ref[TAPS - 1 : TAPS, :] * grad_pre
    sums = [None] * TAPS
    sums[TAPS - 1] = jnp.sum(grad_pre * shared_proj, axis=0, keepdims=True)
    for k in range(1, TAPS):
        moved = shared_head[k : k + rows, :] * keeps[k - 1]
        grad_proj = grad_proj + conv_shared_ref[TAPS - 1 - k : TAPS - k, :] * moved
        sums[TAPS - 1 - k] = jnp.sum(moved * shared_proj, axis=0, keepdims=True)
    sums.append(jnp.sum(grad_pre, axis=0, keepdims=True))
    sums.append(jnp.zeros((TAIL - len(sums), width), f32))
    sums_ref[:, channels : channels + width] += jnp.concatenate(sums, axis=0)
    split = mm(lower, halves(by_head, 1), TN)
    grad_log = split[:, :LANES] + split[:, LANES:] + leaving[0:1, :]
    grad_step = (step_terms + rate * grad_log) * sigmoid(step_raw)
    grads_ref[:, channels : channels + width] = grad_proj.astype(bf16)
    grads_ref[:, channels + width :] = grad_step.astype(bf16)
    sums_ref[:, channels + width :] += jnp.concatenate(
        [
            jnp.sum(grad_step, axis=0, keepdims=True),
            rate * jnp.sum(step * grad_log, axis=0, keepdims=True),
            leaving[1:2, :],
            jnp.zeros((TAIL - 3, LANES), f32),
        ],
        axis=0,
    )

    @pl.when(turn == pl.num_programs(0) - 1)
    def _():
        inner_out_ref[...] = inner_head[0:TAIL, :]
        shared_out_ref[...] = shared_head[0:TAIL, :]


def mixer_backward(
    lengths, upstream, saved, conv_inner, conv_shared, rate, skip, spread, carry, blocks, span
):
    ssm, inner, pre_inner, shared, pre_shared, step_raw, entering = saved
    rows, channels = upstream.shape
    width = conv_shared.shape[1]
    states = width // 2
    begin, end = blocks
    known = channels + width + LANES
    by_row = lambda cols: pl.BlockSpec((span, cols), lambda i: (end - 1 - i, 0))
    small = ((TAIL, known), (TAIL, channels), (TAIL, width), (states, channels))
    results = pl.pallas_call(
        partial(backward_kernel, begin, rows),
        grid=(end - begin,),
        in_specs=[
            pl.BlockSpec(memory_space=pltpu.SMEM),
            by_row(channels), by_row(channels), by_row(channels), by_row(channels),
            by_row(width), by_row(width), by_row(LANES),
            pl.BlockSpec((1, states, channels), lambda i: (end - 1 - i, 0, 0)),
            full(conv_inner.shape),
            full(conv_shared.shape),
            full(rate.shape),
            full(skip.shape),
            full(spread.shape),
            *[full(shape) for shape in small],
        ],
        out_specs=[
            pl.BlockSpec((span, known), lambda i: (end - begin - 1 - i, 0)),
            *[full(shape) for shape in small],
        ],
        out_shape=[
            jax.ShapeDtypeStruct(((end - begin) * span, known), bf16),
            *[jax.ShapeDtypeStruct(shape, f32) for shape in small],
        ],
        scratch_shapes=[
            pltpu.VMEM((TAIL + span, channels), f32),
            pltpu.VMEM((TAIL + span, width), f32),
        ],
        compiler_params=pltpu.CompilerParams(
            dimension_semantics=("arbitrary",), vmem_limit_bytes=LIMIT
        ),
        name="mixer_backward",
    )(
        lengths, upstream, ssm, inner, pre_inner, shared, pre_shared, step_raw, entering,
        conv_inner, conv_shared, rate, skip, spread, *carry,
    )
    return results[0], tuple(results[1:])


def product_kernel(normed_ref, *refs):
    grads, out_ref = refs[:-1], refs[-1]
    total, at = 0.0, 0
    for ref in grads:
        rows = ref.shape[0]
        total = total + mm(normed_ref[at : at + rows, :], ref[...], TN)
        at += rows
    out_ref[...] = total.astype(bf16)


def weight_products(normed, grads):
    known = grads[0].shape[1]
    return pl.pallas_call(
        product_kernel,
        out_shape=jax.ShapeDtypeStruct((normed.shape[1], known), bf16),
        compiler_params=pltpu.CompilerParams(vmem_limit_bytes=LIMIT),
        name="weight_products",
    )(normed, *grads)


def gate_kernel(normed_ref, gate_w_ref, upstream_ref, out_w_ref, gain_ref, ssm_ref,
                gate_ref, grad_ref, sums_ref):
    rows = normed_ref.shape[0]
    gate = mm(normed_ref[...], gate_w_ref[...], NN)
    grad = mm(upstream_ref[...], out_w_ref[...], NN)
    gate_ref[...] = gate
    grad_ref[...] = grad
    gated = ssm_ref[...] * (gate * sigmoid(gate))
    square = jnp.sum(gated * gated, axis=1, keepdims=True)
    cross = jnp.sum(grad * gain_ref[...] * gated, axis=1, keepdims=True)
    lane = lax.broadcasted_iota(jnp.int32, (rows, LANES), 1)
    both = jnp.where(lane == 0, square, jnp.where(lane == 1, cross, 0.0))
    sums_ref[...] = jnp.transpose(both)[0:TAIL, :]


def gate_forward(normed, upstream, weight, gain, ssm, span):
    rows, model = normed.shape
    channels = ssm.shape[1]
    by_row = lambda cols: pl.BlockSpec((span, cols), lambda i: (i, 0))
    return pl.pallas_call(
        gate_kernel,
        grid=(rows // span,),
        in_specs=[
            by_row(model), pl.BlockSpec((model, channels), lambda i: (0, 0)), by_row(model),
            pl.BlockSpec((model, channels), lambda i: (0, 1)), full(gain.shape), by_row(channels),
        ],
        out_specs=[by_row(channels), by_row(channels), pl.BlockSpec((TAIL, span), lambda i: (0, i))],
        out_shape=[
            jax.ShapeDtypeStruct((rows, channels), f32),
            jax.ShapeDtypeStruct((rows, channels), f32),
            jax.ShapeDtypeStruct((TAIL, rows), f32),
        ],
        compiler_params=pltpu.CompilerParams(
            dimension_semantics=("arbitrary",), vmem_limit_bytes=LIMIT
        ),
        name="gate_forward",
    )(normed, weight, upstream, weight, gain, ssm)


def norm_kernel(full_inner, sums_ref, gate_ref, grad_ref, ssm_ref, gain_ref, normed_ref,
                upstream_ref, out_w_ref, grad_gate_ref, grad_ssm_ref, gain_sum_ref, branch_ref,
                products_ref, scaled, totals):
    rows, channels = gate_ref.shape

    @pl.when(pl.program_id(0) == 0)
    def _():
        gain_sum_ref[...] = jnp.zeros_like(gain_sum_ref)
        totals[...] = jnp.zeros_like(totals)

    padded = jnp.concatenate([sums_ref[...], jnp.zeros((LANES - TAIL, rows), f32)], axis=0)
    sums = jnp.transpose(padded)
    scale = lax.rsqrt(sums[:, 0:1] / full_inner + EPSILON)
    pull = scale * scale * scale * (sums[:, 1:2] / full_inner)
    for lo in range(0, channels, LANES):
        hi = lo + LANES
        gain = gain_ref[:, lo:hi]
        gate, grad, ssm = gate_ref[:, lo:hi], grad_ref[:, lo:hi], ssm_ref[:, lo:hi]
        sig = sigmoid(gate)
        silu = gate * sig
        gated = ssm * silu
        normal = gated * scale
        scaled[:, lo:hi] = (normal * gain).astype(bf16)
        gain_sum_ref[:, lo:hi] += jnp.broadcast_to(
            jnp.sum(grad * normal, axis=0, keepdims=True), (TAIL, LANES)
        )
        grad_gated = scale * (grad * gain) - gated * pull
        grad_ssm_ref[:, lo:hi] = grad_gated * silu
        grad_gate_ref[:, lo:hi] = (grad_gated * ssm * (sig * (1.0 + gate * (1.0 - sig)))).astype(bf16)
    scaled_out = scaled[...]
    branch_ref[...] = mm(scaled_out, out_w_ref[...], NT).astype(bf16)
    totals[:, :channels] += mm(normed_ref[...], grad_gate_ref[...], TN)
    totals[:, channels:] += mm(upstream_ref[...], scaled_out, TN)

    @pl.when(pl.program_id(0) == pl.num_programs(0) - 1)
    def _():
        products_ref[...] = totals[...].astype(bf16)


def gate_norm(sums, gate, grad, ssm, gain, normed, upstream, weight, full_inner, span):
    rows, channels = gate.shape
    model = normed.shape[1]
    by_row = lambda cols: pl.BlockSpec((span, cols), lambda i: (i, 0))
    return pl.pallas_call(
        partial(norm_kernel, float(full_inner)),
        grid=(rows // span,),
        in_specs=[
            pl.BlockSpec((TAIL, span), lambda i: (0, i)), by_row(channels), by_row(channels),
            by_row(channels), full(gain.shape), by_row(model), by_row(model),
            pl.BlockSpec((model, channels), lambda i: (0, 1)),
        ],
        out_specs=[
            by_row(channels), by_row(channels), full((TAIL, channels)), by_row(model),
            full((model, 2 * channels)),
        ],
        out_shape=[
            jax.ShapeDtypeStruct((rows, channels), bf16),
            jax.ShapeDtypeStruct((rows, channels), f32),
            jax.ShapeDtypeStruct((TAIL, channels), f32),
            jax.ShapeDtypeStruct((rows, model), bf16),
            jax.ShapeDtypeStruct((model, 2 * channels), bf16),
        ],
        scratch_shapes=[
            pltpu.VMEM((span, channels), bf16),
            pltpu.VMEM((model, 2 * channels), f32),
        ],
        compiler_params=pltpu.CompilerParams(
            dimension_semantics=("arbitrary",), vmem_limit_bytes=LIMIT
        ),
        name="gate_norm",
    )(sums, gate, grad, ssm, gain, normed, upstream, weight)


def lanes_of(vector):
    return jnp.pad(vector, (0, LANES - vector.shape[0]))[None, :]


def spread_map(heads, channels):
    size = channels // heads
    row = lax.broadcasted_iota(jnp.int32, (2 * LANES, channels), 0) % LANES
    col = lax.broadcasted_iota(jnp.int32, (2 * LANES, channels), 1) // size
    return (row == col).astype(bf16)


def input_kernel(grad_gate_ref, grads_ref, gate_w_ref, weight_ref, normed_ref, gain_ref, sums_ref,
                 before_ref, terms_ref, packed_ref):
    known = sums_ref.shape[1]
    terms = mm(grad_gate_ref[...], gate_w_ref[...], NT)
    terms = terms + mm(grads_ref[...], weight_ref[...], NT)
    terms_ref[...] = terms.astype(bf16)

    @pl.when(pl.program_id(0) == 0)
    def _():
        packed_ref[:, :known] = sums_ref[...]
        packed_ref[:, known:] = before_ref[:, known:]

    total = jnp.sum(terms * normed_ref[...].astype(f32), axis=0, keepdims=True) / gain_ref[...]
    packed_ref[0:1, known:] += total


def input_terms(grad_gate, grads, weight_late, weight, normed, gain, sums, before, begin, span):
    model = normed.shape[1]
    channels = grad_gate.shape[1]
    rows, known = grads.shape
    by_row = lambda cols: pl.BlockSpec((span, cols), lambda i: (i + begin, 0))
    here = lambda cols: pl.BlockSpec((span, cols), lambda i: (i, 0))
    return pl.pallas_call(
        input_kernel,
        grid=(rows // span,),
        in_specs=[
            by_row(channels), here(known), pl.BlockSpec((model, channels), lambda i: (0, 0)),
            full(weight.shape), by_row(model), full(gain.shape), full(sums.shape),
            full(before.shape),
        ],
        out_specs=[here(model), full((TAIL, known + model))],
        out_shape=[
            jax.ShapeDtypeStruct((rows, model), bf16),
            jax.ShapeDtypeStruct((TAIL, known + model), f32),
        ],
        compiler_params=pltpu.CompilerParams(
            dimension_semantics=("arbitrary",), vmem_limit_bytes=LIMIT
        ),
        name="input_terms",
    )(grad_gate, grads, weight_late, weight, normed, gain, sums, before)


def dp_send(value, bit):
    size = lax.axis_size("dp")
    return lax.ppermute(value, "dp", [(i, i ^ bit) for i in range(size)])


def chip_bits():
    return [4 * k for k in range(1, lax.axis_size("dp") // 4)]


def choose(stacked, index, axis):
    return lax.dynamic_index_in_dim(stacked, index, axis, keepdims=False)


def interleave(mine, other, upper, axis):
    return jnp.stack([jnp.where(upper, other, mine), jnp.where(upper, mine, other)], axis=axis)


def gather_long(shard):
    me = lax.axis_index("dp")
    rows, cols = shard.shape
    pieces = [shard] + [dp_send(shard, bit) for bit in chip_bits()]
    stacked = jnp.zeros((len(pieces), rows, cols), shard.dtype)
    for k, piece in enumerate(pieces):
        stacked = lax.dynamic_update_index_in_dim(stacked, piece, (me // 4) ^ k, 0)
    return stacked


def gather_x(stacked):
    return interleave(stacked, dp_send(stacked, 2), (lax.axis_index("dp") // 2) % 2 == 1, 1)


def gather_cores(chips):
    whole = interleave(chips, dp_send(chips, 1), lax.axis_index("dp") % 2 == 1, 2)
    return whole.reshape(-1, chips.shape[-1])


def fold(parts, bit, axis):
    mine = (lax.axis_index("dp") // bit) % 2
    got = dp_send(choose(parts, 1 - mine, axis), bit)
    return choose(parts, mine, axis).astype(f32) + got.astype(f32)


def fold_chips(parts):
    place = lax.axis_index("dp") // 4
    sends = parts.astype(bf16)
    total = choose(parts, place, 0)
    got = [dp_send(choose(sends, place ^ (bit // 4), 0), bit) for bit in chip_bits()]
    for piece in got:
        total = total + piece.astype(f32)
    return total


def tensor_swap(value):
    return lax.ppermute(value, "tensor", [(0, 1), (1, 0)])


def sum_dp(value):
    value = value + dp_send(value, 1)
    value = value + dp_send(value, 2)
    bits = chip_bits()
    pieces = [value] + [dp_send(value, bit) for bit in bits]
    while len(pieces) > 1:
        pieces = [a + b for a, b in zip(pieces[0::2], pieces[1::2])]
    return pieces[0]


def gather_other(own, size):
    if size != 2:
        return lax.all_gather(own, "tensor", axis=0, tiled=True)
    return tensor_swap(own)


def join_halves(own, other, size):
    if size != 2:
        return other
    upper = lax.axis_index("tensor") == 1
    return jnp.concatenate([jnp.where(upper, other, own), jnp.where(upper, own, other)], axis=0)


def join_pieces(own, top, bottom, size):
    if size != 2:
        top = top.reshape(size, -1, own.shape[1])
        bottom = bottom.reshape(size, -1, own.shape[1])
        return jnp.concatenate([top, bottom], axis=1).reshape(-1, own.shape[1])
    return join_halves(own, jnp.concatenate([top, bottom], axis=0), size)


def pick_half(lower, upper, size):
    if size != 2:
        return lower
    return jnp.where(lax.axis_index("tensor") == 0, lower, upper)


def sum_quarters(quarters, other0, other1, size):
    if size != 2:
        whole = jnp.concatenate(quarters, axis=0)
        return lax.psum_scatter(whole, "tensor", scatter_dimension=0, tiled=True).astype(f32)
    first = lax.axis_index("tensor") == 0
    top = jnp.where(first, quarters[0], quarters[2]).astype(f32) + other0.astype(f32)
    bottom = jnp.where(first, quarters[1], quarters[3]).astype(f32) + other1.astype(f32)
    return jnp.concatenate([top, bottom], axis=0)


def tensor_sum(value, size):
    if size != 2:
        return lax.psum(value, "tensor")
    return value + tensor_swap(value)


def send_half(value, size):
    if size != 2:
        total = lax.psum_scatter(value, "tensor", scatter_dimension=0, tiled=True)
        return total, jnp.zeros_like(total)
    me = lax.axis_index("tensor")
    halved = value.reshape(2, -1, value.shape[1])
    return choose(halved, me, 0), tensor_swap(choose(halved, 1 - me, 0))


def shards(
    tokens, lengths, norm_gain, zx_weight, bc_weight, dt_weight, conv_inner, bias_inner,
    conv_shared, bias_shared, step_bias, log_rate, skip_gain, gate_gain, out_weight, cotangent,
):
    size = lax.axis_size("tensor")
    channels = zx_weight.shape[2]
    heads = step_bias.shape[0]
    width = bc_weight.shape[1]
    inputs = tokens.astype(f32)
    norm_scale = lax.rsqrt(jnp.mean(inputs * inputs, axis=1, keepdims=True) + EPSILON)
    normed_rows = (inputs * norm_scale * norm_gain[None, :]).astype(bf16)
    step_weight = jnp.pad(dt_weight, ((0, 0), (0, LANES - heads)))
    early = jnp.concatenate([zx_weight[:, 1, :], bc_weight, step_weight], axis=1)
    late = jnp.concatenate([zx_weight[:, 0, :], out_weight], axis=1)
    weight_late = lax.all_gather(late, "dp", axis=0, tiled=True)
    half = normed_rows.shape[0] // 2
    stacked, upper_rows = lax.optimization_barrier(
        (gather_long(early), gather_other(normed_rows[:half], size))
    )
    chips, lower_rows = lax.optimization_barrier(
        (gather_x(stacked), gather_other(normed_rows[half:], size))
    )
    normed = join_pieces(normed_rows, upper_rows, lower_rows, size)
    weight = gather_cores(chips)
    spread = spread_map(heads, channels)
    rate = lanes_of(-jnp.exp(log_rate))
    skip = jnp.repeat(skip_gain, channels // heads)[None, :]
    saved = mixer_forward(
        lengths, normed, weight, conv_inner, bias_inner[None, :], conv_shared,
        bias_shared[None, :], lanes_of(step_bias), rate, skip, spread, SPAN,
    )
    gain = gate_gain[None, :]
    other, ssm, weight_late = lax.optimization_barrier(
        (gather_other(cotangent, size), saved[0], weight_late)
    )
    upstream = join_halves(cotangent, other, size)
    gate, grad, sums = gate_forward(normed, upstream, weight_late, gain, ssm, SPAN)
    sums = tensor_sum(sums, size)
    grad_gate, grad_ssm, gain_sum, branch, first = gate_norm(
        sums, gate, grad, ssm, gain, normed, upstream, weight_late, channels * size, SPAN
    )
    branch_own, branch_other = send_half(branch, size)
    count = len(chip_bits()) + 1
    first = first.reshape(count, 2, 2, -1, first.shape[1])
    blocks = grad_ssm.shape[0] // SPAN
    quarter = blocks // 4
    known = channels + width + LANES
    carry = (
        jnp.pad(gain_sum[:1], ((TAIL - 1, 0), (0, known - channels))),
        jnp.zeros((TAIL, channels), f32),
        jnp.zeros((TAIL, width), f32),
        jnp.zeros((width // 2, channels), f32),
    )
    packed = jnp.zeros((TAIL, known + normed.shape[1]), f32)

    def part(index, carry, packed):
        begin = index * quarter
        grads, carry = mixer_backward(
            lengths, grad_ssm, saved, conv_inner, conv_shared, rate, skip, spread, carry,
            (begin, begin + quarter), SPAN,
        )
        return grads, carry

    def terms_of(index, grads, sums, packed):
        return input_terms(
            grad_gate, grads, weight_late, weight, normed, norm_gain[None, :], sums, packed,
            index * quarter, SPAN,
        )

    grads3, carry = part(3, carry, packed)
    first = fold(first, 1, 2).astype(bf16)
    carry, first = lax.optimization_barrier((carry, first))
    first_gate, first_out = first[..., :channels], first[..., channels:]
    grads2, carry = part(2, carry, packed)
    terms3, packed = terms_of(3, grads3, carry[0], packed)
    terms2, packed = terms_of(2, grads2, carry[0], packed)
    carry, packed = lax.optimization_barrier((carry, packed))
    grads1, carry = part(1, carry, packed)
    terms1, packed = terms_of(1, grads1, carry[0], packed)
    first_gate = fold(first_gate, 2, 1)
    first_out = fold_chips(first_out).astype(bf16)
    send1 = pick_half(terms3, terms1, size)
    carry, first_gate, first_out, send1, branch_other = lax.optimization_barrier(
        (carry, first_gate, first_out, send1, branch_other)
    )
    other1 = gather_other(send1, size)
    part_gate = fold_chips(first_gate)
    part_out = fold(first_out, 2, 0)
    block_out = (inputs + (branch_own.astype(f32) + branch_other.astype(f32))).astype(bf16)
    grads0, carry = part(0, carry, packed)
    products = weight_products(normed, (grads0, grads1, grads2, grads3))
    parts = fold(products.reshape(count, 2, 2, -1, known), 1, 2).astype(bf16)
    terms0, packed = terms_of(0, grads0, carry[0], packed)
    parts, packed, terms0 = lax.optimization_barrier((parts, packed, terms0))
    other0 = gather_other(pick_half(terms2, terms0, size), size)
    cut = (known // (2 * LANES)) * LANES
    parts_a = fold_chips(fold(parts[..., :cut], 2, 1))
    parts_b = fold(fold_chips(parts[..., cut:]).astype(bf16), 2, 0)
    part_small = jnp.concatenate([parts_a, parts_b], axis=1)
    packed = sum_dp(packed)
    grad_normed = sum_quarters((terms0, terms1, terms2, terms3), other0, other1, size)
    packed_all = tensor_sum(packed, size)
    part_inner = part_small[:, :channels]
    part_step = part_small[:, channels + width : channels + width + heads]
    part_shared = tensor_sum(part_small[:, channels : channels + width], size)
    scaled_grad = grad_normed * norm_gain[None, :]
    grad_inputs = norm_scale * scaled_grad - inputs * norm_scale**3 * jnp.mean(
        scaled_grad * inputs, axis=1, keepdims=True
    )
    grad_tokens = (cotangent.astype(f32) + grad_inputs).astype(bf16)
    part_in = jnp.stack([part_gate, part_inner], axis=1)
    at_step = channels + width
    at_norm = at_step + LANES
    return (
        block_out,
        grad_tokens,
        packed_all[0, at_norm:],
        part_in,
        part_shared,
        part_step,
        packed[:TAPS, :channels],
        packed[TAPS, :channels],
        packed_all[:TAPS, channels:at_step],
        packed_all[TAPS, channels:at_step],
        packed[0, at_step : at_step + heads],
        packed[1, at_step : at_step + heads],
        packed[2, at_step : at_step + heads],
        packed[TAIL - 1, :channels],
        part_out,
    )


def solution(mesh):
    return jax.shard_map(
        shards,
        mesh=mesh,
        in_specs=(
            P(("dp", "tensor"), None),
            P("dp", None),
            P(),
            P("dp", None, "tensor"),
            P("dp", None),
            P("dp", "tensor"),
            P(None, "tensor"),
            P("tensor"),
            P(),
            P(),
            P("tensor"),
            P("tensor"),
            P("tensor"),
            P("tensor"),
            P("dp", "tensor"),
            P(("dp", "tensor"), None),
        ),
        out_specs=(
            P(("dp", "tensor"), None),
            P(("dp", "tensor"), None),
            P(),
            P("dp", None, "tensor"),
            P("dp", None),
            P("dp", "tensor"),
            P(None, "tensor"),
            P("tensor"),
            P(),
            P(),
            P("tensor"),
            P("tensor"),
            P("tensor"),
            P("tensor"),
            P("dp", "tensor"),
        ),
        check_vma=False,
    )
```

profile of v0, /device:TPU:0, one launch (start us, length us, event | category | flops | bytes accessed | tf_op | source)
XLA Modules:
  0.0 327.5 jit_solution(13892481820495681923)
XLA Ops:
  11.4 3.0 collective-permute-start
  14.4 2.6 collective-permute-start.1
  23.2 11.2 %collective-permute-done.1 = bf16[64,1408]{1,0:T(8,128)(2,1)} collective-permute-done((bf16[64,1408]{1,0:T(8,128)(2,1)}, bf16[64,1408]{1,0:T(8,128)(2,1)}, u32[]{:S(2)}, u32[]{:S(2)}) %collective-permute-start.1) | collective-permute-done | bytes 180256 | tf_op jit(solution)/shard_map/ppermute | solution.py:611
  40.4 10.3 %collective-permute-done.4 = bf16[4,64,1408]{2,1,0:T(8,128)(2,1)S(1)} collective-permute-done((bf16[4,64,1408]{2,1,0:T(8,128)(2,1)S(1)}, bf16[4,64,1408]{2,1,0:T(8,128)(2,1)S(1)}, u32[]{:S(2)}, u32[]{:S(2)}) %collective-permute-start.4) | collective-permute-done | bytes 720928 | tf_op jit(solution)/shard_map/ppermute | solution.py:611
  65.6 20.7 %mixer_forward.1 = (f32[1024,1024]{1,0:T(8,128)}, f32[1024,1024]{1,0:T(8,128)}, f32[1024,1024]{1,0:T(8,128)}, f32[1024,256]{1,0:T(8,128)}, f32[1024,256]{1,0:T(8...) custom-call(s32[1,4]{1,0:T(1,128)} %lengths_ref.9, bf16[1024,1024]{1,0:T(8,128)(2,1)} %pad_maximum_fusion.1.normed_ref, ...), custom_call_target="tpu_custom_call" | custom-call | tf_op jit(solution)/shard_map/mixer_forward/pallas_call | solution.py:185
  89.2 10.6 %gate_forward.1 = (f32[1024,1024]{1,0:T(8,128)}, f32[1024,1024]{1,0:T(8,128)}, f32[8,1024]{1,0:T(8,128)}) custom-call(bf16[1024,1024]{1,0:T(8,128)(2,1)} %pad_maximum_fusion.1.normed_ref, bf16[1024,2048]{1,0:T(8,128)(2,1)} %all-gather.2.cloned.1.call-done.gate_w_ref.out_w_ref, bf16[1024,1024]{1,0:T(8,128)(2,1)} %pad_maximum_fusion.2.upstream_ref, ...), custom_call_target="tpu_custom_call" | custom-call | tf_op jit(solution)/shard_map/gate_forward/pallas_call | solution.py:463
  101.3 2.6 collective-permute-done.8
  105.3 18.8 %gate_norm.1 = (bf16[1024,1024]{1,0:T(8,128)(2,1)}, f32[1024,1024]{1,0:T(8,128)}, f32[8,1024]{1,0:T(8,128)}, bf16[1024,1024]{1,0:T(8,128)(2,1)}, bf16[1024,2048]{1,0:T(8,128)(2,1)}) custom-call(f32[8,1024]{1,0:T(8,128)} %add.228.sums_ref, f32[1024,1024]{1,0:T(8,128)} %get-tuple-element.92.gate_ref, f32[1024,1024]{1,0:T(8,128)} %get-tuple-element.93.grad_ref, ...), custom_call_target="tpu_custom_call" | custom-call | tf_op jit(solution)/shard_map/gate_norm/pallas_call | solution.py:526
  124.1 2.6 constant_dynamic-slice_fusion.1
  135.6 11.4 %mixer_backward.4 = (bf16[256,1408]{1,0:T(8,128)(2,1)}, f32[8,1408]{1,0:T(8,128)}, f32[8,1024]{1,0:T(8,128)}, f32[8,256]{1,0:T(8,128)}, f32[128,1024]{1,0:T(8,128)}) custom-call(s32[1,4]{1,0:T(1,128)} %lengths_ref.9, f32[1024,1024]{1,0:T(8,128)} %get-tuple-element.95.upstream_ref, f32[1024,1024]{1,0:T(8,128)} %get-tuple-element.90.ssm_ref, ...), custom_call_target="tpu_custom_call" | custom-call | tf_op jit(solution)/shard_map/mixer_backward/pallas_call | solution.py:386
  147.0 2.4 fusion
  151.9 11.6 %mixer_backward.5 = (bf16[256,1408]{1,0:T(8,128)(2,1)}, f32[8,1408]{1,0:T(8,128)}, f32[8,1024]{1,0:T(8,128)}, f32[8,256]{1,0:T(8,128)}, f32[128,1024]{1,0:T(8,128)}) custom-call(s32[1,4]{1,0:T(1,128)} %lengths_ref.9, f32[1024,1024]{1,0:T(8,128)} %get-tuple-element.95.upstream_ref, f32[1024,1024]{1,0:T(8,128)} %get-tuple-element.90.ssm_ref, ...), custom_call_target="tpu_custom_call" | custom-call | tf_op jit(solution)/shard_map/mixer_backward/pallas_call | solution.py:386
  164.1 5.3 %input_terms.4 = (bf16[256,1024]{1,0:T(8,128)(2,1)}, f32[8,2432]{1,0:T(8,128)}) custom-call(bf16[1024,1024]{1,0:T(8,128)(2,1)} %get-tuple-element.116.grad_gate_ref, bf16[256,1408]{1,0:T(8,128)(2,1)} %get-tuple-element.118.grads_ref.refs_3_, bf16[1024,2048]{1,0:T(8,128)(2,1)} %all-gather.2.cloned.1.call-done.gate_w_ref.out_w_ref, ...), custom_call_target="tpu_custom_call" | custom-call | tf_op jit(solution)/shard_map/input_terms/pallas_call | solution.py:589
  169.4 5.3 %input_terms.5 = (bf16[256,1024]{1,0:T(8,128)(2,1)}, f32[8,2432]{1,0:T(8,128)}) custom-call(bf16[1024,1024]{1,0:T(8,128)(2,1)} %get-tuple-element.116.grad_gate_ref, bf16[256,1408]{1,0:T(8,128)(2,1)} %get-tuple-element.117.grads_ref.refs_2_, bf16[1024,2048]{1,0:T(8,128)(2,1)} %all-gather.2.cloned.1.call-done.gate_w_ref.out_w_ref, ...), custom_call_target="tpu_custom_call" | custom-call | tf_op jit(solution)/shard_map/input_terms/pallas_call | solution.py:589
  174.7 16.6 %collective-permute-start.11 = (bf16[2,64,1024]{2,1,0:T(8,128)(2,1)}, bf16[2,64,1024]{2,1,0:T(8,128)(2,1)}, u32[]{:S(2)}, u32[]{:S(2)}) collective-permute-start(bf16[2,64,1024]{2,1,0:T(8,128)(2,1)} %get-tuple-element.197), channel_id=1, source_target_pairs={{0,8},{2,10},{4,12},{6,14},{8,0},{10,2},{12,4},{14,6},{16,24},{18,... | collective-permute-start | bytes 786440 | tf_op jit(solution)/shard_map/ppermute | solution.py:611
  191.3 2.7 collective-permute-start.12
  195.4 11.6 %mixer_backward.6 = (bf16[256,1408]{1,0:T(8,128)(2,1)}, f32[8,1408]{1,0:T(8,128)}, f32[8,1024]{1,0:T(8,128)}, f32[8,256]{1,0:T(8,128)}, f32[128,1024]{1,0:T(8,128)}) custom-call(s32[1,4]{1,0:T(1,128)} %lengths_ref.9, f32[1024,1024]{1,0:T(8,128)} %get-tuple-element.95.upstream_ref, f32[1024,1024]{1,0:T(8,128)} %get-tuple-element.90.ssm_ref, ...), custom_call_target="tpu_custom_call" | custom-call | tf_op jit(solution)/shard_map/mixer_backward/pallas_call | solution.py:386
  207.0 5.4 %input_terms.6 = (bf16[256,1024]{1,0:T(8,128)(2,1)}, f32[8,2432]{1,0:T(8,128)}) custom-call(bf16[1024,1024]{1,0:T(8,128)(2,1)} %get-tuple-element.116.grad_gate_ref, bf16[256,1408]{1,0:T(8,128)(2,1)} %get-tuple-element.131.grads_ref.refs_1_, bf16[1024,2048]{1,0:T(8,128)(2,1)} %all-gather.2.cloned.1.call-done.gate_w_ref.out_w_ref, ...), custom_call_target="tpu_custom_call" | custom-call | tf_op jit(solution)/shard_map/input_terms/pallas_call | solution.py:589
  215.8 11.7 %mixer_backward.7 = (bf16[256,1408]{1,0:T(8,128)(2,1)}, f32[8,1408]{1,0:T(8,128)}, f32[8,1024]{1,0:T(8,128)}, f32[8,256]{1,0:T(8,128)}, f32[128,1024]{1,0:T(8,128)}) custom-call(s32[1,4]{1,0:T(1,128)} %lengths_ref.9, f32[1024,1024]{1,0:T(8,128)} %get-tuple-element.95.upstream_ref, f32[1024,1024]{1,0:T(8,128)} %get-tuple-element.90.ssm_ref, ...), custom_call_target="tpu_custom_call" | custom-call | tf_op jit(solution)/shard_map/mixer_backward/pallas_call | solution.py:386
  227.6 7.5 %weight_products.1 = bf16[1024,1408]{1,0:T(8,128)(2,1)} custom-call(bf16[1024,1024]{1,0:T(8,128)(2,1)} %pad_maximum_fusion.1.normed_ref, bf16[256,1408]{1,0:T(8,128)(2,1)} %get-tuple-element.139.refs_0_.grads_ref, bf16[256,1408]{1,0:T(8,128)(2,1)} %get-tuple-element.131.grads_ref.refs_1_, bf16[256,1408]{1,0:T(8,128)(2,1)} %get-tuple-element.117.grads_ref.refs_2_, ...), custom_call_target="tpu_custom_call" | custom-call | tf_op jit(solution)/shard_map/weight_products/pallas_call | solution.py:436
  235.0 2.6 dynamic-slice_bitcast_fusion
  240.6 4.1 %collective-permute-start.24 = (bf16[64,1024]{1,0:T(8,128)(2,1)}, bf16[64,1024]{1,0:T(8,128)(2,1)S(1)}, u32[]{:S(2)}, u32[]{:S(2)}) collective-permute-start(bf16[64,1024]{1,0:T(8,128)(2,1)} %get-tuple-element.205), channel_id=1, source_target_pairs={{0,8},{2,10},{4,12},{6,14},{8,0},{10,2},{12,4},{14,6},{16,24},{18,... | collective-permute-start | bytes 393224 | tf_op jit(solution)/shard_map/ppermute | solution.py:611
  246.8 5.4 %input_terms.7 = (bf16[256,1024]{1,0:T(8,128)(2,1)}, f32[8,2432]{1,0:T(8,128)}) custom-call(bf16[1024,1024]{1,0:T(8,128)(2,1)} %get-tuple-element.116.grad_gate_ref, bf16[256,1408]{1,0:T(8,128)(2,1)} %get-tuple-element.139.refs_0_.grads_ref, bf16[1024,2048]{1,0:T(8,128)(2,1)} %all-gather.2.cloned.1.call-done.gate_w_ref.out_w_ref, ...), custom_call_target="tpu_custom_call" | custom-call | tf_op jit(solution)/shard_map/input_terms/pallas_call | solution.py:589
  254.4 5.0 %collective-permute-done.26 = bf16[64,1024]{1,0:T(8,128)(2,1)S(1)} collective-permute-done((bf16[64,1024]{1,0:T(8,128)(2,1)}, bf16[64,1024]{1,0:T(8,128)(2,1)S(1)}, u32[]{:S(2)}, u32[]{:S(2)}) %collective-permute-start.26) | collective-permute-done | bytes 131104 | tf_op jit(solution)/shard_map/ppermute | solution.py:611
  263.5 2.7 collective-permute-start.31
  266.2 2.4 collective-permute-start.33
  272.3 9.0 %collective-permute-done.19 = f32[8,2432]{1,0:T(8,128)S(1)} collective-permute-done((f32[8,2432]{1,0:T(8,128)S(1)}, f32[8,2432]{1,0:T(8,128)S(1)}, u32[]{:S(2)}, u32[]{:S(2)}) %collective-permute-start.19) | collective-permute-done | bytes 77856 | tf_op jit(solution)/shard_map/ppermute | solution.py:611
  284.9 2.4 collective-permute-start.22
  289.7 2.8 collective-permute-done.21
  304.8 2.6 collective-permute-start.30
  309.1 3.0 collective-permute-done.29
  316.7 3.5 %fusion.9 = (bf16[512,1024]{1,0:T(8,128)(2,1)}, bf16[512,1024]{1,0:T(8,128)(2,1)}) fusion(bf16[512,1024]{1,0:T(8,128)(2,1)S(1)} %copy-done, bf16[512,1024]{1,0:T(8,128)(2,1)S(1)} %copy-done.3, f32[256,1024]{1,0:T(8,128)S(1)} %convert_add_fusion.5, f32[256,1024]{1,0:T(8,128)S(1)} %convert_add_fusion.6, f32[512]{0:T(512)S(1)} %broadcast_multiply_fusion, ...), kind=kLoop, calls=%fused_computation.17 | loop fusion | flops 7864320 | bytes 8398852 | tf_op jit(solution)/shard_map/convert_element_type | solution.py:836
  (190 shorter events, 93.1 us)
Async XLA Ops:
  7.2 79.1 %all-gather.2.cloned.1.call-start = ((), (), s32[]{:S(2)}) async-start(), calls=%async_computation | async-start | bytes 4456448 | tf_op jit(solution)/shard_map/all_gather | solution.py:741
  11.4 10.8 %collective-permute-start = (bf16[64,1408]{1,0:T(8,128)(2,1)}, bf16[64,1408]{1,0:T(8,128)(2,1)}, u32[]{:S(2)}, u32[]{:S(2)}) collective-permute-start(bf16[64,1408]{1,0:T(8,128)(2,1)} %fusion.23), channel_id=1, source_target_pairs={{0,8},{2,10},{4,12},{6,14},{8,0},{10,2},{12,4},{14,6},{16,24},{18,... | collective-permute-start | bytes 540680 | tf_op jit(solution)/shard_map/ppermute | solution.py:611
  14.4 19.9 %collective-permute-start.1 = (bf16[64,1408]{1,0:T(8,128)(2,1)}, bf16[64,1408]{1,0:T(8,128)(2,1)}, u32[]{:S(2)}, u32[]{:S(2)}) collective-permute-start(bf16[64,1408]{1,0:T(8,128)(2,1)} %fusion.23), channel_id=1, source_target_pairs={{0,16},{2,18},{4,20},{6,22},{8,24},{10,26},{12,28},{14,30},{16,0},... | collective-permute-start | bytes 540680 | tf_op jit(solution)/shard_map/ppermute | solution.py:611
  17.0 18.3 %collective-permute-start.2 = (bf16[64,1408]{1,0:T(8,128)(2,1)}, bf16[64,1408]{1,0:T(8,128)(2,1)}, u32[]{:S(2)}, u32[]{:S(2)}) collective-permute-start(bf16[64,1408]{1,0:T(8,128)(2,1)} %fusion.23), channel_id=1, source_target_pairs={{0,24},{2,26},{4,28},{6,30},{8,16},{10,18},{12,20},{14,22},{16,8},... | collective-permute-start | bytes 540680 | tf_op jit(solution)/shard_map/ppermute | solution.py:611
  19.1 17.2 %collective-permute-start.3 = (bf16[256,1024]{1,0:T(8,128)(2,1)S(1)}, bf16[256,1024]{1,0:T(8,128)(2,1)}, u32[]{:S(2)}, u32[]{:S(2)}) collective-permute-start(bf16[256,1024]{1,0:T(8,128)(2,1)S(1)} %get-tuple-element.201), channel_id=1, source_target_pairs={{0,1},{1,0},{2,3},{3,2},{4,5},{5,4},{6,7},{7,6},{8,9},{9,8},{10,11... | collective-permute-start | bytes 1572872 | tf_op jit(solution)/shard_map/ppermute | solution.py:662
  36.3 14.4 %collective-permute-start.4 = (bf16[4,64,1408]{2,1,0:T(8,128)(2,1)S(1)}, bf16[4,64,1408]{2,1,0:T(8,128)(2,1)S(1)}, u32[]{:S(2)}, u32[]{:S(2)}) collective-permute-start(bf16[4,64,1408]{2,1,0:T(8,128)(2,1)S(1)} %bitcast_dynamic-update-slice_fusion), channel_id=1, source_target_pairs={{0,4},{2,6},{4,0},{6,2},{8,12},{10,14},{12,8},{14,10},{16,20},{18,... | collective-permute-start | bytes 2162696 | tf_op jit(solution)/shard_map/ppermute | solution.py:611
  37.8 15.2 %collective-permute-start.5 = (bf16[256,1024]{1,0:T(8,128)(2,1)}, bf16[256,1024]{1,0:T(8,128)(2,1)}, u32[]{:S(2)}, u32[]{:S(2)}) collective-permute-start(bf16[256,1024]{1,0:T(8,128)(2,1)} %get-tuple-element.200), channel_id=1, source_target_pairs={{0,1},{1,0},{2,3},{3,2},{4,5},{5,4},{6,7},{7,6},{8,9},{9,8},{10,11... | collective-permute-start | bytes 1572872 | tf_op jit(solution)/shard_map/ppermute | solution.py:662
  39.3 46.9 %collective-permute-start.6 = (bf16[512,1024]{1,0:T(8,128)(2,1)S(1)}, bf16[512,1024]{1,0:T(8,128)(2,1)}, u32[]{:S(2)}, u32[]{:S(2)}) collective-permute-start(bf16[512,1024]{1,0:T(8,128)(2,1)S(1)} %copy-done.2), channel_id=1, source_target_pairs={{0,1},{1,0},{2,3},{3,2},{4,5},{5,4},{6,7},{7,6},{8,9},{9,8},{10,11... | collective-permute-start | bytes 3145736 | tf_op jit(solution)/shard_map/ppermute | solution.py:662
  53.0 9.0 %collective-permute-start.7 = (bf16[4,2,64,1408]{3,2,1,0:T(8,128)(2,1)S(1)}, bf16[4,2,64,1408]{3,2,1,0:T(8,128)(2,1)}, u32[]{:S(2)}, u32[]{:S(2)}) collective-permute-start(bf16[4,2,64,1408]{3,2,1,0:T(8,128)(2,1)S(1)} %pad_maximum_fusion.3), channel_id=1, source_target_pairs={{0,2},{2,0},{4,6},{6,4},{8,10},{10,8},{12,14},{14,12},{16,18},{18,... | collective-permute-start | bytes 4325384 | tf_op jit(solution)/shard_map/ppermute | solution.py:611
  128.3 18.7 %collective-permute-start.9 = (bf16[4,2,64,2048]{3,2,0,1:T(8,128)(2,1)}, bf16[4,2,64,2048]{3,2,0,1:T(8,128)(2,1)}, u32[]{:S(2)}, u32[]{:S(2)}) collective-permute-start(bf16[4,2,64,2048]{3,2,0,1:T(8,128)(2,1)} %bitcast.134), channel_id=1, source_target_pairs={{0,2},{2,0},{4,6},{6,4},{8,10},{10,8},{12,14},{14,12},{16,18},{18,... | collective-permute-start | bytes 6291464 | tf_op jit(solution)/shard_map/ppermute | solution.py:611
  131.4 84.5 %collective-permute-start.14 = (bf16[512,1024]{1,0:T(8,128)(2,1)}, bf16[512,1024]{1,0:T(8,128)(2,1)}, u32[]{:S(2)}, u32[]{:S(2)}) collective-permute-start(bf16[512,1024]{1,0:T(8,128)(2,1)} %dynamic-slice_bitcast_fusion.1), channel_id=1, source_target_pairs={{0,1},{1,0},{2,3},{3,2},{4,5},{5,4},{6,7},{7,6},{8,9},{9,8},{10,11... | collective-permute-start | bytes 3145736 | tf_op jit(solution)/shard_map/ppermute | solution.py:662
  150.5 64.1 %collective-permute-start.10 = (bf16[4,64,1024]{2,1,0:T(8,128)(2,1)}, bf16[4,64,1024]{2,1,0:T(8,128)(2,1)}, u32[]{:S(2)}, u32[]{:S(2)}) collective-permute-start(bf16[4,64,1024]{2,1,0:T(8,128)(2,1)} %dynamic-slice_bitcast_fusion.2), channel_id=1, source_target_pairs={{0,4},{2,6},{4,0},{6,2},{8,12},{10,14},{12,8},{14,10},{16,20},{18,... | collective-permute-start | bytes 1572872 | tf_op jit(solution)/shard_map/ppermute | solution.py:611
  174.7 38.6 %collective-permute-start.11 = (bf16[2,64,1024]{2,1,0:T(8,128)(2,1)}, bf16[2,64,1024]{2,1,0:T(8,128)(2,1)}, u32[]{:S(2)}, u32[]{:S(2)}) collective-permute-start(bf16[2,64,1024]{2,1,0:T(8,128)(2,1)} %get-tuple-element.197), channel_id=1, source_target_pairs={{0,8},{2,10},{4,12},{6,14},{8,0},{10,2},{12,4},{14,6},{16,24},{18,... | collective-permute-start | bytes 786440 | tf_op jit(solution)/shard_map/ppermute | solution.py:611
  191.3 22.0 %collective-permute-start.12 = (bf16[2,64,1024]{2,1,0:T(8,128)(2,1)}, bf16[2,64,1024]{2,1,0:T(8,128)(2,1)}, u32[]{:S(2)}, u32[]{:S(2)}) collective-permute-start(bf16[2,64,1024]{2,1,0:T(8,128)(2,1)} %get-tuple-element.199), channel_id=1, source_target_pairs={{0,16},{2,18},{4,20},{6,22},{8,24},{10,26},{12,28},{14,30},{16,0},... | collective-permute-start | bytes 786440 | tf_op jit(solution)/shard_map/ppermute | solution.py:611
  194.0 19.3 %collective-permute-start.13 = (bf16[2,64,1024]{2,1,0:T(8,128)(2,1)S(1)}, bf16[2,64,1024]{2,1,0:T(8,128)(2,1)}, u32[]{:S(2)}, u32[]{:S(2)}) collective-permute-start(bf16[2,64,1024]{2,1,0:T(8,128)(2,1)S(1)} %get-tuple-element.198), channel_id=1, source_target_pairs={{0,24},{2,26},{4,28},{6,30},{8,16},{10,18},{12,20},{14,22},{16,8},... | collective-permute-start | bytes 786440 | tf_op jit(solution)/shard_map/ppermute | solution.py:611
  237.6 23.9 %collective-permute-start.15 = (bf16[4,2,64,1408]{3,2,1,0:T(8,128)(2,1)}, bf16[4,2,64,1408]{3,2,1,0:T(8,128)(2,1)}, u32[]{:S(2)}, u32[]{:S(2)}) collective-permute-start(bf16[4,2,64,1408]{3,2,1,0:T(8,128)(2,1)} %dynamic-slice_bitcast_fusion), channel_id=1, source_target_pairs={{0,2},{2,0},{4,6},{6,4},{8,10},{10,8},{12,14},{14,12},{16,18},{18,... | collective-permute-start | bytes 4325384 | tf_op jit(solution)/shard_map/ppermute | solution.py:611
  237.6 14.6 %collective-permute-start.36 = (bf16[64,1024]{1,0:T(8,128)(2,1)S(1)}, bf16[64,1024]{1,0:T(8,128)(2,1)S(1)}, u32[]{:S(2)}, u32[]{:S(2)}) collective-permute-start(bf16[64,1024]{1,0:T(8,128)(2,1)S(1)} %dynamic-slice_bitcast_fusion.10), channel_id=1, source_target_pairs={{0,4},{2,6},{4,0},{6,2},{8,12},{10,14},{12,8},{14,10},{16,20},{18,... | collective-permute-start | bytes 393224 | tf_op jit(solution)/shard_map/ppermute | solution.py:611
  238.3 21.9 %collective-permute-start.17 = (bf16[256,1024]{1,0:T(8,128)(2,1)}, bf16[256,1024]{1,0:T(8,128)(2,1)}, u32[]{:S(2)}, u32[]{:S(2)}) collective-permute-start(bf16[256,1024]{1,0:T(8,128)(2,1)} %broadcast_select_fusion.5), channel_id=1, source_target_pairs={{0,1},{1,0},{2,3},{3,2},{4,5},{5,4},{6,7},{7,6},{8,9},{9,8},{10,11... | collective-permute-start | bytes 1572872 | tf_op jit(solution)/shard_map/ppermute | solution.py:662
  240.6 13.8 %collective-permute-start.24 = (bf16[64,1024]{1,0:T(8,128)(2,1)}, bf16[64,1024]{1,0:T(8,128)(2,1)S(1)}, u32[]{:S(2)}, u32[]{:S(2)}) collective-permute-start(bf16[64,1024]{1,0:T(8,128)(2,1)} %get-tuple-element.205), channel_id=1, source_target_pairs={{0,8},{2,10},{4,12},{6,14},{8,0},{10,2},{12,4},{14,6},{16,24},{18,... | collective-permute-start | bytes 393224 | tf_op jit(solution)/shard_map/ppermute | solution.py:611
  244.8 9.7 %collective-permute-start.25 = (bf16[64,1024]{1,0:T(8,128)(2,1)}, bf16[64,1024]{1,0:T(8,128)(2,1)S(1)}, u32[]{:S(2)}, u32[]{:S(2)}) collective-permute-start(bf16[64,1024]{1,0:T(8,128)(2,1)} %get-tuple-element.207), channel_id=1, source_target_pairs={{0,16},{2,18},{4,20},{6,22},{8,24},{10,26},{12,28},{14,30},{16,0},... | collective-permute-start | bytes 393224 | tf_op jit(solution)/shard_map/ppermute | solution.py:611
  252.2 7.3 %collective-permute-start.26 = (bf16[64,1024]{1,0:T(8,128)(2,1)}, bf16[64,1024]{1,0:T(8,128)(2,1)S(1)}, u32[]{:S(2)}, u32[]{:S(2)}) collective-permute-start(bf16[64,1024]{1,0:T(8,128)(2,1)} %get-tuple-element.206), channel_id=1, source_target_pairs={{0,24},{2,26},{4,28},{6,30},{8,16},{10,18},{12,20},{14,22},{16,8},... | collective-permute-start | bytes 393224 | tf_op jit(solution)/shard_map/ppermute | solution.py:611
  263.5 19.5 %collective-permute-start.31 = (bf16[2,64,768]{2,1,0:T(8,128)(2,1)S(1)}, bf16[2,64,768]{2,1,0:T(8,128)(2,1)S(1)}, u32[]{:S(2)}, u32[]{:S(2)}) collective-permute-start(bf16[2,64,768]{2,1,0:T(8,128)(2,1)S(1)} %get-tuple-element.202), channel_id=1, source_target_pairs={{0,8},{2,10},{4,12},{6,14},{8,0},{10,2},{12,4},{14,6},{16,24},{18,... | collective-permute-start | bytes 589832 | tf_op jit(solution)/shard_map/ppermute | solution.py:611
  266.2 17.9 %collective-permute-start.32 = (bf16[2,64,768]{2,1,0:T(8,128)(2,1)S(1)}, bf16[2,64,768]{2,1,0:T(8,128)(2,1)S(1)}, u32[]{:S(2)}, u32[]{:S(2)}) collective-permute-start(bf16[2,64,768]{2,1,0:T(8,128)(2,1)S(1)} %get-tuple-element.204), channel_id=1, source_target_pairs={{0,16},{2,18},{4,20},{6,22},{8,24},{10,26},{12,28},{14,30},{16,0},... | collective-permute-start | bytes 589832 | tf_op jit(solution)/shard_map/ppermute | solution.py:611
  266.2 18.8 %collective-permute-start.33 = (bf16[2,64,768]{2,1,0:T(8,128)(2,1)S(1)}, bf16[2,64,768]{2,1,0:T(8,128)(2,1)S(1)}, u32[]{:S(2)}, u32[]{:S(2)}) collective-permute-start(bf16[2,64,768]{2,1,0:T(8,128)(2,1)S(1)} %get-tuple-element.203), channel_id=1, source_target_pairs={{0,24},{2,26},{4,28},{6,30},{8,16},{10,18},{12,20},{14,22},{16,8},... | collective-permute-start | bytes 589832 | tf_op jit(solution)/shard_map/ppermute | solution.py:611
  269.4 32.4 %collective-permute-start.27 = (bf16[4,64,640]{2,1,0:T(8,128)(2,1)}, bf16[4,64,640]{2,1,0:T(8,128)(2,1)}, u32[]{:S(2)}, u32[]{:S(2)}) collective-permute-start(bf16[4,64,640]{2,1,0:T(8,128)(2,1)} %dynamic-slice_bitcast_fusion.3), channel_id=1, source_target_pairs={{0,4},{2,6},{4,0},{6,2},{8,12},{10,14},{12,8},{14,10},{16,20},{18,... | collective-permute-start | bytes 983048 | tf_op jit(solution)/shard_map/ppermute | solution.py:611
  270.9 10.5 %collective-permute-start.19 = (f32[8,2432]{1,0:T(8,128)S(1)}, f32[8,2432]{1,0:T(8,128)S(1)}, u32[]{:S(2)}, u32[]{:S(2)}) collective-permute-start(f32[8,2432]{1,0:T(8,128)S(1)} %add.246), channel_id=1, source_target_pairs={{0,4},{2,6},{4,0},{6,2},{8,12},{10,14},{12,8},{14,10},{16,20},{18,... | collective-permute-start | bytes 233480 | tf_op jit(solution)/shard_map/ppermute | solution.py:611
  281.4 32.1 %collective-permute-start.16 = (bf16[256,1024]{1,0:T(8,128)(2,1)}, bf16[256,1024]{1,0:T(8,128)(2,1)}, u32[]{:S(2)}, u32[]{:S(2)}) collective-permute-start(bf16[256,1024]{1,0:T(8,128)(2,1)} %broadcast_select_fusion.4), channel_id=1, source_target_pairs={{0,1},{1,0},{2,3},{3,2},{4,5},{5,4},{6,7},{7,6},{8,9},{9,8},{10,11... | collective-permute-start | bytes 1572872 | tf_op jit(solution)/shard_map/ppermute | solution.py:662
  284.0 8.5 %collective-permute-start.21 = (f32[8,2432]{1,0:T(8,128)S(1)}, f32[8,2432]{1,0:T(8,128)S(1)}, u32[]{:S(2)}, u32[]{:S(2)}) collective-permute-start(f32[8,2432]{1,0:T(8,128)S(1)} %add.247), channel_id=1, source_target_pairs={{0,16},{2,18},{4,20},{6,22},{8,24},{10,26},{12,28},{14,30},{16,0},... | collective-permute-start | bytes 233480 | tf_op jit(solution)/shard_map/ppermute | solution.py:611
  284.9 7.6 %collective-permute-start.22 = (f32[8,2432]{1,0:T(8,128)S(1)}, f32[8,2432]{1,0:T(8,128)S(1)}, u32[]{:S(2)}, u32[]{:S(2)}) collective-permute-start(f32[8,2432]{1,0:T(8,128)S(1)} %add.247), channel_id=1, source_target_pairs={{0,24},{2,26},{4,28},{6,30},{8,16},{10,18},{12,20},{14,22},{16,8},... | collective-permute-start | bytes 233480 | tf_op jit(solution)/shard_map/ppermute | solution.py:611
  296.1 11.2 %collective-permute-start.35 = (f32[64,256]{1,0:T(8,128)}, f32[64,256]{1,0:T(8,128)}, u32[]{:S(2)}, u32[]{:S(2)}) collective-permute-start(f32[64,256]{1,0:T(8,128)} %slice.87), channel_id=1, source_target_pairs={{0,1},{1,0},{2,3},{3,2},{4,5},{5,4},{6,7},{7,6},{8,9},{9,8},{10,11... | collective-permute-start | bytes 196616 | tf_op jit(solution)/shard_map/ppermute | solution.py:662
  304.4 7.8 %collective-permute-start.29 = (bf16[64,640]{1,0:T(8,128)(2,1)S(1)}, bf16[64,640]{1,0:T(8,128)(2,1)S(1)}, u32[]{:S(2)}, u32[]{:S(2)}) collective-permute-start(bf16[64,640]{1,0:T(8,128)(2,1)S(1)} %get-tuple-element.210), channel_id=1, source_target_pairs={{0,16},{2,18},{4,20},{6,22},{8,24},{10,26},{12,28},{14,30},{16,0},... | collective-permute-start | bytes 245768 | tf_op jit(solution)/shard_map/ppermute | solution.py:611
  304.8 7.4 %collective-permute-start.30 = (bf16[64,640]{1,0:T(8,128)(2,1)S(1)}, bf16[64,640]{1,0:T(8,128)(2,1)S(1)}, u32[]{:S(2)}, u32[]{:S(2)}) collective-permute-start(bf16[64,640]{1,0:T(8,128)(2,1)S(1)} %get-tuple-element.209), channel_id=1, source_target_pairs={{0,24},{2,26},{4,28},{6,30},{8,16},{10,18},{12,20},{14,22},{16,8},... | collective-permute-start | bytes 245768 | tf_op jit(solution)/shard_map/ppermute | solution.py:611
  (27 other events, 239.8 us)
Sparse Core Ops, SparseCore 0:
  10.8 65.9 all-gather.1
where the time goes:
time: 332 us; the launch traced here: 327 us
  Pallas kernels  125 us (38%)
  starting transfers between devices  66.4 us (20%)
  waiting for transfers between devices  48.4 us (15%)
  other arithmetic  36.4 us (11%)
  local copies, waits for them, and re-layouts  36.1 us (11%)
  between operations  15 us (5%)
    ppermute x28, starting transfers between devices, dp_send(): return lax.ppermute(value, 'dp', [(i, i ^ bit) for i in range(size)])  54.4 us
    pallas_call x4, Pallas kernels, mixer_backward(): pl.pallas_call(partial(backward_kernel, begin, rows), grid=(end - begin,)...  46.3 us
    ppermute x28, waiting for transfers between devices, dp_send(): return lax.ppermute(value, 'dp', [(i, i ^ bit) for i in range(size)])  43.6 us
    pallas_call x4, Pallas kernels, input_terms(): pl.pallas_call(input_kernel, grid=(rows // span,), in_specs=[by_row(chann...  21.3 us
    pallas_call x1, Pallas kernels, mixer_forward(): pl.pallas_call(forward_kernel, grid=(blocks,), in_specs=[pl.BlockSpec(mem...  20.7 us
    pallas_call x1, Pallas kernels, gate_norm(): pl.pallas_call(partial(norm_kernel, float(full_inner)), grid=(rows // spa...  18.8 us
    ppermute x9, starting transfers between devices, tensor_swap(): return lax.ppermute(value, 'tensor', [(0, 1), (1, 0)])  12 us
    pallas_call x1, Pallas kernels, gate_forward(): pl.pallas_call(gate_kernel, grid=(rows // span,), in_specs=[by_row(model)...  10.6 us
  transfers between devices with their start and end apart: 38, of which 11 were waited for; matrix products, arithmetic and copies ran while one was open for 15% of the time, Pallas kernels for 23%

commit v1 on v0

--- a/solution.py
+++ b/solution.py
@@ -81,12 +81,58 @@
     return down == across
 
 
+def rows_of(block, blocks, spot_ref, own_ref, others):
+    if not others:
+        return own_ref[...]
+    half = blocks // 2
+    local = lax.rem(block, half)
+    span = own_ref.shape[0] // half
+    each = half // len(others)
+    value = None
+    for i, ref in enumerate(others):
+        at = lax.rem(local, each) * span
+        piece = ref[pl.ds(pl.multiple_of(at, span), span), :]
+        value = piece if i == 0 else jnp.where(local >= i * each, piece, value)
+    mine = own_ref[pl.ds(pl.multiple_of(local * span, span), span), :]
+    return jnp.where(block // half == spot_ref[0, 0], mine, value)
+
+
+def own_specs(own, others, span):
+    if not others:
+        return [pl.BlockSpec((span, own.shape[1]), lambda i: (i, 0))]
+    return [full(own.shape), *[full(other.shape) for other in others]]
+
+
+def place_weights(spot_ref, weight_ref, sources, count):
+    rows = weight_ref.shape[0] // (4 * count)
+    for i, ref in enumerate(sources):
+        along = spot_ref[0, 2] ^ (i % 2)
+        core = spot_ref[0, 3] ^ (i // 2)
+        for k in range(count):
+            at = (((spot_ref[0, 1] ^ k) * 2 + along) * 2 + core) * rows
+            weight_ref[pl.ds(pl.multiple_of(at, rows), rows), :] = ref[k * rows : (k + 1) * rows, :]
+
+
+def split_cores(spot_ref, value_ref, keep_ref, send_ref, chips):
+    rows = keep_ref.shape[0] // chips
+    core = spot_ref[0, 3]
+    for chip in range(chips):
+        here = pl.ds(pl.multiple_of((2 * chip + core) * rows, rows), rows)
+        there = pl.ds(pl.multiple_of((2 * chip + 1 - core) * rows, rows), rows)
+        keep_ref[chip * rows : (chip + 1) * rows, :] = value_ref[here, :].astype(bf16)
+        send_ref[chip * rows : (chip + 1) * rows, :] = value_ref[there, :].astype(bf16)
+
+
 def forward_kernel(
-    lengths_ref, normed_ref, weight_ref, conv_inner_ref, bias_inner_ref,
-    conv_shared_ref, bias_shared_ref, step_bias_ref, rate_ref, skip_ref, spread_ref,
-    ssm_ref, inner_ref, pre_inner_ref, shared_ref, pre_shared_ref, step_ref, entering_ref,
-    inner_tail, shared_tail, state,
+    pieces, count, spot_ref, lengths_ref, *refs
 ):
+    own_ref, others = refs[0], refs[1:pieces]
+    sources = refs[pieces : pieces + 4]
+    (
+        conv_inner_ref, bias_inner_ref, conv_shared_ref, bias_shared_ref, step_bias_ref, rate_ref,
+        skip_ref, spread_ref, normed_ref, weight_ref, ssm_ref, inner_ref, pre_inner_ref, shared_ref,
+        pre_shared_ref, step_ref, entering_ref, inner_tail, shared_tail, state,
+    ) = refs[pieces + 4 :]
     block = pl.program_id(0)
     rows = normed_ref.shape[0]
     channels = conv_inner_ref.shape[1]
@@ -98,13 +144,15 @@
         inner_tail[0:TAIL, :] = jnp.zeros((TAIL, channels), f32)
         shared_tail[0:TAIL, :] = jnp.zeros((TAIL, shared_tail.shape[1]), f32)
         state[...] = jnp.zeros_like(state)
+        place_weights(spot_ref, weight_ref, sources, count)
 
     @pl.when(block > 0)
     def _():
         inner_tail[0:TAIL, :] = inner_tail[rows : rows + TAIL, :]
         shared_tail[0:TAIL, :] = shared_tail[rows : rows + TAIL, :]
 
-    normed = normed_ref[...]
+    normed = rows_of(block, pl.num_programs(0), spot_ref, own_ref, others)
+    normed_ref[...] = normed
     small = mm(normed, weight_ref[:, channels:], NN)
     width = conv_shared_ref.shape[1]
     shared_proj = small[:, :width]
@@ -172,37 +220,34 @@
 
 
 def mixer_forward(
-    lengths, normed, weight, conv_inner, bias_inner, conv_shared, bias_shared,
+    spot, lengths, own, others, sources, count, conv_inner, bias_inner, conv_shared, bias_shared,
     step_bias, rate, skip, spread, span,
 ):
-    rows, model = normed.shape
+    rows = own.shape[0] * (2 if others else 1)
+    model = own.shape[1]
     channels = conv_inner.shape[1]
     width = conv_shared.shape[1]
+    known = channels + width + LANES
     blocks = rows // span
     by_row = lambda cols: pl.BlockSpec((span, cols), lambda i: (i, 0))
     shape = lambda cols: jax.ShapeDtypeStruct((rows, cols), f32)
     states = width // 2
+    smem = pl.BlockSpec(memory_space=pltpu.SMEM)
+    fixed = (conv_inner, bias_inner, conv_shared, bias_shared, step_bias, rate, skip, spread)
     return pl.pallas_call(
-        forward_kernel,
+        partial(forward_kernel, 1 + len(others), count),
         grid=(blocks,),
         in_specs=[
-            pl.BlockSpec(memory_space=pltpu.SMEM),
-            by_row(model),
-            full(weight.shape),
-            full(conv_inner.shape),
-            full(bias_inner.shape),
-            full(conv_shared.shape),
-            full(bias_shared.shape),
-            full(step_bias.shape),
-            full(rate.shape),
-            full(skip.shape),
-            full(spread.shape),
+            smem, smem, *own_specs(own, others, span), *[full(x.shape) for x in sources],
+            *[full(x.shape) for x in fixed],
         ],
         out_specs=[
-            by_row(channels), by_row(channels), by_row(channels), by_row(width), by_row(width),
-            by_row(LANES), pl.BlockSpec((1, states, channels), lambda i: (i, 0, 0)),
+            by_row(model), full((model, known)), by_row(channels), by_row(channels),
+            by_row(channels), by_row(width), by_row(width), by_row(LANES),
+            pl.BlockSpec((1, states, channels), lambda i: (i, 0, 0)),
         ],
         out_shape=[
+            jax.ShapeDtypeStruct((rows, model), bf16), jax.ShapeDtypeStruct((model, known), bf16),
             shape(channels), shape(channels), shape(channels), shape(width), shape(width),
             shape(LANES), jax.ShapeDtypeStruct((blocks, states, channels), f32),
         ],
@@ -215,10 +260,7 @@
             dimension_semantics=("arbitrary",), vmem_limit_bytes=LIMIT
         ),
         name="mixer_forward",
-    )(
-        lengths, normed, weight, conv_inner, bias_inner, conv_shared, bias_shared,
-        step_bias, rate, skip, spread,
-    )
+    )(spot, lengths, own, *others, *sources, *fixed)
 
 
 def backward_kernel(
@@ -421,54 +463,92 @@
     return results[0], tuple(results[1:])
 
 
-def product_kernel(normed_ref, *refs):
-    grads, out_ref = refs[:-1], refs[-1]
-    total, at = 0.0, 0
-    for ref in grads:
+def gain_row(weight_ref, total_ref, columns):
+    rows = weight_ref.shape[0]
+    added = jnp.zeros((rows, LANES), f32)
+    for lo in range(0, columns, LANES):
+        added = added + weight_ref[:, lo : lo + LANES].astype(f32) * total_ref[:, lo : lo + LANES]
+    return jnp.sum(jnp.transpose(added), axis=0, keepdims=True)
+
+
+def product_kernel(chips, spot_ref, normed_ref, weight_ref, gain_ref, sums_ref, norm_sum_ref, *refs):
+    grads, (keep_ref, send_ref, packed_ref, total) = refs[:-4], refs[-4:]
+    known = sums_ref.shape[1]
+    at = 0
+    for i, ref in enumerate(grads):
         rows = ref.shape[0]
-        total = total + mm(normed_ref[at : at + rows, :], ref[...], TN)
+        added = mm(normed_ref[at : at + rows, :], ref[...], TN)
+        total[...] = added if i == 0 else total[...] + added
         at += rows
-    out_ref[...] = total.astype(bf16)
-
-
-def weight_products(normed, grads):
+    split_cores(spot_ref, total, keep_ref, send_ref, chips)
+    packed_ref[:, :known] = sums_ref[...]
+    packed_ref[:, known:] = norm_sum_ref[...]
+    row = norm_sum_ref[0:1, :] + gain_row(weight_ref, total, known)
+    packed_ref[0:1, known:] = row / gain_ref[...]
+
+
+def weight_products(spot, normed, weight, gain, sums, norm_sum, grads, chips):
     known = grads[0].shape[1]
+    model = normed.shape[1]
+    part = jax.ShapeDtypeStruct((model // 2, known), bf16)
+    vmem = pl.BlockSpec(memory_space=pltpu.VMEM)
     return pl.pallas_call(
-        product_kernel,
-        out_shape=jax.ShapeDtypeStruct((normed.shape[1], known), bf16),
+        partial(product_kernel, chips),
+        in_specs=[pl.BlockSpec(memory_space=pltpu.SMEM), *[vmem for _ in range(5 + len(grads))]],
+        out_specs=[vmem, vmem, vmem],
+        out_shape=[part, part, jax.ShapeDtypeStruct((TAIL, known + model), f32)],
+        scratch_shapes=[pltpu.VMEM((model, known), f32)],
         compiler_params=pltpu.CompilerParams(vmem_limit_bytes=LIMIT),
         name="weight_products",
-    )(normed, *grads)
-
-
-def gate_kernel(normed_ref, gate_w_ref, upstream_ref, out_w_ref, gain_ref, ssm_ref,
-                gate_ref, grad_ref, sums_ref):
-    rows = normed_ref.shape[0]
-    gate = mm(normed_ref[...], gate_w_ref[...], NN)
-    grad = mm(upstream_ref[...], out_w_ref[...], NN)
-    gate_ref[...] = gate
-    grad_ref[...] = grad
-    gated = ssm_ref[...] * (gate * sigmoid(gate))
-    square = jnp.sum(gated * gated, axis=1, keepdims=True)
-    cross = jnp.sum(grad * gain_ref[...] * gated, axis=1, keepdims=True)
+    )(spot, normed, weight, gain, sums, norm_sum, *grads)
+
+
+def gate_kernel(pieces, spot_ref, normed_ref, *refs):
+    own_ref, others = refs[0], refs[1:pieces]
+    gate_w_ref, out_w_ref, gain_ref, ssm_ref, upstream_ref, gate_ref, grad_ref, sums_ref = refs[pieces:]
+    rows, channels = ssm_ref.shape
+    normed = normed_ref[...]
+    upstream = rows_of(pl.program_id(0), pl.num_programs(0), spot_ref, own_ref, others)
+    upstream_ref[...] = upstream
+    square = jnp.zeros((rows, LANES), f32)
+    cross = jnp.zeros((rows, LANES), f32)
+    step = 2 * LANES
+    for lo in range(0, channels, step):
+        hi = lo + step
+        gate = mm(normed, gate_w_ref[:, lo:hi], NN)
+        grad = mm(upstream, out_w_ref[:, lo:hi], NN)
+        gate_ref[:, lo:hi] = gate
+        grad_ref[:, lo:hi] = grad
+        gated = ssm_ref[:, lo:hi] * (gate * sigmoid(gate))
+        squares = gated * gated
+        crosses = grad * gain_ref[:, lo:hi] * gated
+        square = square + (squares[:, :LANES] + squares[:, LANES:])
+        cross = cross + (crosses[:, :LANES] + crosses[:, LANES:])
+    square = jnp.sum(square, axis=1, keepdims=True)
+    cross = jnp.sum(cross, axis=1, keepdims=True)
     lane = lax.broadcasted_iota(jnp.int32, (rows, LANES), 1)
     both = jnp.where(lane == 0, square, jnp.where(lane == 1, cross, 0.0))
     sums_ref[...] = jnp.transpose(both)[0:TAIL, :]
 
 
-def gate_forward(normed, upstream, weight, gain, ssm, span):
+def gate_forward(spot, normed, own, others, weight, gain, ssm, span):
     rows, model = normed.shape
     channels = ssm.shape[1]
     by_row = lambda cols: pl.BlockSpec((span, cols), lambda i: (i, 0))
     return pl.pallas_call(
-        gate_kernel,
+        partial(gate_kernel, 1 + len(others)),
         grid=(rows // span,),
         in_specs=[
-            by_row(model), pl.BlockSpec((model, channels), lambda i: (0, 0)), by_row(model),
+            pl.BlockSpec(memory_space=pltpu.SMEM), by_row(model), *own_specs(own, others, span),
+            pl.BlockSpec((model, channels), lambda i: (0, 0)),
             pl.BlockSpec((model, channels), lambda i: (0, 1)), full(gain.shape), by_row(channels),
         ],
-        out_specs=[by_row(channels), by_row(channels), pl.BlockSpec((TAIL, span), lambda i: (0, i))],
+        out_specs=[
+            by_row(model), by_row(channels), by_row(channels),
+            pl.BlockSpec((TAIL, span), lambda i: (0, i)),
+        ],
         out_shape=[
+            jax.ShapeDtypeStruct((rows, model), bf16),
             jax.ShapeDtypeStruct((rows, channels), f32),
             jax.ShapeDtypeStruct((rows, channels), f32),
             jax.ShapeDtypeStruct((TAIL, rows), f32),
@@ -477,70 +557,105 @@
             dimension_semantics=("arbitrary",), vmem_limit_bytes=LIMIT
         ),
         name="gate_forward",
-    )(normed, weight, upstream, weight, gain, ssm)
-
-
-def norm_kernel(full_inner, sums_ref, gate_ref, grad_ref, ssm_ref, gain_ref, normed_ref,
-                upstream_ref, out_w_ref, grad_gate_ref, grad_ssm_ref, gain_sum_ref, branch_ref,
-                products_ref, scaled, totals):
+    )(spot, normed, own, *others, weight, weight, gain, ssm)
+
+
+def norm_kernel(full_inner, chips, split, spot_ref, sums_ref, more_ref, gate_ref, grad_ref, ssm_ref,
+                gain_ref, normed_ref, upstream_ref, gate_w_ref, out_w_ref, grad_gate_ref,
+                grad_ssm_ref, gain_sum_ref, keep_ref, send_ref, mine_ref, theirs_ref, norm_sum_ref,
+                scaled, totals):
     rows, channels = gate_ref.shape
-
-    @pl.when(pl.program_id(0) == 0)
+    block = pl.program_id(0)
+
+    @pl.when(block == 0)
     def _():
         gain_sum_ref[...] = jnp.zeros_like(gain_sum_ref)
         totals[...] = jnp.zeros_like(totals)
 
-    padded = jnp.concatenate([sums_ref[...], jnp.zeros((LANES - TAIL, rows), f32)], axis=0)
-    sums = jnp.transpose(padded)
+    sums = sums_ref[...] + more_ref[...] if split else sums_ref[...]
+    sums = jnp.transpose(jnp.concatenate([sums, jnp.zeros((LANES - TAIL, rows), f32)], axis=0))
     scale = lax.rsqrt(sums[:, 0:1] / full_inner + EPSILON)
     pull = scale * scale * scale * (sums[:, 1:2] / full_inner)
-    for lo in range(0, channels, LANES):
-        hi = lo + LANES
+    normed_t = jnp.transpose(normed_ref[...])
+    upstream_t = jnp.transpose(upstream_ref[...])
+    step = 2 * LANES
+    for lo in range(0, channels, step):
+        hi = lo + step
         gain = gain_ref[:, lo:hi]
         gate, grad, ssm = gate_ref[:, lo:hi], grad_ref[:, lo:hi], ssm_ref[:, lo:hi]
         sig = sigmoid(gate)
         silu = gate * sig
         gated = ssm * silu
         normal = gated * scale
-        scaled[:, lo:hi] = (normal * gain).astype(bf16)
+        scaled_low = (normal * gain).astype(bf16)
+        scaled[:, lo:hi] = scaled_low
         gain_sum_ref[:, lo:hi] += jnp.broadcast_to(
-            jnp.sum(grad * normal, axis=0, keepdims=True), (TAIL, LANES)
+            jnp.sum(grad * normal, axis=0, keepdims=True), (TAIL, step)
         )
         grad_gated = scale * (grad * gain) - gated * pull
         grad_ssm_ref[:, lo:hi] = grad_gated * silu
-        grad_gate_ref[:, lo:hi] = (grad_gated * ssm * (sig * (1.0 + gate * (1.0 - sig)))).astype(bf16)
-    scaled_out = scaled[...]
-    branch_ref[...] = mm(scaled_out, out_w_ref[...], NT).astype(bf16)
-    totals[:, :channels] += mm(normed_ref[...], grad_gate_ref[...], TN)
-    totals[:, channels:] += mm(upstream_ref[...], scaled_out, TN)
-
-    @pl.when(pl.program_id(0) == pl.num_programs(0) - 1)
+        grad_gate = (grad_gated * ssm * (sig * (1.0 + gate * (1.0 - sig)))).astype(bf16)
+        grad_gate_ref[:, lo:hi] = grad_gate
+        totals[:, lo:hi] += mm(normed_t, grad_gate, NN)
+        totals[:, channels + lo : channels + hi] += mm(upstream_t, scaled_low, NN)
+    branch = mm(scaled[...], out_w_ref[...], NT).astype(bf16)
+    if split:
+        half = pl.num_programs(0) // 2
+        at = pl.ds(pl.multiple_of(lax.rem(block, half) * rows, rows), rows)
+
+        @pl.when(block // half == spot_ref[0, 0])
+        def _():
+            mine_ref[at, :] = branch
+
+        @pl.when(block // half != spot_ref[0, 0])
+        def _():
+            theirs_ref[at, :] = branch
+    else:
+        mine_ref[pl.ds(pl.multiple_of(block * rows, rows), rows), :] = branch
+
+        @pl.when(block == 0)
+        def _():
+            theirs_ref[...] = jnp.zeros_like(theirs_ref)
+
+    @pl.when(block == pl.num_programs(0) - 1)
     def _():
-        products_ref[...] = totals[...].astype(bf16)
-
-
-def gate_norm(sums, gate, grad, ssm, gain, normed, upstream, weight, full_inner, span):
+        split_cores(spot_ref, totals, keep_ref, send_ref, chips)
+        norm_sum_ref[...] = jnp.zeros_like(norm_sum_ref)
+        norm_sum_ref[0:1, :] = gain_row(gate_w_ref, totals, channels)
+
+
+def gate_norm(
+    spot, sums, more, gate, grad, ssm, gain, normed, upstream, weight, full_inner, chips, split, span
+):
     rows, channels = gate.shape
     model = normed.shape[1]
     by_row = lambda cols: pl.BlockSpec((span, cols), lambda i: (i, 0))
+    stats = pl.BlockSpec((TAIL, span), lambda i: (0, i))
+    half = (model // 2, 2 * channels)
+    mine = (rows // 2 if split else rows, model)
+    theirs = (rows // 2 if split else TAIL * 2, model)
     return pl.pallas_call(
-        partial(norm_kernel, float(full_inner)),
+        partial(norm_kernel, float(full_inner), chips, split),
         grid=(rows // span,),
         in_specs=[
-            pl.BlockSpec((TAIL, span), lambda i: (0, i)), by_row(channels), by_row(channels),
+            pl.BlockSpec(memory_space=pltpu.SMEM), stats, stats, by_row(channels), by_row(channels),
             by_row(channels), full(gain.shape), by_row(model), by_row(model),
+            pl.BlockSpec((model, channels), lambda i: (0, 0)),
             pl.BlockSpec((model, channels), lambda i: (0, 1)),
         ],
         out_specs=[
-            by_row(channels), by_row(channels), full((TAIL, channels)), by_row(model),
-            full((model, 2 * channels)),
+            by_row(channels), by_row(channels), full((TAIL, channels)), full(half), full(half),
+            full(mine), full(theirs), full((TAIL, model)),
         ],
         out_shape=[
             jax.ShapeDtypeStruct((rows, channels), bf16),
             jax.ShapeDtypeStruct((rows, channels), f32),
             jax.ShapeDtypeStruct((TAIL, channels), f32),
-            jax.ShapeDtypeStruct((rows, model), bf16),
-            jax.ShapeDtypeStruct((model, 2 * channels), bf16),
+            jax.ShapeDtypeStruct(half, bf16),
+            jax.ShapeDtypeStruct(half, bf16),
+            jax.ShapeDtypeStruct(mine, bf16),
+            jax.ShapeDtypeStruct(theirs, bf16),
+            jax.ShapeDtypeStruct((TAIL, model), f32),
         ],
         scratch_shapes=[
             pltpu.VMEM((span, channels), bf16),
@@ -550,7 +665,7 @@
             dimension_semantics=("arbitrary",), vmem_limit_bytes=LIMIT
         ),
         name="gate_norm",
-    )(sums, gate, grad, ssm, gain, normed, upstream, weight)
+    )(spot, sums, more, gate, grad, ssm, gain, normed, upstream, weight, weight)
 
 
 def lanes_of(vector):
@@ -564,46 +679,31 @@
     return (row == col).astype(bf16)
 
 
-def input_kernel(grad_gate_ref, grads_ref, gate_w_ref, weight_ref, normed_ref, gain_ref, sums_ref,
-                 before_ref, terms_ref, packed_ref):
-    known = sums_ref.shape[1]
+def input_kernel(grad_gate_ref, grads_ref, gate_w_ref, weight_ref, terms_ref):
     terms = mm(grad_gate_ref[...], gate_w_ref[...], NT)
     terms = terms + mm(grads_ref[...], weight_ref[...], NT)
     terms_ref[...] = terms.astype(bf16)
 
-    @pl.when(pl.program_id(0) == 0)
-    def _():
-        packed_ref[:, :known] = sums_ref[...]
-        packed_ref[:, known:] = before_ref[:, known:]
-
-    total = jnp.sum(terms * normed_ref[...].astype(f32), axis=0, keepdims=True) / gain_ref[...]
-    packed_ref[0:1, known:] += total
-
-
-def input_terms(grad_gate, grads, weight_late, weight, normed, gain, sums, before, begin, span):
-    model = normed.shape[1]
+
+def input_terms(grad_gate, grads, weight_late, weight, begin, span):
+    model = weight.shape[0]
     channels = grad_gate.shape[1]
     rows, known = grads.shape
-    by_row = lambda cols: pl.BlockSpec((span, cols), lambda i: (i + begin, 0))
-    here = lambda cols: pl.BlockSpec((span, cols), lambda i: (i, 0))
     return pl.pallas_call(
         input_kernel,
         grid=(rows // span,),
         in_specs=[
-            by_row(channels), here(known), pl.BlockSpec((model, channels), lambda i: (0, 0)),
-            full(weight.shape), by_row(model), full(gain.shape), full(sums.shape),
-            full(before.shape),
-        ],
-        out_specs=[here(model), full((TAIL, known + model))],
-        out_shape=[
-            jax.ShapeDtypeStruct((rows, model), bf16),
-            jax.ShapeDtypeStruct((TAIL, known + model), f32),
-        ],
+            pl.BlockSpec((span, channels), lambda i: (i + begin, 0)),
+            pl.BlockSpec((span, known), lambda i: (i, 0)),
+            pl.BlockSpec((model, channels), lambda i: (0, 0)), full(weight.shape),
+        ],
+        out_specs=pl.BlockSpec((span, model), lambda i: (i, 0)),
+        out_shape=jax.ShapeDtypeStruct((rows, model), bf16),
         compiler_params=pltpu.CompilerParams(
             dimension_semantics=("arbitrary",), vmem_limit_bytes=LIMIT
         ),
         name="input_terms",
-    )(grad_gate, grads, weight_late, weight, normed, gain, sums, before)
+    )(grad_gate, grads, weight_late, weight)
 
 
 def dp_send(value, bit):
@@ -617,29 +717,6 @@
 
 def choose(stacked, index, axis):
     return lax.dynamic_index_in_dim(stacked, index, axis, keepdims=False)
-
-
-def interleave(mine, other, upper, axis):
-    return jnp.stack([jnp.where(upper, other, mine), jnp.where(upper, mine, other)], axis=axis)
-
-
-def gather_long(shard):
-    me = lax.axis_index("dp")
-    rows, cols = shard.shape
-    pieces = [shard] + [dp_send(shard, bit) for bit in chip_bits()]
-    stacked = jnp.zeros((len(pieces), rows, cols), shard.dtype)
-    for k, piece in enumerate(pieces):
-        stacked = lax.dynamic_update_index_in_dim(stacked, piece, (me // 4) ^ k, 0)
-    return stacked
-
-
-def gather_x(stacked):
-    return interleave(stacked, dp_send(stacked, 2), (lax.axis_index("dp") // 2) % 2 == 1, 1)
-
-
-def gather_cores(chips):
-    whole = interleave(chips, dp_send(chips, 1), lax.axis_index("dp") % 2 == 1, 2)
-    return whole.reshape(-1, chips.shape[-1])
 
 
 def fold(parts, bit, axis):
@@ -662,9 +739,7 @@
     return lax.ppermute(value, "tensor", [(0, 1), (1, 0)])
 
 
-def sum_dp(value):
-    value = value + dp_send(value, 1)
-    value = value + dp_send(value, 2)
+def sum_chips(value):
     bits = chip_bits()
     pieces = [value] + [dp_send(value, bit) for bit in bits]
     while len(pieces) > 1:
@@ -678,19 +753,10 @@
     return tensor_swap(own)
 
 
-def join_halves(own, other, size):
-    if size != 2:
-        return other
-    upper = lax.axis_index("tensor") == 1
-    return jnp.concatenate([jnp.where(upper, other, own), jnp.where(upper, own, other)], axis=0)
-
-
 def join_pieces(own, top, bottom, size):
-    if size != 2:
-        top = top.reshape(size, -1, own.shape[1])
-        bottom = bottom.reshape(size, -1, own.shape[1])
-        return jnp.concatenate([top, bottom], axis=1).reshape(-1, own.shape[1])
-    return join_halves(own, jnp.concatenate([top, bottom], axis=0), size)
+    top = top.reshape(size, -1, own.shape[1])
+    bottom = bottom.reshape(size, -1, own.shape[1])
+    return jnp.concatenate([top, bottom], axis=1).reshape(-1, own.shape[1])
 
 
 def pick_half(lower, upper, size):
@@ -704,24 +770,15 @@
         whole = jnp.concatenate(quarters, axis=0)
         return lax.psum_scatter(whole, "tensor", scatter_dimension=0, tiled=True).astype(f32)
     first = lax.axis_index("tensor") == 0
-    top = jnp.where(first, quarters[0], quarters[2]).astype(f32) + other0.astype(f32)
-    bottom = jnp.where(first, quarters[1], quarters[3]).astype(f32) + other1.astype(f32)
-    return jnp.concatenate([top, bottom], axis=0)
+    lower = jnp.concatenate(quarters[:2], axis=0)
+    others = jnp.concatenate([other0, other1], axis=0)
+    return jnp.where(first, lower, quarters[2]).astype(f32) + others.astype(f32)
 
 
 def tensor_sum(value, size):
     if size != 2:
         return lax.psum(value, "tensor")
     return value + tensor_swap(value)
-
-
-def send_half(value, size):
-    if size != 2:
-        total = lax.psum_scatter(value, "tensor", scatter_dimension=0, tiled=True)
-        return total, jnp.zeros_like(total)
-    me = lax.axis_index("tensor")
-    halved = value.reshape(2, -1, value.shape[1])
-    return choose(halved, me, 0), tensor_swap(choose(halved, 1 - me, 0))
 
 
 def shards(
@@ -729,129 +786,149 @@
     conv_shared, bias_shared, step_bias, log_rate, skip_gain, gate_gain, out_weight, cotangent,
 ):
     size = lax.axis_size("tensor")
+    split = size == 2
+    me = lax.axis_index("dp")
+    count = len(chip_bits()) + 1
+    spot = jnp.stack([lax.axis_index("tensor"), me // 4, (me // 2) % 2, me % 2])[None, :]
+    spot = spot.astype(jnp.int32)
     channels = zx_weight.shape[2]
     heads = step_bias.shape[0]
     width = bc_weight.shape[1]
+    known = channels + width + LANES
+    step_weight = jnp.pad(dt_weight, ((0, 0), (0, LANES - heads)))
+    early = jnp.concatenate([zx_weight[:, 1, :], bc_weight, step_weight], axis=1)
     inputs = tokens.astype(f32)
     norm_scale = lax.rsqrt(jnp.mean(inputs * inputs, axis=1, keepdims=True) + EPSILON)
     normed_rows = (inputs * norm_scale * norm_gain[None, :]).astype(bf16)
-    step_weight = jnp.pad(dt_weight, ((0, 0), (0, LANES - heads)))
-    early = jnp.concatenate([zx_weight[:, 1, :], bc_weight, step_weight], axis=1)
+    half = normed_rows.shape[0] // 2
+    fixed = (
+        conv_inner, bias_inner[None, :], conv_shared, bias_shared[None, :], lanes_of(step_bias),
+        lanes_of(-jnp.exp(log_rate)), jnp.repeat(skip_gain, channels // heads)[None, :],
+        spread_map(heads, channels),
+    )
     late = jnp.concatenate([zx_weight[:, 0, :], out_weight], axis=1)
+    column = jnp.concatenate([early] + [dp_send(early, bit) for bit in chip_bits()], axis=0)
+    column, late, top, fixed = lax.optimization_barrier(
+        (column, late, gather_other(normed_rows[:half], size), fixed)
+    )
     weight_late = lax.all_gather(late, "dp", axis=0, tiled=True)
-    half = normed_rows.shape[0] // 2
-    stacked, upper_rows = lax.optimization_barrier(
-        (gather_long(early), gather_other(normed_rows[:half], size))
-    )
-    chips, lower_rows = lax.optimization_barrier(
-        (gather_x(stacked), gather_other(normed_rows[half:], size))
-    )
-    normed = join_pieces(normed_rows, upper_rows, lower_rows, size)
-    weight = gather_cores(chips)
-    spread = spread_map(heads, channels)
-    rate = lanes_of(-jnp.exp(log_rate))
-    skip = jnp.repeat(skip_gain, channels // heads)[None, :]
-    saved = mixer_forward(
-        lengths, normed, weight, conv_inner, bias_inner[None, :], conv_shared,
-        bias_shared[None, :], lanes_of(step_bias), rate, skip, spread, SPAN,
-    )
+    by_core = dp_send(column, 1)
+    by_x, bottom = lax.optimization_barrier(
+        (dp_send(column, 2), gather_other(normed_rows[half:], size))
+    )
+    sources = (column, by_x, by_core, dp_send(by_x, 1))
+    own, others = normed_rows, (top, bottom)
+    if not split:
+        own, others = join_pieces(normed_rows, top, bottom, size), ()
+    normed, weight, *saved = mixer_forward(
+        spot, lengths, own, others, sources, count, *fixed, SPAN
+    )
+    _, _, _, _, _, rate, skip, spread = fixed
     gain = gate_gain[None, :]
     other, ssm, weight_late = lax.optimization_barrier(
         (gather_other(cotangent, size), saved[0], weight_late)
     )
-    upstream = join_halves(cotangent, other, size)
-    gate, grad, sums = gate_forward(normed, upstream, weight_late, gain, ssm, SPAN)
-    sums = tensor_sum(sums, size)
-    grad_gate, grad_ssm, gain_sum, branch, first = gate_norm(
-        sums, gate, grad, ssm, gain, normed, upstream, weight_late, channels * size, SPAN
-    )
-    branch_own, branch_other = send_half(branch, size)
-    count = len(chip_bits()) + 1
-    first = first.reshape(count, 2, 2, -1, first.shape[1])
-    blocks = grad_ssm.shape[0] // SPAN
-    quarter = blocks // 4
-    known = channels + width + LANES
+    own, others = (cotangent, (other,)) if split else (other, ())
+    upstream, gate, grad, sums = gate_forward(
+        spot, normed, own, others, weight_late, gain, ssm, SPAN
+    )
+    more = gather_other(sums, size) if split else sums
+    sums = sums if split else lax.psum(sums, "tensor")
+    chips = 2 * count
+    grad_gate, grad_ssm, gain_sum, keep, send, branch_own, branch_send, norm_sum = gate_norm(
+        spot, sums, more, gate, grad, ssm, gain, normed, upstream, weight_late, channels * size,
+        chips, split, SPAN,
+    )
+    if split:
+        branch_other = gather_other(branch_send, size)
+    else:
+        branch_own = lax.psum_scatter(branch_own, "tensor", scatter_dimension=0, tiled=True)
+        branch_other = jnp.zeros_like(branch_own)
+    quarter = grad_ssm.shape[0] // SPAN // 4
     carry = (
         jnp.pad(gain_sum[:1], ((TAIL - 1, 0), (0, known - channels))),
         jnp.zeros((TAIL, channels), f32),
         jnp.zeros((TAIL, width), f32),
         jnp.zeros((width // 2, channels), f32),
     )
-    packed = jnp.zeros((TAIL, known + normed.shape[1]), f32)
-
-    def part(index, carry, packed):
-        begin = index * quarter
-        grads, carry = mixer_backward(
+    def back(begin, end, carry):
+        return mixer_backward(
             lengths, grad_ssm, saved, conv_inner, conv_shared, rate, skip, spread, carry,
-            (begin, begin + quarter), SPAN,
+            (begin * quarter, end * quarter), SPAN,
         )
-        return grads, carry
-
-    def terms_of(index, grads, sums, packed):
-        return input_terms(
-            grad_gate, grads, weight_late, weight, normed, norm_gain[None, :], sums, packed,
-            index * quarter, SPAN,
-        )
-
-    grads3, carry = part(3, carry, packed)
-    first = fold(first, 1, 2).astype(bf16)
-    carry, first = lax.optimization_barrier((carry, first))
+
+    def terms_of(begin, grads):
+        return input_terms(grad_gate, grads, weight_late, weight, begin * quarter, SPAN)
+
+    first = dp_send(send, 1)
+    grads2, carry = back(2, 4, carry)
+    first = (keep.astype(f32) + first.astype(f32)).astype(bf16)
+    first = first.reshape(count, 2, -1, first.shape[1])
+    carry, first, grads2 = lax.optimization_barrier((carry, first, grads2))
     first_gate, first_out = first[..., :channels], first[..., channels:]
-    grads2, carry = part(2, carry, packed)
-    terms3, packed = terms_of(3, grads3, carry[0], packed)
-    terms2, packed = terms_of(2, grads2, carry[0], packed)
-    carry, packed = lax.optimization_barrier((carry, packed))
-    grads1, carry = part(1, carry, packed)
-    terms1, packed = terms_of(1, grads1, carry[0], packed)
+    terms2 = terms_of(2, grads2)
+    carry, terms2 = lax.optimization_barrier((carry, terms2))
+    grads1, carry = back(1, 2, carry)
+    terms1 = terms_of(1, grads1)
     first_gate = fold(first_gate, 2, 1)
     first_out = fold_chips(first_out).astype(bf16)
-    send1 = pick_half(terms3, terms1, size)
-    carry, first_gate, first_out, send1, branch_other = lax.optimization_barrier(
-        (carry, first_gate, first_out, send1, branch_other)
-    )
-    other1 = gather_other(send1, size)
+    send1 = pick_half(terms2[terms2.shape[0] // 2 :], terms1, size)
+    carry, send1, branch_other, first_gate, first_out = lax.optimization_barrier(
+        (carry, send1, branch_other, first_gate, first_out)
+    )
+    other1 = gather_other(send1, size) if split else send1
+    block_out = (inputs + (branch_own.astype(f32) + branch_other.astype(f32))).astype(bf16)
     part_gate = fold_chips(first_gate)
     part_out = fold(first_out, 2, 0)
-    block_out = (inputs + (branch_own.astype(f32) + branch_other.astype(f32))).astype(bf16)
-    grads0, carry = part(0, carry, packed)
-    products = weight_products(normed, (grads0, grads1, grads2, grads3))
-    parts = fold(products.reshape(count, 2, 2, -1, known), 1, 2).astype(bf16)
-    terms0, packed = terms_of(0, grads0, carry[0], packed)
-    parts, packed, terms0 = lax.optimization_barrier((parts, packed, terms0))
-    other0 = gather_other(pick_half(terms2, terms0, size), size)
+    grads0, carry = back(0, 1, carry)
+    sums, part_gate, part_out, grads0, other1, block_out = lax.optimization_barrier(
+        (carry[0], part_gate, part_out, grads0, other1, block_out)
+    )
+    keep, send, sums = weight_products(
+        spot, normed, weight, norm_gain[None, :], sums, norm_sum, (grads0, grads1, grads2), chips
+    )
+    got = dp_send(send, 1)
+    sums = (sums + dp_send(sums, 1)) + (dp_send(sums, 2) + dp_send(sums, 3))
+    terms0 = terms_of(0, grads0)
+    send0 = pick_half(terms2[: terms2.shape[0] // 2], terms0, size)
+    parts = (keep.astype(f32) + got.astype(f32)).astype(bf16).reshape(count, 2, -1, known)
+    parts, sums, send0 = lax.optimization_barrier((parts, sums, send0))
+    other0 = gather_other(send0, size) if split else send0
     cut = (known // (2 * LANES)) * LANES
-    parts_a = fold_chips(fold(parts[..., :cut], 2, 1))
-    parts_b = fold(fold_chips(parts[..., cut:]).astype(bf16), 2, 0)
-    part_small = jnp.concatenate([parts_a, parts_b], axis=1)
-    packed = sum_dp(packed)
-    grad_normed = sum_quarters((terms0, terms1, terms2, terms3), other0, other1, size)
-    packed_all = tensor_sum(packed, size)
-    part_inner = part_small[:, :channels]
-    part_step = part_small[:, channels + width : channels + width + heads]
-    part_shared = tensor_sum(part_small[:, channels : channels + width], size)
+    parts_a = fold(parts[..., :cut], 2, 1)
+    parts_b = fold_chips(parts[..., cut:]).astype(bf16)
+    sums = sum_chips(sums)
+    parts_a, parts_b, other0, sums = lax.optimization_barrier((parts_a, parts_b, other0, sums))
+    shared_sums = tensor_sum(sums[:, channels:], size)
+    norm_sum = shared_sums[0, known - channels :]
+    grad_normed = sum_quarters((terms0, terms1, terms2), other0, other1, size)
     scaled_grad = grad_normed * norm_gain[None, :]
     grad_inputs = norm_scale * scaled_grad - inputs * norm_scale**3 * jnp.mean(
         scaled_grad * inputs, axis=1, keepdims=True
     )
     grad_tokens = (cotangent.astype(f32) + grad_inputs).astype(bf16)
+    parts_a = fold_chips(parts_a)
+    parts_b = fold(parts_b, 2, 0)
+    part_inner = jnp.concatenate([parts_a, parts_b[:, : channels - cut]], axis=1)
+    at_step = channels + width
+    part_shared = tensor_sum(parts_b[:, channels - cut : at_step - cut], size)
+    part_step = parts_b[:, at_step - cut : at_step - cut + heads]
     part_in = jnp.stack([part_gate, part_inner], axis=1)
-    at_step = channels + width
-    at_norm = at_step + LANES
     return (
         block_out,
         grad_tokens,
-        packed_all[0, at_norm:],
+        norm_sum,
         part_in,
         part_shared,
         part_step,
-        packed[:TAPS, :channels],
-        packed[TAPS, :channels],
-        packed_all[:TAPS, channels:at_step],
-        packed_all[TAPS, channels:at_step],
-        packed[0, at_step : at_step + heads],
-        packed[1, at_step : at_step + heads],
-        packed[2, at_step : at_step + heads],
-        packed[TAIL - 1, :channels],
+        sums[:TAPS, :channels],
+        sums[TAPS, :channels],
+        shared_sums[:TAPS, :width],
+        shared_sums[TAPS, :width],
+        sums[0, at_step : at_step + heads],
+        sums[1, at_step : at_step + heads],
+        sums[2, at_step : at_step + heads],
+        sums[TAIL - 1, :channels],
         part_out,
     )
 

time: 332 us -> 289 us (0.87)
  starting transfers between devices: 66.4 us -> 49 us
  local copies, waits for them, and re-layouts: 36.1 us -> 20.5 us
  other arithmetic: 36.4 us -> 24.3 us
  waiting for transfers between devices: 48.4 us -> 52 us
    ppermute x28 -> x30, waiting for transfers between devices: 43.6 us -> 26.2 us  [dp_send(): return lax.ppermute(value, 'dp', [(i, i ^ bit) for i in range(size)])]
    ppermute x28 -> x30, starting transfers between devices: 54.4 us -> 38.1 us  [dp_send(): return lax.ppermute(value, 'dp', [(i, i ^ bit) for i in range(size)])]
    ppermute x9, waiting for transfers between devices: 4.68 us -> 16.6 us  [tensor_swap(): return lax.ppermute(value, 'tensor', [(0, 1), (1, 0)])]
    all_gather x1, waiting for transfers between devices: 0.02 us -> 9.22 us  [shards(): weight_late = lax.all_gather(late, 'dp', axis=0, tiled=True)]
    squeeze x10 -> x8, local copies, waits for them, and re-layouts: 8.19 us -> 3.28 us  [choose(): return lax.dynamic_index_in_dim(stacked, index, axis, keepdims=False)]
    dynamic_slice x2 -> x0, local copies, waits for them, and re-layouts: 4.23 us -> none  [choose(): return lax.dynamic_index_in_dim(stacked, index, axis, keepdims=False)]
    another operation x4 -> x0, other arithmetic: 3.83 us -> none  [interleave(): jnp.stack([jnp.where(upper, other, mine), jnp.where(upper, mine, other)],...]
    convert_element_type x3 -> x4, other arithmetic: 4.2 us -> 7.03 us  [the longest x1 2.83 us: shards(): (inputs + (branch_own.astype(f32) + branch_other.astype(f32))).astype(bf16)]
  transfers between devices with their start and end apart: 38 -> 40, of which waited for: 11 -> 12; matrix products, arithmetic and copies ran while one was open for 15% -> 12% of each run, Pallas kernels for 23% -> 29%
where the time goes in v1:
time: 289 us; the launch traced here: 286 us
  Pallas kernels  125 us (43%)
  waiting for transfers between devices  52 us (18%)
  starting transfers between devices  49 us (17%)
  other arithmetic  24.3 us (8%)
  local copies, waits for them, and re-layouts  20.5 us (7%)
  between operations  15.2 us (5%)
    pallas_call x3, Pallas kernels, mixer_backward(): pl.pallas_call(partial(backward_kernel, begin, rows), grid=(end - begin,)...  43.7 us
    ppermute x30, starting transfers between devices, dp_send(): return lax.ppermute(value, 'dp', [(i, i ^ bit) for i in range(size)])  38.1 us
    ppermute x30, waiting for transfers between devices, dp_send(): return lax.ppermute(value, 'dp', [(i, i ^ bit) for i in range(size)])  26.2 us
    pallas_call x1, Pallas kernels, mixer_forward(): pl.pallas_call(partial(forward_kernel, 1 + len(others), count), grid=(blo...  23.1 us
    pallas_call x1, Pallas kernels, gate_norm(): pl.pallas_call(partial(norm_kernel, float(full_inner), chips, split), gri...  19.8 us
    pallas_call x3, Pallas kernels, input_terms(): pl.pallas_call(input_kernel, grid=(rows // span,), in_specs=[pl.BlockSpec...  17.4 us
    ppermute x9, waiting for transfers between devices, tensor_swap(): return lax.ppermute(value, 'tensor', [(0, 1), (1, 0)])  16.6 us
    pallas_call x1, Pallas kernels, gate_forward(): pl.pallas_call(partial(gate_kernel, 1 + len(others)), grid=(rows // span,...  11.9 us
  transfers between devices with their start and end apart: 40, of which 12 were waited for; matrix products, arithmetic and copies ran while one was open for 12% of the time, Pallas kernels for 29%

profile of v1, /device:TPU:0, one launch (start us, length us, event | category | flops | bytes accessed | tf_op | source)
XLA Modules:
  0.0 285.5 jit_solution(8404971415627603413)
XLA Ops:
  11.1 3.0 %collective-permute-start = (bf16[64,1408]{1,0:T(8,128)(2,1)}, bf16[64,1408]{1,0:T(8,128)(2,1)}, u32[]{:S(2)}, u32[]{:S(2)}) collective-permute-start(bf16[64,1408]{1,0:T(8,128)(2,1)} %pad_maximum_fusion.4), channel_id=1, source_target_pairs={{0,8},{2,10},{4,12},{6,14},{8,0},{10,2},{12,4},{14,6},{16,24},{18,... | collective-permute-start | bytes 540680 | tf_op jit(solution)/shard_map/ppermute | solution.py:711
  14.1 2.6 collective-permute-start.1
  25.7 4.8 %collective-permute-done.1 = bf16[64,1408]{1,0:T(8,128)(2,1)} collective-permute-done((bf16[64,1408]{1,0:T(8,128)(2,1)}, bf16[64,1408]{1,0:T(8,128)(2,1)}, u32[]{:S(2)}, u32[]{:S(2)}) %collective-permute-start.1) | collective-permute-done | bytes 180256 | tf_op jit(solution)/shard_map/ppermute | solution.py:711
  30.6 2.0 pad_maximum_fusion.1.refs_3_
  36.3 13.1 %collective-permute-done.5.refs_2_ = bf16[256,1024]{1,0:T(8,128)(2,1)} collective-permute-done((bf16[256,1024]{1,0:T(8,128)(2,1)}, bf16[256,1024]{1,0:T(8,128)(2,1)}, u32[]{:S(2)}, u32[]{:S(2)}) %collective-permute-start.5) | collective-permute-done | bytes 524320 | tf_op jit(solution)/shard_map/ppermute | solution.py:739
  49.5 2.8 collective-permute-done.4.refs_4_
  54.9 23.1 %mixer_forward.1 = (bf16[1024,1024]{1,0:T(8,128)(2,1)}, bf16[1024,1408]{1,0:T(8,128)(2,1)}, f32[1024,1024]{1,0:T(8,128)}, f32[1024,1024]{1,0:T(8,128)}, f32[1024...) custom-call(s32[1,4]{1,0:T(1,128)} %add_bitcast_fusion.spot_ref, ...), custom_call_target="tpu_custom_call" | custom-call | tf_op jit(solution)/shard_map/mixer_forward/pallas_call | solution.py:237
  78.0 9.2 %all-gather.2.cloned.1.call-done.refs_2_.refs_3_.gate_w_ref.out_w_ref = bf16[1024,2048]{1,0:T(8,128)(2,1)} async-done(((bf16[64,2048]{1,0:T(8,128)(2,1)}), bf16[1024,2048]{1,0:T(8,128)(2,1)}) %all-gather.2.cloned.1.call-update) | async-done | bytes 4194320 | tf_op jit(solution)/shard_map/all_gather | solution.py:814
  87.2 11.9 %gate_forward.1 = (bf16[1024,1024]{1,0:T(8,128)(2,1)}, f32[1024,1024]{1,0:T(8,128)}, f32[1024,1024]{1,0:T(8,128)}, f32[8,1024]{1,0:T(8,128)}) custom-call(s32[1,4]{1,0:T(1,128)} %add_bitcast_fusion.spot_ref, bf16[1024,1024]{1,0:T(8,128)(2,1)} %get-tuple-element.111.normed_ref, bf16[512,1024]{1,0:T(8,128)(2,1)} %refs_0_.1, bf16[512,1024]{1,0:T(8,128)(2,1)} %copy-done.11, ...), custom_call_target="tpu_custom_call" | custom-call | tf_op jit(solution)/shard_map/gate_forward/pallas_call | solution.py:538
  100.7 2.7 collective-permute-done.9.more_ref
  104.0 19.8 %gate_norm.1 = (bf16[1024,1024]{1,0:T(8,128)(2,1)}, f32[1024,1024]{1,0:T(8,128)}, f32[8,1024]{1,0:T(8,128)}, bf16[512,2048]{1,0:T(8,128)(2,1)}, bf16[512,2048]{1...) custom-call(s32[1,4]{1,0:T(1,128)} %add_bitcast_fusion.spot_ref, ...), custom_call_target="tpu_custom_call" | custom-call | tf_op jit(solution)/shard_map/gate_norm/pallas_call | solution.py:637
  128.8 20.6 %mixer_backward.3 = (bf16[512,1408]{1,0:T(8,128)(2,1)}, f32[8,1408]{1,0:T(8,128)}, f32[8,1024]{1,0:T(8,128)}, f32[8,256]{1,0:T(8,128)}, f32[128,1024]{1,0:T(8,128)}) custom-call(s32[1,4]{1,0:T(1,128)} %lengths_ref.7, f32[1024,1024]{1,0:T(8,128)} %get-tuple-element.121.upstream_ref, f32[1024,1024]{1,0:T(8,128)} %get-tuple-element.116.refs_5_.ssm_ref, ...), custom_call_target="tpu_custom_call" | custom-call | tf_op jit(solution)/shard_map/mixer_backward/pallas_call | solution.py:428
  149.4 2.4 add_convert_fusion
  157.6 2.0 collective-permute-start.15
  159.6 6.9 %input_terms.3 = bf16[512,1024]{1,0:T(8,128)(2,1)} custom-call(bf16[1024,1024]{1,0:T(8,128)(2,1)} %get-tuple-element.140.grad_gate_ref, bf16[512,1408]{1,0:T(8,128)(2,1)} %get-tuple-element.141.grads_ref.refs_2_, bf16[1024,2048]{1,0:T(8,128)(2,1)} %all-gather.2.cloned.1.call-done.refs_2_.refs_3_.gate_w_ref.out_w_ref, ...), custom_call_target="tpu_custom_call" | custom-call | tf_op jit(solution)/shard_map/input_terms/pallas_call | solution.py:692
  166.6 11.4 %mixer_backward.4 = (bf16[256,1408]{1,0:T(8,128)(2,1)}, f32[8,1408]{1,0:T(8,128)}, f32[8,1024]{1,0:T(8,128)}, f32[8,256]{1,0:T(8,128)}, f32[128,1024]{1,0:T(8,128)}) custom-call(s32[1,4]{1,0:T(1,128)} %lengths_ref.7, f32[1024,1024]{1,0:T(8,128)} %get-tuple-element.121.upstream_ref, f32[1024,1024]{1,0:T(8,128)} %get-tuple-element.116.refs_5_.ssm_ref, ...), custom_call_target="tpu_custom_call" | custom-call | tf_op jit(solution)/shard_map/mixer_backward/pallas_call | solution.py:428
  178.0 5.3 %input_terms.4 = bf16[256,1024]{1,0:T(8,128)(2,1)} custom-call(bf16[1024,1024]{1,0:T(8,128)(2,1)} %get-tuple-element.140.grad_gate_ref, bf16[256,1408]{1,0:T(8,128)(2,1)} %get-tuple-element.152.grads_ref.refs_1_, bf16[1024,2048]{1,0:T(8,128)(2,1)} %all-gather.2.cloned.1.call-done.refs_2_.refs_3_.gate_w_ref.out_w_ref, ...), custom_call_target="tpu_custom_call" | custom-call | tf_op jit(solution)/shard_map/input_terms/pallas_call | solution.py:692
  191.7 2.0 collective-permute-start.18
  195.4 2.8 fusion.3
  198.3 11.7 %mixer_backward.5 = (bf16[256,1408]{1,0:T(8,128)(2,1)}, f32[8,1408]{1,0:T(8,128)}, f32[8,1024]{1,0:T(8,128)}, f32[8,256]{1,0:T(8,128)}, f32[128,1024]{1,0:T(8,128)}) custom-call(s32[1,4]{1,0:T(1,128)} %lengths_ref.7, f32[1024,1024]{1,0:T(8,128)} %get-tuple-element.121.upstream_ref, f32[1024,1024]{1,0:T(8,128)} %get-tuple-element.116.refs_5_.ssm_ref, ...), custom_call_target="tpu_custom_call" | custom-call | tf_op jit(solution)/shard_map/mixer_backward/pallas_call | solution.py:428
  212.7 8.7 %weight_products.1 = (bf16[512,1408]{1,0:T(8,128)(2,1)}, bf16[512,1408]{1,0:T(8,128)(2,1)}, f32[8,2432]{1,0:T(8,128)}) custom-call(s32[1,4]{1,0:T(1,128)} %add_bitcast_fusion.spot_ref, bf16[1024,1024]{1,0:T(8,128)(2,1)} %get-tuple-element.111.normed_ref, bf16[1024,1408]{1,0:T(8,128)(2,1)} %get-tuple-element.142.weight_ref, f32[1,1024]{1,0:T(1,128)} %bitcast.104, ...), custom_call_target="tpu_custom_call" | custom-call | tf_op jit(solution)/shard_map/weight_products/pallas_call | solution.py:495
  221.3 5.2 %input_terms.5 = bf16[256,1024]{1,0:T(8,128)(2,1)} custom-call(bf16[1024,1024]{1,0:T(8,128)(2,1)} %get-tuple-element.140.grad_gate_ref, bf16[256,1408]{1,0:T(8,128)(2,1)} %get-tuple-element.167.grads_ref.refs_0_, bf16[1024,2048]{1,0:T(8,128)(2,1)} %all-gather.2.cloned.1.call-done.refs_2_.refs_3_.gate_w_ref.out_w_ref, ...), custom_call_target="tpu_custom_call" | custom-call | tf_op jit(solution)/shard_map/input_terms/pallas_call | solution.py:692
  228.5 3.7 %collective-permute-done.23 = f32[8,2432]{1,0:T(8,128)S(1)} collective-permute-done((f32[8,2432]{1,0:T(8,128)S(1)}, f32[8,2432]{1,0:T(8,128)S(1)}, u32[]{:S(2)}, u32[]{:S(2)}) %collective-permute-start.23) | collective-permute-done | bytes 77856 | tf_op jit(solution)/shard_map/ppermute | solution.py:711
  234.1 2.4 collective-permute-start.31
  236.5 2.0 collective-permute-start.32
  238.7 2.4 collective-permute-start.27
  241.4 2.1 collective-permute-start.28
  245.4 4.0 %collective-permute-done.26 = bf16[2,64,768]{2,1,0:T(8,128)(2,1)S(1)} collective-permute-done((bf16[2,64,768]{2,1,0:T(8,128)(2,1)S(1)}, bf16[2,64,768]{2,1,0:T(8,128)(2,1)S(1)}, u32[]{:S(2)}, u32[]{:S(2)}) %collective-permute-start.26) | collective-permute-done | bytes 196640 | tf_op jit(solution)/shard_map/ppermute | solution.py:711
  249.5 8.5 %collective-permute-done.27 = bf16[2,64,768]{2,1,0:T(8,128)(2,1)S(1)} collective-permute-done((bf16[2,64,768]{2,1,0:T(8,128)(2,1)S(1)}, bf16[2,64,768]{2,1,0:T(8,128)(2,1)S(1)}, u32[]{:S(2)}, u32[]{:S(2)}) %collective-permute-start.27) | collective-permute-done | bytes 196640 | tf_op jit(solution)/shard_map/ppermute | solution.py:711
  260.3 4.0 %collective-permute-start.34 = (bf16[64,640]{1,0:T(8,128)(2,1)S(1)}, bf16[64,640]{1,0:T(8,128)(2,1)S(1)}, u32[]{:S(2)}, u32[]{:S(2)}) collective-permute-start(bf16[64,640]{1,0:T(8,128)(2,1)S(1)} %get-tuple-element.226), channel_id=1, source_target_pairs={{0,8},{2,10},{4,12},{6,14},{8,0},{10,2},{12,4},{14,6},{16,24},{18,... | collective-permute-start | bytes 245768 | tf_op jit(solution)/shard_map/ppermute | solution.py:711
  264.7 2.0 collective-permute-start.36
  267.8 2.6 fusion.7
  (181 shorter events, 62.5 us)
Async XLA Ops:
  7.2 80.0 %all-gather.2.cloned.1.call-start = ((), (), s32[]{:S(2)}) async-start(), calls=%async_computation | async-start | bytes 4456448 | tf_op jit(solution)/shard_map/all_gather | solution.py:814
  11.1 14.6 %collective-permute-start = (bf16[64,1408]{1,0:T(8,128)(2,1)}, bf16[64,1408]{1,0:T(8,128)(2,1)}, u32[]{:S(2)}, u32[]{:S(2)}) collective-permute-start(bf16[64,1408]{1,0:T(8,128)(2,1)} %pad_maximum_fusion.4), channel_id=1, source_target_pairs={{0,8},{2,10},{4,12},{6,14},{8,0},{10,2},{12,4},{14,6},{16,24},{18,... | collective-permute-start | bytes 540680 | tf_op jit(solution)/shard_map/ppermute | solution.py:711
  14.1 16.4 %collective-permute-start.1 = (bf16[64,1408]{1,0:T(8,128)(2,1)}, bf16[64,1408]{1,0:T(8,128)(2,1)}, u32[]{:S(2)}, u32[]{:S(2)}) collective-permute-start(bf16[64,1408]{1,0:T(8,128)(2,1)} %pad_maximum_fusion.4), channel_id=1, source_target_pairs={{0,16},{2,18},{4,20},{6,22},{8,24},{10,26},{12,28},{14,30},{16,0},... | collective-permute-start | bytes 540680 | tf_op jit(solution)/shard_map/ppermute | solution.py:711
  16.7 13.8 %collective-permute-start.2 = (bf16[64,1408]{1,0:T(8,128)(2,1)}, bf16[64,1408]{1,0:T(8,128)(2,1)}, u32[]{:S(2)}, u32[]{:S(2)}) collective-permute-start(bf16[64,1408]{1,0:T(8,128)(2,1)} %pad_maximum_fusion.4), channel_id=1, source_target_pairs={{0,24},{2,26},{4,28},{6,30},{8,16},{10,18},{12,20},{14,22},{16,8},... | collective-permute-start | bytes 540680 | tf_op jit(solution)/shard_map/ppermute | solution.py:711
  19.3 13.4 %collective-permute-start.3 = (bf16[256,1024]{1,0:T(8,128)(2,1)}, bf16[256,1024]{1,0:T(8,128)(2,1)}, u32[]{:S(2)}, u32[]{:S(2)}) collective-permute-start(bf16[256,1024]{1,0:T(8,128)(2,1)} %get-tuple-element.219), channel_id=1, source_target_pairs={{0,1},{1,0},{2,3},{3,2},{4,5},{5,4},{6,7},{7,6},{8,9},{9,8},{10,11... | collective-permute-start | bytes 1572872 | tf_op jit(solution)/shard_map/ppermute | solution.py:739
  32.7 19.6 %collective-permute-start.4 = (bf16[256,1408]{1,0:T(8,128)(2,1)}, bf16[256,1408]{1,0:T(8,128)(2,1)}, u32[]{:S(2)}, u32[]{:S(2)}) collective-permute-start(bf16[256,1408]{1,0:T(8,128)(2,1)} %pad_maximum_fusion.1.refs_3_), channel_id=1, source_target_pairs={{0,4},{2,6},{4,0},{6,2},{8,12},{10,14},{12,8},{14,10},{16,20},{18,... | collective-permute-start | bytes 2162696 | tf_op jit(solution)/shard_map/ppermute | solution.py:711
  34.3 15.2 %collective-permute-start.5 = (bf16[256,1024]{1,0:T(8,128)(2,1)}, bf16[256,1024]{1,0:T(8,128)(2,1)}, u32[]{:S(2)}, u32[]{:S(2)}) collective-permute-start(bf16[256,1024]{1,0:T(8,128)(2,1)} %get-tuple-element.218), channel_id=1, source_target_pairs={{0,1},{1,0},{2,3},{3,2},{4,5},{5,4},{6,7},{7,6},{8,9},{9,8},{10,11... | collective-permute-start | bytes 1572872 | tf_op jit(solution)/shard_map/ppermute | solution.py:739
  35.8 42.2 %collective-permute-start.8 = (bf16[512,1024]{1,0:T(8,128)(2,1)S(1)}, bf16[512,1024]{1,0:T(8,128)(2,1)S(1)}, u32[]{:S(2)}, u32[]{:S(2)}) collective-permute-start(bf16[512,1024]{1,0:T(8,128)(2,1)S(1)} %copy-done.5), channel_id=1, source_target_pairs={{0,1},{1,0},{2,3},{3,2},{4,5},{5,4},{6,7},{7,6},{8,9},{9,8},{10,11... | collective-permute-start | bytes 3145736 | tf_op jit(solution)/shard_map/ppermute | solution.py:739
  36.3 16.6 %collective-permute-start.6 = (bf16[256,1408]{1,0:T(8,128)(2,1)}, bf16[256,1408]{1,0:T(8,128)(2,1)}, u32[]{:S(2)}, u32[]{:S(2)}) collective-permute-start(bf16[256,1408]{1,0:T(8,128)(2,1)} %pad_maximum_fusion.1.refs_3_), channel_id=1, source_target_pairs={{0,2},{2,0},{4,6},{6,4},{8,10},{10,8},{12,14},{14,12},{16,18},{18,... | collective-permute-start | bytes 2162696 | tf_op jit(solution)/shard_map/ppermute | solution.py:711
  123.8 25.6 %collective-permute-start.10 = (bf16[512,2048]{1,0:T(8,128)(2,1)}, bf16[512,2048]{1,0:T(8,128)(2,1)}, u32[]{:S(2)}, u32[]{:S(2)}) collective-permute-start(bf16[512,2048]{1,0:T(8,128)(2,1)} %get-tuple-element.134), channel_id=1, source_target_pairs={{0,2},{2,0},{4,6},{6,4},{8,10},{10,8},{12,14},{14,12},{16,18},{18,... | collective-permute-start | bytes 6291464 | tf_op jit(solution)/shard_map/ppermute | solution.py:711
  124.7 61.7 %collective-permute-start.11 = (bf16[512,1024]{1,0:T(8,128)(2,1)}, bf16[512,1024]{1,0:T(8,128)(2,1)}, u32[]{:S(2)}, u32[]{:S(2)}) collective-permute-start(bf16[512,1024]{1,0:T(8,128)(2,1)} %get-tuple-element.153), channel_id=1, source_target_pairs={{0,1},{1,0},{2,3},{3,2},{4,5},{5,4},{6,7},{7,6},{8,9},{9,8},{10,11... | collective-permute-start | bytes 3145736 | tf_op jit(solution)/shard_map/ppermute | solution.py:739
  153.8 32.4 %collective-permute-start.12 = (bf16[4,64,1024]{2,1,0:T(8,128)(2,1)}, bf16[4,64,1024]{2,1,0:T(8,128)(2,1)S(1)}, u32[]{:S(2)}, u32[]{:S(2)}) collective-permute-start(bf16[4,64,1024]{2,1,0:T(8,128)(2,1)} %dynamic-slice_bitcast_fusion), channel_id=1, source_target_pairs={{0,4},{2,6},{4,0},{6,2},{8,12},{10,14},{12,8},{14,10},{16,20},{18,... | collective-permute-start | bytes 1572872 | tf_op jit(solution)/shard_map/ppermute | solution.py:711
  155.2 28.9 %collective-permute-start.13 = (bf16[2,64,1024]{2,1,0:T(8,128)(2,1)}, bf16[2,64,1024]{2,1,0:T(8,128)(2,1)S(1)}, u32[]{:S(2)}, u32[]{:S(2)}) collective-permute-start(bf16[2,64,1024]{2,1,0:T(8,128)(2,1)} %get-tuple-element.215), channel_id=1, source_target_pairs={{0,8},{2,10},{4,12},{6,14},{8,0},{10,2},{12,4},{14,6},{16,24},{18,... | collective-permute-start | bytes 786440 | tf_op jit(solution)/shard_map/ppermute | solution.py:711
  156.7 27.5 %collective-permute-start.14 = (bf16[2,64,1024]{2,1,0:T(8,128)(2,1)}, bf16[2,64,1024]{2,1,0:T(8,128)(2,1)}, u32[]{:S(2)}, u32[]{:S(2)}) collective-permute-start(bf16[2,64,1024]{2,1,0:T(8,128)(2,1)} %get-tuple-element.217), channel_id=1, source_target_pairs={{0,16},{2,18},{4,20},{6,22},{8,24},{10,26},{12,28},{14,30},{16,0},... | collective-permute-start | bytes 786440 | tf_op jit(solution)/shard_map/ppermute | solution.py:711
  157.6 27.3 %collective-permute-start.15 = (bf16[2,64,1024]{2,1,0:T(8,128)(2,1)}, bf16[2,64,1024]{2,1,0:T(8,128)(2,1)}, u32[]{:S(2)}, u32[]{:S(2)}) collective-permute-start(bf16[2,64,1024]{2,1,0:T(8,128)(2,1)} %get-tuple-element.216), channel_id=1, source_target_pairs={{0,24},{2,26},{4,28},{6,30},{8,16},{10,18},{12,20},{14,22},{16,8},... | collective-permute-start | bytes 786440 | tf_op jit(solution)/shard_map/ppermute | solution.py:711
  187.1 22.9 %collective-permute-start.19 = (bf16[64,1024]{1,0:T(8,128)(2,1)}, bf16[64,1024]{1,0:T(8,128)(2,1)}, u32[]{:S(2)}, u32[]{:S(2)}) collective-permute-start(bf16[64,1024]{1,0:T(8,128)(2,1)} %dynamic-slice_bitcast_fusion.8), channel_id=1, source_target_pairs={{0,4},{2,6},{4,0},{6,2},{8,12},{10,14},{12,8},{14,10},{16,20},{18,... | collective-permute-start | bytes 393224 | tf_op jit(solution)/shard_map/ppermute | solution.py:711
  189.4 22.2 %collective-permute-start.16 = (bf16[64,1024]{1,0:T(8,128)(2,1)}, bf16[64,1024]{1,0:T(8,128)(2,1)S(1)}, u32[]{:S(2)}, u32[]{:S(2)}) collective-permute-start(bf16[64,1024]{1,0:T(8,128)(2,1)} %get-tuple-element.223), channel_id=1, source_target_pairs={{0,8},{2,10},{4,12},{6,14},{8,0},{10,2},{12,4},{14,6},{16,24},{18,... | collective-permute-start | bytes 393224 | tf_op jit(solution)/shard_map/ppermute | solution.py:711
  190.0 21.6 %collective-permute-start.17 = (bf16[64,1024]{1,0:T(8,128)(2,1)}, bf16[64,1024]{1,0:T(8,128)(2,1)}, u32[]{:S(2)}, u32[]{:S(2)}) collective-permute-start(bf16[64,1024]{1,0:T(8,128)(2,1)} %get-tuple-element.225), channel_id=1, source_target_pairs={{0,16},{2,18},{4,20},{6,22},{8,24},{10,26},{12,28},{14,30},{16,0},... | collective-permute-start | bytes 393224 | tf_op jit(solution)/shard_map/ppermute | solution.py:711
  191.7 19.9 %collective-permute-start.18 = (bf16[64,1024]{1,0:T(8,128)(2,1)}, bf16[64,1024]{1,0:T(8,128)(2,1)}, u32[]{:S(2)}, u32[]{:S(2)}) collective-permute-start(bf16[64,1024]{1,0:T(8,128)(2,1)} %get-tuple-element.224), channel_id=1, source_target_pairs={{0,24},{2,26},{4,28},{6,30},{8,16},{10,18},{12,20},{14,22},{16,8},... | collective-permute-start | bytes 393224 | tf_op jit(solution)/shard_map/ppermute | solution.py:711
  193.7 18.9 %collective-permute-start.20 = (bf16[256,1024]{1,0:T(8,128)(2,1)}, bf16[256,1024]{1,0:T(8,128)(2,1)S(1)}, u32[]{:S(2)}, u32[]{:S(2)}) collective-permute-start(bf16[256,1024]{1,0:T(8,128)(2,1)} %slice_select_fusion.1), channel_id=1, source_target_pairs={{0,1},{1,0},{2,3},{3,2},{4,5},{5,4},{6,7},{7,6},{8,9},{9,8},{10,11... | collective-permute-start | bytes 1572872 | tf_op jit(solution)/shard_map/ppermute | solution.py:739
  221.3 10.9 %collective-permute-start.21 = (bf16[512,1408]{1,0:T(8,128)(2,1)}, bf16[512,1408]{1,0:T(8,128)(2,1)}, u32[]{:S(2)}, u32[]{:S(2)}) collective-permute-start(bf16[512,1408]{1,0:T(8,128)(2,1)} %get-tuple-element.171), channel_id=1, source_target_pairs={{0,2},{2,0},{4,6},{6,4},{8,10},{10,8},{12,14},{14,12},{16,18},{18,... | collective-permute-start | bytes 4325384 | tf_op jit(solution)/shard_map/ppermute | solution.py:711
  234.1 9.6 %collective-permute-start.31 = (f32[8,2432]{1,0:T(8,128)S(1)}, f32[8,2432]{1,0:T(8,128)S(1)}, u32[]{:S(2)}, u32[]{:S(2)}) collective-permute-start(f32[8,2432]{1,0:T(8,128)S(1)} %add_add_fusion.1), channel_id=1, source_target_pairs={{0,16},{2,18},{4,20},{6,22},{8,24},{10,26},{12,28},{14,30},{16,0},... | collective-permute-start | bytes 233480 | tf_op jit(solution)/shard_map/ppermute | solution.py:711
  236.5 8.6 %collective-permute-start.32 = (f32[8,2432]{1,0:T(8,128)S(1)}, f32[8,2432]{1,0:T(8,128)S(1)}, u32[]{:S(2)}, u32[]{:S(2)}) collective-permute-start(f32[8,2432]{1,0:T(8,128)S(1)} %add_add_fusion.1), channel_id=1, source_target_pairs={{0,24},{2,26},{4,28},{6,30},{8,16},{10,18},{12,20},{14,22},{16,8},... | collective-permute-start | bytes 233480 | tf_op jit(solution)/shard_map/ppermute | solution.py:711
  238.7 10.8 %collective-permute-start.26 = (bf16[2,64,768]{2,1,0:T(8,128)(2,1)S(1)}, bf16[2,64,768]{2,1,0:T(8,128)(2,1)S(1)}, u32[]{:S(2)}, u32[]{:S(2)}) collective-permute-start(bf16[2,64,768]{2,1,0:T(8,128)(2,1)S(1)} %get-tuple-element.220), channel_id=1, source_target_pairs={{0,8},{2,10},{4,12},{6,14},{8,0},{10,2},{12,4},{14,6},{16,24},{18,... | collective-permute-start | bytes 589832 | tf_op jit(solution)/shard_map/ppermute | solution.py:711
  238.7 19.3 %collective-permute-start.27 = (bf16[2,64,768]{2,1,0:T(8,128)(2,1)S(1)}, bf16[2,64,768]{2,1,0:T(8,128)(2,1)S(1)}, u32[]{:S(2)}, u32[]{:S(2)}) collective-permute-start(bf16[2,64,768]{2,1,0:T(8,128)(2,1)S(1)} %get-tuple-element.222), channel_id=1, source_target_pairs={{0,16},{2,18},{4,20},{6,22},{8,24},{10,26},{12,28},{14,30},{16,0},... | collective-permute-start | bytes 589832 | tf_op jit(solution)/shard_map/ppermute | solution.py:711
  241.4 16.6 %collective-permute-start.28 = (bf16[2,64,768]{2,1,0:T(8,128)(2,1)S(1)}, bf16[2,64,768]{2,1,0:T(8,128)(2,1)S(1)}, u32[]{:S(2)}, u32[]{:S(2)}) collective-permute-start(bf16[2,64,768]{2,1,0:T(8,128)(2,1)S(1)} %get-tuple-element.221), channel_id=1, source_target_pairs={{0,24},{2,26},{4,28},{6,30},{8,16},{10,18},{12,20},{14,22},{16,8},... | collective-permute-start | bytes 589832 | tf_op jit(solution)/shard_map/ppermute | solution.py:711
  243.7 14.4 %collective-permute-start.25 = (bf16[4,64,640]{2,1,0:T(8,128)(2,1)S(1)}, bf16[4,64,640]{2,1,0:T(8,128)(2,1)S(1)}, u32[]{:S(2)}, u32[]{:S(2)}) collective-permute-start(bf16[4,64,640]{2,1,0:T(8,128)(2,1)S(1)} %dynamic-slice_bitcast_fusion.1), channel_id=1, source_target_pairs={{0,4},{2,6},{4,0},{6,2},{8,12},{10,14},{12,8},{14,10},{16,20},{18,... | collective-permute-start | bytes 983048 | tf_op jit(solution)/shard_map/ppermute | solution.py:711
  245.0 13.2 %collective-permute-start.29 = (bf16[256,1024]{1,0:T(8,128)(2,1)S(1)}, bf16[256,1024]{1,0:T(8,128)(2,1)S(1)}, u32[]{:S(2)}, u32[]{:S(2)}) collective-permute-start(bf16[256,1024]{1,0:T(8,128)(2,1)S(1)} %slice_select_fusion), channel_id=1, source_target_pairs={{0,1},{1,0},{2,3},{3,2},{4,5},{5,4},{6,7},{7,6},{8,9},{9,8},{10,11... | collective-permute-start | bytes 1572872 | tf_op jit(solution)/shard_map/ppermute | solution.py:739
  258.9 14.5 %collective-permute-start.37 = (bf16[64,768]{1,0:T(8,128)(2,1)S(1)}, bf16[64,768]{1,0:T(8,128)(2,1)S(1)}, u32[]{:S(2)}, u32[]{:S(2)}) collective-permute-start(bf16[64,768]{1,0:T(8,128)(2,1)S(1)} %dynamic-slice_bitcast_fusion.12), channel_id=1, source_target_pairs={{0,4},{2,6},{4,0},{6,2},{8,12},{10,14},{12,8},{14,10},{16,20},{18,... | collective-permute-start | bytes 294920 | tf_op jit(solution)/shard_map/ppermute | solution.py:711
  260.3 13.0 %collective-permute-start.34 = (bf16[64,640]{1,0:T(8,128)(2,1)S(1)}, bf16[64,640]{1,0:T(8,128)(2,1)S(1)}, u32[]{:S(2)}, u32[]{:S(2)}) collective-permute-start(bf16[64,640]{1,0:T(8,128)(2,1)S(1)} %get-tuple-element.226), channel_id=1, source_target_pairs={{0,8},{2,10},{4,12},{6,14},{8,0},{10,2},{12,4},{14,6},{16,24},{18,... | collective-permute-start | bytes 245768 | tf_op jit(solution)/shard_map/ppermute | solution.py:711
  264.3 9.0 %collective-permute-start.35 = (bf16[64,640]{1,0:T(8,128)(2,1)S(1)}, bf16[64,640]{1,0:T(8,128)(2,1)S(1)}, u32[]{:S(2)}, u32[]{:S(2)}) collective-permute-start(bf16[64,640]{1,0:T(8,128)(2,1)S(1)} %get-tuple-element.228), channel_id=1, source_target_pairs={{0,16},{2,18},{4,20},{6,22},{8,24},{10,26},{12,28},{14,30},{16,0},... | collective-permute-start | bytes 245768 | tf_op jit(solution)/shard_map/ppermute | solution.py:711
  264.7 8.6 %collective-permute-start.36 = (bf16[64,640]{1,0:T(8,128)(2,1)S(1)}, bf16[64,640]{1,0:T(8,128)(2,1)S(1)}, u32[]{:S(2)}, u32[]{:S(2)}) collective-permute-start(bf16[64,640]{1,0:T(8,128)(2,1)S(1)} %get-tuple-element.227), channel_id=1, source_target_pairs={{0,24},{2,26},{4,28},{6,30},{8,16},{10,18},{12,20},{14,22},{16,8},... | collective-permute-start | bytes 245768 | tf_op jit(solution)/shard_map/ppermute | solution.py:711
  (32 other events, 234.8 us)
Sparse Core Ops, SparseCore 0:
  32.9 54.3 all-gather.1

commit v2 on v1

--- a/solution.py
+++ b/solution.py
@@ -110,7 +110,19 @@
         core = spot_ref[0, 3] ^ (i // 2)
         for k in range(count):
             at = (((spot_ref[0, 1] ^ k) * 2 + along) * 2 + core) * rows
-            weight_ref[pl.ds(pl.multiple_of(at, rows), rows), :] = ref[k * rows : (k + 1) * rows, :]
+            at = pl.ds(pl.multiple_of(at, rows), rows)
+            weight_ref[at, :] = ref[k * rows : (k + 1) * rows, :]
+
+
+def place_pairs(spot_ref, weight_ref, sources, count, lo):
+    rows = weight_ref.shape[0] // (4 * count)
+    for i, (ref, begin) in enumerate(sources):
+        core = spot_ref[0, 3] ^ (i // count)
+        for j in range(2):
+            at = (((spot_ref[0, 1] ^ (i % count)) * 2 + (spot_ref[0, 2] ^ j)) * 2 + core) * rows
+            at = pl.ds(pl.multiple_of(at, rows), rows)
+            here = begin + j * rows
+            weight_ref[at, lo : lo + ref.shape[1]] = ref[here : here + rows, :]
 
 
 def split_cores(spot_ref, value_ref, keep_ref, send_ref, chips):
@@ -465,47 +477,67 @@
 
 def gain_row(weight_ref, total_ref, columns):
     rows = weight_ref.shape[0]
+    begin, end = columns
     added = jnp.zeros((rows, LANES), f32)
-    for lo in range(0, columns, LANES):
-        added = added + weight_ref[:, lo : lo + LANES].astype(f32) * total_ref[:, lo : lo + LANES]
+    for lo in range(begin, end, LANES):
+        weight = weight_ref[:, lo : lo + LANES].astype(f32)
+        added = added + weight * total_ref[:, lo - begin : lo - begin + LANES]
     return jnp.sum(jnp.transpose(added), axis=0, keepdims=True)
 
 
-def product_kernel(chips, spot_ref, normed_ref, weight_ref, gain_ref, sums_ref, norm_sum_ref, *refs):
+def product_kernel(chips, columns, last, spot_ref, normed_ref, weight_ref, gain_ref, sums_ref,
+                   norm_sum_ref, *refs):
     grads, (keep_ref, send_ref, packed_ref, total) = refs[:-4], refs[-4:]
-    known = sums_ref.shape[1]
+    lo, hi = columns
     at = 0
     for i, ref in enumerate(grads):
         rows = ref.shape[0]
-        added = mm(normed_ref[at : at + rows, :], ref[...], TN)
+        added = mm(normed_ref[at : at + rows, :], ref[:, lo:hi], TN)
         total[...] = added if i == 0 else total[...] + added
         at += rows
     split_cores(spot_ref, total, keep_ref, send_ref, chips)
-    packed_ref[:, :known] = sums_ref[...]
-    packed_ref[:, known:] = norm_sum_ref[...]
-    row = norm_sum_ref[0:1, :] + gain_row(weight_ref, total, known)
-    packed_ref[0:1, known:] = row / gain_ref[...]
-
-
-def weight_products(spot, normed, weight, gain, sums, norm_sum, grads, chips):
+    row = norm_sum_ref[0:1, :] + gain_row(weight_ref, total, columns)
+    known = sums_ref.shape[1]
+    if last:
+        packed_ref[:, :known] = sums_ref[...]
+        packed_ref[:, known:] = jnp.broadcast_to(row / gain_ref[...], norm_sum_ref.shape)
+    else:
+        packed_ref[...] = jnp.broadcast_to(row, norm_sum_ref.shape)
+
+
+def weight_products(spot, normed, weight, gain, sums, norm_sum, grads, chips, columns, last):
     known = grads[0].shape[1]
     model = normed.shape[1]
-    part = jax.ShapeDtypeStruct((model // 2, known), bf16)
+    size = columns[1] - columns[0]
+    part = jax.ShapeDtypeStruct((model // 2, size), bf16)
     vmem = pl.BlockSpec(memory_space=pltpu.VMEM)
     return pl.pallas_call(
-        partial(product_kernel, chips),
+        partial(product_kernel, chips, columns, last),
         in_specs=[pl.BlockSpec(memory_space=pltpu.SMEM), *[vmem for _ in range(5 + len(grads))]],
         out_specs=[vmem, vmem, vmem],
-        out_shape=[part, part, jax.ShapeDtypeStruct((TAIL, known + model), f32)],
-        scratch_shapes=[pltpu.VMEM((model, known), f32)],
+        out_shape=[
+            part, part, jax.ShapeDtypeStruct((TAIL, known + model if last else model), f32),
+        ],
+        scratch_shapes=[pltpu.VMEM((model, size), f32)],
         compiler_params=pltpu.CompilerParams(vmem_limit_bytes=LIMIT),
         name="weight_products",
     )(spot, normed, weight, gain, sums, norm_sum, *grads)
 
 
-def gate_kernel(pieces, spot_ref, normed_ref, *refs):
+def gate_kernel(pieces, count, spot_ref, normed_ref, *refs):
     own_ref, others = refs[0], refs[1:pieces]
-    gate_w_ref, out_w_ref, gain_ref, ssm_ref, upstream_ref, gate_ref, grad_ref, sums_ref = refs[pieces:]
+    joined, sources = refs[pieces : pieces + 2], refs[pieces + 2 : pieces + 2 + 2 * count]
+    (
+        gain_ref, ssm_ref, upstream_ref, weight_ref, gate_ref, grad_ref, sums_ref
+    ) = refs[pieces + 2 + 2 * count :]
+
+    @pl.when(pl.program_id(0) == 0)
+    def _():
+        each = joined[0].shape[0] // count
+        rows = [(ref, k * each) for ref in joined for k in range(count)]
+        place_pairs(spot_ref, weight_ref, rows, count, 0)
+        place_pairs(spot_ref, weight_ref, [(ref, 0) for ref in sources], count, joined[0].shape[1])
+
     rows, channels = ssm_ref.shape
     normed = normed_ref[...]
     upstream = rows_of(pl.program_id(0), pl.num_programs(0), spot_ref, own_ref, others)
@@ -515,8 +547,8 @@
     step = 2 * LANES
     for lo in range(0, channels, step):
         hi = lo + step
-        gate = mm(normed, gate_w_ref[:, lo:hi], NN)
-        grad = mm(upstream, out_w_ref[:, lo:hi], NN)
+        gate = mm(normed, weight_ref[:, lo:hi], NN)
+        grad = mm(upstream, weight_ref[:, channels + lo : channels + hi], NN)
         gate_ref[:, lo:hi] = gate
         grad_ref[:, lo:hi] = grad
         gated = ssm_ref[:, lo:hi] * (gate * sigmoid(gate))
@@ -531,24 +563,24 @@
     sums_ref[...] = jnp.transpose(both)[0:TAIL, :]
 
 
-def gate_forward(spot, normed, own, others, weight, gain, ssm, span):
+def gate_forward(spot, normed, own, others, sources, count, gain, ssm, span):
     rows, model = normed.shape
     channels = ssm.shape[1]
     by_row = lambda cols: pl.BlockSpec((span, cols), lambda i: (i, 0))
     return pl.pallas_call(
-        partial(gate_kernel, 1 + len(others)),
+        partial(gate_kernel, 1 + len(others), count),
         grid=(rows // span,),
         in_specs=[
             pl.BlockSpec(memory_space=pltpu.SMEM), by_row(model), *own_specs(own, others, span),
-            pl.BlockSpec((model, channels), lambda i: (0, 0)),
-            pl.BlockSpec((model, channels), lambda i: (0, 1)), full(gain.shape), by_row(channels),
+            *[full(x.shape) for x in sources], full(gain.shape), by_row(channels),
         ],
         out_specs=[
-            by_row(model), by_row(channels), by_row(channels),
+            by_row(model), full((model, 2 * channels)), by_row(channels), by_row(channels),
             pl.BlockSpec((TAIL, span), lambda i: (0, i)),
         ],
         out_shape=[
             jax.ShapeDtypeStruct((rows, model), bf16),
+            jax.ShapeDtypeStruct((model, 2 * channels), bf16),
             jax.ShapeDtypeStruct((rows, channels), f32),
             jax.ShapeDtypeStruct((rows, channels), f32),
             jax.ShapeDtypeStruct((TAIL, rows), f32),
@@ -557,7 +589,7 @@
             dimension_semantics=("arbitrary",), vmem_limit_bytes=LIMIT
         ),
         name="gate_forward",
-    )(spot, normed, own, *others, weight, weight, gain, ssm)
+    )(spot, normed, own, *others, *sources, gain, ssm)
 
 
 def norm_kernel(full_inner, chips, split, spot_ref, sums_ref, more_ref, gate_ref, grad_ref, ssm_ref,
@@ -589,9 +621,7 @@
         normal = gated * scale
         scaled_low = (normal * gain).astype(bf16)
         scaled[:, lo:hi] = scaled_low
-        gain_sum_ref[:, lo:hi] += jnp.broadcast_to(
-            jnp.sum(grad * normal, axis=0, keepdims=True), (TAIL, step)
-        )
+        gain_sum_ref[TAIL - 1 : TAIL, lo:hi] += jnp.sum(grad * normal, axis=0, keepdims=True)
         grad_gated = scale * (grad * gain) - gated * pull
         grad_ssm_ref[:, lo:hi] = grad_gated * silu
         grad_gate = (grad_gated * ssm * (sig * (1.0 + gate * (1.0 - sig)))).astype(bf16)
@@ -621,11 +651,11 @@
     def _():
         split_cores(spot_ref, totals, keep_ref, send_ref, chips)
         norm_sum_ref[...] = jnp.zeros_like(norm_sum_ref)
-        norm_sum_ref[0:1, :] = gain_row(gate_w_ref, totals, channels)
+        norm_sum_ref[0:1, :] = gain_row(gate_w_ref, totals, (0, channels))
 
 
 def gate_norm(
-    spot, sums, more, gate, grad, ssm, gain, normed, upstream, weight, full_inner, chips, split, span
+    spot, sums, more, gate, grad, ssm, gain, normed, upstream, weight, known, full_inner, chips, split, span
 ):
     rows, channels = gate.shape
     model = normed.shape[1]
@@ -644,13 +674,13 @@
             pl.BlockSpec((model, channels), lambda i: (0, 1)),
         ],
         out_specs=[
-            by_row(channels), by_row(channels), full((TAIL, channels)), full(half), full(half),
+            by_row(channels), by_row(channels), full((TAIL, known)), full(half), full(half),
             full(mine), full(theirs), full((TAIL, model)),
         ],
         out_shape=[
             jax.ShapeDtypeStruct((rows, channels), bf16),
             jax.ShapeDtypeStruct((rows, channels), f32),
-            jax.ShapeDtypeStruct((TAIL, channels), f32),
+            jax.ShapeDtypeStruct((TAIL, known), f32),
             jax.ShapeDtypeStruct(half, bf16),
             jax.ShapeDtypeStruct(half, bf16),
             jax.ShapeDtypeStruct(mine, bf16),
@@ -715,36 +745,51 @@
     return [4 * k for k in range(1, lax.axis_size("dp") // 4)]
 
 
+def long_bits():
+    bits, bit = [], 4
+    while bit < lax.axis_size("dp"):
+        bits.append(bit)
+        bit *= 2
+    return bits
+
+
 def choose(stacked, index, axis):
     return lax.dynamic_index_in_dim(stacked, index, axis, keepdims=False)
 
 
+def send_fold(parts, bit, axis):
+    mine = (lax.axis_index("dp") // bit) % 2
+    return dp_send(choose(parts, 1 - mine, axis), bit)
+
+
+def keep_fold(parts, got, bit, axis):
+    mine = (lax.axis_index("dp") // bit) % 2
+    return choose(parts, mine, axis).astype(f32) + got.astype(f32)
+
+
 def fold(parts, bit, axis):
-    mine = (lax.axis_index("dp") // bit) % 2
-    got = dp_send(choose(parts, 1 - mine, axis), bit)
-    return choose(parts, mine, axis).astype(f32) + got.astype(f32)
-
-
-def fold_chips(parts):
+    return keep_fold(parts, send_fold(parts, bit, axis), bit, axis)
+
+
+def send_chips(parts):
     place = lax.axis_index("dp") // 4
     sends = parts.astype(bf16)
-    total = choose(parts, place, 0)
-    got = [dp_send(choose(sends, place ^ (bit // 4), 0), bit) for bit in chip_bits()]
+    return [dp_send(choose(sends, place ^ (bit // 4), 0), bit) for bit in chip_bits()]
+
+
+def keep_chips(parts, got):
+    total = choose(parts, lax.axis_index("dp") // 4, 0).astype(f32)
     for piece in got:
         total = total + piece.astype(f32)
     return total
 
 
+def fold_chips(parts):
+    return keep_chips(parts, send_chips(parts))
+
+
 def tensor_swap(value):
     return lax.ppermute(value, "tensor", [(0, 1), (1, 0)])
-
-
-def sum_chips(value):
-    bits = chip_bits()
-    pieces = [value] + [dp_send(value, bit) for bit in bits]
-    while len(pieces) > 1:
-        pieces = [a + b for a, b in zip(pieces[0::2], pieces[1::2])]
-    return pieces[0]
 
 
 def gather_other(own, size):
@@ -807,15 +852,27 @@
         spread_map(heads, channels),
     )
     late = jnp.concatenate([zx_weight[:, 0, :], out_weight], axis=1)
-    column = jnp.concatenate([early] + [dp_send(early, bit) for bit in chip_bits()], axis=0)
-    column, late, top, fixed = lax.optimization_barrier(
-        (column, late, gather_other(normed_rows[:half], size), fixed)
-    )
-    weight_late = lax.all_gather(late, "dp", axis=0, tiled=True)
+    zeros = (
+        jnp.zeros((TAIL, channels), f32), jnp.zeros((TAIL, width), f32),
+        jnp.zeros((width // 2, channels), f32),
+    )
+
+    def along(value):
+        return [value] + [dp_send(value, bit) for bit in chip_bits()]
+
+    column = jnp.concatenate(along(early), axis=0)
+    column, pair, top, fixed, zeros, spot = lax.optimization_barrier((
+        column, jnp.concatenate([late, dp_send(late, 2)], axis=0),
+        gather_other(normed_rows[:half], size), fixed, zeros, spot,
+    ))
+    cut_late = (2 * channels * 3 // 8) // LANES * LANES
+    joined = along(pair[:, :cut_late])
+    by_x, column, bottom, joined, pair = lax.optimization_barrier(
+        (dp_send(column, 2), column, gather_other(normed_rows[half:], size), joined, pair)
+    )
+    joined = jnp.concatenate(joined, axis=0)
+    pairs = along(pair[:, cut_late:])
     by_core = dp_send(column, 1)
-    by_x, bottom = lax.optimization_barrier(
-        (dp_send(column, 2), gather_other(normed_rows[half:], size))
-    )
     sources = (column, by_x, by_core, dp_send(by_x, 1))
     own, others = normed_rows, (top, bottom)
     if not split:
@@ -825,18 +882,19 @@
     )
     _, _, _, _, _, rate, skip, spread = fixed
     gain = gate_gain[None, :]
-    other, ssm, weight_late = lax.optimization_barrier(
-        (gather_other(cotangent, size), saved[0], weight_late)
-    )
+    other, ssm, joined_core, pairs = lax.optimization_barrier(
+        (gather_other(cotangent, size), saved[0], dp_send(joined, 1), pairs)
+    )
+    sources = (joined, joined_core, *pairs, *[dp_send(pair, 1) for pair in pairs])
     own, others = (cotangent, (other,)) if split else (other, ())
-    upstream, gate, grad, sums = gate_forward(
-        spot, normed, own, others, weight_late, gain, ssm, SPAN
+    upstream, weight_late, gate, grad, sums = gate_forward(
+        spot, normed, own, others, sources, count, gain, ssm, SPAN
     )
     more = gather_other(sums, size) if split else sums
     sums = sums if split else lax.psum(sums, "tensor")
     chips = 2 * count
     grad_gate, grad_ssm, gain_sum, keep, send, branch_own, branch_send, norm_sum = gate_norm(
-        spot, sums, more, gate, grad, ssm, gain, normed, upstream, weight_late, channels * size,
+        spot, sums, more, gate, grad, ssm, gain, normed, upstream, weight_late, known, channels * size,
         chips, split, SPAN,
     )
     if split:
@@ -845,12 +903,8 @@
         branch_own = lax.psum_scatter(branch_own, "tensor", scatter_dimension=0, tiled=True)
         branch_other = jnp.zeros_like(branch_own)
     quarter = grad_ssm.shape[0] // SPAN // 4
-    carry = (
-        jnp.pad(gain_sum[:1], ((TAIL - 1, 0), (0, known - channels))),
-        jnp.zeros((TAIL, channels), f32),
-        jnp.zeros((TAIL, width), f32),
-        jnp.zeros((width // 2, channels), f32),
-    )
+    carry = (gain_sum, *zeros)
+
     def back(begin, end, carry):
         return mixer_backward(
             lengths, grad_ssm, saved, conv_inner, conv_shared, rate, skip, spread, carry,
@@ -885,20 +939,31 @@
         (carry[0], part_gate, part_out, grads0, other1, block_out)
     )
     keep, send, sums = weight_products(
-        spot, normed, weight, norm_gain[None, :], sums, norm_sum, (grads0, grads1, grads2), chips
+        spot, normed, weight, norm_gain[None, :], sums, norm_sum, (grads0, grads1, grads2), chips,
+        (0, known), True,
     )
     got = dp_send(send, 1)
-    sums = (sums + dp_send(sums, 1)) + (dp_send(sums, 2) + dp_send(sums, 3))
     terms0 = terms_of(0, grads0)
     send0 = pick_half(terms2[: terms2.shape[0] // 2], terms0, size)
     parts = (keep.astype(f32) + got.astype(f32)).astype(bf16).reshape(count, 2, -1, known)
     parts, sums, send0 = lax.optimization_barrier((parts, sums, send0))
+    cut = min((known * 2 // 3) // LANES * LANES, channels)
+    parts_a, parts_b = parts[..., :cut], parts[..., cut:]
+    got_b = send_chips(parts_b)
+    sums = sums + dp_send(sums, 1)
+    got_a = send_fold(parts_a, 2, 1)
+    sums = sums + dp_send(sums, 2)
+    sums = sums + dp_send(sums, 4)
+    send0, sums = lax.optimization_barrier((send0, sums))
     other0 = gather_other(send0, size) if split else send0
-    cut = (known // (2 * LANES)) * LANES
-    parts_a = fold(parts[..., :cut], 2, 1)
-    parts_b = fold_chips(parts[..., cut:]).astype(bf16)
-    sums = sum_chips(sums)
-    parts_a, parts_b, other0, sums = lax.optimization_barrier((parts_a, parts_b, other0, sums))
+    got_a, got_b, sums = lax.optimization_barrier((got_a, got_b, sums))
+    parts_a = keep_fold(parts_a, got_a, 2, 1)
+    parts_b = keep_chips(parts_b, got_b).astype(bf16)
+    got_a = send_chips(parts_a)
+    parts_b = fold(parts_b, 2, 0)
+    for bit in long_bits()[1:]:
+        sums = sums + dp_send(sums, bit)
+    parts_a = keep_chips(parts_a, got_a)
     shared_sums = tensor_sum(sums[:, channels:], size)
     norm_sum = shared_sums[0, known - channels :]
     grad_normed = sum_quarters((terms0, terms1, terms2), other0, other1, size)
@@ -907,8 +972,6 @@
         scaled_grad * inputs, axis=1, keepdims=True
     )
     grad_tokens = (cotangent.astype(f32) + grad_inputs).astype(bf16)
-    parts_a = fold_chips(parts_a)
-    parts_b = fold(parts_b, 2, 0)
     part_inner = jnp.concatenate([parts_a, parts_b[:, : channels - cut]], axis=1)
     at_step = channels + width
     part_shared = tensor_sum(parts_b[:, channels - cut : at_step - cut], size)

time: 289 us -> 286 us (0.990)
  between operations: 15.2 us -> 1.54 us
  waiting for transfers between devices: 52 us -> 38.7 us
  other arithmetic: 24.3 us -> 33.9 us
  starting transfers between devices: 49 us -> 56.1 us
  local copies, waits for them, and re-layouts: 20.5 us -> 26.1 us
    all_gather x1 -> x0, waiting for transfers between devices: 9.22 us -> none  [shards(): weight_late = lax.all_gather(late, 'dp', axis=0, tiled=True)]
    ppermute x30 -> x40, starting transfers between devices: 38.1 us -> 47.2 us  [dp_send(): return lax.ppermute(value, 'dp', [(i, i ^ bit) for i in range(size)])]
    ppermute x9, waiting for transfers between devices: 16.6 us -> 10.3 us  [tensor_swap(): return lax.ppermute(value, 'tensor', [(0, 1), (1, 0)])]
    add x8 -> x9, other arithmetic: 3.03 us -> 6.33 us  [the longest x2 2.89 us: keep_chips(): total = total + piece.astype(f32)]
    ppermute x30 -> x40, waiting for transfers between devices: 26.2 us -> 28.3 us  [dp_send(): return lax.ppermute(value, 'dp', [(i, i ^ bit) for i in range(size)])]
    unnamed x53 -> x78, local copies, waits for them, and re-layouts: 5.99 us -> 7.78 us
  transfers between devices with their start and end apart: 40 -> 49, of which waited for: 12 -> 12; matrix products, arithmetic and copies ran while one was open for 12% -> 16% of each run, Pallas kernels for 29% -> 30%
where the time goes in v2:
time: 286 us; the launch traced here: 282 us
  Pallas kernels  126 us (44%)
  starting transfers between devices  56.1 us (20%)
  waiting for transfers between devices  38.7 us (14%)
  other arithmetic  33.9 us (12%)
  local copies, waits for them, and re-layouts  26.1 us (9%)
    ppermute x40, starting transfers between devices, dp_send(): return lax.ppermute(value, 'dp', [(i, i ^ bit) for i in range(size)])  47.2 us
    pallas_call x3, Pallas kernels, mixer_backward(): pl.pallas_call(partial(backward_kernel, begin, rows), grid=(end - begin,)...  43.5 us
    ppermute x40, waiting for transfers between devices, dp_send(): return lax.ppermute(value, 'dp', [(i, i ^ bit) for i in range(size)])  28.3 us
    pallas_call x1, Pallas kernels, mixer_forward(): pl.pallas_call(partial(forward_kernel, 1 + len(others), count), grid=(blo...  23.2 us
    pallas_call x1, Pallas kernels, gate_norm(): pl.pallas_call(partial(norm_kernel, float(full_inner), chips, split), gri...  19.9 us
    pallas_call x3, Pallas kernels, input_terms(): pl.pallas_call(input_kernel, grid=(rows // span,), in_specs=[pl.BlockSpec...  17.4 us
    pallas_call x1, Pallas kernels, gate_forward(): pl.pallas_call(partial(gate_kernel, 1 + len(others), count), grid=(rows /...  13.3 us
    ppermute x9, waiting for transfers between devices, tensor_swap(): return lax.ppermute(value, 'tensor', [(0, 1), (1, 0)])  10.3 us
  transfers between devices with their start and end apart: 49, of which 12 were waited for; matrix products, arithmetic and copies ran while one was open for 16% of the time, Pallas kernels for 30%

profile of v2, /device:TPU:0, one launch (start us, length us, event | category | flops | bytes accessed | tf_op | source)
XLA Modules:
  0.0 282.4 jit_solution(10691456212620190884)
XLA Ops:
  4.5 3.0 %collective-permute-start = (bf16[64,1408]{1,0:T(8,128)(2,1)}, bf16[64,1408]{1,0:T(8,128)(2,1)}, u32[]{:S(2)}, u32[]{:S(2)}) collective-permute-start(bf16[64,1408]{1,0:T(8,128)(2,1)} %pad_maximum_fusion.5), channel_id=1, source_target_pairs={{0,8},{2,10},{4,12},{6,14},{8,0},{10,2},{12,4},{14,6},{16,24},{18,... | collective-permute-start | bytes 540680 | tf_op jit(solution)/shard_map/ppermute | solution.py:741
  7.6 2.6 collective-permute-start.1
  12.5 1.7 collective-permute-start.4
  19.9 1.7 fusion.9.refs_14_.spread_ref
  29.5 3.0 %collective-permute-start.7 = (bf16[128,768]{1,0:T(8,128)(2,1)S(1)}, bf16[128,768]{1,0:T(8,128)(2,1)S(1)}, u32[]{:S(2)}, u32[]{:S(2)}) collective-permute-start(bf16[128,768]{1,0:T(8,128)(2,1)S(1)} %slice.79), channel_id=1, source_target_pairs={{0,8},{2,10},{4,12},{6,14},{8,0},{10,2},{12,4},{14,6},{16,24},{18,... | collective-permute-start | bytes 589832 | tf_op jit(solution)/shard_map/ppermute | solution.py:741
  35.0 6.3 %collective-permute-done.6.refs_2_ = bf16[256,1024]{1,0:T(8,128)(2,1)S(1)} collective-permute-done((bf16[256,1024]{1,0:T(8,128)(2,1)S(1)}, bf16[256,1024]{1,0:T(8,128)(2,1)S(1)}, u32[]{:S(2)}, u32[]{:S(2)}) %collective-permute-start.6) | collective-permute-done | bytes 524320 | tf_op jit(solution)/shard_map/ppermute | solution.py:792
  41.8 6.9 %collective-permute-done.8 = bf16[128,768]{1,0:T(8,128)(2,1)S(1)} collective-permute-done((bf16[128,768]{1,0:T(8,128)(2,1)S(1)}, bf16[128,768]{1,0:T(8,128)(2,1)S(1)}, u32[]{:S(2)}, u32[]{:S(2)}) %collective-permute-start.8) | collective-permute-done | bytes 196640 | tf_op jit(solution)/shard_map/ppermute | solution.py:741
  49.6 2.7 collective-permute-start.14
  52.3 2.3 collective-permute-start.15
  56.9 23.2 %mixer_forward.1 = (bf16[1024,1024]{1,0:T(8,128)(2,1)}, bf16[1024,1408]{1,0:T(8,128)(2,1)}, f32[1024,1024]{1,0:T(8,128)}, f32[1024,1024]{1,0:T(8,128)}, f32[1024...) custom-call(s32[1,4]{1,0:T(1,128)} %add_bitcast_fusion.spot_ref, ...), custom_call_target="tpu_custom_call" | custom-call | tf_op jit(solution)/shard_map/mixer_forward/pallas_call | solution.py:249
  84.2 13.3 %gate_forward.1 = (bf16[1024,1024]{1,0:T(8,128)(2,1)}, bf16[1024,2048]{1,0:T(8,128)(2,1)}, f32[1024,1024]{1,0:T(8,128)}, f32[1024,1024]{1,0:T(8,128)}, f32[8,1024]{1,0:T(8,128)}) custom-call(s32[1,4]{1,0:T(1,128)} %add_bitcast_fusion.spot_ref, bf16[1024,1024]{1,0:T(8,128)(2,1)} %get-tuple-element.132.normed_ref, bf16[512,1024]{1,0:T(8,128)(2,1)} %refs_0_.1, ...), custom_call_target="tpu_custom_call" | custom-call | tf_op jit(solution)/shard_map/gate_forward/pallas_call | solution.py:570
  98.0 3.7 %collective-permute-done.21.more_ref = f32[8,1024]{1,0:T(8,128)S(1)} collective-permute-done((f32[8,1024]{1,0:T(8,128)}, f32[8,1024]{1,0:T(8,128)S(1)}, u32[]{:S(2)}, u32[]{:S(2)}) %collective-permute-start.21) | collective-permute-done | bytes 32800 | tf_op jit(solution)/shard_map/ppermute | solution.py:792
  102.3 19.9 %gate_norm.1 = (bf16[1024,1024]{1,0:T(8,128)(2,1)}, f32[1024,1024]{1,0:T(8,128)}, f32[8,1408]{1,0:T(8,128)}, bf16[512,2048]{1,0:T(8,128)(2,1)}, bf16[512,2048]{1...) custom-call(s32[1,4]{1,0:T(1,128)} %add_bitcast_fusion.spot_ref, ...), custom_call_target="tpu_custom_call" | custom-call | tf_op jit(solution)/shard_map/gate_norm/pallas_call | solution.py:667
  125.0 20.2 %mixer_backward.3 = (bf16[512,1408]{1,0:T(8,128)(2,1)}, f32[8,1408]{1,0:T(8,128)}, f32[8,1024]{1,0:T(8,128)}, f32[8,256]{1,0:T(8,128)}, f32[128,1024]{1,0:T(8,128)}) custom-call(s32[1,4]{1,0:T(1,128)} %lengths_ref.7, f32[1024,1024]{1,0:T(8,128)} %get-tuple-element.151.upstream_ref, f32[1024,1024]{1,0:T(8,128)} %get-tuple-element.145.refs_13_.ssm_ref, ...), custom_call_target="tpu_custom_call" | custom-call | tf_op jit(solution)/shard_map/mixer_backward/pallas_call | solution.py:440
  145.2 2.4 add_convert_fusion
  151.4 4.6 %collective-permute-start.25 = (bf16[2,64,1024]{2,1,0:T(8,128)(2,1)}, bf16[2,64,1024]{2,1,0:T(8,128)(2,1)}, u32[]{:S(2)}, u32[]{:S(2)}) collective-permute-start(bf16[2,64,1024]{2,1,0:T(8,128)(2,1)} %get-tuple-element.253), channel_id=1, source_target_pairs={{0,8},{2,10},{4,12},{6,14},{8,0},{10,2},{12,4},{14,6},{16,24},{18,... | collective-permute-start | bytes 786440 | tf_op jit(solution)/shard_map/ppermute | solution.py:741
  158.5 7.0 %input_terms.3 = bf16[512,1024]{1,0:T(8,128)(2,1)} custom-call(bf16[1024,1024]{1,0:T(8,128)(2,1)} %get-tuple-element.173.grad_gate_ref, bf16[512,1408]{1,0:T(8,128)(2,1)} %get-tuple-element.174.grads_ref.refs_2_, bf16[1024,2048]{1,0:T(8,128)(2,1)} %get-tuple-element.150.gate_w_ref.out_w_ref, bf16[1024,1408]{1,0:T(8,128)(2,1)} %get-tuple-element.175.weight_ref), custom_call_target="tpu_custom_call" | custom-call | tf_op jit(solution)/shard_map/input_terms/pallas_call | solution.py:722
  165.5 11.5 %mixer_backward.4 = (bf16[256,1408]{1,0:T(8,128)(2,1)}, f32[8,1408]{1,0:T(8,128)}, f32[8,1024]{1,0:T(8,128)}, f32[8,256]{1,0:T(8,128)}, f32[128,1024]{1,0:T(8,128)}) custom-call(s32[1,4]{1,0:T(1,128)} %lengths_ref.7, f32[1024,1024]{1,0:T(8,128)} %get-tuple-element.151.upstream_ref, f32[1024,1024]{1,0:T(8,128)} %get-tuple-element.145.refs_13_.ssm_ref, ...), custom_call_target="tpu_custom_call" | custom-call | tf_op jit(solution)/shard_map/mixer_backward/pallas_call | solution.py:440
  176.9 5.3 %input_terms.4 = bf16[256,1024]{1,0:T(8,128)(2,1)} custom-call(bf16[1024,1024]{1,0:T(8,128)(2,1)} %get-tuple-element.173.grad_gate_ref, bf16[256,1408]{1,0:T(8,128)(2,1)} %get-tuple-element.185.grads_ref.refs_1_, bf16[1024,2048]{1,0:T(8,128)(2,1)} %get-tuple-element.150.gate_w_ref.out_w_ref, bf16[1024,1408]{1,0:T(8,128)(2,1)} %get-tuple-element.175.weight_ref), custom_call_target="tpu_custom_call" | custom-call | tf_op jit(solution)/shard_map/input_terms/pallas_call | solution.py:722
  188.2 1.9 collective-permute-start.29
  191.5 2.6 collective-permute-start.32
  194.2 2.8 %fusion.3 = bf16[512,1024]{1,0:T(8,128)(2,1)} fusion(bf16[512,1024]{1,0:T(8,128)(2,1)S(1)} %copy-done, bf16[512,1024]{1,0:T(8,128)(2,1)} %collective-permute-done.23, bf16[512,1024]{1,0:T(8,128)(2,1)S(1)} %copy-done.17), kind=kLoop, calls=%fused_computation.10 | loop fusion | flops 3145728 | bytes 4194304 | tf_op jit(solution)/shard_map/convert_element_type | solution.py:934
  197.0 11.9 %mixer_backward.5 = (bf16[256,1408]{1,0:T(8,128)(2,1)}, f32[8,1408]{1,0:T(8,128)}, f32[8,1024]{1,0:T(8,128)}, f32[8,256]{1,0:T(8,128)}, f32[128,1024]{1,0:T(8,128)}) custom-call(s32[1,4]{1,0:T(1,128)} %lengths_ref.7, f32[1024,1024]{1,0:T(8,128)} %get-tuple-element.151.upstream_ref, f32[1024,1024]{1,0:T(8,128)} %get-tuple-element.145.refs_13_.ssm_ref, ...), custom_call_target="tpu_custom_call" | custom-call | tf_op jit(solution)/shard_map/mixer_backward/pallas_call | solution.py:440
  212.3 8.9 %weight_products.1 = (bf16[512,1408]{1,0:T(8,128)(2,1)}, bf16[512,1408]{1,0:T(8,128)(2,1)}, f32[8,2432]{1,0:T(8,128)}) custom-call(s32[1,4]{1,0:T(1,128)} %add_bitcast_fusion.spot_ref, bf16[1024,1024]{1,0:T(8,128)(2,1)} %get-tuple-element.132.normed_ref, bf16[1024,1408]{1,0:T(8,128)(2,1)} %get-tuple-element.175.weight_ref, f32[1,1024]{1,0:T(1,128)} %bitcast.106, ...), custom_call_target="tpu_custom_call" | custom-call | tf_op jit(solution)/shard_map/weight_products/pallas_call | solution.py:514
  221.2 5.2 %input_terms.5 = bf16[256,1024]{1,0:T(8,128)(2,1)} custom-call(bf16[1024,1024]{1,0:T(8,128)(2,1)} %get-tuple-element.173.grad_gate_ref, bf16[256,1408]{1,0:T(8,128)(2,1)} %get-tuple-element.200.grads_ref.refs_0_, bf16[1024,2048]{1,0:T(8,128)(2,1)} %get-tuple-element.150.gate_w_ref.out_w_ref, bf16[1024,1408]{1,0:T(8,128)(2,1)} %get-tuple-element.175.weight_ref), custom_call_target="tpu_custom_call" | custom-call | tf_op jit(solution)/shard_map/input_terms/pallas_call | solution.py:722
  232.1 2.8 collective-permute-start.40
  236.4 6.7 %collective-permute-done.35 = f32[8,2432]{1,0:T(8,128)S(1)} collective-permute-done((f32[8,2432]{1,0:T(8,128)S(1)}, f32[8,2432]{1,0:T(8,128)S(1)}, u32[]{:S(2)}, u32[]{:S(2)}) %collective-permute-start.35) | collective-permute-done | bytes 77856 | tf_op jit(solution)/shard_map/ppermute | solution.py:741
  243.3 4.2 %collective-permute-done.36 = f32[8,2432]{1,0:T(8,128)S(1)} collective-permute-done((f32[8,2432]{1,0:T(8,128)S(1)}, f32[8,2432]{1,0:T(8,128)S(1)}, u32[]{:S(2)}, u32[]{:S(2)}) %collective-permute-start.36) | collective-permute-done | bytes 77856 | tf_op jit(solution)/shard_map/ppermute | solution.py:741
  251.5 2.8 collective-permute-start.45
  259.4 7.3 %collective-permute-done.42 = f32[8,2432]{1,0:T(8,128)} collective-permute-done((f32[8,2432]{1,0:T(8,128)}, f32[8,2432]{1,0:T(8,128)}, u32[]{:S(2)}, u32[]{:S(2)}) %collective-permute-start.42) | collective-permute-done | bytes 77856 | tf_op jit(solution)/shard_map/ppermute | solution.py:741
  277.4 1.8 fusion.8
  279.3 3.0 %fusion.7 = bf16[512,1024]{1,0:T(8,128)(2,1)} fusion(bf16[512,1024]{1,0:T(8,128)(2,1)S(1)} %copy-done, bf16[512,1024]{1,0:T(8,128)(2,1)S(1)} %copy-done.6, f32[512]{0:T(512)S(1)} %broadcast_multiply_fusion, f32[512]{0:T(512)S(1)} %copy-done.34, f32[1024]{0:T(1024)S(1)} %copy-done.30, f32[512]{0:T(512)S(1)} %copy-done.33, ...), kind=kLoop, calls=%fused_computation.14 | loop fusion | flops 10485760 | bytes 6301697 | tf_op jit(solution)/shard_map/convert_element_type | solution.py:974
  (226 shorter events, 77.8 us)
Async XLA Ops:
  4.5 21.6 %collective-permute-start = (bf16[64,1408]{1,0:T(8,128)(2,1)}, bf16[64,1408]{1,0:T(8,128)(2,1)}, u32[]{:S(2)}, u32[]{:S(2)}) collective-permute-start(bf16[64,1408]{1,0:T(8,128)(2,1)} %pad_maximum_fusion.5), channel_id=1, source_target_pairs={{0,8},{2,10},{4,12},{6,14},{8,0},{10,2},{12,4},{14,6},{16,24},{18,... | collective-permute-start | bytes 540680 | tf_op jit(solution)/shard_map/ppermute | solution.py:741
  7.6 18.6 %collective-permute-start.1 = (bf16[64,1408]{1,0:T(8,128)(2,1)}, bf16[64,1408]{1,0:T(8,128)(2,1)}, u32[]{:S(2)}, u32[]{:S(2)}) collective-permute-start(bf16[64,1408]{1,0:T(8,128)(2,1)} %pad_maximum_fusion.5), channel_id=1, source_target_pairs={{0,16},{2,18},{4,20},{6,22},{8,24},{10,26},{12,28},{14,30},{16,0},... | collective-permute-start | bytes 540680 | tf_op jit(solution)/shard_map/ppermute | solution.py:741
  10.2 16.0 %collective-permute-start.2 = (bf16[64,1408]{1,0:T(8,128)(2,1)}, bf16[64,1408]{1,0:T(8,128)(2,1)}, u32[]{:S(2)}, u32[]{:S(2)}) collective-permute-start(bf16[64,1408]{1,0:T(8,128)(2,1)} %pad_maximum_fusion.5), channel_id=1, source_target_pairs={{0,24},{2,26},{4,28},{6,30},{8,16},{10,18},{12,20},{14,22},{16,8},... | collective-permute-start | bytes 540680 | tf_op jit(solution)/shard_map/ppermute | solution.py:741
  12.5 16.1 %collective-permute-start.4 = (bf16[256,1024]{1,0:T(8,128)(2,1)}, bf16[256,1024]{1,0:T(8,128)(2,1)}, u32[]{:S(2)}, u32[]{:S(2)}) collective-permute-start(bf16[256,1024]{1,0:T(8,128)(2,1)} %get-tuple-element.257), channel_id=1, source_target_pairs={{0,1},{1,0},{2,3},{3,2},{4,5},{5,4},{6,7},{7,6},{8,9},{9,8},{10,11... | collective-permute-start | bytes 1572872 | tf_op jit(solution)/shard_map/ppermute | solution.py:792
  28.6 20.1 %collective-permute-start.5 = (bf16[256,1408]{1,0:T(8,128)(2,1)S(1)}, bf16[256,1408]{1,0:T(8,128)(2,1)S(1)}, u32[]{:S(2)}, u32[]{:S(2)}) collective-permute-start(bf16[256,1408]{1,0:T(8,128)(2,1)S(1)} %pad_maximum_fusion.1.refs_3_), channel_id=1, source_target_pairs={{0,4},{2,6},{4,0},{6,2},{8,12},{10,14},{12,8},{14,10},{16,20},{18,... | collective-permute-start | bytes 2162696 | tf_op jit(solution)/shard_map/ppermute | solution.py:741
  32.6 16.1 %collective-permute-start.8 = (bf16[128,768]{1,0:T(8,128)(2,1)S(1)}, bf16[128,768]{1,0:T(8,128)(2,1)S(1)}, u32[]{:S(2)}, u32[]{:S(2)}) collective-permute-start(bf16[128,768]{1,0:T(8,128)(2,1)S(1)} %slice.79), channel_id=1, source_target_pairs={{0,16},{2,18},{4,20},{6,22},{8,24},{10,26},{12,28},{14,30},{16,0},... | collective-permute-start | bytes 589832 | tf_op jit(solution)/shard_map/ppermute | solution.py:741
  34.0 14.7 %collective-permute-start.9 = (bf16[128,768]{1,0:T(8,128)(2,1)S(1)}, bf16[128,768]{1,0:T(8,128)(2,1)S(1)}, u32[]{:S(2)}, u32[]{:S(2)}) collective-permute-start(bf16[128,768]{1,0:T(8,128)(2,1)S(1)} %slice.79), channel_id=1, source_target_pairs={{0,24},{2,26},{4,28},{6,30},{8,16},{10,18},{12,20},{14,22},{16,8},... | collective-permute-start | bytes 589832 | tf_op jit(solution)/shard_map/ppermute | solution.py:741
  41.3 38.8 %collective-permute-start.12 = (bf16[512,1024]{1,0:T(8,128)(2,1)S(1)}, bf16[512,1024]{1,0:T(8,128)(2,1)}, u32[]{:S(2)}, u32[]{:S(2)}) collective-permute-start(bf16[512,1024]{1,0:T(8,128)(2,1)S(1)} %copy-done.5), channel_id=1, source_target_pairs={{0,1},{1,0},{2,3},{3,2},{4,5},{5,4},{6,7},{7,6},{8,9},{9,8},{10,11... | collective-permute-start | bytes 3145736 | tf_op jit(solution)/shard_map/ppermute | solution.py:792
  49.4 30.8 %collective-permute-start.13 = (bf16[512,768]{1,0:T(8,128)(2,1)S(1)}, bf16[512,768]{1,0:T(8,128)(2,1)}, u32[]{:S(2)}, u32[]{:S(2)}) collective-permute-start(bf16[512,768]{1,0:T(8,128)(2,1)S(1)} %constant_dynamic-update-slice_fusion.refs_2_), channel_id=1, source_target_pairs={{0,2},{2,0},{4,6},{6,4},{8,10},{10,8},{12,14},{14,12},{16,18},{18,... | collective-permute-start | bytes 2359304 | tf_op jit(solution)/shard_map/ppermute | solution.py:741
  49.6 30.6 %collective-permute-start.14 = (bf16[128,1280]{1,0:T(8,128)(2,1)S(1)}, bf16[128,1280]{1,0:T(8,128)(2,1)}, u32[]{:S(2)}, u32[]{:S(2)}) collective-permute-start(bf16[128,1280]{1,0:T(8,128)(2,1)S(1)} %slice.80.refs_4_), channel_id=1, source_target_pairs={{0,8},{2,10},{4,12},{6,14},{8,0},{10,2},{12,4},{14,6},{16,24},{18,... | collective-permute-start | bytes 983048 | tf_op jit(solution)/shard_map/ppermute | solution.py:741
  52.3 27.8 %collective-permute-start.15 = (bf16[128,1280]{1,0:T(8,128)(2,1)S(1)}, bf16[128,1280]{1,0:T(8,128)(2,1)}, u32[]{:S(2)}, u32[]{:S(2)}) collective-permute-start(bf16[128,1280]{1,0:T(8,128)(2,1)S(1)} %slice.80.refs_4_), channel_id=1, source_target_pairs={{0,16},{2,18},{4,20},{6,22},{8,24},{10,26},{12,28},{14,30},{16,0},... | collective-permute-start | bytes 983048 | tf_op jit(solution)/shard_map/ppermute | solution.py:741
  55.5 24.7 %collective-permute-start.16 = (bf16[128,1280]{1,0:T(8,128)(2,1)S(1)}, bf16[128,1280]{1,0:T(8,128)(2,1)}, u32[]{:S(2)}, u32[]{:S(2)}) collective-permute-start(bf16[128,1280]{1,0:T(8,128)(2,1)S(1)} %slice.80.refs_4_), channel_id=1, source_target_pairs={{0,24},{2,26},{4,28},{6,30},{8,16},{10,18},{12,20},{14,22},{16,8},... | collective-permute-start | bytes 983048 | tf_op jit(solution)/shard_map/ppermute | solution.py:741
  122.2 22.9 %collective-permute-start.22 = (bf16[512,2048]{1,0:T(8,128)(2,1)}, bf16[512,2048]{1,0:T(8,128)(2,1)}, u32[]{:S(2)}, u32[]{:S(2)}) collective-permute-start(bf16[512,2048]{1,0:T(8,128)(2,1)} %get-tuple-element.167), channel_id=1, source_target_pairs={{0,2},{2,0},{4,6},{6,4},{8,10},{10,8},{12,14},{14,12},{16,18},{18,... | collective-permute-start | bytes 6291464 | tf_op jit(solution)/shard_map/ppermute | solution.py:741
  122.4 62.2 %collective-permute-start.23 = (bf16[512,1024]{1,0:T(8,128)(2,1)}, bf16[512,1024]{1,0:T(8,128)(2,1)}, u32[]{:S(2)}, u32[]{:S(2)}) collective-permute-start(bf16[512,1024]{1,0:T(8,128)(2,1)} %get-tuple-element.186), channel_id=1, source_target_pairs={{0,1},{1,0},{2,3},{3,2},{4,5},{5,4},{6,7},{7,6},{8,9},{9,8},{10,11... | collective-permute-start | bytes 3145736 | tf_op jit(solution)/shard_map/ppermute | solution.py:792
  149.6 34.8 %collective-permute-start.24 = (bf16[4,64,1024]{2,1,0:T(8,128)(2,1)}, bf16[4,64,1024]{2,1,0:T(8,128)(2,1)S(1)}, u32[]{:S(2)}, u32[]{:S(2)}) collective-permute-start(bf16[4,64,1024]{2,1,0:T(8,128)(2,1)} %dynamic-slice_bitcast_fusion), channel_id=1, source_target_pairs={{0,4},{2,6},{4,0},{6,2},{8,12},{10,14},{12,8},{14,10},{16,20},{18,... | collective-permute-start | bytes 1572872 | tf_op jit(solution)/shard_map/ppermute | solution.py:741
  151.4 31.6 %collective-permute-start.25 = (bf16[2,64,1024]{2,1,0:T(8,128)(2,1)}, bf16[2,64,1024]{2,1,0:T(8,128)(2,1)}, u32[]{:S(2)}, u32[]{:S(2)}) collective-permute-start(bf16[2,64,1024]{2,1,0:T(8,128)(2,1)} %get-tuple-element.253), channel_id=1, source_target_pairs={{0,8},{2,10},{4,12},{6,14},{8,0},{10,2},{12,4},{14,6},{16,24},{18,... | collective-permute-start | bytes 786440 | tf_op jit(solution)/shard_map/ppermute | solution.py:741
  156.0 27.1 %collective-permute-start.26 = (bf16[2,64,1024]{2,1,0:T(8,128)(2,1)}, bf16[2,64,1024]{2,1,0:T(8,128)(2,1)}, u32[]{:S(2)}, u32[]{:S(2)}) collective-permute-start(bf16[2,64,1024]{2,1,0:T(8,128)(2,1)} %get-tuple-element.255), channel_id=1, source_target_pairs={{0,16},{2,18},{4,20},{6,22},{8,24},{10,26},{12,28},{14,30},{16,0},... | collective-permute-start | bytes 786440 | tf_op jit(solution)/shard_map/ppermute | solution.py:741
  157.0 26.0 %collective-permute-start.27 = (bf16[2,64,1024]{2,1,0:T(8,128)(2,1)S(1)}, bf16[2,64,1024]{2,1,0:T(8,128)(2,1)}, u32[]{:S(2)}, u32[]{:S(2)}) collective-permute-start(bf16[2,64,1024]{2,1,0:T(8,128)(2,1)S(1)} %get-tuple-element.254), channel_id=1, source_target_pairs={{0,24},{2,26},{4,28},{6,30},{8,16},{10,18},{12,20},{14,22},{16,8},... | collective-permute-start | bytes 786440 | tf_op jit(solution)/shard_map/ppermute | solution.py:741
  185.3 23.6 %collective-permute-start.31 = (bf16[64,1024]{1,0:T(8,128)(2,1)}, bf16[64,1024]{1,0:T(8,128)(2,1)}, u32[]{:S(2)}, u32[]{:S(2)}) collective-permute-start(bf16[64,1024]{1,0:T(8,128)(2,1)} %dynamic-slice_bitcast_fusion.8), channel_id=1, source_target_pairs={{0,4},{2,6},{4,0},{6,2},{8,12},{10,14},{12,8},{14,10},{16,20},{18,... | collective-permute-start | bytes 393224 | tf_op jit(solution)/shard_map/ppermute | solution.py:741
  187.2 23.4 %collective-permute-start.28 = (bf16[64,1024]{1,0:T(8,128)(2,1)}, bf16[64,1024]{1,0:T(8,128)(2,1)S(1)}, u32[]{:S(2)}, u32[]{:S(2)}) collective-permute-start(bf16[64,1024]{1,0:T(8,128)(2,1)} %get-tuple-element.261), channel_id=1, source_target_pairs={{0,8},{2,10},{4,12},{6,14},{8,0},{10,2},{12,4},{14,6},{16,24},{18,... | collective-permute-start | bytes 393224 | tf_op jit(solution)/shard_map/ppermute | solution.py:741
  188.2 22.3 %collective-permute-start.29 = (bf16[64,1024]{1,0:T(8,128)(2,1)}, bf16[64,1024]{1,0:T(8,128)(2,1)}, u32[]{:S(2)}, u32[]{:S(2)}) collective-permute-start(bf16[64,1024]{1,0:T(8,128)(2,1)} %get-tuple-element.263), channel_id=1, source_target_pairs={{0,16},{2,18},{4,20},{6,22},{8,24},{10,26},{12,28},{14,30},{16,0},... | collective-permute-start | bytes 393224 | tf_op jit(solution)/shard_map/ppermute | solution.py:741
  190.1 20.5 %collective-permute-start.30 = (bf16[64,1024]{1,0:T(8,128)(2,1)}, bf16[64,1024]{1,0:T(8,128)(2,1)}, u32[]{:S(2)}, u32[]{:S(2)}) collective-permute-start(bf16[64,1024]{1,0:T(8,128)(2,1)} %get-tuple-element.262), channel_id=1, source_target_pairs={{0,24},{2,26},{4,28},{6,30},{8,16},{10,18},{12,20},{14,22},{16,8},... | collective-permute-start | bytes 393224 | tf_op jit(solution)/shard_map/ppermute | solution.py:741
  191.5 20.7 %collective-permute-start.32 = (bf16[256,1024]{1,0:T(8,128)(2,1)}, bf16[256,1024]{1,0:T(8,128)(2,1)S(1)}, u32[]{:S(2)}, u32[]{:S(2)}) collective-permute-start(bf16[256,1024]{1,0:T(8,128)(2,1)} %slice_select_fusion.1), channel_id=1, source_target_pairs={{0,1},{1,0},{2,3},{3,2},{4,5},{5,4},{6,7},{7,6},{8,9},{9,8},{10,11... | collective-permute-start | bytes 1572872 | tf_op jit(solution)/shard_map/ppermute | solution.py:792
  228.4 20.4 %collective-permute-start.38 = (bf16[4,64,896]{2,1,0:T(8,128)(2,1)S(1)}, bf16[4,64,896]{2,1,0:T(8,128)(2,1)S(1)}, u32[]{:S(2)}, u32[]{:S(2)}) collective-permute-start(bf16[4,64,896]{2,1,0:T(8,128)(2,1)S(1)} %dynamic-slice_bitcast_fusion.1), channel_id=1, source_target_pairs={{0,4},{2,6},{4,0},{6,2},{8,12},{10,14},{12,8},{14,10},{16,20},{18,... | collective-permute-start | bytes 1376264 | tf_op jit(solution)/shard_map/ppermute | solution.py:741
  230.6 12.5 %collective-permute-start.35 = (f32[8,2432]{1,0:T(8,128)S(1)}, f32[8,2432]{1,0:T(8,128)S(1)}, u32[]{:S(2)}, u32[]{:S(2)}) collective-permute-start(f32[8,2432]{1,0:T(8,128)S(1)} %add.200), channel_id=1, source_target_pairs={{0,4},{2,6},{4,0},{6,2},{8,12},{10,14},{12,8},{14,10},{16,20},{18,... | collective-permute-start | bytes 233480 | tf_op jit(solution)/shard_map/ppermute | solution.py:741
  231.9 16.9 %collective-permute-start.39 = (bf16[2,64,512]{2,1,0:T(8,128)(2,1)S(1)}, bf16[2,64,512]{2,1,0:T(8,128)(2,1)S(1)}, u32[]{:S(2)}, u32[]{:S(2)}) collective-permute-start(bf16[2,64,512]{2,1,0:T(8,128)(2,1)S(1)} %get-tuple-element.260), channel_id=1, source_target_pairs={{0,8},{2,10},{4,12},{6,14},{8,0},{10,2},{12,4},{14,6},{16,24},{18,... | collective-permute-start | bytes 393224 | tf_op jit(solution)/shard_map/ppermute | solution.py:741
  232.1 16.7 %collective-permute-start.40 = (bf16[2,64,512]{2,1,0:T(8,128)(2,1)S(1)}, bf16[2,64,512]{2,1,0:T(8,128)(2,1)S(1)}, u32[]{:S(2)}, u32[]{:S(2)}) collective-permute-start(bf16[2,64,512]{2,1,0:T(8,128)(2,1)S(1)} %get-tuple-element.259), channel_id=1, source_target_pairs={{0,16},{2,18},{4,20},{6,22},{8,24},{10,26},{12,28},{14,30},{16,0},... | collective-permute-start | bytes 393224 | tf_op jit(solution)/shard_map/ppermute | solution.py:741
  234.9 13.9 %collective-permute-start.41 = (bf16[2,64,512]{2,1,0:T(8,128)(2,1)S(1)}, bf16[2,64,512]{2,1,0:T(8,128)(2,1)S(1)}, u32[]{:S(2)}, u32[]{:S(2)}) collective-permute-start(bf16[2,64,512]{2,1,0:T(8,128)(2,1)S(1)} %get-tuple-element.258), channel_id=1, source_target_pairs={{0,24},{2,26},{4,28},{6,30},{8,16},{10,18},{12,20},{14,22},{16,8},... | collective-permute-start | bytes 393224 | tf_op jit(solution)/shard_map/ppermute | solution.py:741
  248.2 29.2 %collective-permute-start.37 = (bf16[256,1024]{1,0:T(8,128)(2,1)}, bf16[256,1024]{1,0:T(8,128)(2,1)}, u32[]{:S(2)}, u32[]{:S(2)}) collective-permute-start(bf16[256,1024]{1,0:T(8,128)(2,1)} %slice_select_fusion), channel_id=1, source_target_pairs={{0,1},{1,0},{2,3},{3,2},{4,5},{5,4},{6,7},{7,6},{8,9},{9,8},{10,11... | collective-permute-start | bytes 1572872 | tf_op jit(solution)/shard_map/ppermute | solution.py:792
  251.4 19.5 %collective-permute-start.44 = (bf16[64,896]{1,0:T(8,128)(2,1)}, bf16[64,896]{1,0:T(8,128)(2,1)}, u32[]{:S(2)}, u32[]{:S(2)}) collective-permute-start(bf16[64,896]{1,0:T(8,128)(2,1)} %get-tuple-element.264), channel_id=1, source_target_pairs={{0,8},{2,10},{4,12},{6,14},{8,0},{10,2},{12,4},{14,6},{16,24},{18,... | collective-permute-start | bytes 344072 | tf_op jit(solution)/shard_map/ppermute | solution.py:741
  251.5 19.9 %collective-permute-start.45 = (bf16[64,896]{1,0:T(8,128)(2,1)}, bf16[64,896]{1,0:T(8,128)(2,1)}, u32[]{:S(2)}, u32[]{:S(2)}) collective-permute-start(bf16[64,896]{1,0:T(8,128)(2,1)} %get-tuple-element.266), channel_id=1, source_target_pairs={{0,16},{2,18},{4,20},{6,22},{8,24},{10,26},{12,28},{14,30},{16,0},... | collective-permute-start | bytes 344072 | tf_op jit(solution)/shard_map/ppermute | solution.py:741
  254.3 17.1 %collective-permute-start.46 = (bf16[64,896]{1,0:T(8,128)(2,1)}, bf16[64,896]{1,0:T(8,128)(2,1)}, u32[]{:S(2)}, u32[]{:S(2)}) collective-permute-start(bf16[64,896]{1,0:T(8,128)(2,1)} %get-tuple-element.265), channel_id=1, source_target_pairs={{0,24},{2,26},{4,28},{6,30},{8,16},{10,18},{12,20},{14,22},{16,8},... | collective-permute-start | bytes 344072 | tf_op jit(solution)/shard_map/ppermute | solution.py:741
  (52 other events, 442.1 us)

commit v3 on v2

--- a/solution.py
+++ b/solution.py
@@ -103,15 +103,27 @@
     return [full(own.shape), *[full(other.shape) for other in others]]
 
 
-def place_weights(spot_ref, weight_ref, sources, count):
+def run_copies(copies):
+    for copy in copies:
+        copy.start()
+    for copy in copies:
+        copy.wait()
+
+
+def place_weights(spot_ref, weight_ref, sources, count, done):
     rows = weight_ref.shape[0] // (4 * count)
+    copies = []
     for i, ref in enumerate(sources):
         along = spot_ref[0, 2] ^ (i % 2)
         core = spot_ref[0, 3] ^ (i // 2)
         for k in range(count):
             at = (((spot_ref[0, 1] ^ k) * 2 + along) * 2 + core) * rows
-            at = pl.ds(pl.multiple_of(at, rows), rows)
-            weight_ref[at, :] = ref[k * rows : (k + 1) * rows, :]
+            copies.append(pltpu.make_async_copy(
+                ref.at[pl.ds(k * rows, rows), :],
+                weight_ref.at[pl.ds(pl.multiple_of(at, rows), rows), :],
+                done.at[i * count + k],
+            ))
+    run_copies(copies)
 
 
 def place_pairs(spot_ref, weight_ref, sources, count, lo):
@@ -143,7 +155,7 @@
     (
         conv_inner_ref, bias_inner_ref, conv_shared_ref, bias_shared_ref, step_bias_ref, rate_ref,
         skip_ref, spread_ref, normed_ref, weight_ref, ssm_ref, inner_ref, pre_inner_ref, shared_ref,
-        pre_shared_ref, step_ref, entering_ref, inner_tail, shared_tail, state,
+        pre_shared_ref, step_ref, entering_ref, inner_tail, shared_tail, state, done,
     ) = refs[pieces + 4 :]
     block = pl.program_id(0)
     rows = normed_ref.shape[0]
@@ -156,7 +168,7 @@
         inner_tail[0:TAIL, :] = jnp.zeros((TAIL, channels), f32)
         shared_tail[0:TAIL, :] = jnp.zeros((TAIL, shared_tail.shape[1]), f32)
         state[...] = jnp.zeros_like(state)
-        place_weights(spot_ref, weight_ref, sources, count)
+        place_weights(spot_ref, weight_ref, sources, count, done)
 
     @pl.when(block > 0)
     def _():
@@ -184,6 +196,7 @@
         ((segment_at(ends, position - k) == segment) & (position >= k)).astype(f32)
         for k in range(1, TAPS)
     ]
+    keeps = [jnp.broadcast_to(keep, (rows, LANES)) for keep in keeps]
 
     def conv(tail, taps_ref, bias_ref, lo, hi):
         total = bias_ref[:, lo:hi] + taps_ref[TAPS - 1 : TAPS, lo:hi] * tail[TAIL : TAIL + rows, lo:hi]
@@ -192,7 +205,13 @@
             total = total + taps_ref[TAPS - 1 - k : TAPS - k, lo:hi] * (shifted * keeps[k - 1])
         return total
 
-    pre_shared = conv(shared_tail, conv_shared_ref, bias_shared_ref, 0, width)
+    pre_shared = jnp.concatenate(
+        [
+            conv(shared_tail, conv_shared_ref, bias_shared_ref, lo, lo + LANES)
+            for lo in range(0, width, LANES)
+        ],
+        axis=1,
+    )
     pre_shared_ref[...] = pre_shared
     shared = pre_shared * sigmoid(pre_shared)
     in_map = shared[:, : width // 2].astype(bf16)
@@ -207,17 +226,19 @@
         pre = conv(inner_tail, conv_inner_ref, bias_inner_ref, lo, hi)
         pre_inner_ref[:, lo:hi] = pre
         head_in = pre * sigmoid(pre)
-        spread = spread_ref[:, lo:hi]
-        scaled = head_in * mm(step2, spread, NN)
+        side = (pair % 2) * LANES
+        if side == 0:
+            spread = spread_ref[:, lo : min(lo + 2 * LANES, channels)]
+            wide = [mm(value, spread, NN) for value in (step2, entry2, leave2)]
+        step_wide, entry_wide, leave_wide = [x[:, side : side + LANES] for x in wide]
+        scaled = head_in * step_wide
         scaled_low = scaled.astype(bf16)
-        entry_wide = mm(entry2, spread, NN)
-        leave_wide = mm(leave2, spread, NN)
         held = state[:, lo:hi]
         entering_ref[0, :, lo:hi] = held
         carried_out = mm(out_map, held.astype(bf16), NN) * entry_wide
         parts = []
-        for side in range(2):
-            head = 2 * pair + side
+        for parity in range(2):
+            head = 2 * pair + parity
             gap = running[:, head : head + 1] - running_t[head : head + 1, :]
             mixed = (scores * jnp.exp(gap + allowed)).astype(bf16)
             parts.append(mm(mixed, scaled_low, NN))
@@ -250,7 +271,8 @@
         partial(forward_kernel, 1 + len(others), count),
         grid=(blocks,),
         in_specs=[
-            smem, smem, *own_specs(own, others, span), *[full(x.shape) for x in sources],
+            smem, smem, *own_specs(own, others, span),
+            *[pl.BlockSpec(memory_space=pl.ANY) for _ in sources],
             *[full(x.shape) for x in fixed],
         ],
         out_specs=[
@@ -267,6 +289,7 @@
             pltpu.VMEM((TAIL + span, channels), f32),
             pltpu.VMEM((TAIL + span, width), f32),
             pltpu.VMEM((states, channels), f32),
+            pltpu.SemaphoreType.DMA((4 * count,)),
         ],
         compiler_params=pltpu.CompilerParams(
             dimension_semantics=("arbitrary",), vmem_limit_bytes=LIMIT
@@ -278,8 +301,9 @@
 def backward_kernel(
     first_block, total_rows, lengths_ref, upstream_ref, ssm_ref, inner_ref, pre_inner_ref, shared_ref, pre_shared_ref,
     step_ref, entering_ref, conv_inner_ref, conv_shared_ref, rate_ref, skip_ref, spread_ref,
-    sums_in_ref, inner_in_ref, shared_in_ref, adjoint_in_ref,
-    grads_ref, sums_ref, inner_out_ref, shared_out_ref, adjoint, inner_head, shared_head,
+    grad_gate_ref, gate_w_ref, weight_ref, sums_in_ref, inner_in_ref, shared_in_ref, adjoint_in_ref,
+    grads_ref, terms_ref, sums_ref, inner_out_ref, shared_out_ref, adjoint, inner_head, shared_head,
+    gate_w, weight, done,
 ):
     turn = pl.program_id(0)
     block = first_block + pl.num_programs(0) - 1 - turn
@@ -288,12 +312,20 @@
     base = block * rows
     ends = sequence_ends(lengths_ref)
 
+    def weight_copies():
+        return (
+            pltpu.make_async_copy(gate_w_ref.at[:, pl.ds(0, channels)], gate_w, done.at[0]),
+            pltpu.make_async_copy(weight_ref, weight, done.at[1]),
+        )
+
     @pl.when(turn == 0)
     def _():
         inner_head[rows : rows + TAIL, :] = inner_in_ref[...]
         shared_head[rows : rows + TAIL, :] = shared_in_ref[...]
         adjoint[...] = adjoint_in_ref[...]
         sums_ref[...] = sums_in_ref[...]
+        for copy in weight_copies():
+            copy.start()
 
     @pl.when(turn > 0)
     def _():
@@ -308,6 +340,7 @@
         ((segment_at(ends, position + k) == segment) & (position + k < total_rows)).astype(f32)
         for k in range(1, TAPS)
     ]
+    keeps = [jnp.broadcast_to(keep, (rows, LANES)) for keep in keeps]
     pre_shared = pre_shared_ref[...]
     shared_gate = sigmoid(pre_shared)
     shared = pre_shared * shared_gate
@@ -328,10 +361,12 @@
     leaving = jnp.zeros((TAIL, LANES), f32)
     for pair in range(channels // LANES):
         lo, hi = pair * LANES, (pair + 1) * LANES
-        spread = spread_ref[:, lo:hi]
-        step_wide = mm(step2, spread, NN)
-        entry_wide = mm(entry2, spread, NN)
-        leave_wide = mm(leave2, spread, NN)
+        side = (pair % 2) * LANES
+        if side == 0:
+            spread = spread_ref[:, lo : min(lo + 2 * LANES, channels)]
+            wide = [mm(value, spread, NN) for value in (step2, entry2, leave2)]
+            products = []
+        step_wide, entry_wide, leave_wide = [x[:, side : side + LANES] for x in wide]
         pre = pre_inner_ref[:, lo:hi]
         gate = sigmoid(pre)
         head_in = pre * gate
@@ -356,21 +391,24 @@
         )
         adjoint[:, lo:hi] = ahead * through + mm(out_map, entry_up, TN)
         parts = []
-        for side in range(2):
-            head = 2 * pair + side
+        for parity in range(2):
+            head = 2 * pair + parity
             gap = running_t[head : head + 1, :] - running[:, head : head + 1]
             decay = jnp.exp(gap + allowed_t)
             mixed = (scores_t * decay).astype(bf16)
             parts.append(mm(mixed, upstream_low, NN))
-            mine = first_half if side == 0 else jnp.logical_not(first_half)
+            mine = first_half if parity == 0 else jnp.logical_not(first_half)
             chosen = jnp.where(mine, scaled_back, 0.0).astype(bf16)
             grad_scores_t = grad_scores_t + mm(chosen, upstream_low, NT) * decay
         grad_scaled = grad_scaled + jnp.where(first_half, parts[0], parts[1])
-        spread_one = spread[:LANES, :]
+        spread_one = spread[:LANES, side : side + LANES]
         spread_both = jnp.concatenate([spread_one, spread_one], axis=1)
         balance = upstream_back * (ssm_ref[:, lo:hi] - skip * head_in) - scaled_back * grad_scaled
         by_head = by_head + mm(halves(balance, 1), spread_both, NT)
-        step_terms = step_terms + mm(halves(head_in * grad_scaled, 1), spread_both, NT)
+        products.append((head_in * grad_scaled).astype(bf16))
+        if hi == channels or side > 0:
+            joined = jnp.concatenate(products, axis=1)
+            step_terms = step_terms + mm(joined, spread[:LANES, :], NT)
         skip_terms = jnp.sum(upstream * head_in, axis=0, keepdims=True)
         edge = jnp.concatenate([tail_terms, skip_terms, jnp.zeros((TAIL - 2, LANES), f32)], axis=0)
         leaving = leaving + mm(halves(edge, 1), spread_both, NT)
@@ -399,7 +437,8 @@
     sums = [None] * TAPS
     sums[TAPS - 1] = jnp.sum(grad_pre * shared_proj, axis=0, keepdims=True)
     for k in range(1, TAPS):
-        moved = shared_head[k : k + rows, :] * keeps[k - 1]
+        keep = jnp.concatenate([keeps[k - 1]] * (width // LANES), axis=1)
+        moved = shared_head[k : k + rows, :] * keep
         grad_proj = grad_proj + conv_shared_ref[TAPS - 1 - k : TAPS - k, :] * moved
         sums[TAPS - 1 - k] = jnp.sum(moved * shared_proj, axis=0, keepdims=True)
     sums.append(jnp.sum(grad_pre, axis=0, keepdims=True))
@@ -410,6 +449,14 @@
     grad_step = (step_terms + rate * grad_log) * sigmoid(step_raw)
     grads_ref[:, channels : channels + width] = grad_proj.astype(bf16)
     grads_ref[:, channels + width :] = grad_step.astype(bf16)
+
+    @pl.when(turn == 0)
+    def _():
+        for copy in weight_copies():
+            copy.wait()
+
+    terms = mm(grad_gate_ref[...], gate_w[...], NT) + mm(grads_ref[...], weight[...], NT)
+    terms_ref[...] = terms.astype(bf16)
     sums_ref[:, channels + width :] += jnp.concatenate(
         [
             jnp.sum(grad_step, axis=0, keepdims=True),
@@ -427,7 +474,8 @@
 
 
 def mixer_backward(
-    lengths, upstream, saved, conv_inner, conv_shared, rate, skip, spread, carry, blocks, span
+    lengths, upstream, saved, conv_inner, conv_shared, rate, skip, spread, grad_gate, weight_late,
+    weight, carry, blocks, span
 ):
     ssm, inner, pre_inner, shared, pre_shared, step_raw, entering = saved
     rows, channels = upstream.shape
@@ -435,6 +483,7 @@
     states = width // 2
     begin, end = blocks
     known = channels + width + LANES
+    model = weight.shape[0]
     by_row = lambda cols: pl.BlockSpec((span, cols), lambda i: (end - 1 - i, 0))
     small = ((TAIL, known), (TAIL, channels), (TAIL, width), (states, channels))
     results = pl.pallas_call(
@@ -450,19 +499,27 @@
             full(rate.shape),
             full(skip.shape),
             full(spread.shape),
+            by_row(channels),
+            pl.BlockSpec(memory_space=pl.ANY),
+            pl.BlockSpec(memory_space=pl.ANY),
             *[full(shape) for shape in small],
         ],
         out_specs=[
             pl.BlockSpec((span, known), lambda i: (end - begin - 1 - i, 0)),
+            pl.BlockSpec((span, model), lambda i: (end - begin - 1 - i, 0)),
             *[full(shape) for shape in small],
         ],
         out_shape=[
             jax.ShapeDtypeStruct(((end - begin) * span, known), bf16),
+            jax.ShapeDtypeStruct(((end - begin) * span, model), bf16),
             *[jax.ShapeDtypeStruct(shape, f32) for shape in small],
         ],
         scratch_shapes=[
             pltpu.VMEM((TAIL + span, channels), f32),
             pltpu.VMEM((TAIL + span, width), f32),
+            pltpu.VMEM((model, channels), bf16),
+            pltpu.VMEM((model, known), bf16),
+            pltpu.SemaphoreType.DMA((2,)),
         ],
         compiler_params=pltpu.CompilerParams(
             dimension_semantics=("arbitrary",), vmem_limit_bytes=LIMIT
@@ -470,9 +527,9 @@
         name="mixer_backward",
     )(
         lengths, upstream, ssm, inner, pre_inner, shared, pre_shared, step_raw, entering,
-        conv_inner, conv_shared, rate, skip, spread, *carry,
-    )
-    return results[0], tuple(results[1:])
+        conv_inner, conv_shared, rate, skip, spread, grad_gate, weight_late, weight, *carry,
+    )
+    return results[0], results[1], tuple(results[2:])
 
 
 def gain_row(weight_ref, total_ref, columns):
@@ -709,33 +766,6 @@
     return (row == col).astype(bf16)
 
 
-def input_kernel(grad_gate_ref, grads_ref, gate_w_ref, weight_ref, terms_ref):
-    terms = mm(grad_gate_ref[...], gate_w_ref[...], NT)
-    terms = terms + mm(grads_ref[...], weight_ref[...], NT)
-    terms_ref[...] = terms.astype(bf16)
-
-
-def input_terms(grad_gate, grads, weight_late, weight, begin, span):
-    model = weight.shape[0]
-    channels = grad_gate.shape[1]
-    rows, known = grads.shape
-    return pl.pallas_call(
-        input_kernel,
-        grid=(rows // span,),
-        in_specs=[
-            pl.BlockSpec((span, channels), lambda i: (i + begin, 0)),
-            pl.BlockSpec((span, known), lambda i: (i, 0)),
-            pl.BlockSpec((model, channels), lambda i: (0, 0)), full(weight.shape),
-        ],
-        out_specs=pl.BlockSpec((span, model), lambda i: (i, 0)),
-        out_shape=jax.ShapeDtypeStruct((rows, model), bf16),
-        compiler_params=pltpu.CompilerParams(
-            dimension_semantics=("arbitrary",), vmem_limit_bytes=LIMIT
-        ),
-        name="input_terms",
-    )(grad_gate, grads, weight_late, weight)
-
-
 def dp_send(value, bit):
     size = lax.axis_size("dp")
     return lax.ppermute(value, "dp", [(i, i ^ bit) for i in range(size)])
@@ -815,9 +845,12 @@
         whole = jnp.concatenate(quarters, axis=0)
         return lax.psum_scatter(whole, "tensor", scatter_dimension=0, tiled=True).astype(f32)
     first = lax.axis_index("tensor") == 0
-    lower = jnp.concatenate(quarters[:2], axis=0)
+    each = other0.shape[0]
+    low, middle, high = quarters
+    lower = jnp.concatenate([low, middle[:each]], axis=0)
+    upper = jnp.concatenate([middle[each:], high], axis=0)
     others = jnp.concatenate([other0, other1], axis=0)
-    return jnp.where(first, lower, quarters[2]).astype(f32) + others.astype(f32)
+    return jnp.where(first, lower, upper).astype(f32) + others.astype(f32)
 
 
 def tensor_sum(value, size):
@@ -907,26 +940,21 @@
 
     def back(begin, end, carry):
         return mixer_backward(
-            lengths, grad_ssm, saved, conv_inner, conv_shared, rate, skip, spread, carry,
-            (begin * quarter, end * quarter), SPAN,
+            lengths, grad_ssm, saved, conv_inner, conv_shared, rate, skip, spread, grad_gate,
+            weight_late, weight, carry, (begin * quarter, end * quarter), SPAN,
         )
 
-    def terms_of(begin, grads):
-        return input_terms(grad_gate, grads, weight_late, weight, begin * quarter, SPAN)
-
     first = dp_send(send, 1)
-    grads2, carry = back(2, 4, carry)
+    grads3, terms3, carry = back(3, 4, carry)
     first = (keep.astype(f32) + first.astype(f32)).astype(bf16)
     first = first.reshape(count, 2, -1, first.shape[1])
-    carry, first, grads2 = lax.optimization_barrier((carry, first, grads2))
+    carry, first = lax.optimization_barrier((carry, first))
     first_gate, first_out = first[..., :channels], first[..., channels:]
-    terms2 = terms_of(2, grads2)
-    carry, terms2 = lax.optimization_barrier((carry, terms2))
-    grads1, carry = back(1, 2, carry)
-    terms1 = terms_of(1, grads1)
+    grads1, terms1, carry = back(1, 3, carry)
     first_gate = fold(first_gate, 2, 1)
     first_out = fold_chips(first_out).astype(bf16)
-    send1 = pick_half(terms2[terms2.shape[0] // 2 :], terms1, size)
+    each = terms3.shape[0]
+    send1 = pick_half(terms3, terms1[:each], size)
     carry, send1, branch_other, first_gate, first_out = lax.optimization_barrier(
         (carry, send1, branch_other, first_gate, first_out)
     )
@@ -934,44 +962,46 @@
     block_out = (inputs + (branch_own.astype(f32) + branch_other.astype(f32))).astype(bf16)
     part_gate = fold_chips(first_gate)
     part_out = fold(first_out, 2, 0)
-    grads0, carry = back(0, 1, carry)
-    sums, part_gate, part_out, grads0, other1, block_out = lax.optimization_barrier(
-        (carry[0], part_gate, part_out, grads0, other1, block_out)
-    )
+    grads0, terms0, carry = back(0, 1, carry)
+    send0 = pick_half(terms1[each:], terms0, size)
+    sums, part_gate, part_out, grads0, other1, block_out, send0 = lax.optimization_barrier(
+        (carry[0], part_gate, part_out, grads0, other1, block_out, send0)
+    )
+    other0 = gather_other(send0, size) if split else send0
     keep, send, sums = weight_products(
-        spot, normed, weight, norm_gain[None, :], sums, norm_sum, (grads0, grads1, grads2), chips,
+        spot, normed, weight, norm_gain[None, :], sums, norm_sum, (grads0, grads1, grads3), chips,
         (0, known), True,
     )
-    got = dp_send(send, 1)
-    terms0 = terms_of(0, grads0)
-    send0 = pick_half(terms2[: terms2.shape[0] // 2], terms0, size)
+    each = send.shape[0] // 4
+    got = [dp_send(send[i * each : (i + 1) * each], 1) for i in range(4)]
+    *got, other0, sums, keep = lax.optimization_barrier((*got, other0, sums, keep))
+    got = jnp.concatenate(got, axis=0)
     parts = (keep.astype(f32) + got.astype(f32)).astype(bf16).reshape(count, 2, -1, known)
-    parts, sums, send0 = lax.optimization_barrier((parts, sums, send0))
     cut = min((known * 2 // 3) // LANES * LANES, channels)
     parts_a, parts_b = parts[..., :cut], parts[..., cut:]
+    got_a = send_fold(parts_a, 2, 1)
     got_b = send_chips(parts_b)
+    shared_sums = tensor_sum(sums[:, channels:], size)
+    step_sums = sums[:, channels + width : known]
+    sums = jnp.concatenate([sums[:, :channels], step_sums, shared_sums], axis=1)
     sums = sums + dp_send(sums, 1)
-    got_a = send_fold(parts_a, 2, 1)
     sums = sums + dp_send(sums, 2)
-    sums = sums + dp_send(sums, 4)
-    send0, sums = lax.optimization_barrier((send0, sums))
-    other0 = gather_other(send0, size) if split else send0
-    got_a, got_b, sums = lax.optimization_barrier((got_a, got_b, sums))
+    grad_normed = sum_quarters((terms0, terms1, terms3), other0, other1, size)
+    scaled_grad = grad_normed * norm_gain[None, :]
+    grad_inputs = norm_scale * scaled_grad - inputs * norm_scale**3 * jnp.mean(
+        scaled_grad * inputs, axis=1, keepdims=True
+    )
+    grad_tokens = (cotangent.astype(f32) + grad_inputs).astype(bf16)
+    got_a, got_b, sums, grad_tokens = lax.optimization_barrier((got_a, got_b, sums, grad_tokens))
     parts_a = keep_fold(parts_a, got_a, 2, 1)
     parts_b = keep_chips(parts_b, got_b).astype(bf16)
     got_a = send_chips(parts_a)
     parts_b = fold(parts_b, 2, 0)
-    for bit in long_bits()[1:]:
+    for bit in long_bits():
         sums = sums + dp_send(sums, bit)
     parts_a = keep_chips(parts_a, got_a)
-    shared_sums = tensor_sum(sums[:, channels:], size)
+    shared_sums = sums[:, channels + LANES :]
     norm_sum = shared_sums[0, known - channels :]
-    grad_normed = sum_quarters((terms0, terms1, terms2), other0, other1, size)
-    scaled_grad = grad_normed * norm_gain[None, :]
-    grad_inputs = norm_scale * scaled_grad - inputs * norm_scale**3 * jnp.mean(
-        scaled_grad * inputs, axis=1, keepdims=True
-    )
-    grad_tokens = (cotangent.astype(f32) + grad_inputs).astype(bf16)
     part_inner = jnp.concatenate([parts_a, parts_b[:, : channels - cut]], axis=1)
     at_step = channels + width
     part_shared = tensor_sum(parts_b[:, channels - cut : at_step - cut], size)
@@ -988,9 +1018,9 @@
         sums[TAPS, :channels],
         shared_sums[:TAPS, :width],
         shared_sums[TAPS, :width],
-        sums[0, at_step : at_step + heads],
-        sums[1, at_step : at_step + heads],
-        sums[2, at_step : at_step + heads],
+        sums[0, channels : channels + heads],
+        sums[1, channels : channels + heads],
+        sums[2, channels : channels + heads],
         sums[TAIL - 1, :channels],
         part_out,
     )

time: 286 us -> 271 us (0.948)
  Pallas kernels: 126 us -> 112 us
  starting transfers between devices: 56.1 us -> 62.2 us
  local copies, waits for them, and re-layouts: 26.1 us -> 21.2 us
  other arithmetic: 33.9 us -> 30.6 us
    pallas_call x3 -> x0, Pallas kernels: 17.4 us -> none  [input_terms(): pl.pallas_call(input_kernel, grid=(rows // span,), in_specs=[pl.BlockSpec...]
    ppermute x40 -> x43, starting transfers between devices: 47.2 us -> 53.4 us  [dp_send(): return lax.ppermute(value, 'dp', [(i, i ^ bit) for i in range(size)])]
    pallas_call x3, Pallas kernels: 43.5 us -> 46.5 us  [mixer_backward(): pl.pallas_call(partial(backward_kernel, begin, rows), grid=(end - begin,)...]
    unnamed x78 -> x72, local copies, waits for them, and re-layouts: 7.78 us -> 5.1 us
    ppermute x40 -> x43, waiting for transfers between devices: 28.3 us -> 29 us  [dp_send(): return lax.ppermute(value, 'dp', [(i, i ^ bit) for i in range(size)])]
  transfers between devices with their start and end apart: 49 -> 52, of which waited for: 12 -> 18; matrix products, arithmetic and copies ran while one was open for 16% -> 15% of each run, Pallas kernels for 30% -> 29%
where the time goes in v3:
time: 271 us; the launch traced here: 268 us
  Pallas kernels  112 us (41%)
  starting transfers between devices  62.2 us (23%)
  waiting for transfers between devices  40 us (15%)
  other arithmetic  30.6 us (11%)
  local copies, waits for them, and re-layouts  21.2 us (8%)
    ppermute x43, starting transfers between devices, dp_send(): return lax.ppermute(value, 'dp', [(i, i ^ bit) for i in range(size)])  53.4 us
    pallas_call x3, Pallas kernels, mixer_backward(): pl.pallas_call(partial(backward_kernel, begin, rows), grid=(end - begin,)...  46.5 us
    ppermute x43, waiting for transfers between devices, dp_send(): return lax.ppermute(value, 'dp', [(i, i ^ bit) for i in range(size)])  29 us
    pallas_call x1, Pallas kernels, mixer_forward(): pl.pallas_call(partial(forward_kernel, 1 + len(others), count), grid=(blo...  23 us
    pallas_call x1, Pallas kernels, gate_norm(): pl.pallas_call(partial(norm_kernel, float(full_inner), chips, split), gri...  20.4 us
    pallas_call x1, Pallas kernels, gate_forward(): pl.pallas_call(partial(gate_kernel, 1 + len(others), count), grid=(rows /...  13.3 us
    ppermute x9, waiting for transfers between devices, tensor_swap(): return lax.ppermute(value, 'tensor', [(0, 1), (1, 0)])  11 us
    pallas_call x1, Pallas kernels, weight_products(): pl.pallas_call(partial(product_kernel, chips, columns, last), in_specs=[p...  9.02 us
  transfers between devices with their start and end apart: 52, of which 18 were waited for; matrix products, arithmetic and copies ran while one was open for 15% of the time, Pallas kernels for 29%

profile of v3, /device:TPU:0, one launch (start us, length us, event | category | flops | bytes accessed | tf_op | source)
XLA Modules:
  0.0 267.8 jit_solution(4265473924140936245)
XLA Ops:
  4.5 3.0 %collective-permute-start = (bf16[64,1408]{1,0:T(8,128)(2,1)}, bf16[64,1408]{1,0:T(8,128)(2,1)}, u32[]{:S(2)}, u32[]{:S(2)}) collective-permute-start(bf16[64,1408]{1,0:T(8,128)(2,1)} %pad_maximum_fusion.5), channel_id=1, source_target_pairs={{0,8},{2,10},{4,12},{6,14},{8,0},{10,2},{12,4},{14,6},{16,24},{18,... | collective-permute-start | bytes 540680 | tf_op jit(solution)/shard_map/ppermute | solution.py:771
  7.6 2.6 collective-permute-start.1
  12.4 1.7 collective-permute-start.4
  29.5 3.0 %collective-permute-start.7 = (bf16[128,768]{1,0:T(8,128)(2,1)S(1)}, bf16[128,768]{1,0:T(8,128)(2,1)S(1)}, u32[]{:S(2)}, u32[]{:S(2)}) collective-permute-start(bf16[128,768]{1,0:T(8,128)(2,1)S(1)} %slice.103), channel_id=1, source_target_pairs={{0,8},{2,10},{4,12},{6,14},{8,0},{10,2},{12,4},{14,6},{16,24},{18,... | collective-permute-start | bytes 589832 | tf_op jit(solution)/shard_map/ppermute | solution.py:771
  35.0 6.3 %collective-permute-done.6.refs_2_ = bf16[256,1024]{1,0:T(8,128)(2,1)S(1)} collective-permute-done((bf16[256,1024]{1,0:T(8,128)(2,1)S(1)}, bf16[256,1024]{1,0:T(8,128)(2,1)S(1)}, u32[]{:S(2)}, u32[]{:S(2)}) %collective-permute-start.6) | collective-permute-done | bytes 524320 | tf_op jit(solution)/shard_map/ppermute | solution.py:822
  41.8 6.9 %collective-permute-done.8 = bf16[128,768]{1,0:T(8,128)(2,1)S(1)} collective-permute-done((bf16[128,768]{1,0:T(8,128)(2,1)S(1)}, bf16[128,768]{1,0:T(8,128)(2,1)S(1)}, u32[]{:S(2)}, u32[]{:S(2)}) %collective-permute-start.8) | collective-permute-done | bytes 196640 | tf_op jit(solution)/shard_map/ppermute | solution.py:771
  49.6 2.7 %collective-permute-start.14 = (bf16[128,1280]{1,0:T(8,128)(2,1)S(1)}, bf16[128,1280]{1,0:T(8,128)(2,1)}, u32[]{:S(2)}, u32[]{:S(2)}) collective-permute-start(bf16[128,1280]{1,0:T(8,128)(2,1)S(1)} %slice.104.refs_4_), channel_id=1, source_target_pairs={{0,8},{2,10},{4,12},{6,14},{8,0},{10,2},{12,4},{14,6},{16,24},{18,... | collective-permute-start | bytes 983048 | tf_op jit(solution)/shard_map/ppermute | solution.py:771
  52.3 2.3 collective-permute-start.15
  56.9 23.0 %mixer_forward.1 = (bf16[1024,1024]{1,0:T(8,128)(2,1)}, bf16[1024,1408]{1,0:T(8,128)(2,1)}, f32[1024,1024]{1,0:T(8,128)}, f32[1024,1024]{1,0:T(8,128)}, f32[1024...) custom-call(s32[1,4]{1,0:T(1,128)} %add_bitcast_fusion.spot_ref, ...), custom_call_target="tpu_custom_call" | custom-call | tf_op jit(solution)/shard_map/mixer_forward/pallas_call | solution.py:270
  84.0 13.3 %gate_forward.1 = (bf16[1024,1024]{1,0:T(8,128)(2,1)}, bf16[1024,2048]{1,0:T(8,128)(2,1)}, f32[1024,1024]{1,0:T(8,128)}, f32[1024,1024]{1,0:T(8,128)}, f32[8,1024]{1,0:T(8,128)}) custom-call(s32[1,4]{1,0:T(1,128)} %add_bitcast_fusion.spot_ref, bf16[1024,1024]{1,0:T(8,128)(2,1)} %get-tuple-element.133.normed_ref, bf16[512,1024]{1,0:T(8,128)(2,1)} %refs_0_.1, ...), custom_call_target="tpu_custom_call" | custom-call | tf_op jit(solution)/shard_map/gate_forward/pallas_call | solution.py:627
  97.8 3.6 %collective-permute-done.21.more_ref = f32[8,1024]{1,0:T(8,128)S(1)} collective-permute-done((f32[8,1024]{1,0:T(8,128)}, f32[8,1024]{1,0:T(8,128)S(1)}, u32[]{:S(2)}, u32[]{:S(2)}) %collective-permute-start.21) | collective-permute-done | bytes 32800 | tf_op jit(solution)/shard_map/ppermute | solution.py:822
  102.1 20.4 %gate_norm.1 = (bf16[1024,1024]{1,0:T(8,128)(2,1)}, f32[1024,1024]{1,0:T(8,128)}, f32[8,1408]{1,0:T(8,128)}, bf16[512,2048]{1,0:T(8,128)(2,1)}, bf16[512,2048]{1...) custom-call(s32[1,4]{1,0:T(1,128)} %add_bitcast_fusion.spot_ref, ...), custom_call_target="tpu_custom_call" | custom-call | tf_op jit(solution)/shard_map/gate_norm/pallas_call | solution.py:724
  125.3 12.3 %mixer_backward.3 = (bf16[256,1408]{1,0:T(8,128)(2,1)}, bf16[256,1024]{1,0:T(8,128)(2,1)}, f32[8,1408]{1,0:T(8,128)}, f32[8,1024]{1,0:T(8,128)}, f32[8,256]{1,0:T(8,128)}, /*index=5*/f32[128,1024]{1,0:T(8,128)}) custom-call(s32[1,4]{1,0:T(1,128)} %lengths_ref.7, f32[1024,1024]{1,0:T(8,128)} %get-tuple-element.152.upstream_ref, ...), custom_call_target="tpu_custom_call" | custom-call | tf_op jit(solution)/shard_map/mixer_backward/pallas_call | solution.py:489
  137.6 2.4 add_convert_fusion
  141.1 4.8 %collective-permute-start.25 = (bf16[2,64,1024]{2,1,0:T(8,128)(2,1)}, bf16[2,64,1024]{2,1,0:T(8,128)(2,1)}, u32[]{:S(2)}, u32[]{:S(2)}) collective-permute-start(bf16[2,64,1024]{2,1,0:T(8,128)(2,1)} %get-tuple-element.262), channel_id=1, source_target_pairs={{0,8},{2,10},{4,12},{6,14},{8,0},{10,2},{12,4},{14,6},{16,24},{18,... | collective-permute-start | bytes 786440 | tf_op jit(solution)/shard_map/ppermute | solution.py:771
  150.2 22.1 %mixer_backward.4 = (bf16[512,1408]{1,0:T(8,128)(2,1)}, bf16[512,1024]{1,0:T(8,128)(2,1)}, f32[8,1408]{1,0:T(8,128)}, f32[8,1024]{1,0:T(8,128)}, f32[8,256]{1,0:T(8,128)}, /*index=5*/f32[128,1024]{1,0:T(8,128)}) custom-call(s32[1,4]{1,0:T(1,128)} %lengths_ref.7, f32[1024,1024]{1,0:T(8,128)} %get-tuple-element.152.upstream_ref, ...), custom_call_target="tpu_custom_call" | custom-call | tf_op jit(solution)/shard_map/mixer_backward/pallas_call | solution.py:489
  172.4 2.2 fusion.28
  179.0 2.8 %fusion.3 = bf16[512,1024]{1,0:T(8,128)(2,1)} fusion(bf16[512,1024]{1,0:T(8,128)(2,1)S(1)} %copy-done, bf16[512,1024]{1,0:T(8,128)(2,1)} %collective-permute-done.23, bf16[512,1024]{1,0:T(8,128)(2,1)S(1)} %copy-done.13), kind=kLoop, calls=%fused_computation.10 | loop fusion | flops 3145728 | bytes 4194304 | tf_op jit(solution)/shard_map/convert_element_type | solution.py:962
  181.8 12.1 %mixer_backward.5 = (bf16[256,1408]{1,0:T(8,128)(2,1)}, bf16[256,1024]{1,0:T(8,128)(2,1)}, f32[8,1408]{1,0:T(8,128)}, f32[8,1024]{1,0:T(8,128)}, f32[8,256]{1,0:T(8,128)}, /*index=5*/f32[128,1024]{1,0:T(8,128)}) custom-call(s32[1,4]{1,0:T(1,128)} %lengths_ref.7, f32[1024,1024]{1,0:T(8,128)} %get-tuple-element.152.upstream_ref, ...), custom_call_target="tpu_custom_call" | custom-call | tf_op jit(solution)/shard_map/mixer_backward/pallas_call | solution.py:489
  193.9 2.0 broadcast_select_fusion
  198.8 1.9 collective-permute-start.29
  203.3 7.0 %collective-permute-done.29 = bf16[64,1024]{1,0:T(8,128)(2,1)S(1)} collective-permute-done((bf16[64,1024]{1,0:T(8,128)(2,1)S(1)}, bf16[64,1024]{1,0:T(8,128)(2,1)S(1)}, u32[]{:S(2)}, u32[]{:S(2)}) %collective-permute-start.29) | collective-permute-done | bytes 131104 | tf_op jit(solution)/shard_map/ppermute | solution.py:771
  210.8 9.0 %weight_products.1 = (bf16[512,1408]{1,0:T(8,128)(2,1)}, bf16[512,1408]{1,0:T(8,128)(2,1)}, f32[8,2432]{1,0:T(8,128)}) custom-call(s32[1,4]{1,0:T(1,128)} %add_bitcast_fusion.spot_ref, bf16[1024,1024]{1,0:T(8,128)(2,1)} %get-tuple-element.133.normed_ref, bf16[1024,1408]{1,0:T(8,128)(2,1)} %get-tuple-element.160.weight_ref, f32[1,1024]{1,0:T(1,128)} %bitcast.106, ...), custom_call_target="tpu_custom_call" | custom-call | tf_op jit(solution)/shard_map/weight_products/pallas_call | solution.py:571
  224.6 1.8 fusion.8
  226.5 1.7 collective-permute-start.42
  230.7 2.0 collective-permute-start.39
  236.4 2.9 %fusion.7 = bf16[512,1024]{1,0:T(8,128)(2,1)} fusion(bf16[512,1024]{1,0:T(8,128)(2,1)S(1)} %copy-done, bf16[512,1024]{1,0:T(8,128)(2,1)S(1)} %copy-done.5, f32[512]{0:T(512)S(1)} %broadcast_multiply_fusion, f32[512]{0:T(512)S(1)} %copy-done.31, f32[1024]{0:T(1024)S(1)} %copy-done.27, f32[512]{0:T(512)S(1)} %copy-done.30, ...), kind=kLoop, calls=%fused_computation.14 | loop fusion | flops 12582912 | bytes 6301697 | tf_op jit(solution)/shard_map/convert_element_type | solution.py:994
  239.2 3.8 %collective-permute-done.44 = f32[8,2560]{1,0:T(8,128)S(1)} collective-permute-done((f32[8,2560]{1,0:T(8,128)S(1)}, f32[8,2560]{1,0:T(8,128)S(1)}, u32[]{:S(2)}, u32[]{:S(2)}) %collective-permute-start.44) | collective-permute-done | bytes 81952 | tf_op jit(solution)/shard_map/ppermute | solution.py:771
  243.0 2.7 collective-permute-done.40
  247.1 2.7 %collective-permute-start.47 = (bf16[64,896]{1,0:T(8,128)(2,1)S(1)}, bf16[64,896]{1,0:T(8,128)(2,1)S(1)}, u32[]{:S(2)}, u32[]{:S(2)}) collective-permute-start(bf16[64,896]{1,0:T(8,128)(2,1)S(1)} %get-tuple-element.273), channel_id=1, source_target_pairs={{0,8},{2,10},{4,12},{6,14},{8,0},{10,2},{12,4},{14,6},{16,24},{18,... | collective-permute-start | bytes 344072 | tf_op jit(solution)/shard_map/ppermute | solution.py:771
  255.3 2.8 %collective-permute-done.45 = f32[8,2560]{1,0:T(8,128)S(1)} collective-permute-done((f32[8,2560]{1,0:T(8,128)S(1)}, f32[8,2560]{1,0:T(8,128)S(1)}, u32[]{:S(2)}, u32[]{:S(2)}) %collective-permute-start.45) | collective-permute-done | bytes 81952 | tf_op jit(solution)/shard_map/ppermute | solution.py:771
  258.1 3.6 %collective-permute-start.46 = (f32[8,2560]{1,0:T(8,128)S(1)}, f32[8,2560]{1,0:T(8,128)S(1)}, u32[]{:S(2)}, u32[]{:S(2)}) collective-permute-start(f32[8,2560]{1,0:T(8,128)S(1)} %add.205), channel_id=1, source_target_pairs={{0,16},{2,18},{4,20},{6,22},{8,24},{10,26},{12,28},{14,30},{16,0},... | collective-permute-start | bytes 245768 | tf_op jit(solution)/shard_map/ppermute | solution.py:771
  (226 shorter events, 74.6 us)
Async XLA Ops:
  4.5 21.6 %collective-permute-start = (bf16[64,1408]{1,0:T(8,128)(2,1)}, bf16[64,1408]{1,0:T(8,128)(2,1)}, u32[]{:S(2)}, u32[]{:S(2)}) collective-permute-start(bf16[64,1408]{1,0:T(8,128)(2,1)} %pad_maximum_fusion.5), channel_id=1, source_target_pairs={{0,8},{2,10},{4,12},{6,14},{8,0},{10,2},{12,4},{14,6},{16,24},{18,... | collective-permute-start | bytes 540680 | tf_op jit(solution)/shard_map/ppermute | solution.py:771
  7.6 18.6 %collective-permute-start.1 = (bf16[64,1408]{1,0:T(8,128)(2,1)}, bf16[64,1408]{1,0:T(8,128)(2,1)}, u32[]{:S(2)}, u32[]{:S(2)}) collective-permute-start(bf16[64,1408]{1,0:T(8,128)(2,1)} %pad_maximum_fusion.5), channel_id=1, source_target_pairs={{0,16},{2,18},{4,20},{6,22},{8,24},{10,26},{12,28},{14,30},{16,0},... | collective-permute-start | bytes 540680 | tf_op jit(solution)/shard_map/ppermute | solution.py:771
  10.1 16.0 %collective-permute-start.2 = (bf16[64,1408]{1,0:T(8,128)(2,1)}, bf16[64,1408]{1,0:T(8,128)(2,1)}, u32[]{:S(2)}, u32[]{:S(2)}) collective-permute-start(bf16[64,1408]{1,0:T(8,128)(2,1)} %pad_maximum_fusion.5), channel_id=1, source_target_pairs={{0,24},{2,26},{4,28},{6,30},{8,16},{10,18},{12,20},{14,22},{16,8},... | collective-permute-start | bytes 540680 | tf_op jit(solution)/shard_map/ppermute | solution.py:771
  12.4 16.1 %collective-permute-start.4 = (bf16[256,1024]{1,0:T(8,128)(2,1)}, bf16[256,1024]{1,0:T(8,128)(2,1)}, u32[]{:S(2)}, u32[]{:S(2)}) collective-permute-start(bf16[256,1024]{1,0:T(8,128)(2,1)} %get-tuple-element.266), channel_id=1, source_target_pairs={{0,1},{1,0},{2,3},{3,2},{4,5},{5,4},{6,7},{7,6},{8,9},{9,8},{10,11... | collective-permute-start | bytes 1572872 | tf_op jit(solution)/shard_map/ppermute | solution.py:822
  15.0 12.4 %collective-permute-start.3 = (bf16[64,2048]{1,0:T(8,128)(2,1)}, bf16[64,2048]{1,0:T(8,128)(2,1)}, u32[]{:S(2)}, u32[]{:S(2)}) collective-permute-start(bf16[64,2048]{1,0:T(8,128)(2,1)} %pad_maximum_fusion.4), channel_id=1, source_target_pairs={{0,4},{2,6},{4,0},{6,2},{8,12},{10,14},{12,8},{14,10},{16,20},{18,... | collective-permute-start | bytes 786440 | tf_op jit(solution)/shard_map/ppermute | solution.py:771
  28.6 20.1 %collective-permute-start.5 = (bf16[256,1408]{1,0:T(8,128)(2,1)S(1)}, bf16[256,1408]{1,0:T(8,128)(2,1)S(1)}, u32[]{:S(2)}, u32[]{:S(2)}) collective-permute-start(bf16[256,1408]{1,0:T(8,128)(2,1)S(1)} %pad_maximum_fusion.1.refs_3_), channel_id=1, source_target_pairs={{0,4},{2,6},{4,0},{6,2},{8,12},{10,14},{12,8},{14,10},{16,20},{18,... | collective-permute-start | bytes 2162696 | tf_op jit(solution)/shard_map/ppermute | solution.py:771
  29.2 12.1 %collective-permute-start.6 = (bf16[256,1024]{1,0:T(8,128)(2,1)S(1)}, bf16[256,1024]{1,0:T(8,128)(2,1)S(1)}, u32[]{:S(2)}, u32[]{:S(2)}) collective-permute-start(bf16[256,1024]{1,0:T(8,128)(2,1)S(1)} %copy-done.18), channel_id=1, source_target_pairs={{0,1},{1,0},{2,3},{3,2},{4,5},{5,4},{6,7},{7,6},{8,9},{9,8},{10,11... | collective-permute-start | bytes 1572872 | tf_op jit(solution)/shard_map/ppermute | solution.py:822
  29.5 12.2 %collective-permute-start.7 = (bf16[128,768]{1,0:T(8,128)(2,1)S(1)}, bf16[128,768]{1,0:T(8,128)(2,1)S(1)}, u32[]{:S(2)}, u32[]{:S(2)}) collective-permute-start(bf16[128,768]{1,0:T(8,128)(2,1)S(1)} %slice.103), channel_id=1, source_target_pairs={{0,8},{2,10},{4,12},{6,14},{8,0},{10,2},{12,4},{14,6},{16,24},{18,... | collective-permute-start | bytes 589832 | tf_op jit(solution)/shard_map/ppermute | solution.py:771
  32.6 16.1 %collective-permute-start.8 = (bf16[128,768]{1,0:T(8,128)(2,1)S(1)}, bf16[128,768]{1,0:T(8,128)(2,1)S(1)}, u32[]{:S(2)}, u32[]{:S(2)}) collective-permute-start(bf16[128,768]{1,0:T(8,128)(2,1)S(1)} %slice.103), channel_id=1, source_target_pairs={{0,16},{2,18},{4,20},{6,22},{8,24},{10,26},{12,28},{14,30},{16,0},... | collective-permute-start | bytes 589832 | tf_op jit(solution)/shard_map/ppermute | solution.py:771
  34.0 14.7 %collective-permute-start.9 = (bf16[128,768]{1,0:T(8,128)(2,1)S(1)}, bf16[128,768]{1,0:T(8,128)(2,1)S(1)}, u32[]{:S(2)}, u32[]{:S(2)}) collective-permute-start(bf16[128,768]{1,0:T(8,128)(2,1)S(1)} %slice.103), channel_id=1, source_target_pairs={{0,24},{2,26},{4,28},{6,30},{8,16},{10,18},{12,20},{14,22},{16,8},... | collective-permute-start | bytes 589832 | tf_op jit(solution)/shard_map/ppermute | solution.py:771
  41.3 38.6 %collective-permute-start.12 = (bf16[512,1024]{1,0:T(8,128)(2,1)S(1)}, bf16[512,1024]{1,0:T(8,128)(2,1)}, u32[]{:S(2)}, u32[]{:S(2)}) collective-permute-start(bf16[512,1024]{1,0:T(8,128)(2,1)S(1)} %copy-done.4), channel_id=1, source_target_pairs={{0,1},{1,0},{2,3},{3,2},{4,5},{5,4},{6,7},{7,6},{8,9},{9,8},{10,11... | collective-permute-start | bytes 3145736 | tf_op jit(solution)/shard_map/ppermute | solution.py:822
  49.4 30.5 %collective-permute-start.13 = (bf16[512,768]{1,0:T(8,128)(2,1)S(1)}, bf16[512,768]{1,0:T(8,128)(2,1)}, u32[]{:S(2)}, u32[]{:S(2)}) collective-permute-start(bf16[512,768]{1,0:T(8,128)(2,1)S(1)} %constant_dynamic-update-slice_fusion.refs_2_), channel_id=1, source_target_pairs={{0,2},{2,0},{4,6},{6,4},{8,10},{10,8},{12,14},{14,12},{16,18},{18,... | collective-permute-start | bytes 2359304 | tf_op jit(solution)/shard_map/ppermute | solution.py:771
  49.6 30.3 %collective-permute-start.14 = (bf16[128,1280]{1,0:T(8,128)(2,1)S(1)}, bf16[128,1280]{1,0:T(8,128)(2,1)}, u32[]{:S(2)}, u32[]{:S(2)}) collective-permute-start(bf16[128,1280]{1,0:T(8,128)(2,1)S(1)} %slice.104.refs_4_), channel_id=1, source_target_pairs={{0,8},{2,10},{4,12},{6,14},{8,0},{10,2},{12,4},{14,6},{16,24},{18,... | collective-permute-start | bytes 983048 | tf_op jit(solution)/shard_map/ppermute | solution.py:771
  52.3 27.6 %collective-permute-start.15 = (bf16[128,1280]{1,0:T(8,128)(2,1)S(1)}, bf16[128,1280]{1,0:T(8,128)(2,1)}, u32[]{:S(2)}, u32[]{:S(2)}) collective-permute-start(bf16[128,1280]{1,0:T(8,128)(2,1)S(1)} %slice.104.refs_4_), channel_id=1, source_target_pairs={{0,16},{2,18},{4,20},{6,22},{8,24},{10,26},{12,28},{14,30},{16,0},... | collective-permute-start | bytes 983048 | tf_op jit(solution)/shard_map/ppermute | solution.py:771
  55.5 24.4 %collective-permute-start.16 = (bf16[128,1280]{1,0:T(8,128)(2,1)S(1)}, bf16[128,1280]{1,0:T(8,128)(2,1)}, u32[]{:S(2)}, u32[]{:S(2)}) collective-permute-start(bf16[128,1280]{1,0:T(8,128)(2,1)S(1)} %slice.104.refs_4_), channel_id=1, source_target_pairs={{0,24},{2,26},{4,28},{6,30},{8,16},{10,18},{12,20},{14,22},{16,8},... | collective-permute-start | bytes 983048 | tf_op jit(solution)/shard_map/ppermute | solution.py:771
  122.5 15.0 %collective-permute-start.22 = (bf16[512,2048]{1,0:T(8,128)(2,1)}, bf16[512,2048]{1,0:T(8,128)(2,1)}, u32[]{:S(2)}, u32[]{:S(2)}) collective-permute-start(bf16[512,2048]{1,0:T(8,128)(2,1)} %get-tuple-element.170), channel_id=1, source_target_pairs={{0,2},{2,0},{4,6},{6,4},{8,10},{10,8},{12,14},{14,12},{16,18},{18,... | collective-permute-start | bytes 6291464 | tf_op jit(solution)/shard_map/ppermute | solution.py:771
  122.6 54.6 %collective-permute-start.23 = (bf16[512,1024]{1,0:T(8,128)(2,1)}, bf16[512,1024]{1,0:T(8,128)(2,1)}, u32[]{:S(2)}, u32[]{:S(2)}) collective-permute-start(bf16[512,1024]{1,0:T(8,128)(2,1)} %get-tuple-element.181), channel_id=1, source_target_pairs={{0,1},{1,0},{2,3},{3,2},{4,5},{5,4},{6,7},{7,6},{8,9},{9,8},{10,11... | collective-permute-start | bytes 3145736 | tf_op jit(solution)/shard_map/ppermute | solution.py:822
  141.1 33.5 %collective-permute-start.25 = (bf16[2,64,1024]{2,1,0:T(8,128)(2,1)}, bf16[2,64,1024]{2,1,0:T(8,128)(2,1)}, u32[]{:S(2)}, u32[]{:S(2)}) collective-permute-start(bf16[2,64,1024]{2,1,0:T(8,128)(2,1)} %get-tuple-element.262), channel_id=1, source_target_pairs={{0,8},{2,10},{4,12},{6,14},{8,0},{10,2},{12,4},{14,6},{16,24},{18,... | collective-permute-start | bytes 786440 | tf_op jit(solution)/shard_map/ppermute | solution.py:771
  145.9 28.7 %collective-permute-start.26 = (bf16[2,64,1024]{2,1,0:T(8,128)(2,1)}, bf16[2,64,1024]{2,1,0:T(8,128)(2,1)}, u32[]{:S(2)}, u32[]{:S(2)}) collective-permute-start(bf16[2,64,1024]{2,1,0:T(8,128)(2,1)} %get-tuple-element.264), channel_id=1, source_target_pairs={{0,16},{2,18},{4,20},{6,22},{8,24},{10,26},{12,28},{14,30},{16,0},... | collective-permute-start | bytes 786440 | tf_op jit(solution)/shard_map/ppermute | solution.py:771
  146.9 27.8 %collective-permute-start.27 = (bf16[2,64,1024]{2,1,0:T(8,128)(2,1)S(1)}, bf16[2,64,1024]{2,1,0:T(8,128)(2,1)}, u32[]{:S(2)}, u32[]{:S(2)}) collective-permute-start(bf16[2,64,1024]{2,1,0:T(8,128)(2,1)S(1)} %get-tuple-element.263), channel_id=1, source_target_pairs={{0,24},{2,26},{4,28},{6,30},{8,16},{10,18},{12,20},{14,22},{16,8},... | collective-permute-start | bytes 786440 | tf_op jit(solution)/shard_map/ppermute | solution.py:771
  149.2 26.8 %collective-permute-start.24 = (bf16[4,64,1024]{2,1,0:T(8,128)(2,1)}, bf16[4,64,1024]{2,1,0:T(8,128)(2,1)}, u32[]{:S(2)}, u32[]{:S(2)}) collective-permute-start(bf16[4,64,1024]{2,1,0:T(8,128)(2,1)} %dynamic-slice_bitcast_fusion), channel_id=1, source_target_pairs={{0,4},{2,6},{4,0},{6,2},{8,12},{10,14},{12,8},{14,10},{16,20},{18,... | collective-permute-start | bytes 1572872 | tf_op jit(solution)/shard_map/ppermute | solution.py:771
  178.0 24.2 %collective-permute-start.31 = (bf16[64,1024]{1,0:T(8,128)(2,1)}, bf16[64,1024]{1,0:T(8,128)(2,1)S(1)}, u32[]{:S(2)}, u32[]{:S(2)}) collective-permute-start(bf16[64,1024]{1,0:T(8,128)(2,1)} %dynamic-slice_bitcast_fusion.8), channel_id=1, source_target_pairs={{0,4},{2,6},{4,0},{6,2},{8,12},{10,14},{12,8},{14,10},{16,20},{18,... | collective-permute-start | bytes 393224 | tf_op jit(solution)/shard_map/ppermute | solution.py:771
  195.9 14.4 %collective-permute-start.32 = (bf16[256,1024]{1,0:T(8,128)(2,1)S(1)}, bf16[256,1024]{1,0:T(8,128)(2,1)}, u32[]{:S(2)}, u32[]{:S(2)}) collective-permute-start(bf16[256,1024]{1,0:T(8,128)(2,1)S(1)} %copy-done.19), channel_id=1, source_target_pairs={{0,1},{1,0},{2,3},{3,2},{4,5},{5,4},{6,7},{7,6},{8,9},{9,8},{10,11... | collective-permute-start | bytes 1572872 | tf_op jit(solution)/shard_map/ppermute | solution.py:822
  198.8 11.4 %collective-permute-start.29 = (bf16[64,1024]{1,0:T(8,128)(2,1)S(1)}, bf16[64,1024]{1,0:T(8,128)(2,1)S(1)}, u32[]{:S(2)}, u32[]{:S(2)}) collective-permute-start(bf16[64,1024]{1,0:T(8,128)(2,1)S(1)} %get-tuple-element.272), channel_id=1, source_target_pairs={{0,16},{2,18},{4,20},{6,22},{8,24},{10,26},{12,28},{14,30},{16,0},... | collective-permute-start | bytes 393224 | tf_op jit(solution)/shard_map/ppermute | solution.py:771
  210.4 14.2 %collective-permute-start.37 = (bf16[256,1024]{1,0:T(8,128)(2,1)}, bf16[256,1024]{1,0:T(8,128)(2,1)S(1)}, u32[]{:S(2)}, u32[]{:S(2)}) collective-permute-start(bf16[256,1024]{1,0:T(8,128)(2,1)} %broadcast_select_fusion), channel_id=1, source_target_pairs={{0,1},{1,0},{2,3},{3,2},{4,5},{5,4},{6,7},{7,6},{8,9},{9,8},{10,11... | collective-permute-start | bytes 1572872 | tf_op jit(solution)/shard_map/ppermute | solution.py:822
  228.9 16.8 %collective-permute-start.38 = (bf16[4,64,896]{2,1,0:T(8,128)(2,1)S(1)}, bf16[4,64,896]{2,1,0:T(8,128)(2,1)S(1)}, u32[]{:S(2)}, u32[]{:S(2)}) collective-permute-start(bf16[4,64,896]{2,1,0:T(8,128)(2,1)S(1)} %dynamic-slice_bitcast_fusion.1), channel_id=1, source_target_pairs={{0,4},{2,6},{4,0},{6,2},{8,12},{10,14},{12,8},{14,10},{16,20},{18,... | collective-permute-start | bytes 1376264 | tf_op jit(solution)/shard_map/ppermute | solution.py:771
  230.7 12.3 %collective-permute-start.39 = (bf16[2,64,512]{2,1,0:T(8,128)(2,1)S(1)}, bf16[2,64,512]{2,1,0:T(8,128)(2,1)S(1)}, u32[]{:S(2)}, u32[]{:S(2)}) collective-permute-start(bf16[2,64,512]{2,1,0:T(8,128)(2,1)S(1)} %get-tuple-element.269), channel_id=1, source_target_pairs={{0,8},{2,10},{4,12},{6,14},{8,0},{10,2},{12,4},{14,6},{16,24},{18,... | collective-permute-start | bytes 393224 | tf_op jit(solution)/shard_map/ppermute | solution.py:771
  232.8 12.9 %collective-permute-start.40 = (bf16[2,64,512]{2,1,0:T(8,128)(2,1)S(1)}, bf16[2,64,512]{2,1,0:T(8,128)(2,1)S(1)}, u32[]{:S(2)}, u32[]{:S(2)}) collective-permute-start(bf16[2,64,512]{2,1,0:T(8,128)(2,1)S(1)} %get-tuple-element.268), channel_id=1, source_target_pairs={{0,16},{2,18},{4,20},{6,22},{8,24},{10,26},{12,28},{14,30},{16,0},... | collective-permute-start | bytes 393224 | tf_op jit(solution)/shard_map/ppermute | solution.py:771
  233.8 11.8 %collective-permute-start.41 = (bf16[2,64,512]{2,1,0:T(8,128)(2,1)S(1)}, bf16[2,64,512]{2,1,0:T(8,128)(2,1)S(1)}, u32[]{:S(2)}, u32[]{:S(2)}) collective-permute-start(bf16[2,64,512]{2,1,0:T(8,128)(2,1)S(1)} %get-tuple-element.267), channel_id=1, source_target_pairs={{0,24},{2,26},{4,28},{6,30},{8,16},{10,18},{12,20},{14,22},{16,8},... | collective-permute-start | bytes 393224 | tf_op jit(solution)/shard_map/ppermute | solution.py:771
  247.1 14.6 %collective-permute-start.47 = (bf16[64,896]{1,0:T(8,128)(2,1)S(1)}, bf16[64,896]{1,0:T(8,128)(2,1)S(1)}, u32[]{:S(2)}, u32[]{:S(2)}) collective-permute-start(bf16[64,896]{1,0:T(8,128)(2,1)S(1)} %get-tuple-element.273), channel_id=1, source_target_pairs={{0,8},{2,10},{4,12},{6,14},{8,0},{10,2},{12,4},{14,6},{16,24},{18,... | collective-permute-start | bytes 344072 | tf_op jit(solution)/shard_map/ppermute | solution.py:771
  249.8 11.9 %collective-permute-start.48 = (bf16[64,896]{1,0:T(8,128)(2,1)S(1)}, bf16[64,896]{1,0:T(8,128)(2,1)S(1)}, u32[]{:S(2)}, u32[]{:S(2)}) collective-permute-start(bf16[64,896]{1,0:T(8,128)(2,1)S(1)} %get-tuple-element.275), channel_id=1, source_target_pairs={{0,16},{2,18},{4,20},{6,22},{8,24},{10,26},{12,28},{14,30},{16,0},... | collective-permute-start | bytes 344072 | tf_op jit(solution)/shard_map/ppermute | solution.py:771
  250.9 10.8 %collective-permute-start.49 = (bf16[64,896]{1,0:T(8,128)(2,1)S(1)}, bf16[64,896]{1,0:T(8,128)(2,1)S(1)}, u32[]{:S(2)}, u32[]{:S(2)}) collective-permute-start(bf16[64,896]{1,0:T(8,128)(2,1)S(1)} %get-tuple-element.274), channel_id=1, source_target_pairs={{0,24},{2,26},{4,28},{6,30},{8,16},{10,18},{12,20},{14,22},{16,8},... | collective-permute-start | bytes 344072 | tf_op jit(solution)/shard_map/ppermute | solution.py:771
  (52 other events, 366.2 us)

commit v4 on v3

--- a/solution.py
+++ b/solution.py
@@ -137,14 +137,16 @@
             weight_ref[at, lo : lo + ref.shape[1]] = ref[here : here + rows, :]
 
 
-def split_cores(spot_ref, value_ref, keep_ref, send_ref, chips):
+def split_cores(spot_ref, value_ref, keep_ref, send_refs, chips):
     rows = keep_ref.shape[0] // chips
+    each = chips // len(send_refs)
     core = spot_ref[0, 3]
     for chip in range(chips):
         here = pl.ds(pl.multiple_of((2 * chip + core) * rows, rows), rows)
         there = pl.ds(pl.multiple_of((2 * chip + 1 - core) * rows, rows), rows)
         keep_ref[chip * rows : (chip + 1) * rows, :] = value_ref[here, :].astype(bf16)
-        send_ref[chip * rows : (chip + 1) * rows, :] = value_ref[there, :].astype(bf16)
+        at = (chip % each) * rows
+        send_refs[chip // each][at : at + rows, :] = value_ref[there, :].astype(bf16)
 
 
 def forward_kernel(
@@ -544,7 +546,7 @@
 
 def product_kernel(chips, columns, last, spot_ref, normed_ref, weight_ref, gain_ref, sums_ref,
                    norm_sum_ref, *refs):
-    grads, (keep_ref, send_ref, packed_ref, total) = refs[:-4], refs[-4:]
+    grads, (keep_ref, *send_refs, packed_ref, total) = refs[:-7], refs[-7:]
     lo, hi = columns
     at = 0
     for i, ref in enumerate(grads):
@@ -552,7 +554,7 @@
         added = mm(normed_ref[at : at + rows, :], ref[:, lo:hi], TN)
         total[...] = added if i == 0 else total[...] + added
         at += rows
-    split_cores(spot_ref, total, keep_ref, send_ref, chips)
+    split_cores(spot_ref, total, keep_ref, send_refs, chips)
     row = norm_sum_ref[0:1, :] + gain_row(weight_ref, total, columns)
     known = sums_ref.shape[1]
     if last:
@@ -567,13 +569,14 @@
     model = normed.shape[1]
     size = columns[1] - columns[0]
     part = jax.ShapeDtypeStruct((model // 2, size), bf16)
+    piece = jax.ShapeDtypeStruct((model // 8, size), bf16)
     vmem = pl.BlockSpec(memory_space=pltpu.VMEM)
     return pl.pallas_call(
         partial(product_kernel, chips, columns, last),
         in_specs=[pl.BlockSpec(memory_space=pltpu.SMEM), *[vmem for _ in range(5 + len(grads))]],
-        out_specs=[vmem, vmem, vmem],
+        out_specs=[vmem] * 6,
         out_shape=[
-            part, part, jax.ShapeDtypeStruct((TAIL, known + model if last else model), f32),
+            part, *[piece] * 4, jax.ShapeDtypeStruct((TAIL, known + model if last else model), f32),
         ],
         scratch_shapes=[pltpu.VMEM((model, size), f32)],
         compiler_params=pltpu.CompilerParams(vmem_limit_bytes=LIMIT),
@@ -706,7 +709,7 @@
 
     @pl.when(block == pl.num_programs(0) - 1)
     def _():
-        split_cores(spot_ref, totals, keep_ref, send_ref, chips)
+        split_cores(spot_ref, totals, keep_ref, [send_ref], chips)
         norm_sum_ref[...] = jnp.zeros_like(norm_sum_ref)
         norm_sum_ref[0:1, :] = gain_row(gate_w_ref, totals, (0, channels))
 
@@ -963,17 +966,17 @@
     part_gate = fold_chips(first_gate)
     part_out = fold(first_out, 2, 0)
     grads0, terms0, carry = back(0, 1, carry)
+    sums, part_gate, part_out, grads0, other1, block_out, terms0 = lax.optimization_barrier(
+        (carry[0], part_gate, part_out, grads0, other1, block_out, terms0)
+    )
     send0 = pick_half(terms1[each:], terms0, size)
-    sums, part_gate, part_out, grads0, other1, block_out, send0 = lax.optimization_barrier(
-        (carry[0], part_gate, part_out, grads0, other1, block_out, send0)
-    )
+    send0, grads0 = lax.optimization_barrier((send0, grads0))
     other0 = gather_other(send0, size) if split else send0
-    keep, send, sums = weight_products(
+    keep, *send, sums = weight_products(
         spot, normed, weight, norm_gain[None, :], sums, norm_sum, (grads0, grads1, grads3), chips,
         (0, known), True,
     )
-    each = send.shape[0] // 4
-    got = [dp_send(send[i * each : (i + 1) * each], 1) for i in range(4)]
+    got = [dp_send(piece, 1) for piece in send]
     *got, other0, sums, keep = lax.optimization_barrier((*got, other0, sums, keep))
     got = jnp.concatenate(got, axis=0)
     parts = (keep.astype(f32) + got.astype(f32)).astype(bf16).reshape(count, 2, -1, known)
@@ -983,6 +986,7 @@
     got_b = send_chips(parts_b)
     shared_sums = tensor_sum(sums[:, channels:], size)
     step_sums = sums[:, channels + width : known]
+    shared_sums, other0 = lax.optimization_barrier((shared_sums, other0))
     sums = jnp.concatenate([sums[:, :channels], step_sums, shared_sums], axis=1)
     sums = sums + dp_send(sums, 1)
     sums = sums + dp_send(sums, 2)

time: 271 us -> 262 us (0.967)
  waiting for transfers between devices: 40 us -> 27.9 us
    ppermute x43, waiting for transfers between devices: 29 us -> 18 us  [dp_send(): return lax.ppermute(value, 'dp', [(i, i ^ bit) for i in range(size)])]
  transfers between devices with their start and end apart: 52 -> 52, of which waited for: 18 -> 14; matrix products, arithmetic and copies ran while one was open for 15% -> 16% of each run, Pallas kernels for 29% -> 30%
where the time goes in v4:
time: 262 us; the launch traced here: 258 us
  Pallas kernels  112 us (43%)
  starting transfers between devices  61 us (23%)
  other arithmetic  32.8 us (13%)
  waiting for transfers between devices  27.9 us (11%)
  local copies, waits for them, and re-layouts  22.7 us (9%)
    ppermute x43, starting transfers between devices, dp_send(): return lax.ppermute(value, 'dp', [(i, i ^ bit) for i in range(size)])  52.9 us
    pallas_call x3, Pallas kernels, mixer_backward(): pl.pallas_call(partial(backward_kernel, begin, rows), grid=(end - begin,)...  46.7 us
    pallas_call x1, Pallas kernels, mixer_forward(): pl.pallas_call(partial(forward_kernel, 1 + len(others), count), grid=(blo...  22.9 us
    pallas_call x1, Pallas kernels, gate_norm(): pl.pallas_call(partial(norm_kernel, float(full_inner), chips, split), gri...  20.2 us
    ppermute x43, waiting for transfers between devices, dp_send(): return lax.ppermute(value, 'dp', [(i, i ^ bit) for i in range(size)])  18 us
    pallas_call x1, Pallas kernels, gate_forward(): pl.pallas_call(partial(gate_kernel, 1 + len(others), count), grid=(rows /...  13.3 us
    ppermute x9, waiting for transfers between devices, tensor_swap(): return lax.ppermute(value, 'tensor', [(0, 1), (1, 0)])  9.89 us
    pallas_call x1, Pallas kernels, weight_products(): pl.pallas_call(partial(product_kernel, chips, columns, last), in_specs=[p...  8.83 us
  transfers between devices with their start and end apart: 52, of which 14 were waited for; matrix products, arithmetic and copies ran while one was open for 16% of the time, Pallas kernels for 30%

profile of v4, /device:TPU:0, one launch (start us, length us, event | category | flops | bytes accessed | tf_op | source)
XLA Modules:
  0.0 258.0 jit_solution(16438012477606247090)
XLA Ops:
  0.7 1.6 fusion.29
  4.5 3.0 %collective-permute-start = (bf16[64,1408]{1,0:T(8,128)(2,1)}, bf16[64,1408]{1,0:T(8,128)(2,1)}, u32[]{:S(2)}, u32[]{:S(2)}) collective-permute-start(bf16[64,1408]{1,0:T(8,128)(2,1)} %pad_maximum_fusion.5), channel_id=1, source_target_pairs={{0,8},{2,10},{4,12},{6,14},{8,0},{10,2},{12,4},{14,6},{16,24},{18,... | collective-permute-start | bytes 540680 | tf_op jit(solution)/shard_map/ppermute | solution.py:774
  7.5 2.6 %collective-permute-start.1 = (bf16[64,1408]{1,0:T(8,128)(2,1)}, bf16[64,1408]{1,0:T(8,128)(2,1)}, u32[]{:S(2)}, u32[]{:S(2)}) collective-permute-start(bf16[64,1408]{1,0:T(8,128)(2,1)} %pad_maximum_fusion.5), channel_id=1, source_target_pairs={{0,16},{2,18},{4,20},{6,22},{8,24},{10,26},{12,28},{14,30},{16,0},... | collective-permute-start | bytes 540680 | tf_op jit(solution)/shard_map/ppermute | solution.py:774
  12.5 1.7 collective-permute-start.4
  19.9 1.7 fusion.9.refs_14_.spread_ref
  29.5 3.0 %collective-permute-start.7 = (bf16[128,768]{1,0:T(8,128)(2,1)S(1)}, bf16[128,768]{1,0:T(8,128)(2,1)S(1)}, u32[]{:S(2)}, u32[]{:S(2)}) collective-permute-start(bf16[128,768]{1,0:T(8,128)(2,1)S(1)} %slice.91), channel_id=1, source_target_pairs={{0,8},{2,10},{4,12},{6,14},{8,0},{10,2},{12,4},{14,6},{16,24},{18,... | collective-permute-start | bytes 589832 | tf_op jit(solution)/shard_map/ppermute | solution.py:774
  35.0 6.2 %collective-permute-done.6.refs_2_ = bf16[256,1024]{1,0:T(8,128)(2,1)S(1)} collective-permute-done((bf16[256,1024]{1,0:T(8,128)(2,1)S(1)}, bf16[256,1024]{1,0:T(8,128)(2,1)S(1)}, u32[]{:S(2)}, u32[]{:S(2)}) %collective-permute-start.6) | collective-permute-done | bytes 524320 | tf_op jit(solution)/shard_map/ppermute | solution.py:825
  41.7 7.0 %collective-permute-done.8 = bf16[128,768]{1,0:T(8,128)(2,1)S(1)} collective-permute-done((bf16[128,768]{1,0:T(8,128)(2,1)S(1)}, bf16[128,768]{1,0:T(8,128)(2,1)S(1)}, u32[]{:S(2)}, u32[]{:S(2)}) %collective-permute-start.8) | collective-permute-done | bytes 196640 | tf_op jit(solution)/shard_map/ppermute | solution.py:774
  49.6 2.7 %collective-permute-start.14 = (bf16[128,1280]{1,0:T(8,128)(2,1)S(1)}, bf16[128,1280]{1,0:T(8,128)(2,1)}, u32[]{:S(2)}, u32[]{:S(2)}) collective-permute-start(bf16[128,1280]{1,0:T(8,128)(2,1)S(1)} %slice.92.refs_4_), channel_id=1, source_target_pairs={{0,8},{2,10},{4,12},{6,14},{8,0},{10,2},{12,4},{14,6},{16,24},{18,... | collective-permute-start | bytes 983048 | tf_op jit(solution)/shard_map/ppermute | solution.py:774
  52.3 2.3 collective-permute-start.15
  56.9 22.9 %mixer_forward.1 = (bf16[1024,1024]{1,0:T(8,128)(2,1)}, bf16[1024,1408]{1,0:T(8,128)(2,1)}, f32[1024,1024]{1,0:T(8,128)}, f32[1024,1024]{1,0:T(8,128)}, f32[1024...) custom-call(s32[1,4]{1,0:T(1,128)} %add_bitcast_fusion.spot_ref, ...), custom_call_target="tpu_custom_call" | custom-call | tf_op jit(solution)/shard_map/mixer_forward/pallas_call | solution.py:272
  84.0 13.3 %gate_forward.1 = (bf16[1024,1024]{1,0:T(8,128)(2,1)}, bf16[1024,2048]{1,0:T(8,128)(2,1)}, f32[1024,1024]{1,0:T(8,128)}, f32[1024,1024]{1,0:T(8,128)}, f32[8,1024]{1,0:T(8,128)}) custom-call(s32[1,4]{1,0:T(1,128)} %add_bitcast_fusion.spot_ref, bf16[1024,1024]{1,0:T(8,128)(2,1)} %get-tuple-element.140.normed_ref, bf16[512,1024]{1,0:T(8,128)(2,1)} %refs_0_.1, ...), custom_call_target="tpu_custom_call" | custom-call | tf_op jit(solution)/shard_map/gate_forward/pallas_call | solution.py:630
  97.8 3.6 %collective-permute-done.21.more_ref = f32[8,1024]{1,0:T(8,128)S(1)} collective-permute-done((f32[8,1024]{1,0:T(8,128)}, f32[8,1024]{1,0:T(8,128)S(1)}, u32[]{:S(2)}, u32[]{:S(2)}) %collective-permute-start.21) | collective-permute-done | bytes 32800 | tf_op jit(solution)/shard_map/ppermute | solution.py:825
  102.0 20.2 %gate_norm.1 = (bf16[1024,1024]{1,0:T(8,128)(2,1)}, f32[1024,1024]{1,0:T(8,128)}, f32[8,1408]{1,0:T(8,128)}, bf16[512,2048]{1,0:T(8,128)(2,1)}, bf16[512,2048]{1...) custom-call(s32[1,4]{1,0:T(1,128)} %add_bitcast_fusion.spot_ref, ...), custom_call_target="tpu_custom_call" | custom-call | tf_op jit(solution)/shard_map/gate_norm/pallas_call | solution.py:727
  125.0 12.2 %mixer_backward.3 = (bf16[256,1408]{1,0:T(8,128)(2,1)}, bf16[256,1024]{1,0:T(8,128)(2,1)}, f32[8,1408]{1,0:T(8,128)}, f32[8,1024]{1,0:T(8,128)}, f32[8,256]{1,0:T(8,128)}, /*index=5*/f32[128,1024]{1,0:T(8,128)}) custom-call(s32[1,4]{1,0:T(1,128)} %lengths_ref.7, f32[1024,1024]{1,0:T(8,128)} %get-tuple-element.159.upstream_ref, ...), custom_call_target="tpu_custom_call" | custom-call | tf_op jit(solution)/shard_map/mixer_backward/pallas_call | solution.py:491
  137.2 2.4 add_convert_fusion
  140.8 4.8 %collective-permute-start.25 = (bf16[2,64,1024]{2,1,0:T(8,128)(2,1)}, bf16[2,64,1024]{2,1,0:T(8,128)(2,1)}, u32[]{:S(2)}, u32[]{:S(2)}) collective-permute-start(bf16[2,64,1024]{2,1,0:T(8,128)(2,1)} %get-tuple-element.272), channel_id=1, source_target_pairs={{0,8},{2,10},{4,12},{6,14},{8,0},{10,2},{12,4},{14,6},{16,24},{18,... | collective-permute-start | bytes 786440 | tf_op jit(solution)/shard_map/ppermute | solution.py:774
  149.9 22.5 %mixer_backward.4 = (bf16[512,1408]{1,0:T(8,128)(2,1)}, bf16[512,1024]{1,0:T(8,128)(2,1)}, f32[8,1408]{1,0:T(8,128)}, f32[8,1024]{1,0:T(8,128)}, f32[8,256]{1,0:T(8,128)}, /*index=5*/f32[128,1024]{1,0:T(8,128)}) custom-call(s32[1,4]{1,0:T(1,128)} %lengths_ref.7, f32[1024,1024]{1,0:T(8,128)} %get-tuple-element.159.upstream_ref, ...), custom_call_target="tpu_custom_call" | custom-call | tf_op jit(solution)/shard_map/mixer_backward/pallas_call | solution.py:491
  172.4 2.2 fusion.27
  180.9 1.9 collective-permute-start.29
  185.7 2.8 %fusion.3 = bf16[512,1024]{1,0:T(8,128)(2,1)} fusion(bf16[512,1024]{1,0:T(8,128)(2,1)S(1)} %copy-done, bf16[512,1024]{1,0:T(8,128)(2,1)} %collective-permute-done.23, bf16[512,1024]{1,0:T(8,128)(2,1)S(1)} %copy-done.12), kind=kLoop, calls=%fused_computation.10 | loop fusion | flops 3145728 | bytes 4194304 | tf_op jit(solution)/shard_map/convert_element_type | solution.py:965
  188.6 12.1 %mixer_backward.5 = (bf16[256,1408]{1,0:T(8,128)(2,1)}, bf16[256,1024]{1,0:T(8,128)(2,1)}, f32[8,1408]{1,0:T(8,128)}, f32[8,1024]{1,0:T(8,128)}, f32[8,256]{1,0:T(8,128)}, /*index=5*/f32[128,1024]{1,0:T(8,128)}) custom-call(s32[1,4]{1,0:T(1,128)} %lengths_ref.7, f32[1024,1024]{1,0:T(8,128)} %get-tuple-element.159.upstream_ref, ...), custom_call_target="tpu_custom_call" | custom-call | tf_op jit(solution)/shard_map/mixer_backward/pallas_call | solution.py:491
  200.7 1.6 convert_add_fusion.5
  205.2 8.8 %weight_products.1 = (bf16[512,1408]{1,0:T(8,128)(2,1)}, bf16[128,1408]{1,0:T(8,128)(2,1)}, bf16[128,1408]{1,0:T(8,128)(2,1)}, bf16[128,1408]{1,0:T(8,128)(2,1)}...) custom-call(s32[1,4]{1,0:T(1,128)} %add_bitcast_fusion.spot_ref, bf16[1024,1024]{1,0:T(8,128)(2,1)} %get-tuple-element.140.normed_ref, ...), custom_call_target="tpu_custom_call" | custom-call | tf_op jit(solution)/shard_map/weight_products/pallas_call | solution.py:574
  219.7 1.7 add_convert_fusion.1
  224.0 2.8 %collective-permute-start.40 = (bf16[2,64,512]{2,1,0:T(8,128)(2,1)S(1)}, bf16[2,64,512]{2,1,0:T(8,128)(2,1)S(1)}, u32[]{:S(2)}, u32[]{:S(2)}) collective-permute-start(bf16[2,64,512]{2,1,0:T(8,128)(2,1)S(1)} %get-tuple-element.278), channel_id=1, source_target_pairs={{0,16},{2,18},{4,20},{6,22},{8,24},{10,26},{12,28},{14,30},{16,0},... | collective-permute-start | bytes 393224 | tf_op jit(solution)/shard_map/ppermute | solution.py:774
  228.4 1.8 fusion.8
  231.8 2.9 %fusion.7 = bf16[512,1024]{1,0:T(8,128)(2,1)} fusion(bf16[512,1024]{1,0:T(8,128)(2,1)S(1)} %copy-done, bf16[512,1024]{1,0:T(8,128)(2,1)S(1)} %copy-done.5, f32[512]{0:T(512)S(1)} %broadcast_multiply_fusion, f32[512]{0:T(512)S(1)} %copy-done.29, f32[1024]{0:T(1024)S(1)} %copy-done.25, f32[512]{0:T(512)S(1)} %copy-done.28, ...), kind=kLoop, calls=%fused_computation.14 | loop fusion | flops 12582912 | bytes 6301697 | tf_op jit(solution)/shard_map/convert_element_type | solution.py:998
  234.7 2.5 collective-permute-done.44
  238.6 2.1 collective-permute-start.47
  245.7 2.8 %collective-permute-done.45 = f32[8,2560]{1,0:T(8,128)S(1)} collective-permute-done((f32[8,2560]{1,0:T(8,128)S(1)}, f32[8,2560]{1,0:T(8,128)S(1)}, u32[]{:S(2)}, u32[]{:S(2)}) %collective-permute-start.45) | collective-permute-done | bytes 81952 | tf_op jit(solution)/shard_map/ppermute | solution.py:774
  248.5 3.4 %collective-permute-start.46 = (f32[8,2560]{1,0:T(8,128)S(1)}, f32[8,2560]{1,0:T(8,128)S(1)}, u32[]{:S(2)}, u32[]{:S(2)}) collective-permute-start(f32[8,2560]{1,0:T(8,128)S(1)} %add.205), channel_id=1, source_target_pairs={{0,16},{2,18},{4,20},{6,22},{8,24},{10,26},{12,28},{14,30},{16,0},... | collective-permute-start | bytes 245768 | tf_op jit(solution)/shard_map/ppermute | solution.py:774
  (221 shorter events, 73.0 us)
Async XLA Ops:
  4.5 21.6 %collective-permute-start = (bf16[64,1408]{1,0:T(8,128)(2,1)}, bf16[64,1408]{1,0:T(8,128)(2,1)}, u32[]{:S(2)}, u32[]{:S(2)}) collective-permute-start(bf16[64,1408]{1,0:T(8,128)(2,1)} %pad_maximum_fusion.5), channel_id=1, source_target_pairs={{0,8},{2,10},{4,12},{6,14},{8,0},{10,2},{12,4},{14,6},{16,24},{18,... | collective-permute-start | bytes 540680 | tf_op jit(solution)/shard_map/ppermute | solution.py:774
  7.5 18.5 %collective-permute-start.1 = (bf16[64,1408]{1,0:T(8,128)(2,1)}, bf16[64,1408]{1,0:T(8,128)(2,1)}, u32[]{:S(2)}, u32[]{:S(2)}) collective-permute-start(bf16[64,1408]{1,0:T(8,128)(2,1)} %pad_maximum_fusion.5), channel_id=1, source_target_pairs={{0,16},{2,18},{4,20},{6,22},{8,24},{10,26},{12,28},{14,30},{16,0},... | collective-permute-start | bytes 540680 | tf_op jit(solution)/shard_map/ppermute | solution.py:774
  10.1 16.0 %collective-permute-start.2 = (bf16[64,1408]{1,0:T(8,128)(2,1)}, bf16[64,1408]{1,0:T(8,128)(2,1)}, u32[]{:S(2)}, u32[]{:S(2)}) collective-permute-start(bf16[64,1408]{1,0:T(8,128)(2,1)} %pad_maximum_fusion.5), channel_id=1, source_target_pairs={{0,24},{2,26},{4,28},{6,30},{8,16},{10,18},{12,20},{14,22},{16,8},... | collective-permute-start | bytes 540680 | tf_op jit(solution)/shard_map/ppermute | solution.py:774
  12.5 16.1 %collective-permute-start.4 = (bf16[256,1024]{1,0:T(8,128)(2,1)}, bf16[256,1024]{1,0:T(8,128)(2,1)}, u32[]{:S(2)}, u32[]{:S(2)}) collective-permute-start(bf16[256,1024]{1,0:T(8,128)(2,1)} %get-tuple-element.276), channel_id=1, source_target_pairs={{0,1},{1,0},{2,3},{3,2},{4,5},{5,4},{6,7},{7,6},{8,9},{9,8},{10,11... | collective-permute-start | bytes 1572872 | tf_op jit(solution)/shard_map/ppermute | solution.py:825
  15.0 12.4 %collective-permute-start.3 = (bf16[64,2048]{1,0:T(8,128)(2,1)}, bf16[64,2048]{1,0:T(8,128)(2,1)}, u32[]{:S(2)}, u32[]{:S(2)}) collective-permute-start(bf16[64,2048]{1,0:T(8,128)(2,1)} %pad_maximum_fusion.4), channel_id=1, source_target_pairs={{0,4},{2,6},{4,0},{6,2},{8,12},{10,14},{12,8},{14,10},{16,20},{18,... | collective-permute-start | bytes 786440 | tf_op jit(solution)/shard_map/ppermute | solution.py:774
  28.6 20.1 %collective-permute-start.5 = (bf16[256,1408]{1,0:T(8,128)(2,1)S(1)}, bf16[256,1408]{1,0:T(8,128)(2,1)S(1)}, u32[]{:S(2)}, u32[]{:S(2)}) collective-permute-start(bf16[256,1408]{1,0:T(8,128)(2,1)S(1)} %pad_maximum_fusion.1.refs_3_), channel_id=1, source_target_pairs={{0,4},{2,6},{4,0},{6,2},{8,12},{10,14},{12,8},{14,10},{16,20},{18,... | collective-permute-start | bytes 2162696 | tf_op jit(solution)/shard_map/ppermute | solution.py:774
  29.2 12.1 %collective-permute-start.6 = (bf16[256,1024]{1,0:T(8,128)(2,1)S(1)}, bf16[256,1024]{1,0:T(8,128)(2,1)S(1)}, u32[]{:S(2)}, u32[]{:S(2)}) collective-permute-start(bf16[256,1024]{1,0:T(8,128)(2,1)S(1)} %copy-done.17), channel_id=1, source_target_pairs={{0,1},{1,0},{2,3},{3,2},{4,5},{5,4},{6,7},{7,6},{8,9},{9,8},{10,11... | collective-permute-start | bytes 1572872 | tf_op jit(solution)/shard_map/ppermute | solution.py:825
  29.5 12.2 %collective-permute-start.7 = (bf16[128,768]{1,0:T(8,128)(2,1)S(1)}, bf16[128,768]{1,0:T(8,128)(2,1)S(1)}, u32[]{:S(2)}, u32[]{:S(2)}) collective-permute-start(bf16[128,768]{1,0:T(8,128)(2,1)S(1)} %slice.91), channel_id=1, source_target_pairs={{0,8},{2,10},{4,12},{6,14},{8,0},{10,2},{12,4},{14,6},{16,24},{18,... | collective-permute-start | bytes 589832 | tf_op jit(solution)/shard_map/ppermute | solution.py:774
  32.6 16.1 %collective-permute-start.8 = (bf16[128,768]{1,0:T(8,128)(2,1)S(1)}, bf16[128,768]{1,0:T(8,128)(2,1)S(1)}, u32[]{:S(2)}, u32[]{:S(2)}) collective-permute-start(bf16[128,768]{1,0:T(8,128)(2,1)S(1)} %slice.91), channel_id=1, source_target_pairs={{0,16},{2,18},{4,20},{6,22},{8,24},{10,26},{12,28},{14,30},{16,0},... | collective-permute-start | bytes 589832 | tf_op jit(solution)/shard_map/ppermute | solution.py:774
  33.9 14.8 %collective-permute-start.9 = (bf16[128,768]{1,0:T(8,128)(2,1)S(1)}, bf16[128,768]{1,0:T(8,128)(2,1)S(1)}, u32[]{:S(2)}, u32[]{:S(2)}) collective-permute-start(bf16[128,768]{1,0:T(8,128)(2,1)S(1)} %slice.91), channel_id=1, source_target_pairs={{0,24},{2,26},{4,28},{6,30},{8,16},{10,18},{12,20},{14,22},{16,8},... | collective-permute-start | bytes 589832 | tf_op jit(solution)/shard_map/ppermute | solution.py:774
  41.3 38.6 %collective-permute-start.12 = (bf16[512,1024]{1,0:T(8,128)(2,1)S(1)}, bf16[512,1024]{1,0:T(8,128)(2,1)}, u32[]{:S(2)}, u32[]{:S(2)}) collective-permute-start(bf16[512,1024]{1,0:T(8,128)(2,1)S(1)} %copy-done.4), channel_id=1, source_target_pairs={{0,1},{1,0},{2,3},{3,2},{4,5},{5,4},{6,7},{7,6},{8,9},{9,8},{10,11... | collective-permute-start | bytes 3145736 | tf_op jit(solution)/shard_map/ppermute | solution.py:825
  49.4 30.5 %collective-permute-start.13 = (bf16[512,768]{1,0:T(8,128)(2,1)S(1)}, bf16[512,768]{1,0:T(8,128)(2,1)}, u32[]{:S(2)}, u32[]{:S(2)}) collective-permute-start(bf16[512,768]{1,0:T(8,128)(2,1)S(1)} %constant_dynamic-update-slice_fusion.refs_2_), channel_id=1, source_target_pairs={{0,2},{2,0},{4,6},{6,4},{8,10},{10,8},{12,14},{14,12},{16,18},{18,... | collective-permute-start | bytes 2359304 | tf_op jit(solution)/shard_map/ppermute | solution.py:774
  49.6 30.3 %collective-permute-start.14 = (bf16[128,1280]{1,0:T(8,128)(2,1)S(1)}, bf16[128,1280]{1,0:T(8,128)(2,1)}, u32[]{:S(2)}, u32[]{:S(2)}) collective-permute-start(bf16[128,1280]{1,0:T(8,128)(2,1)S(1)} %slice.92.refs_4_), channel_id=1, source_target_pairs={{0,8},{2,10},{4,12},{6,14},{8,0},{10,2},{12,4},{14,6},{16,24},{18,... | collective-permute-start | bytes 983048 | tf_op jit(solution)/shard_map/ppermute | solution.py:774
  52.3 27.6 %collective-permute-start.15 = (bf16[128,1280]{1,0:T(8,128)(2,1)S(1)}, bf16[128,1280]{1,0:T(8,128)(2,1)}, u32[]{:S(2)}, u32[]{:S(2)}) collective-permute-start(bf16[128,1280]{1,0:T(8,128)(2,1)S(1)} %slice.92.refs_4_), channel_id=1, source_target_pairs={{0,16},{2,18},{4,20},{6,22},{8,24},{10,26},{12,28},{14,30},{16,0},... | collective-permute-start | bytes 983048 | tf_op jit(solution)/shard_map/ppermute | solution.py:774
  55.5 24.4 %collective-permute-start.16 = (bf16[128,1280]{1,0:T(8,128)(2,1)S(1)}, bf16[128,1280]{1,0:T(8,128)(2,1)}, u32[]{:S(2)}, u32[]{:S(2)}) collective-permute-start(bf16[128,1280]{1,0:T(8,128)(2,1)S(1)} %slice.92.refs_4_), channel_id=1, source_target_pairs={{0,24},{2,26},{4,28},{6,30},{8,16},{10,18},{12,20},{14,22},{16,8},... | collective-permute-start | bytes 983048 | tf_op jit(solution)/shard_map/ppermute | solution.py:774
  122.2 15.0 %collective-permute-start.22 = (bf16[512,2048]{1,0:T(8,128)(2,1)}, bf16[512,2048]{1,0:T(8,128)(2,1)}, u32[]{:S(2)}, u32[]{:S(2)}) collective-permute-start(bf16[512,2048]{1,0:T(8,128)(2,1)} %get-tuple-element.177), channel_id=1, source_target_pairs={{0,2},{2,0},{4,6},{6,4},{8,10},{10,8},{12,14},{14,12},{16,18},{18,... | collective-permute-start | bytes 6291464 | tf_op jit(solution)/shard_map/ppermute | solution.py:774
  122.4 54.9 %collective-permute-start.23 = (bf16[512,1024]{1,0:T(8,128)(2,1)}, bf16[512,1024]{1,0:T(8,128)(2,1)}, u32[]{:S(2)}, u32[]{:S(2)}) collective-permute-start(bf16[512,1024]{1,0:T(8,128)(2,1)} %get-tuple-element.188), channel_id=1, source_target_pairs={{0,1},{1,0},{2,3},{3,2},{4,5},{5,4},{6,7},{7,6},{8,9},{9,8},{10,11... | collective-permute-start | bytes 3145736 | tf_op jit(solution)/shard_map/ppermute | solution.py:825
  140.8 33.8 %collective-permute-start.25 = (bf16[2,64,1024]{2,1,0:T(8,128)(2,1)}, bf16[2,64,1024]{2,1,0:T(8,128)(2,1)}, u32[]{:S(2)}, u32[]{:S(2)}) collective-permute-start(bf16[2,64,1024]{2,1,0:T(8,128)(2,1)} %get-tuple-element.272), channel_id=1, source_target_pairs={{0,8},{2,10},{4,12},{6,14},{8,0},{10,2},{12,4},{14,6},{16,24},{18,... | collective-permute-start | bytes 786440 | tf_op jit(solution)/shard_map/ppermute | solution.py:774
  145.6 29.0 %collective-permute-start.26 = (bf16[2,64,1024]{2,1,0:T(8,128)(2,1)}, bf16[2,64,1024]{2,1,0:T(8,128)(2,1)}, u32[]{:S(2)}, u32[]{:S(2)}) collective-permute-start(bf16[2,64,1024]{2,1,0:T(8,128)(2,1)} %get-tuple-element.274), channel_id=1, source_target_pairs={{0,16},{2,18},{4,20},{6,22},{8,24},{10,26},{12,28},{14,30},{16,0},... | collective-permute-start | bytes 786440 | tf_op jit(solution)/shard_map/ppermute | solution.py:774
  146.6 28.0 %collective-permute-start.27 = (bf16[2,64,1024]{2,1,0:T(8,128)(2,1)S(1)}, bf16[2,64,1024]{2,1,0:T(8,128)(2,1)}, u32[]{:S(2)}, u32[]{:S(2)}) collective-permute-start(bf16[2,64,1024]{2,1,0:T(8,128)(2,1)S(1)} %get-tuple-element.273), channel_id=1, source_target_pairs={{0,24},{2,26},{4,28},{6,30},{8,16},{10,18},{12,20},{14,22},{16,8},... | collective-permute-start | bytes 786440 | tf_op jit(solution)/shard_map/ppermute | solution.py:774
  148.9 27.0 %collective-permute-start.24 = (bf16[4,64,1024]{2,1,0:T(8,128)(2,1)}, bf16[4,64,1024]{2,1,0:T(8,128)(2,1)}, u32[]{:S(2)}, u32[]{:S(2)}) collective-permute-start(bf16[4,64,1024]{2,1,0:T(8,128)(2,1)} %dynamic-slice_bitcast_fusion), channel_id=1, source_target_pairs={{0,4},{2,6},{4,0},{6,2},{8,12},{10,14},{12,8},{14,10},{16,20},{18,... | collective-permute-start | bytes 1572872 | tf_op jit(solution)/shard_map/ppermute | solution.py:774
  177.9 22.7 %collective-permute-start.31 = (bf16[64,1024]{1,0:T(8,128)(2,1)}, bf16[64,1024]{1,0:T(8,128)(2,1)}, u32[]{:S(2)}, u32[]{:S(2)}) collective-permute-start(bf16[64,1024]{1,0:T(8,128)(2,1)} %dynamic-slice_bitcast_fusion.8), channel_id=1, source_target_pairs={{0,4},{2,6},{4,0},{6,2},{8,12},{10,14},{12,8},{14,10},{16,20},{18,... | collective-permute-start | bytes 393224 | tf_op jit(solution)/shard_map/ppermute | solution.py:774
  179.8 22.5 %collective-permute-start.28 = (bf16[64,1024]{1,0:T(8,128)(2,1)}, bf16[64,1024]{1,0:T(8,128)(2,1)S(1)}, u32[]{:S(2)}, u32[]{:S(2)}) collective-permute-start(bf16[64,1024]{1,0:T(8,128)(2,1)} %get-tuple-element.280), channel_id=1, source_target_pairs={{0,8},{2,10},{4,12},{6,14},{8,0},{10,2},{12,4},{14,6},{16,24},{18,... | collective-permute-start | bytes 393224 | tf_op jit(solution)/shard_map/ppermute | solution.py:774
  180.9 21.4 %collective-permute-start.29 = (bf16[64,1024]{1,0:T(8,128)(2,1)}, bf16[64,1024]{1,0:T(8,128)(2,1)}, u32[]{:S(2)}, u32[]{:S(2)}) collective-permute-start(bf16[64,1024]{1,0:T(8,128)(2,1)} %get-tuple-element.282), channel_id=1, source_target_pairs={{0,16},{2,18},{4,20},{6,22},{8,24},{10,26},{12,28},{14,30},{16,0},... | collective-permute-start | bytes 393224 | tf_op jit(solution)/shard_map/ppermute | solution.py:774
  182.8 19.5 %collective-permute-start.30 = (bf16[64,1024]{1,0:T(8,128)(2,1)}, bf16[64,1024]{1,0:T(8,128)(2,1)}, u32[]{:S(2)}, u32[]{:S(2)}) collective-permute-start(bf16[64,1024]{1,0:T(8,128)(2,1)} %get-tuple-element.281), channel_id=1, source_target_pairs={{0,24},{2,26},{4,28},{6,30},{8,16},{10,18},{12,20},{14,22},{16,8},... | collective-permute-start | bytes 393224 | tf_op jit(solution)/shard_map/ppermute | solution.py:774
  184.2 19.1 %collective-permute-start.32 = (bf16[256,1024]{1,0:T(8,128)(2,1)}, bf16[256,1024]{1,0:T(8,128)(2,1)}, u32[]{:S(2)}, u32[]{:S(2)}) collective-permute-start(bf16[256,1024]{1,0:T(8,128)(2,1)} %get-tuple-element.198), channel_id=1, source_target_pairs={{0,1},{1,0},{2,3},{3,2},{4,5},{5,4},{6,7},{7,6},{8,9},{9,8},{10,11... | collective-permute-start | bytes 1572872 | tf_op jit(solution)/shard_map/ppermute | solution.py:825
  204.5 13.0 %collective-permute-start.37 = (bf16[256,1024]{1,0:T(8,128)(2,1)S(1)}, bf16[256,1024]{1,0:T(8,128)(2,1)S(1)}, u32[]{:S(2)}, u32[]{:S(2)}) collective-permute-start(bf16[256,1024]{1,0:T(8,128)(2,1)S(1)} %broadcast_select_fusion), channel_id=1, source_target_pairs={{0,1},{1,0},{2,3},{3,2},{4,5},{5,4},{6,7},{7,6},{8,9},{9,8},{10,11... | collective-permute-start | bytes 1572872 | tf_op jit(solution)/shard_map/ppermute | solution.py:825
  223.1 14.2 %collective-permute-start.38 = (bf16[4,64,896]{2,1,0:T(8,128)(2,1)S(1)}, bf16[4,64,896]{2,1,0:T(8,128)(2,1)S(1)}, u32[]{:S(2)}, u32[]{:S(2)}) collective-permute-start(bf16[4,64,896]{2,1,0:T(8,128)(2,1)S(1)} %dynamic-slice_bitcast_fusion.1), channel_id=1, source_target_pairs={{0,4},{2,6},{4,0},{6,2},{8,12},{10,14},{12,8},{14,10},{16,20},{18,... | collective-permute-start | bytes 1376264 | tf_op jit(solution)/shard_map/ppermute | solution.py:774
  223.7 13.5 %collective-permute-start.39 = (bf16[2,64,512]{2,1,0:T(8,128)(2,1)S(1)}, bf16[2,64,512]{2,1,0:T(8,128)(2,1)S(1)}, u32[]{:S(2)}, u32[]{:S(2)}) collective-permute-start(bf16[2,64,512]{2,1,0:T(8,128)(2,1)S(1)} %get-tuple-element.279), channel_id=1, source_target_pairs={{0,8},{2,10},{4,12},{6,14},{8,0},{10,2},{12,4},{14,6},{16,24},{18,... | collective-permute-start | bytes 393224 | tf_op jit(solution)/shard_map/ppermute | solution.py:774
  224.0 13.2 %collective-permute-start.40 = (bf16[2,64,512]{2,1,0:T(8,128)(2,1)S(1)}, bf16[2,64,512]{2,1,0:T(8,128)(2,1)S(1)}, u32[]{:S(2)}, u32[]{:S(2)}) collective-permute-start(bf16[2,64,512]{2,1,0:T(8,128)(2,1)S(1)} %get-tuple-element.278), channel_id=1, source_target_pairs={{0,16},{2,18},{4,20},{6,22},{8,24},{10,26},{12,28},{14,30},{16,0},... | collective-permute-start | bytes 393224 | tf_op jit(solution)/shard_map/ppermute | solution.py:774
  238.6 13.4 %collective-permute-start.47 = (bf16[64,896]{1,0:T(8,128)(2,1)S(1)}, bf16[64,896]{1,0:T(8,128)(2,1)S(1)}, u32[]{:S(2)}, u32[]{:S(2)}) collective-permute-start(bf16[64,896]{1,0:T(8,128)(2,1)S(1)} %get-tuple-element.283), channel_id=1, source_target_pairs={{0,8},{2,10},{4,12},{6,14},{8,0},{10,2},{12,4},{14,6},{16,24},{18,... | collective-permute-start | bytes 344072 | tf_op jit(solution)/shard_map/ppermute | solution.py:774
  240.7 11.3 %collective-permute-start.48 = (bf16[64,896]{1,0:T(8,128)(2,1)S(1)}, bf16[64,896]{1,0:T(8,128)(2,1)S(1)}, u32[]{:S(2)}, u32[]{:S(2)}) collective-permute-start(bf16[64,896]{1,0:T(8,128)(2,1)S(1)} %get-tuple-element.285), channel_id=1, source_target_pairs={{0,16},{2,18},{4,20},{6,22},{8,24},{10,26},{12,28},{14,30},{16,0},... | collective-permute-start | bytes 344072 | tf_op jit(solution)/shard_map/ppermute | solution.py:774
  (50 other events, 366.2 us)

commit v5 on v4

--- a/solution.py
+++ b/solution.py
@@ -219,9 +219,10 @@
     in_map = shared[:, : width // 2].astype(bf16)
     out_map = shared[:, width // 2 :].astype(bf16)
     scores = mm(out_map, in_map, NT)
+    in_map_t = jnp.transpose(in_map)
     allowed = jnp.where((row >= col) & same_rows(ends, base, rows), 0.0, MASKED)
     running_t = jnp.transpose(running)
-    step2, entry2, leave2 = halves(step, 1), halves(entry, 1), halves(leave, 1)
+    factors = jnp.concatenate([halves(x, 1) for x in (step, entry, leave)], axis=0)
     lane = lax.broadcasted_iota(jnp.int32, (rows, LANES), 1)
     for pair in range(channels // LANES):
         lo, hi = pair * LANES, (pair + 1) * LANES
@@ -231,8 +232,10 @@
         side = (pair % 2) * LANES
         if side == 0:
             spread = spread_ref[:, lo : min(lo + 2 * LANES, channels)]
-            wide = [mm(value, spread, NN) for value in (step2, entry2, leave2)]
-        step_wide, entry_wide, leave_wide = [x[:, side : side + LANES] for x in wide]
+            wide = mm(factors, spread, NN)
+        step_wide, entry_wide, leave_wide = [
+            wide[i * rows : (i + 1) * rows, side : side + LANES] for i in range(3)
+        ]
         scaled = head_in * step_wide
         scaled_low = scaled.astype(bf16)
         held = state[:, lo:hi]
@@ -242,11 +245,11 @@
         for parity in range(2):
             head = 2 * pair + parity
             gap = running[:, head : head + 1] - running_t[head : head + 1, :]
-            mixed = (scores * jnp.exp(gap + allowed)).astype(bf16)
-            parts.append(mm(mixed, scaled_low, NN))
-        intra = jnp.where(lane < LANES // 2, parts[0], parts[1])
+            parts.append((scores * jnp.exp(gap + allowed)).astype(bf16))
+        both = mm(jnp.concatenate(parts, axis=0), scaled_low, NN)
+        intra = jnp.where(lane < LANES // 2, both[:rows], both[rows:])
         ssm_ref[:, lo:hi] = carried_out + intra + skip_ref[:, lo:hi] * head_in
-        added = mm(in_map, (scaled * leave_wide).astype(bf16), TN)
+        added = mm(in_map_t, (scaled * leave_wide).astype(bf16), NN)
         state[:, lo:hi] = held * entry_wide[rows - 1 :, :] + added
 
 
@@ -301,12 +304,15 @@
 
 
 def backward_kernel(
-    first_block, total_rows, lengths_ref, upstream_ref, ssm_ref, inner_ref, pre_inner_ref, shared_ref, pre_shared_ref,
-    step_ref, entering_ref, conv_inner_ref, conv_shared_ref, rate_ref, skip_ref, spread_ref,
-    grad_gate_ref, gate_w_ref, weight_ref, sums_in_ref, inner_in_ref, shared_in_ref, adjoint_in_ref,
-    grads_ref, terms_ref, sums_ref, inner_out_ref, shared_out_ref, adjoint, inner_head, shared_head,
-    gate_w, weight, done,
+    first_block, total_rows, lengths_ref, upstream_ref, ssm_ref, inner_ref, pre_inner_ref,
+    shared_ref, pre_shared_ref, step_ref, entering_ref, conv_inner_ref, conv_shared_ref, rate_ref, skip_ref, spread_ref,
+    grad_gate_ref, gate_w_ref, weight_ref, sums_in_ref, *refs,
 ):
+    carried_in, refs = refs[:-11], refs[-11:]
+    (
+        grads_ref, terms_ref, sums_ref, inner_out_ref, shared_out_ref, adjoint, inner_head,
+        shared_head, gate_w, weight, done,
+    ) = refs
     turn = pl.program_id(0)
     block = first_block + pl.num_programs(0) - 1 - turn
     rows, channels = upstream_ref.shape
@@ -322,9 +328,14 @@
 
     @pl.when(turn == 0)
     def _():
-        inner_head[rows : rows + TAIL, :] = inner_in_ref[...]
-        shared_head[rows : rows + TAIL, :] = shared_in_ref[...]
-        adjoint[...] = adjoint_in_ref[...]
+        if carried_in:
+            inner_head[rows : rows + TAIL, :] = carried_in[0][...]
+            shared_head[rows : rows + TAIL, :] = carried_in[1][...]
+            adjoint[...] = carried_in[2][...]
+        else:
+            inner_head[rows : rows + TAIL, :] = jnp.zeros((TAIL, channels), f32)
+            shared_head[rows : rows + TAIL, :] = jnp.zeros((TAIL, width), f32)
+            adjoint[...] = jnp.zeros_like(adjoint)
         sums_ref[...] = sums_in_ref[...]
         for copy in weight_copies():
             copy.start()
@@ -350,25 +361,27 @@
     in_map = shared[:, :half].astype(bf16)
     out_map = shared[:, half:].astype(bf16)
     scores_t = mm(in_map, out_map, NT)
+    out_map_t = jnp.transpose(out_map)
     allowed_t = jnp.where((col >= row) & same_rows(ends, base, rows), 0.0, MASKED)
     running_t = jnp.transpose(running)
-    step2, entry2, leave2 = halves(step, 1), halves(entry, 1), halves(leave, 1)
+    factors = jnp.concatenate([halves(x, 1) for x in (step, entry, leave)], axis=0)
     lane = lax.broadcasted_iota(jnp.int32, (rows, LANES), 1)
     first_half = lane < LANES // 2
     grad_scores_t = jnp.zeros((rows, rows), f32)
     grad_in = jnp.zeros((rows, half), f32)
     grad_out = jnp.zeros((rows, half), f32)
-    by_head = jnp.zeros((rows, LANES), f32)
+    by_head = jnp.zeros((rows + TAIL, LANES), f32)
     step_terms = jnp.zeros((rows, LANES), f32)
-    leaving = jnp.zeros((TAIL, LANES), f32)
     for pair in range(channels // LANES):
         lo, hi = pair * LANES, (pair + 1) * LANES
         side = (pair % 2) * LANES
         if side == 0:
             spread = spread_ref[:, lo : min(lo + 2 * LANES, channels)]
-            wide = [mm(value, spread, NN) for value in (step2, entry2, leave2)]
+            wide = mm(factors, spread, NN)
             products = []
-        step_wide, entry_wide, leave_wide = [x[:, side : side + LANES] for x in wide]
+        step_wide, entry_wide, leave_wide = [
+            wide[i * rows : (i + 1) * rows, side : side + LANES] for i in range(3)
+        ]
         pre = pre_inner_ref[:, lo:hi]
         gate = sigmoid(pre)
         head_in = pre * gate
@@ -391,29 +404,31 @@
         tail_terms = jnp.sum(scaled_back * grad_scaled, axis=0, keepdims=True) + through * jnp.sum(
             ahead * held, axis=0, keepdims=True
         )
-        adjoint[:, lo:hi] = ahead * through + mm(out_map, entry_up, TN)
-        parts = []
+        adjoint[:, lo:hi] = ahead * through + mm(out_map_t, entry_up, NN)
+        parts, decays, chosen = [], [], []
         for parity in range(2):
             head = 2 * pair + parity
             gap = running_t[head : head + 1, :] - running[:, head : head + 1]
-            decay = jnp.exp(gap + allowed_t)
-            mixed = (scores_t * decay).astype(bf16)
-            parts.append(mm(mixed, upstream_low, NN))
+            decays.append(jnp.exp(gap + allowed_t))
+            parts.append((scores_t * decays[parity]).astype(bf16))
             mine = first_half if parity == 0 else jnp.logical_not(first_half)
-            chosen = jnp.where(mine, scaled_back, 0.0).astype(bf16)
-            grad_scores_t = grad_scores_t + mm(chosen, upstream_low, NT) * decay
-        grad_scaled = grad_scaled + jnp.where(first_half, parts[0], parts[1])
+            chosen.append(jnp.where(mine, scaled_back, 0.0).astype(bf16))
+        both = mm(jnp.concatenate(parts, axis=0), upstream_low, NN)
+        pulled = mm(jnp.concatenate(chosen, axis=0), upstream_low, NT)
+        grad_scores_t = grad_scores_t + (pulled[:rows] * decays[0] + pulled[rows:] * decays[1])
+        grad_scaled = grad_scaled + jnp.where(first_half, both[:rows], both[rows:])
         spread_one = spread[:LANES, side : side + LANES]
         spread_both = jnp.concatenate([spread_one, spread_one], axis=1)
         balance = upstream_back * (ssm_ref[:, lo:hi] - skip * head_in) - scaled_back * grad_scaled
-        by_head = by_head + mm(halves(balance, 1), spread_both, NT)
         products.append((head_in * grad_scaled).astype(bf16))
         if hi == channels or side > 0:
             joined = jnp.concatenate(products, axis=1)
             step_terms = step_terms + mm(joined, spread[:LANES, :], NT)
         skip_terms = jnp.sum(upstream * head_in, axis=0, keepdims=True)
         edge = jnp.concatenate([tail_terms, skip_terms, jnp.zeros((TAIL - 2, LANES), f32)], axis=0)
-        leaving = leaving + mm(halves(edge, 1), spread_both, NT)
+        by_head = by_head + mm(
+            halves(jnp.concatenate([balance, edge], axis=0), 1), spread_both, NT
+        )
         grad_pre = (grad_scaled * step_wide + skip * upstream) * (gate * (1.0 + pre * (1.0 - gate)))
         inner_head[0:rows, lo:hi] = grad_pre
         inner_proj = inner_ref[:, lo:hi]
@@ -446,7 +461,8 @@
     sums.append(jnp.sum(grad_pre, axis=0, keepdims=True))
     sums.append(jnp.zeros((TAIL - len(sums), width), f32))
     sums_ref[:, channels : channels + width] += jnp.concatenate(sums, axis=0)
-    split = mm(lower, halves(by_head, 1), TN)
+    leaving = by_head[rows:]
+    split = mm(lower, halves(by_head[:rows], 1), TN)
     grad_log = split[:, :LANES] + split[:, LANES:] + leaving[0:1, :]
     grad_step = (step_terms + rate * grad_log) * sigmoid(step_raw)
     grads_ref[:, channels : channels + width] = grad_proj.astype(bf16)
@@ -504,7 +520,7 @@
             by_row(channels),
             pl.BlockSpec(memory_space=pl.ANY),
             pl.BlockSpec(memory_space=pl.ANY),
-            *[full(shape) for shape in small],
+            *[full(x.shape) for x in carry],
         ],
         out_specs=[
             pl.BlockSpec((span, known), lambda i: (end - begin - 1 - i, 0)),
@@ -544,9 +560,9 @@
     return jnp.sum(jnp.transpose(added), axis=0, keepdims=True)
 
 
-def product_kernel(chips, columns, last, spot_ref, normed_ref, weight_ref, gain_ref, sums_ref,
+def product_kernel(chips, columns, spot_ref, normed_ref, weight_ref, gain_ref, sums_ref,
                    norm_sum_ref, *refs):
-    grads, (keep_ref, *send_refs, packed_ref, total) = refs[:-7], refs[-7:]
+    grads, (keep_ref, *send_refs, heads_ref, shared_ref, total) = refs[:-8], refs[-8:]
     lo, hi = columns
     at = 0
     for i, ref in enumerate(grads):
@@ -556,27 +572,28 @@
         at += rows
     split_cores(spot_ref, total, keep_ref, send_refs, chips)
     row = norm_sum_ref[0:1, :] + gain_row(weight_ref, total, columns)
-    known = sums_ref.shape[1]
-    if last:
-        packed_ref[:, :known] = sums_ref[...]
-        packed_ref[:, known:] = jnp.broadcast_to(row / gain_ref[...], norm_sum_ref.shape)
-    else:
-        packed_ref[...] = jnp.broadcast_to(row, norm_sum_ref.shape)
-
-
-def weight_products(spot, normed, weight, gain, sums, norm_sum, grads, chips, columns, last):
+    width = shared_ref.shape[1] - norm_sum_ref.shape[1]
+    inner = heads_ref.shape[1] - LANES
+    heads_ref[:, :inner] = sums_ref[:, :inner]
+    heads_ref[:, inner:] = sums_ref[:, inner + width :]
+    shared_ref[:, :width] = sums_ref[:, inner : inner + width]
+    shared_ref[:, width:] = jnp.broadcast_to(row / gain_ref[...], norm_sum_ref.shape)
+
+
+def weight_products(spot, normed, weight, gain, sums, norm_sum, grads, chips, width):
     known = grads[0].shape[1]
     model = normed.shape[1]
-    size = columns[1] - columns[0]
+    size = known
     part = jax.ShapeDtypeStruct((model // 2, size), bf16)
     piece = jax.ShapeDtypeStruct((model // 8, size), bf16)
     vmem = pl.BlockSpec(memory_space=pltpu.VMEM)
     return pl.pallas_call(
-        partial(product_kernel, chips, columns, last),
+        partial(product_kernel, chips, (0, known)),
         in_specs=[pl.BlockSpec(memory_space=pltpu.SMEM), *[vmem for _ in range(5 + len(grads))]],
-        out_specs=[vmem] * 6,
+        out_specs=[vmem] * 7,
         out_shape=[
-            part, *[piece] * 4, jax.ShapeDtypeStruct((TAIL, known + model if last else model), f32),
+            part, *[piece] * 4, jax.ShapeDtypeStruct((TAIL, known - width), f32),
+            jax.ShapeDtypeStruct((TAIL, width + model), f32),
         ],
         scratch_shapes=[pltpu.VMEM((model, size), f32)],
         compiler_params=pltpu.CompilerParams(vmem_limit_bytes=LIMIT),
@@ -888,18 +905,13 @@
         spread_map(heads, channels),
     )
     late = jnp.concatenate([zx_weight[:, 0, :], out_weight], axis=1)
-    zeros = (
-        jnp.zeros((TAIL, channels), f32), jnp.zeros((TAIL, width), f32),
-        jnp.zeros((width // 2, channels), f32),
-    )
-
     def along(value):
         return [value] + [dp_send(value, bit) for bit in chip_bits()]
 
     column = jnp.concatenate(along(early), axis=0)
-    column, pair, top, fixed, zeros, spot = lax.optimization_barrier((
+    column, pair, top, fixed, spot = lax.optimization_barrier((
         column, jnp.concatenate([late, dp_send(late, 2)], axis=0),
-        gather_other(normed_rows[:half], size), fixed, zeros, spot,
+        gather_other(normed_rows[:half], size), fixed, spot,
     ))
     cut_late = (2 * channels * 3 // 8) // LANES * LANES
     joined = along(pair[:, :cut_late])
@@ -939,7 +951,7 @@
         branch_own = lax.psum_scatter(branch_own, "tensor", scatter_dimension=0, tiled=True)
         branch_other = jnp.zeros_like(branch_own)
     quarter = grad_ssm.shape[0] // SPAN // 4
-    carry = (gain_sum, *zeros)
+    carry = (gain_sum,)
 
     def back(begin, end, carry):
         return mixer_backward(
@@ -962,32 +974,32 @@
         (carry, send1, branch_other, first_gate, first_out)
     )
     other1 = gather_other(send1, size) if split else send1
-    block_out = (inputs + (branch_own.astype(f32) + branch_other.astype(f32))).astype(bf16)
     part_gate = fold_chips(first_gate)
     part_out = fold(first_out, 2, 0)
     grads0, terms0, carry = back(0, 1, carry)
-    sums, part_gate, part_out, grads0, other1, block_out, terms0 = lax.optimization_barrier(
-        (carry[0], part_gate, part_out, grads0, other1, block_out, terms0)
+    sums, part_gate, part_out, grads0, other1, terms0 = lax.optimization_barrier(
+        (carry[0], part_gate, part_out, grads0, other1, terms0)
     )
     send0 = pick_half(terms1[each:], terms0, size)
     send0, grads0 = lax.optimization_barrier((send0, grads0))
     other0 = gather_other(send0, size) if split else send0
-    keep, *send, sums = weight_products(
+    keep, *send, sums, shared_sums = weight_products(
         spot, normed, weight, norm_gain[None, :], sums, norm_sum, (grads0, grads1, grads3), chips,
-        (0, known), True,
+        width,
     )
     got = [dp_send(piece, 1) for piece in send]
-    *got, other0, sums, keep = lax.optimization_barrier((*got, other0, sums, keep))
+    *got, other0, sums, shared_sums, keep = lax.optimization_barrier(
+        (*got, other0, sums, shared_sums, keep)
+    )
     got = jnp.concatenate(got, axis=0)
     parts = (keep.astype(f32) + got.astype(f32)).astype(bf16).reshape(count, 2, -1, known)
     cut = min((known * 2 // 3) // LANES * LANES, channels)
     parts_a, parts_b = parts[..., :cut], parts[..., cut:]
     got_a = send_fold(parts_a, 2, 1)
     got_b = send_chips(parts_b)
-    shared_sums = tensor_sum(sums[:, channels:], size)
-    step_sums = sums[:, channels + width : known]
+    shared_sums = tensor_sum(shared_sums, size)
     shared_sums, other0 = lax.optimization_barrier((shared_sums, other0))
-    sums = jnp.concatenate([sums[:, :channels], step_sums, shared_sums], axis=1)
+    sums = jnp.concatenate([sums, shared_sums], axis=1)
     sums = sums + dp_send(sums, 1)
     sums = sums + dp_send(sums, 2)
     grad_normed = sum_quarters((terms0, terms1, terms3), other0, other1, size)
@@ -996,7 +1008,10 @@
         scaled_grad * inputs, axis=1, keepdims=True
     )
     grad_tokens = (cotangent.astype(f32) + grad_inputs).astype(bf16)
-    got_a, got_b, sums, grad_tokens = lax.optimization_barrier((got_a, got_b, sums, grad_tokens))
+    got_a, got_b, sums, grad_tokens, branch_other = lax.optimization_barrier(
+        (got_a, got_b, sums, grad_tokens, branch_other)
+    )
+    block_out = (inputs + (branch_own.astype(f32) + branch_other.astype(f32))).astype(bf16)
     parts_a = keep_fold(parts_a, got_a, 2, 1)
     parts_b = keep_chips(parts_b, got_b).astype(bf16)
     got_a = send_chips(parts_a)
@@ -1005,7 +1020,7 @@
         sums = sums + dp_send(sums, bit)
     parts_a = keep_chips(parts_a, got_a)
     shared_sums = sums[:, channels + LANES :]
-    norm_sum = shared_sums[0, known - channels :]
+    norm_sum = shared_sums[0, width:]
     part_inner = jnp.concatenate([parts_a, parts_b[:, : channels - cut]], axis=1)
     at_step = channels + width
     part_shared = tensor_sum(parts_b[:, channels - cut : at_step - cut], size)

time: 262 us -> 256 us (0.977)
  waiting for transfers between devices: 27.9 us -> 24.2 us
  local copies, waits for them, and re-layouts: 22.7 us -> 19.7 us
    ppermute x43, waiting for transfers between devices: 18 us -> 14.3 us  [dp_send(): return lax.ppermute(value, 'dp', [(i, i ^ bit) for i in range(size)])]
    unnamed x68 -> x71, local copies, waits for them, and re-layouts: 5.1 us -> 5.69 us
  transfers between devices with their start and end apart: 52 -> 52, of which waited for: 14 -> 13; matrix products, arithmetic and copies ran while one was open for 16% -> 16% of each run, Pallas kernels for 30% -> 31%
where the time goes in v5:
time: 256 us; the launch traced here: 252 us
  Pallas kernels  111 us (43%)
  starting transfers between devices  61.2 us (24%)
  other arithmetic  33.7 us (13%)
  waiting for transfers between devices  24.2 us (9%)
  local copies, waits for them, and re-layouts  19.7 us (8%)
    ppermute x43, starting transfers between devices, dp_send(): return lax.ppermute(value, 'dp', [(i, i ^ bit) for i in range(size)])  53.2 us
    pallas_call x3, Pallas kernels, mixer_backward(): pl.pallas_call(partial(backward_kernel, begin, rows), grid=(end - begin,)...  46.1 us
    pallas_call x1, Pallas kernels, mixer_forward(): pl.pallas_call(partial(forward_kernel, 1 + len(others), count), grid=(blo...  22.7 us
    pallas_call x1, Pallas kernels, gate_norm(): pl.pallas_call(partial(norm_kernel, float(full_inner), chips, split), gri...  20.2 us
    ppermute x43, waiting for transfers between devices, dp_send(): return lax.ppermute(value, 'dp', [(i, i ^ bit) for i in range(size)])  14.3 us
    pallas_call x1, Pallas kernels, gate_forward(): pl.pallas_call(partial(gate_kernel, 1 + len(others), count), grid=(rows /...  13.3 us
    ppermute x9, waiting for transfers between devices, tensor_swap(): return lax.ppermute(value, 'tensor', [(0, 1), (1, 0)])  9.9 us
    pallas_call x1, Pallas kernels, weight_products(): pl.pallas_call(partial(product_kernel, chips, (0, known)), in_specs=[pl.B...  8.8 us
  transfers between devices with their start and end apart: 52, of which 13 were waited for; matrix products, arithmetic and copies ran while one was open for 16% of the time, Pallas kernels for 31%

profile of v5, /device:TPU:0, one launch (start us, length us, event | category | flops | bytes accessed | tf_op | source)
XLA Modules:
  0.0 251.5 jit_solution(6617808872363101320)
XLA Ops:
  0.7 1.6 fusion.28
  4.5 3.0 %collective-permute-start = (bf16[64,1408]{1,0:T(8,128)(2,1)}, bf16[64,1408]{1,0:T(8,128)(2,1)}, u32[]{:S(2)}, u32[]{:S(2)}) collective-permute-start(bf16[64,1408]{1,0:T(8,128)(2,1)} %pad_maximum_fusion.5), channel_id=1, source_target_pairs={{0,8},{2,10},{4,12},{6,14},{8,0},{10,2},{12,4},{14,6},{16,24},{18,... | collective-permute-start | bytes 540680 | tf_op jit(solution)/shard_map/ppermute | solution.py:791
  7.6 2.6 %collective-permute-start.1 = (bf16[64,1408]{1,0:T(8,128)(2,1)}, bf16[64,1408]{1,0:T(8,128)(2,1)}, u32[]{:S(2)}, u32[]{:S(2)}) collective-permute-start(bf16[64,1408]{1,0:T(8,128)(2,1)} %pad_maximum_fusion.5), channel_id=1, source_target_pairs={{0,16},{2,18},{4,20},{6,22},{8,24},{10,26},{12,28},{14,30},{16,0},... | collective-permute-start | bytes 540680 | tf_op jit(solution)/shard_map/ppermute | solution.py:791
  12.5 1.7 collective-permute-start.4
  19.9 1.7 fusion.9.refs_14_.spread_ref
  29.5 3.0 %collective-permute-start.7 = (bf16[128,768]{1,0:T(8,128)(2,1)S(1)}, bf16[128,768]{1,0:T(8,128)(2,1)S(1)}, u32[]{:S(2)}, u32[]{:S(2)}) collective-permute-start(bf16[128,768]{1,0:T(8,128)(2,1)S(1)} %slice.82), channel_id=1, source_target_pairs={{0,8},{2,10},{4,12},{6,14},{8,0},{10,2},{12,4},{14,6},{16,24},{18,... | collective-permute-start | bytes 589832 | tf_op jit(solution)/shard_map/ppermute | solution.py:791
  35.0 6.2 %collective-permute-done.6.refs_2_ = bf16[256,1024]{1,0:T(8,128)(2,1)S(1)} collective-permute-done((bf16[256,1024]{1,0:T(8,128)(2,1)S(1)}, bf16[256,1024]{1,0:T(8,128)(2,1)S(1)}, u32[]{:S(2)}, u32[]{:S(2)}) %collective-permute-start.6) | collective-permute-done | bytes 524320 | tf_op jit(solution)/shard_map/ppermute | solution.py:842
  41.8 6.9 %collective-permute-done.8 = bf16[128,768]{1,0:T(8,128)(2,1)S(1)} collective-permute-done((bf16[128,768]{1,0:T(8,128)(2,1)S(1)}, bf16[128,768]{1,0:T(8,128)(2,1)S(1)}, u32[]{:S(2)}, u32[]{:S(2)}) %collective-permute-start.8) | collective-permute-done | bytes 196640 | tf_op jit(solution)/shard_map/ppermute | solution.py:791
  49.6 2.7 %collective-permute-start.14 = (bf16[128,1280]{1,0:T(8,128)(2,1)S(1)}, bf16[128,1280]{1,0:T(8,128)(2,1)}, u32[]{:S(2)}, u32[]{:S(2)}) collective-permute-start(bf16[128,1280]{1,0:T(8,128)(2,1)S(1)} %slice.83.refs_4_), channel_id=1, source_target_pairs={{0,8},{2,10},{4,12},{6,14},{8,0},{10,2},{12,4},{14,6},{16,24},{18,... | collective-permute-start | bytes 983048 | tf_op jit(solution)/shard_map/ppermute | solution.py:791
  52.3 2.3 collective-permute-start.15
  56.9 22.7 %mixer_forward.1 = (bf16[1024,1024]{1,0:T(8,128)(2,1)}, bf16[1024,1408]{1,0:T(8,128)(2,1)}, f32[1024,1024]{1,0:T(8,128)}, f32[1024,1024]{1,0:T(8,128)}, f32[1024...) custom-call(s32[1,4]{1,0:T(1,128)} %add_bitcast_fusion.spot_ref, ...), custom_call_target="tpu_custom_call" | custom-call | tf_op jit(solution)/shard_map/mixer_forward/pallas_call | solution.py:275
  83.7 13.3 %gate_forward.1 = (bf16[1024,1024]{1,0:T(8,128)(2,1)}, bf16[1024,2048]{1,0:T(8,128)(2,1)}, f32[1024,1024]{1,0:T(8,128)}, f32[1024,1024]{1,0:T(8,128)}, f32[8,1024]{1,0:T(8,128)}) custom-call(s32[1,4]{1,0:T(1,128)} %add_bitcast_fusion.spot_ref, bf16[1024,1024]{1,0:T(8,128)(2,1)} %get-tuple-element.139.normed_ref, bf16[512,1024]{1,0:T(8,128)(2,1)} %refs_0_.1, ...), custom_call_target="tpu_custom_call" | custom-call | tf_op jit(solution)/shard_map/gate_forward/pallas_call | solution.py:647
  97.6 3.6 %collective-permute-done.21.more_ref = f32[8,1024]{1,0:T(8,128)S(1)} collective-permute-done((f32[8,1024]{1,0:T(8,128)}, f32[8,1024]{1,0:T(8,128)S(1)}, u32[]{:S(2)}, u32[]{:S(2)}) %collective-permute-start.21) | collective-permute-done | bytes 32800 | tf_op jit(solution)/shard_map/ppermute | solution.py:842
  101.8 20.2 %gate_norm.1 = (bf16[1024,1024]{1,0:T(8,128)(2,1)}, f32[1024,1024]{1,0:T(8,128)}, f32[8,1408]{1,0:T(8,128)}, bf16[512,2048]{1,0:T(8,128)(2,1)}, bf16[512,2048]{1...) custom-call(s32[1,4]{1,0:T(1,128)} %add_bitcast_fusion.spot_ref, ...), custom_call_target="tpu_custom_call" | custom-call | tf_op jit(solution)/shard_map/gate_norm/pallas_call | solution.py:744
  122.7 11.9 %mixer_backward.3 = (bf16[256,1408]{1,0:T(8,128)(2,1)}, bf16[256,1024]{1,0:T(8,128)(2,1)}, f32[8,1408]{1,0:T(8,128)}, f32[8,1024]{1,0:T(8,128)}, f32[8,256]{1,0:T(8,128)}, /*index=5*/f32[128,1024]{1,0:T(8,128)}) custom-call(s32[1,4]{1,0:T(1,128)} %lengths_ref.7, f32[1024,1024]{1,0:T(8,128)} %get-tuple-element.160.upstream_ref, ...), custom_call_target="tpu_custom_call" | custom-call | tf_op jit(solution)/shard_map/mixer_backward/pallas_call | solution.py:507
  134.6 2.4 add_convert_fusion
  138.3 5.0 %collective-permute-start.25 = (bf16[2,64,1024]{2,1,0:T(8,128)(2,1)}, bf16[2,64,1024]{2,1,0:T(8,128)(2,1)}, u32[]{:S(2)}, u32[]{:S(2)}) collective-permute-start(bf16[2,64,1024]{2,1,0:T(8,128)(2,1)} %get-tuple-element.270), channel_id=1, source_target_pairs={{0,8},{2,10},{4,12},{6,14},{8,0},{10,2},{12,4},{14,6},{16,24},{18,... | collective-permute-start | bytes 786440 | tf_op jit(solution)/shard_map/ppermute | solution.py:791
  147.6 22.1 %mixer_backward.4 = (bf16[512,1408]{1,0:T(8,128)(2,1)}, bf16[512,1024]{1,0:T(8,128)(2,1)}, f32[8,1408]{1,0:T(8,128)}, f32[8,1024]{1,0:T(8,128)}, f32[8,256]{1,0:T(8,128)}, /*index=5*/f32[128,1024]{1,0:T(8,128)}) custom-call(s32[1,4]{1,0:T(1,128)} %lengths_ref.7, f32[1024,1024]{1,0:T(8,128)} %get-tuple-element.160.upstream_ref, ...), custom_call_target="tpu_custom_call" | custom-call | tf_op jit(solution)/shard_map/mixer_backward/pallas_call | solution.py:507
  169.8 2.2 fusion.26
  176.3 1.6 collective-permute-start.32
  179.7 1.9 collective-permute-start.29
  183.0 12.0 %mixer_backward.5 = (bf16[256,1408]{1,0:T(8,128)(2,1)}, bf16[256,1024]{1,0:T(8,128)(2,1)}, f32[8,1408]{1,0:T(8,128)}, f32[8,1024]{1,0:T(8,128)}, f32[8,256]{1,0:T(8,128)}, /*index=5*/f32[128,1024]{1,0:T(8,128)}) custom-call(s32[1,4]{1,0:T(1,128)} %lengths_ref.7, f32[1024,1024]{1,0:T(8,128)} %get-tuple-element.160.upstream_ref, ...), custom_call_target="tpu_custom_call" | custom-call | tf_op jit(solution)/shard_map/mixer_backward/pallas_call | solution.py:507
  195.1 1.6 convert_add_fusion.5
  199.6 8.8 %weight_products.1 = (bf16[512,1408]{1,0:T(8,128)(2,1)}, bf16[128,1408]{1,0:T(8,128)(2,1)}, bf16[128,1408]{1,0:T(8,128)(2,1)}, bf16[128,1408]{1,0:T(8,128)(2,1)}...) custom-call(s32[1,4]{1,0:T(1,128)} %add_bitcast_fusion.spot_ref, ...), custom_call_target="tpu_custom_call" | custom-call | tf_op jit(solution)/shard_map/weight_products/pallas_call | solution.py:590
  211.8 1.7 add_convert_fusion.1
  216.6 2.8 %collective-permute-start.40 = (bf16[2,64,512]{2,1,0:T(8,128)(2,1)S(1)}, bf16[2,64,512]{2,1,0:T(8,128)(2,1)S(1)}, u32[]{:S(2)}, u32[]{:S(2)}) collective-permute-start(bf16[2,64,512]{2,1,0:T(8,128)(2,1)S(1)} %get-tuple-element.276), channel_id=1, source_target_pairs={{0,16},{2,18},{4,20},{6,22},{8,24},{10,26},{12,28},{14,30},{16,0},... | collective-permute-start | bytes 393224 | tf_op jit(solution)/shard_map/ppermute | solution.py:791
  221.0 1.8 fusion.7
  224.4 2.9 %fusion.6 = bf16[512,1024]{1,0:T(8,128)(2,1)} fusion(bf16[512,1024]{1,0:T(8,128)(2,1)S(1)} %copy-done, bf16[512,1024]{1,0:T(8,128)(2,1)S(1)} %copy-done.5, f32[512]{0:T(512)S(1)} %broadcast_multiply_fusion, f32[512]{0:T(512)S(1)} %copy-done.30, f32[1024]{0:T(1024)S(1)} %copy-done.24, f32[512]{0:T(512)S(1)} %copy-done.29, ...), kind=kLoop, calls=%fused_computation.13 | loop fusion | flops 12582912 | bytes 6301697 | tf_op jit(solution)/shard_map/convert_element_type | solution.py:1010
  227.3 2.5 collective-permute-done.44
  231.9 2.1 collective-permute-start.47
  237.5 2.8 %fusion.8 = bf16[512,1024]{1,0:T(8,128)(2,1)} fusion(bf16[512,1024]{1,0:T(8,128)(2,1)S(1)} %copy-done, bf16[512,1024]{1,0:T(8,128)(2,1)} %collective-permute-done.23, bf16[512,1024]{1,0:T(8,128)(2,1)S(1)} %copy-done.12), kind=kLoop, calls=%fused_computation.15 | loop fusion | flops 3145728 | bytes 4194304 | tf_op jit(solution)/shard_map/convert_element_type | solution.py:1014
  241.9 3.5 %collective-permute-start.46 = (f32[8,2432]{1,0:T(8,128)S(1)}, f32[8,2432]{1,0:T(8,128)S(1)}, u32[]{:S(2)}, u32[]{:S(2)}) collective-permute-start(f32[8,2432]{1,0:T(8,128)S(1)} %add.205), channel_id=1, source_target_pairs={{0,16},{2,18},{4,20},{6,22},{8,24},{10,26},{12,28},{14,30},{16,0},... | collective-permute-start | bytes 233480 | tf_op jit(solution)/shard_map/ppermute | solution.py:791
  (218 shorter events, 68.6 us)
Async XLA Ops:
  4.5 21.6 %collective-permute-start = (bf16[64,1408]{1,0:T(8,128)(2,1)}, bf16[64,1408]{1,0:T(8,128)(2,1)}, u32[]{:S(2)}, u32[]{:S(2)}) collective-permute-start(bf16[64,1408]{1,0:T(8,128)(2,1)} %pad_maximum_fusion.5), channel_id=1, source_target_pairs={{0,8},{2,10},{4,12},{6,14},{8,0},{10,2},{12,4},{14,6},{16,24},{18,... | collective-permute-start | bytes 540680 | tf_op jit(solution)/shard_map/ppermute | solution.py:791
  7.6 18.6 %collective-permute-start.1 = (bf16[64,1408]{1,0:T(8,128)(2,1)}, bf16[64,1408]{1,0:T(8,128)(2,1)}, u32[]{:S(2)}, u32[]{:S(2)}) collective-permute-start(bf16[64,1408]{1,0:T(8,128)(2,1)} %pad_maximum_fusion.5), channel_id=1, source_target_pairs={{0,16},{2,18},{4,20},{6,22},{8,24},{10,26},{12,28},{14,30},{16,0},... | collective-permute-start | bytes 540680 | tf_op jit(solution)/shard_map/ppermute | solution.py:791
  10.2 16.0 %collective-permute-start.2 = (bf16[64,1408]{1,0:T(8,128)(2,1)}, bf16[64,1408]{1,0:T(8,128)(2,1)}, u32[]{:S(2)}, u32[]{:S(2)}) collective-permute-start(bf16[64,1408]{1,0:T(8,128)(2,1)} %pad_maximum_fusion.5), channel_id=1, source_target_pairs={{0,24},{2,26},{4,28},{6,30},{8,16},{10,18},{12,20},{14,22},{16,8},... | collective-permute-start | bytes 540680 | tf_op jit(solution)/shard_map/ppermute | solution.py:791
  12.5 16.1 %collective-permute-start.4 = (bf16[256,1024]{1,0:T(8,128)(2,1)}, bf16[256,1024]{1,0:T(8,128)(2,1)}, u32[]{:S(2)}, u32[]{:S(2)}) collective-permute-start(bf16[256,1024]{1,0:T(8,128)(2,1)} %get-tuple-element.274), channel_id=1, source_target_pairs={{0,1},{1,0},{2,3},{3,2},{4,5},{5,4},{6,7},{7,6},{8,9},{9,8},{10,11... | collective-permute-start | bytes 1572872 | tf_op jit(solution)/shard_map/ppermute | solution.py:842
  15.0 12.4 %collective-permute-start.3 = (bf16[64,2048]{1,0:T(8,128)(2,1)}, bf16[64,2048]{1,0:T(8,128)(2,1)}, u32[]{:S(2)}, u32[]{:S(2)}) collective-permute-start(bf16[64,2048]{1,0:T(8,128)(2,1)} %pad_maximum_fusion.4), channel_id=1, source_target_pairs={{0,4},{2,6},{4,0},{6,2},{8,12},{10,14},{12,8},{14,10},{16,20},{18,... | collective-permute-start | bytes 786440 | tf_op jit(solution)/shard_map/ppermute | solution.py:791
  28.6 20.1 %collective-permute-start.5 = (bf16[256,1408]{1,0:T(8,128)(2,1)S(1)}, bf16[256,1408]{1,0:T(8,128)(2,1)S(1)}, u32[]{:S(2)}, u32[]{:S(2)}) collective-permute-start(bf16[256,1408]{1,0:T(8,128)(2,1)S(1)} %pad_maximum_fusion.1.refs_3_), channel_id=1, source_target_pairs={{0,4},{2,6},{4,0},{6,2},{8,12},{10,14},{12,8},{14,10},{16,20},{18,... | collective-permute-start | bytes 2162696 | tf_op jit(solution)/shard_map/ppermute | solution.py:791
  29.2 12.1 %collective-permute-start.6 = (bf16[256,1024]{1,0:T(8,128)(2,1)S(1)}, bf16[256,1024]{1,0:T(8,128)(2,1)S(1)}, u32[]{:S(2)}, u32[]{:S(2)}) collective-permute-start(bf16[256,1024]{1,0:T(8,128)(2,1)S(1)} %copy-done.17), channel_id=1, source_target_pairs={{0,1},{1,0},{2,3},{3,2},{4,5},{5,4},{6,7},{7,6},{8,9},{9,8},{10,11... | collective-permute-start | bytes 1572872 | tf_op jit(solution)/shard_map/ppermute | solution.py:842
  29.5 12.2 %collective-permute-start.7 = (bf16[128,768]{1,0:T(8,128)(2,1)S(1)}, bf16[128,768]{1,0:T(8,128)(2,1)S(1)}, u32[]{:S(2)}, u32[]{:S(2)}) collective-permute-start(bf16[128,768]{1,0:T(8,128)(2,1)S(1)} %slice.82), channel_id=1, source_target_pairs={{0,8},{2,10},{4,12},{6,14},{8,0},{10,2},{12,4},{14,6},{16,24},{18,... | collective-permute-start | bytes 589832 | tf_op jit(solution)/shard_map/ppermute | solution.py:791
  32.6 16.1 %collective-permute-start.8 = (bf16[128,768]{1,0:T(8,128)(2,1)S(1)}, bf16[128,768]{1,0:T(8,128)(2,1)S(1)}, u32[]{:S(2)}, u32[]{:S(2)}) collective-permute-start(bf16[128,768]{1,0:T(8,128)(2,1)S(1)} %slice.82), channel_id=1, source_target_pairs={{0,16},{2,18},{4,20},{6,22},{8,24},{10,26},{12,28},{14,30},{16,0},... | collective-permute-start | bytes 589832 | tf_op jit(solution)/shard_map/ppermute | solution.py:791
  34.0 14.8 %collective-permute-start.9 = (bf16[128,768]{1,0:T(8,128)(2,1)S(1)}, bf16[128,768]{1,0:T(8,128)(2,1)S(1)}, u32[]{:S(2)}, u32[]{:S(2)}) collective-permute-start(bf16[128,768]{1,0:T(8,128)(2,1)S(1)} %slice.82), channel_id=1, source_target_pairs={{0,24},{2,26},{4,28},{6,30},{8,16},{10,18},{12,20},{14,22},{16,8},... | collective-permute-start | bytes 589832 | tf_op jit(solution)/shard_map/ppermute | solution.py:791
  41.3 38.4 %collective-permute-start.12 = (bf16[512,1024]{1,0:T(8,128)(2,1)S(1)}, bf16[512,1024]{1,0:T(8,128)(2,1)}, u32[]{:S(2)}, u32[]{:S(2)}) collective-permute-start(bf16[512,1024]{1,0:T(8,128)(2,1)S(1)} %copy-done.4), channel_id=1, source_target_pairs={{0,1},{1,0},{2,3},{3,2},{4,5},{5,4},{6,7},{7,6},{8,9},{9,8},{10,11... | collective-permute-start | bytes 3145736 | tf_op jit(solution)/shard_map/ppermute | solution.py:842
  49.4 30.3 %collective-permute-start.13 = (bf16[512,768]{1,0:T(8,128)(2,1)S(1)}, bf16[512,768]{1,0:T(8,128)(2,1)}, u32[]{:S(2)}, u32[]{:S(2)}) collective-permute-start(bf16[512,768]{1,0:T(8,128)(2,1)S(1)} %constant_dynamic-update-slice_fusion.refs_2_), channel_id=1, source_target_pairs={{0,2},{2,0},{4,6},{6,4},{8,10},{10,8},{12,14},{14,12},{16,18},{18,... | collective-permute-start | bytes 2359304 | tf_op jit(solution)/shard_map/ppermute | solution.py:791
  49.6 30.1 %collective-permute-start.14 = (bf16[128,1280]{1,0:T(8,128)(2,1)S(1)}, bf16[128,1280]{1,0:T(8,128)(2,1)}, u32[]{:S(2)}, u32[]{:S(2)}) collective-permute-start(bf16[128,1280]{1,0:T(8,128)(2,1)S(1)} %slice.83.refs_4_), channel_id=1, source_target_pairs={{0,8},{2,10},{4,12},{6,14},{8,0},{10,2},{12,4},{14,6},{16,24},{18,... | collective-permute-start | bytes 983048 | tf_op jit(solution)/shard_map/ppermute | solution.py:791
  52.3 27.4 %collective-permute-start.15 = (bf16[128,1280]{1,0:T(8,128)(2,1)S(1)}, bf16[128,1280]{1,0:T(8,128)(2,1)}, u32[]{:S(2)}, u32[]{:S(2)}) collective-permute-start(bf16[128,1280]{1,0:T(8,128)(2,1)S(1)} %slice.83.refs_4_), channel_id=1, source_target_pairs={{0,16},{2,18},{4,20},{6,22},{8,24},{10,26},{12,28},{14,30},{16,0},... | collective-permute-start | bytes 983048 | tf_op jit(solution)/shard_map/ppermute | solution.py:791
  55.5 24.2 %collective-permute-start.16 = (bf16[128,1280]{1,0:T(8,128)(2,1)S(1)}, bf16[128,1280]{1,0:T(8,128)(2,1)}, u32[]{:S(2)}, u32[]{:S(2)}) collective-permute-start(bf16[128,1280]{1,0:T(8,128)(2,1)S(1)} %slice.83.refs_4_), channel_id=1, source_target_pairs={{0,24},{2,26},{4,28},{6,30},{8,16},{10,18},{12,20},{14,22},{16,8},... | collective-permute-start | bytes 983048 | tf_op jit(solution)/shard_map/ppermute | solution.py:791
  122.0 12.6 %collective-permute-start.22 = (bf16[512,2048]{1,0:T(8,128)(2,1)}, bf16[512,2048]{1,0:T(8,128)(2,1)}, u32[]{:S(2)}, u32[]{:S(2)}) collective-permute-start(bf16[512,2048]{1,0:T(8,128)(2,1)} %get-tuple-element.174), channel_id=1, source_target_pairs={{0,2},{2,0},{4,6},{6,4},{8,10},{10,8},{12,14},{14,12},{16,18},{18,... | collective-permute-start | bytes 6291464 | tf_op jit(solution)/shard_map/ppermute | solution.py:791
  122.1 52.4 %collective-permute-start.23 = (bf16[512,1024]{1,0:T(8,128)(2,1)}, bf16[512,1024]{1,0:T(8,128)(2,1)}, u32[]{:S(2)}, u32[]{:S(2)}) collective-permute-start(bf16[512,1024]{1,0:T(8,128)(2,1)} %get-tuple-element.185), channel_id=1, source_target_pairs={{0,1},{1,0},{2,3},{3,2},{4,5},{5,4},{6,7},{7,6},{8,9},{9,8},{10,11... | collective-permute-start | bytes 3145736 | tf_op jit(solution)/shard_map/ppermute | solution.py:842
  138.3 33.7 %collective-permute-start.25 = (bf16[2,64,1024]{2,1,0:T(8,128)(2,1)}, bf16[2,64,1024]{2,1,0:T(8,128)(2,1)}, u32[]{:S(2)}, u32[]{:S(2)}) collective-permute-start(bf16[2,64,1024]{2,1,0:T(8,128)(2,1)} %get-tuple-element.270), channel_id=1, source_target_pairs={{0,8},{2,10},{4,12},{6,14},{8,0},{10,2},{12,4},{14,6},{16,24},{18,... | collective-permute-start | bytes 786440 | tf_op jit(solution)/shard_map/ppermute | solution.py:791
  143.3 28.7 %collective-permute-start.26 = (bf16[2,64,1024]{2,1,0:T(8,128)(2,1)}, bf16[2,64,1024]{2,1,0:T(8,128)(2,1)}, u32[]{:S(2)}, u32[]{:S(2)}) collective-permute-start(bf16[2,64,1024]{2,1,0:T(8,128)(2,1)} %get-tuple-element.272), channel_id=1, source_target_pairs={{0,16},{2,18},{4,20},{6,22},{8,24},{10,26},{12,28},{14,30},{16,0},... | collective-permute-start | bytes 786440 | tf_op jit(solution)/shard_map/ppermute | solution.py:791
  144.3 27.7 %collective-permute-start.27 = (bf16[2,64,1024]{2,1,0:T(8,128)(2,1)S(1)}, bf16[2,64,1024]{2,1,0:T(8,128)(2,1)}, u32[]{:S(2)}, u32[]{:S(2)}) collective-permute-start(bf16[2,64,1024]{2,1,0:T(8,128)(2,1)S(1)} %get-tuple-element.271), channel_id=1, source_target_pairs={{0,24},{2,26},{4,28},{6,30},{8,16},{10,18},{12,20},{14,22},{16,8},... | collective-permute-start | bytes 786440 | tf_op jit(solution)/shard_map/ppermute | solution.py:791
  146.6 26.7 %collective-permute-start.24 = (bf16[4,64,1024]{2,1,0:T(8,128)(2,1)}, bf16[4,64,1024]{2,1,0:T(8,128)(2,1)}, u32[]{:S(2)}, u32[]{:S(2)}) collective-permute-start(bf16[4,64,1024]{2,1,0:T(8,128)(2,1)} %dynamic-slice_bitcast_fusion), channel_id=1, source_target_pairs={{0,4},{2,6},{4,0},{6,2},{8,12},{10,14},{12,8},{14,10},{16,20},{18,... | collective-permute-start | bytes 1572872 | tf_op jit(solution)/shard_map/ppermute | solution.py:791
  175.2 19.8 %collective-permute-start.31 = (bf16[64,1024]{1,0:T(8,128)(2,1)}, bf16[64,1024]{1,0:T(8,128)(2,1)}, u32[]{:S(2)}, u32[]{:S(2)}) collective-permute-start(bf16[64,1024]{1,0:T(8,128)(2,1)} %dynamic-slice_bitcast_fusion.8), channel_id=1, source_target_pairs={{0,4},{2,6},{4,0},{6,2},{8,12},{10,14},{12,8},{14,10},{16,20},{18,... | collective-permute-start | bytes 393224 | tf_op jit(solution)/shard_map/ppermute | solution.py:791
  176.3 21.4 %collective-permute-start.32 = (bf16[256,1024]{1,0:T(8,128)(2,1)}, bf16[256,1024]{1,0:T(8,128)(2,1)}, u32[]{:S(2)}, u32[]{:S(2)}) collective-permute-start(bf16[256,1024]{1,0:T(8,128)(2,1)} %get-tuple-element.195), channel_id=1, source_target_pairs={{0,1},{1,0},{2,3},{3,2},{4,5},{5,4},{6,7},{7,6},{8,9},{9,8},{10,11... | collective-permute-start | bytes 1572872 | tf_op jit(solution)/shard_map/ppermute | solution.py:842
  178.6 18.1 %collective-permute-start.28 = (bf16[64,1024]{1,0:T(8,128)(2,1)}, bf16[64,1024]{1,0:T(8,128)(2,1)S(1)}, u32[]{:S(2)}, u32[]{:S(2)}) collective-permute-start(bf16[64,1024]{1,0:T(8,128)(2,1)} %get-tuple-element.278), channel_id=1, source_target_pairs={{0,8},{2,10},{4,12},{6,14},{8,0},{10,2},{12,4},{14,6},{16,24},{18,... | collective-permute-start | bytes 393224 | tf_op jit(solution)/shard_map/ppermute | solution.py:791
  179.7 17.0 %collective-permute-start.29 = (bf16[64,1024]{1,0:T(8,128)(2,1)}, bf16[64,1024]{1,0:T(8,128)(2,1)}, u32[]{:S(2)}, u32[]{:S(2)}) collective-permute-start(bf16[64,1024]{1,0:T(8,128)(2,1)} %get-tuple-element.280), channel_id=1, source_target_pairs={{0,16},{2,18},{4,20},{6,22},{8,24},{10,26},{12,28},{14,30},{16,0},... | collective-permute-start | bytes 393224 | tf_op jit(solution)/shard_map/ppermute | solution.py:791
  181.6 15.1 %collective-permute-start.30 = (bf16[64,1024]{1,0:T(8,128)(2,1)}, bf16[64,1024]{1,0:T(8,128)(2,1)}, u32[]{:S(2)}, u32[]{:S(2)}) collective-permute-start(bf16[64,1024]{1,0:T(8,128)(2,1)} %get-tuple-element.279), channel_id=1, source_target_pairs={{0,24},{2,26},{4,28},{6,30},{8,16},{10,18},{12,20},{14,22},{16,8},... | collective-permute-start | bytes 393224 | tf_op jit(solution)/shard_map/ppermute | solution.py:791
  198.9 13.0 %collective-permute-start.37 = (bf16[256,1024]{1,0:T(8,128)(2,1)S(1)}, bf16[256,1024]{1,0:T(8,128)(2,1)S(1)}, u32[]{:S(2)}, u32[]{:S(2)}) collective-permute-start(bf16[256,1024]{1,0:T(8,128)(2,1)S(1)} %broadcast_select_fusion), channel_id=1, source_target_pairs={{0,1},{1,0},{2,3},{3,2},{4,5},{5,4},{6,7},{7,6},{8,9},{9,8},{10,11... | collective-permute-start | bytes 1572872 | tf_op jit(solution)/shard_map/ppermute | solution.py:842
  215.7 14.1 %collective-permute-start.38 = (bf16[4,64,896]{2,1,0:T(8,128)(2,1)S(1)}, bf16[4,64,896]{2,1,0:T(8,128)(2,1)S(1)}, u32[]{:S(2)}, u32[]{:S(2)}) collective-permute-start(bf16[4,64,896]{2,1,0:T(8,128)(2,1)S(1)} %dynamic-slice_bitcast_fusion.1), channel_id=1, source_target_pairs={{0,4},{2,6},{4,0},{6,2},{8,12},{10,14},{12,8},{14,10},{16,20},{18,... | collective-permute-start | bytes 1376264 | tf_op jit(solution)/shard_map/ppermute | solution.py:791
  216.4 13.4 %collective-permute-start.39 = (bf16[2,64,512]{2,1,0:T(8,128)(2,1)S(1)}, bf16[2,64,512]{2,1,0:T(8,128)(2,1)S(1)}, u32[]{:S(2)}, u32[]{:S(2)}) collective-permute-start(bf16[2,64,512]{2,1,0:T(8,128)(2,1)S(1)} %get-tuple-element.277), channel_id=1, source_target_pairs={{0,8},{2,10},{4,12},{6,14},{8,0},{10,2},{12,4},{14,6},{16,24},{18,... | collective-permute-start | bytes 393224 | tf_op jit(solution)/shard_map/ppermute | solution.py:791
  216.6 13.2 %collective-permute-start.40 = (bf16[2,64,512]{2,1,0:T(8,128)(2,1)S(1)}, bf16[2,64,512]{2,1,0:T(8,128)(2,1)S(1)}, u32[]{:S(2)}, u32[]{:S(2)}) collective-permute-start(bf16[2,64,512]{2,1,0:T(8,128)(2,1)S(1)} %get-tuple-element.276), channel_id=1, source_target_pairs={{0,16},{2,18},{4,20},{6,22},{8,24},{10,26},{12,28},{14,30},{16,0},... | collective-permute-start | bytes 393224 | tf_op jit(solution)/shard_map/ppermute | solution.py:791
  231.9 13.4 %collective-permute-start.47 = (bf16[64,896]{1,0:T(8,128)(2,1)}, bf16[64,896]{1,0:T(8,128)(2,1)}, u32[]{:S(2)}, u32[]{:S(2)}) collective-permute-start(bf16[64,896]{1,0:T(8,128)(2,1)} %get-tuple-element.281), channel_id=1, source_target_pairs={{0,8},{2,10},{4,12},{6,14},{8,0},{10,2},{12,4},{14,6},{16,24},{18,... | collective-permute-start | bytes 344072 | tf_op jit(solution)/shard_map/ppermute | solution.py:791
  234.0 11.4 %collective-permute-start.48 = (bf16[64,896]{1,0:T(8,128)(2,1)}, bf16[64,896]{1,0:T(8,128)(2,1)}, u32[]{:S(2)}, u32[]{:S(2)}) collective-permute-start(bf16[64,896]{1,0:T(8,128)(2,1)} %get-tuple-element.283), channel_id=1, source_target_pairs={{0,16},{2,18},{4,20},{6,22},{8,24},{10,26},{12,28},{14,30},{16,0},... | collective-permute-start | bytes 344072 | tf_op jit(solution)/shard_map/ppermute | solution.py:791
  (51 other events, 365.0 us)

commit v6 on v5

--- a/solution.py
+++ b/solution.py
@@ -124,6 +124,17 @@
                 done.at[i * count + k],
             ))
     run_copies(copies)
+
+
+def place_columns(spot_ref, weight_ref, sources, count):
+    rows = weight_ref.shape[0] // (4 * count)
+    for i, ref in enumerate(sources):
+        along = spot_ref[0, 2] ^ (i % 2)
+        core = spot_ref[0, 3] ^ (i // 2)
+        for k in range(count):
+            at = (((spot_ref[0, 1] ^ k) * 2 + along) * 2 + core) * rows
+            at = pl.ds(pl.multiple_of(at, rows), rows)
+            weight_ref[at, : ref.shape[1]] = ref[k * rows : (k + 1) * rows, :]
 
 
 def place_pairs(spot_ref, weight_ref, sources, count, lo):
@@ -603,17 +614,15 @@
 
 def gate_kernel(pieces, count, spot_ref, normed_ref, *refs):
     own_ref, others = refs[0], refs[1:pieces]
-    joined, sources = refs[pieces : pieces + 2], refs[pieces + 2 : pieces + 2 + 2 * count]
+    columns, sources = refs[pieces : pieces + 4], refs[pieces + 4 : pieces + 4 + 2 * count]
     (
         gain_ref, ssm_ref, upstream_ref, weight_ref, gate_ref, grad_ref, sums_ref
-    ) = refs[pieces + 2 + 2 * count :]
+    ) = refs[pieces + 4 + 2 * count :]
 
     @pl.when(pl.program_id(0) == 0)
     def _():
-        each = joined[0].shape[0] // count
-        rows = [(ref, k * each) for ref in joined for k in range(count)]
-        place_pairs(spot_ref, weight_ref, rows, count, 0)
-        place_pairs(spot_ref, weight_ref, [(ref, 0) for ref in sources], count, joined[0].shape[1])
+        place_columns(spot_ref, weight_ref, columns, count)
+        place_pairs(spot_ref, weight_ref, [(ref, 0) for ref in sources], count, columns[0].shape[1])
 
     rows, channels = ssm_ref.shape
     normed = normed_ref[...]
@@ -775,6 +784,37 @@
     )(spot, sums, more, gate, grad, ssm, gain, normed, upstream, weight, weight)
 
 
+def output_kernel(width, sums_ref, more_ref, *out_refs):
+    sums = sums_ref[...] + more_ref[...]
+    inner = out_refs[0].shape[1]
+    heads = out_refs[4].shape[1]
+    shared = inner + LANES
+    parts = (
+        sums[:TAPS, :inner], sums[TAPS : TAPS + 1, :inner], sums[:TAPS, shared : shared + width],
+        sums[TAPS : TAPS + 1, shared : shared + width], sums[0:1, inner : inner + LANES][:, :heads],
+        sums[1:2, inner : inner + LANES][:, :heads], sums[2:3, inner : inner + LANES][:, :heads],
+        sums[TAIL - 1 :, :inner], sums[0:1, shared + width :],
+    )
+    for ref, part in zip(out_refs, parts):
+        ref[...] = part
+
+
+def sums_outputs(sums, more, channels, width, heads):
+    model = sums.shape[1] - channels - LANES - width
+    shapes = [
+        (TAPS, channels), (1, channels), (TAPS, width), (1, width), (1, heads), (1, heads),
+        (1, heads), (1, channels), (1, model),
+    ]
+    vmem = pl.BlockSpec(memory_space=pltpu.VMEM)
+    return pl.pallas_call(
+        partial(output_kernel, width),
+        in_specs=[vmem, vmem],
+        out_specs=[vmem] * len(shapes),
+        out_shape=[jax.ShapeDtypeStruct(shape, f32) for shape in shapes],
+        name="sums_outputs",
+    )(sums, more)
+
+
 def lanes_of(vector):
     return jnp.pad(vector, (0, LANES - vector.shape[0]))[None, :]
 
@@ -904,22 +944,20 @@
         lanes_of(-jnp.exp(log_rate)), jnp.repeat(skip_gain, channels // heads)[None, :],
         spread_map(heads, channels),
     )
-    late = jnp.concatenate([zx_weight[:, 0, :], out_weight], axis=1)
     def along(value):
         return [value] + [dp_send(value, bit) for bit in chip_bits()]
 
     column = jnp.concatenate(along(early), axis=0)
     column, pair, top, fixed, spot = lax.optimization_barrier((
-        column, jnp.concatenate([late, dp_send(late, 2)], axis=0),
+        column, jnp.concatenate([out_weight, dp_send(out_weight, 2)], axis=0),
         gather_other(normed_rows[:half], size), fixed, spot,
     ))
-    cut_late = (2 * channels * 3 // 8) // LANES * LANES
-    joined = along(pair[:, :cut_late])
-    by_x, column, bottom, joined, pair = lax.optimization_barrier(
-        (dp_send(column, 2), column, gather_other(normed_rows[half:], size), joined, pair)
-    )
-    joined = jnp.concatenate(joined, axis=0)
-    pairs = along(pair[:, cut_late:])
+    by_x, column, bottom, gate_column, pair, late_rows = lax.optimization_barrier((
+        dp_send(column, 2), column, gather_other(normed_rows[half:], size),
+        along(zx_weight[:, 0, :]), pair, cotangent,
+    ))
+    gate_column = jnp.concatenate(gate_column, axis=0)
+    pairs = along(pair)
     by_core = dp_send(column, 1)
     sources = (column, by_x, by_core, dp_send(by_x, 1))
     own, others = normed_rows, (top, bottom)
@@ -930,10 +968,13 @@
     )
     _, _, _, _, _, rate, skip, spread = fixed
     gain = gate_gain[None, :]
-    other, ssm, joined_core, pairs = lax.optimization_barrier(
-        (gather_other(cotangent, size), saved[0], dp_send(joined, 1), pairs)
-    )
-    sources = (joined, joined_core, *pairs, *[dp_send(pair, 1) for pair in pairs])
+    other, ssm, gate_x, gate_column, pairs = lax.optimization_barrier((
+        gather_other(late_rows, size), saved[0], dp_send(gate_column, 2), gate_column, pairs,
+    ))
+    sources = (
+        gate_column, gate_x, dp_send(gate_column, 1), dp_send(gate_x, 1), *pairs,
+        *[dp_send(pair, 1) for pair in pairs],
+    )
     own, others = (cotangent, (other,)) if split else (other, ())
     upstream, weight_late, gate, grad, sums = gate_forward(
         spot, normed, own, others, sources, count, gain, ssm, SPAN
@@ -1016,11 +1057,10 @@
     parts_b = keep_chips(parts_b, got_b).astype(bf16)
     got_a = send_chips(parts_a)
     parts_b = fold(parts_b, 2, 0)
-    for bit in long_bits():
+    for bit in long_bits()[:-1]:
         sums = sums + dp_send(sums, bit)
+    smalls = sums_outputs(sums, dp_send(sums, long_bits()[-1]), channels, width, heads)
     parts_a = keep_chips(parts_a, got_a)
-    shared_sums = sums[:, channels + LANES :]
-    norm_sum = shared_sums[0, width:]
     part_inner = jnp.concatenate([parts_a, parts_b[:, : channels - cut]], axis=1)
     at_step = channels + width
     part_shared = tensor_sum(parts_b[:, channels - cut : at_step - cut], size)
@@ -1029,18 +1069,18 @@
     return (
         block_out,
         grad_tokens,
-        norm_sum,
+        smalls[8][0],
         part_in,
         part_shared,
         part_step,
-        sums[:TAPS, :channels],
-        sums[TAPS, :channels],
-        shared_sums[:TAPS, :width],
-        shared_sums[TAPS, :width],
-        sums[0, channels : channels + heads],
-        sums[1, channels : channels + heads],
-        sums[2, channels : channels + heads],
-        sums[TAIL - 1, :channels],
+        smalls[0],
+        smalls[1][0],
+        smalls[2],
+        smalls[3][0],
+        smalls[4][0],
+        smalls[5][0],
+        smalls[6][0],
+        smalls[7][0],
         part_out,
     )
 

time: 256 us -> 251 us (0.980)
  other arithmetic: 33.7 us -> 27.5 us
    ppermute x43 -> x45, waiting for transfers between devices: 14.3 us -> 19.8 us  [dp_send(): return lax.ppermute(value, 'dp', [(i, i ^ bit) for i in range(size)])]
    ppermute x9, waiting for transfers between devices: 9.9 us -> 4.88 us  [tensor_swap(): return lax.ppermute(value, 'tensor', [(0, 1), (1, 0)])]
    unnamed x71 -> x85, local copies, waits for them, and re-layouts: 5.69 us -> 10.6 us
    ppermute x43 -> x45, starting transfers between devices: 53.2 us -> 50.6 us  [dp_send(): return lax.ppermute(value, 'dp', [(i, i ^ bit) for i in range(size)])]
  transfers between devices with their start and end apart: 52 -> 54, of which waited for: 13 -> 15; matrix products, arithmetic and copies ran while one was open for 16% -> 14% of each run, Pallas kernels for 31% -> 31%
where the time goes in v6:
time: 251 us; the launch traced here: 247 us
  Pallas kernels  112 us (45%)
  starting transfers between devices  60.1 us (24%)
  other arithmetic  27.5 us (11%)
  waiting for transfers between devices  24.6 us (10%)
  local copies, waits for them, and re-layouts  20.8 us (8%)
    ppermute x45, starting transfers between devices, dp_send(): return lax.ppermute(value, 'dp', [(i, i ^ bit) for i in range(size)])  50.6 us
    pallas_call x3, Pallas kernels, mixer_backward(): pl.pallas_call(partial(backward_kernel, begin, rows), grid=(end - begin,)...  46.1 us
    pallas_call x1, Pallas kernels, mixer_forward(): pl.pallas_call(partial(forward_kernel, 1 + len(others), count), grid=(blo...  22.6 us
    pallas_call x1, Pallas kernels, gate_norm(): pl.pallas_call(partial(norm_kernel, float(full_inner), chips, split), gri...  20.2 us
    ppermute x45, waiting for transfers between devices, dp_send(): return lax.ppermute(value, 'dp', [(i, i ^ bit) for i in range(size)])  19.8 us
    pallas_call x1, Pallas kernels, gate_forward(): pl.pallas_call(partial(gate_kernel, 1 + len(others), count), grid=(rows /...  13.2 us
    unnamed x85, local copies, waits for them, and re-layouts  10.6 us
    ppermute x9, starting transfers between devices, tensor_swap(): return lax.ppermute(value, 'tensor', [(0, 1), (1, 0)])  9.57 us
  transfers between devices with their start and end apart: 54, of which 15 were waited for; matrix products, arithmetic and copies ran while one was open for 14% of the time, Pallas kernels for 31%

profile of v6, /device:TPU:0, one launch (start us, length us, event | category | flops | bytes accessed | tf_op | source)
XLA Modules:
  0.0 247.2 jit_solution(11845881424663011965)
XLA Ops:
  4.5 3.0 %collective-permute-start = (bf16[64,1408]{1,0:T(8,128)(2,1)}, bf16[64,1408]{1,0:T(8,128)(2,1)}, u32[]{:S(2)}, u32[]{:S(2)}) collective-permute-start(bf16[64,1408]{1,0:T(8,128)(2,1)} %pad_maximum_fusion.4), channel_id=1, source_target_pairs={{0,8},{2,10},{4,12},{6,14},{8,0},{10,2},{12,4},{14,6},{16,24},{18,... | collective-permute-start | bytes 540680 | tf_op jit(solution)/shard_map/ppermute | solution.py:831
  7.5 2.6 %collective-permute-start.1 = (bf16[64,1408]{1,0:T(8,128)(2,1)}, bf16[64,1408]{1,0:T(8,128)(2,1)}, u32[]{:S(2)}, u32[]{:S(2)}) collective-permute-start(bf16[64,1408]{1,0:T(8,128)(2,1)} %pad_maximum_fusion.4), channel_id=1, source_target_pairs={{0,16},{2,18},{4,20},{6,22},{8,24},{10,26},{12,28},{14,30},{16,0},... | collective-permute-start | bytes 540680 | tf_op jit(solution)/shard_map/ppermute | solution.py:831
  13.0 1.7 collective-permute-start.4
  22.1 1.9 collective-permute-done.1
  29.4 1.9 collective-permute-start.7
  31.4 2.3 collective-permute-start.8
  35.4 7.1 %collective-permute-done.8 = bf16[64,1024]{1,0:T(8,128)(2,1)S(1)} collective-permute-done((bf16[64,1024]{1,0:T(8,128)(2,1)S(1)}, bf16[64,1024]{1,0:T(8,128)(2,1)S(1)}, u32[]{:S(2)}, u32[]{:S(2)}) %collective-permute-start.8) | collective-permute-done | bytes 131104 | tf_op jit(solution)/shard_map/ppermute | solution.py:831
  48.7 2.4 collective-permute-start.14
  53.6 1.7 collective-permute-start.16
  55.3 22.6 %mixer_forward.1 = (bf16[1024,1024]{1,0:T(8,128)(2,1)}, bf16[1024,1408]{1,0:T(8,128)(2,1)}, f32[1024,1024]{1,0:T(8,128)}, f32[1024,1024]{1,0:T(8,128)}, f32[1024...) custom-call(s32[1,4]{1,0:T(1,128)} %add_bitcast_fusion.spot_ref, ...), custom_call_target="tpu_custom_call" | custom-call | tf_op jit(solution)/shard_map/mixer_forward/pallas_call | solution.py:286
  83.6 13.2 %gate_forward.1 = (bf16[1024,1024]{1,0:T(8,128)(2,1)}, bf16[1024,2048]{1,0:T(8,128)(2,1)}, f32[1024,1024]{1,0:T(8,128)}, f32[1024,1024]{1,0:T(8,128)}, f32[8,1024]{1,0:T(8,128)}) custom-call(s32[1,4]{1,0:T(1,128)} %add_bitcast_fusion.spot_ref, bf16[1024,1024]{1,0:T(8,128)(2,1)} %get-tuple-element.150.normed_ref, bf16[512,1024]{1,0:T(8,128)(2,1)} %refs_0_.1, ...), custom_call_target="tpu_custom_call" | custom-call | tf_op jit(solution)/shard_map/gate_forward/pallas_call | solution.py:656
  97.3 3.6 %collective-permute-done.23.more_ref = f32[8,1024]{1,0:T(8,128)S(1)} collective-permute-done((f32[8,1024]{1,0:T(8,128)}, f32[8,1024]{1,0:T(8,128)S(1)}, u32[]{:S(2)}, u32[]{:S(2)}) %collective-permute-start.23) | collective-permute-done | bytes 32800 | tf_op jit(solution)/shard_map/ppermute | solution.py:882
  101.6 20.2 %gate_norm.1 = (bf16[1024,1024]{1,0:T(8,128)(2,1)}, f32[1024,1024]{1,0:T(8,128)}, f32[8,1408]{1,0:T(8,128)}, bf16[512,2048]{1,0:T(8,128)(2,1)}, bf16[512,2048]{1...) custom-call(s32[1,4]{1,0:T(1,128)} %add_bitcast_fusion.spot_ref, ...), custom_call_target="tpu_custom_call" | custom-call | tf_op jit(solution)/shard_map/gate_norm/pallas_call | solution.py:753
  122.4 11.9 %mixer_backward.3 = (bf16[256,1408]{1,0:T(8,128)(2,1)}, bf16[256,1024]{1,0:T(8,128)(2,1)}, f32[8,1408]{1,0:T(8,128)}, f32[8,1024]{1,0:T(8,128)}, f32[8,256]{1,0:T(8,128)}, /*index=5*/f32[128,1024]{1,0:T(8,128)}) custom-call(s32[1,4]{1,0:T(1,128)} %lengths_ref.7, f32[1024,1024]{1,0:T(8,128)} %get-tuple-element.173.upstream_ref, ...), custom_call_target="tpu_custom_call" | custom-call | tf_op jit(solution)/shard_map/mixer_backward/pallas_call | solution.py:518
  134.4 2.4 add_convert_fusion
  138.1 2.5 %collective-permute-start.28 = (bf16[2,64,1024]{2,1,0:T(8,128)(2,1)}, bf16[2,64,1024]{2,1,0:T(8,128)(2,1)}, u32[]{:S(2)}, u32[]{:S(2)}) collective-permute-start(bf16[2,64,1024]{2,1,0:T(8,128)(2,1)} %get-tuple-element.294), channel_id=1, source_target_pairs={{0,16},{2,18},{4,20},{6,22},{8,24},{10,26},{12,28},{14,30},{16,0},... | collective-permute-start | bytes 786440 | tf_op jit(solution)/shard_map/ppermute | solution.py:831
  140.7 1.7 collective-permute-start.29
  144.2 22.1 %mixer_backward.4 = (bf16[512,1408]{1,0:T(8,128)(2,1)}, bf16[512,1024]{1,0:T(8,128)(2,1)}, f32[8,1408]{1,0:T(8,128)}, f32[8,1024]{1,0:T(8,128)}, f32[8,256]{1,0:T(8,128)}, /*index=5*/f32[128,1024]{1,0:T(8,128)}) custom-call(s32[1,4]{1,0:T(1,128)} %lengths_ref.7, f32[1024,1024]{1,0:T(8,128)} %get-tuple-element.173.upstream_ref, ...), custom_call_target="tpu_custom_call" | custom-call | tf_op jit(solution)/shard_map/mixer_backward/pallas_call | solution.py:518
  166.3 2.2 fusion.26
  175.9 2.7 %collective-permute-start.31 = (bf16[64,1024]{1,0:T(8,128)(2,1)}, bf16[64,1024]{1,0:T(8,128)(2,1)}, u32[]{:S(2)}, u32[]{:S(2)}) collective-permute-start(bf16[64,1024]{1,0:T(8,128)(2,1)} %get-tuple-element.302), channel_id=1, source_target_pairs={{0,16},{2,18},{4,20},{6,22},{8,24},{10,26},{12,28},{14,30},{16,0},... | collective-permute-start | bytes 393224 | tf_op jit(solution)/shard_map/ppermute | solution.py:831
  178.6 1.7 collective-permute-start.32
  180.3 12.0 %mixer_backward.5 = (bf16[256,1408]{1,0:T(8,128)(2,1)}, bf16[256,1024]{1,0:T(8,128)(2,1)}, f32[8,1408]{1,0:T(8,128)}, f32[8,1024]{1,0:T(8,128)}, f32[8,256]{1,0:T(8,128)}, /*index=5*/f32[128,1024]{1,0:T(8,128)}) custom-call(s32[1,4]{1,0:T(1,128)} %lengths_ref.7, f32[1024,1024]{1,0:T(8,128)} %get-tuple-element.173.upstream_ref, ...), custom_call_target="tpu_custom_call" | custom-call | tf_op jit(solution)/shard_map/mixer_backward/pallas_call | solution.py:518
  196.9 8.8 %weight_products.1 = (bf16[512,1408]{1,0:T(8,128)(2,1)}, bf16[128,1408]{1,0:T(8,128)(2,1)}, bf16[128,1408]{1,0:T(8,128)(2,1)}, bf16[128,1408]{1,0:T(8,128)(2,1)}...) custom-call(s32[1,4]{1,0:T(1,128)} %add_bitcast_fusion.spot_ref, ...), custom_call_target="tpu_custom_call" | custom-call | tf_op jit(solution)/shard_map/weight_products/pallas_call | solution.py:601
  209.1 1.7 add_convert_fusion.1
  213.7 2.7 %collective-permute-start.42 = (bf16[2,64,512]{2,1,0:T(8,128)(2,1)S(1)}, bf16[2,64,512]{2,1,0:T(8,128)(2,1)S(1)}, u32[]{:S(2)}, u32[]{:S(2)}) collective-permute-start(bf16[2,64,512]{2,1,0:T(8,128)(2,1)S(1)} %get-tuple-element.298), channel_id=1, source_target_pairs={{0,16},{2,18},{4,20},{6,22},{8,24},{10,26},{12,28},{14,30},{16,0},... | collective-permute-start | bytes 393224 | tf_op jit(solution)/shard_map/ppermute | solution.py:831
  218.3 1.8 fusion.7
  221.7 2.9 %fusion.6 = bf16[512,1024]{1,0:T(8,128)(2,1)} fusion(bf16[512,1024]{1,0:T(8,128)(2,1)S(1)} %copy-done, bf16[512,1024]{1,0:T(8,128)(2,1)S(1)} %copy-done.5, f32[512]{0:T(512)S(1)} %broadcast_multiply_fusion, f32[512]{0:T(512)S(1)} %copy-done.35, f32[1024]{0:T(1024)S(1)} %copy-done.29, f32[512]{0:T(512)S(1)} %copy-done.34, ...), kind=kLoop, calls=%fused_computation.13 | loop fusion | flops 12582912 | bytes 6301697 | tf_op jit(solution)/shard_map/convert_element_type | solution.py:1051
  224.6 2.5 collective-permute-done.46
  228.5 2.2 collective-permute-start.49
  231.4 1.7 collective-permute-start.51
  234.1 2.8 %fusion.8 = bf16[512,1024]{1,0:T(8,128)(2,1)} fusion(bf16[512,1024]{1,0:T(8,128)(2,1)S(1)} %copy-done, bf16[512,1024]{1,0:T(8,128)(2,1)} %collective-permute-done.25, bf16[512,1024]{1,0:T(8,128)(2,1)S(1)} %copy-done.12), kind=kLoop, calls=%fused_computation.15 | loop fusion | flops 3145728 | bytes 4194304 | tf_op jit(solution)/shard_map/convert_element_type | solution.py:1055
  238.5 3.2 %collective-permute-start.48 = (f32[8,2432]{1,0:T(8,128)S(1)}, f32[8,2432]{1,0:T(8,128)S(1)}, u32[]{:S(2)}, u32[]{:S(2)}) collective-permute-start(f32[8,2432]{1,0:T(8,128)S(1)} %add.202.sums_ref), channel_id=1, source_target_pairs={{0,16},{2,18},{4,20},{6,22},{8,24},{10,26},{12,28},{14,30},{16,0},... | collective-permute-start | bytes 233480 | tf_op jit(solution)/shard_map/ppermute | solution.py:831
  (228 shorter events, 71.8 us)
Async XLA Ops:
  4.5 17.5 %collective-permute-start = (bf16[64,1408]{1,0:T(8,128)(2,1)}, bf16[64,1408]{1,0:T(8,128)(2,1)}, u32[]{:S(2)}, u32[]{:S(2)}) collective-permute-start(bf16[64,1408]{1,0:T(8,128)(2,1)} %pad_maximum_fusion.4), channel_id=1, source_target_pairs={{0,8},{2,10},{4,12},{6,14},{8,0},{10,2},{12,4},{14,6},{16,24},{18,... | collective-permute-start | bytes 540680 | tf_op jit(solution)/shard_map/ppermute | solution.py:831
  7.5 16.4 %collective-permute-start.1 = (bf16[64,1408]{1,0:T(8,128)(2,1)}, bf16[64,1408]{1,0:T(8,128)(2,1)}, u32[]{:S(2)}, u32[]{:S(2)}) collective-permute-start(bf16[64,1408]{1,0:T(8,128)(2,1)} %pad_maximum_fusion.4), channel_id=1, source_target_pairs={{0,16},{2,18},{4,20},{6,22},{8,24},{10,26},{12,28},{14,30},{16,0},... | collective-permute-start | bytes 540680 | tf_op jit(solution)/shard_map/ppermute | solution.py:831
  10.1 13.8 %collective-permute-start.2 = (bf16[64,1408]{1,0:T(8,128)(2,1)}, bf16[64,1408]{1,0:T(8,128)(2,1)}, u32[]{:S(2)}, u32[]{:S(2)}) collective-permute-start(bf16[64,1408]{1,0:T(8,128)(2,1)} %pad_maximum_fusion.4), channel_id=1, source_target_pairs={{0,24},{2,26},{4,28},{6,30},{8,16},{10,18},{12,20},{14,22},{16,8},... | collective-permute-start | bytes 540680 | tf_op jit(solution)/shard_map/ppermute | solution.py:831
  13.0 13.4 %collective-permute-start.4 = (bf16[256,1024]{1,0:T(8,128)(2,1)}, bf16[256,1024]{1,0:T(8,128)(2,1)}, u32[]{:S(2)}, u32[]{:S(2)}) collective-permute-start(bf16[256,1024]{1,0:T(8,128)(2,1)} %get-tuple-element.296), channel_id=1, source_target_pairs={{0,1},{1,0},{2,3},{3,2},{4,5},{5,4},{6,7},{7,6},{8,9},{9,8},{10,11... | collective-permute-start | bytes 1572872 | tf_op jit(solution)/shard_map/ppermute | solution.py:882
  26.4 17.0 %collective-permute-start.5 = (bf16[256,1408]{1,0:T(8,128)(2,1)S(1)}, bf16[256,1408]{1,0:T(8,128)(2,1)S(1)}, u32[]{:S(2)}, u32[]{:S(2)}) collective-permute-start(bf16[256,1408]{1,0:T(8,128)(2,1)S(1)} %pad_maximum_fusion.1.refs_3_), channel_id=1, source_target_pairs={{0,4},{2,6},{4,0},{6,2},{8,12},{10,14},{12,8},{14,10},{16,20},{18,... | collective-permute-start | bytes 2162696 | tf_op jit(solution)/shard_map/ppermute | solution.py:831
  27.9 14.7 %collective-permute-start.6 = (bf16[256,1024]{1,0:T(8,128)(2,1)}, bf16[256,1024]{1,0:T(8,128)(2,1)S(1)}, u32[]{:S(2)}, u32[]{:S(2)}) collective-permute-start(bf16[256,1024]{1,0:T(8,128)(2,1)} %get-tuple-element.295), channel_id=1, source_target_pairs={{0,1},{1,0},{2,3},{3,2},{4,5},{5,4},{6,7},{7,6},{8,9},{9,8},{10,11... | collective-permute-start | bytes 1572872 | tf_op jit(solution)/shard_map/ppermute | solution.py:882
  31.4 11.2 %collective-permute-start.8 = (bf16[64,1024]{1,0:T(8,128)(2,1)S(1)}, bf16[64,1024]{1,0:T(8,128)(2,1)S(1)}, u32[]{:S(2)}, u32[]{:S(2)}) collective-permute-start(bf16[64,1024]{1,0:T(8,128)(2,1)S(1)} %bitcast.102), channel_id=1, source_target_pairs={{0,16},{2,18},{4,20},{6,22},{8,24},{10,26},{12,28},{14,30},{16,0},... | collective-permute-start | bytes 393224 | tf_op jit(solution)/shard_map/ppermute | solution.py:831
  43.4 34.7 %collective-permute-start.12 = (bf16[512,1024]{1,0:T(8,128)(2,1)S(1)}, bf16[512,1024]{1,0:T(8,128)(2,1)S(1)}, u32[]{:S(2)}, u32[]{:S(2)}) collective-permute-start(bf16[512,1024]{1,0:T(8,128)(2,1)S(1)} %copy-done.4), channel_id=1, source_target_pairs={{0,1},{1,0},{2,3},{3,2},{4,5},{5,4},{6,7},{7,6},{8,9},{9,8},{10,11... | collective-permute-start | bytes 3145736 | tf_op jit(solution)/shard_map/ppermute | solution.py:882
  47.2 30.8 %collective-permute-start.13 = (bf16[256,1024]{1,0:T(8,128)(2,1)}, bf16[256,1024]{1,0:T(8,128)(2,1)}, u32[]{:S(2)}, u32[]{:S(2)}) collective-permute-start(bf16[256,1024]{1,0:T(8,128)(2,1)} %constant_dynamic-update-slice_fusion.refs_2_), channel_id=1, source_target_pairs={{0,4},{2,6},{4,0},{6,2},{8,12},{10,14},{12,8},{14,10},{16,20},{18,... | collective-permute-start | bytes 1572872 | tf_op jit(solution)/shard_map/ppermute | solution.py:831
  48.7 29.2 %collective-permute-start.14 = (bf16[128,1024]{1,0:T(8,128)(2,1)S(1)}, bf16[128,1024]{1,0:T(8,128)(2,1)S(1)}, u32[]{:S(2)}, u32[]{:S(2)}) collective-permute-start(bf16[128,1024]{1,0:T(8,128)(2,1)S(1)} %pad_maximum_fusion.3.refs_6_), channel_id=1, source_target_pairs={{0,8},{2,10},{4,12},{6,14},{8,0},{10,2},{12,4},{14,6},{16,24},{18,... | collective-permute-start | bytes 786440 | tf_op jit(solution)/shard_map/ppermute | solution.py:831
  51.2 26.8 %collective-permute-start.15 = (bf16[128,1024]{1,0:T(8,128)(2,1)S(1)}, bf16[128,1024]{1,0:T(8,128)(2,1)S(1)}, u32[]{:S(2)}, u32[]{:S(2)}) collective-permute-start(bf16[128,1024]{1,0:T(8,128)(2,1)S(1)} %pad_maximum_fusion.3.refs_6_), channel_id=1, source_target_pairs={{0,16},{2,18},{4,20},{6,22},{8,24},{10,26},{12,28},{14,30},{16,0},... | collective-permute-start | bytes 786440 | tf_op jit(solution)/shard_map/ppermute | solution.py:831
  53.6 24.4 %collective-permute-start.16 = (bf16[128,1024]{1,0:T(8,128)(2,1)S(1)}, bf16[128,1024]{1,0:T(8,128)(2,1)}, u32[]{:S(2)}, u32[]{:S(2)}) collective-permute-start(bf16[128,1024]{1,0:T(8,128)(2,1)S(1)} %pad_maximum_fusion.3.refs_6_), channel_id=1, source_target_pairs={{0,24},{2,26},{4,28},{6,30},{8,16},{10,18},{12,20},{14,22},{16,8},... | collective-permute-start | bytes 786440 | tf_op jit(solution)/shard_map/ppermute | solution.py:831
  121.7 12.7 %collective-permute-start.24 = (bf16[512,2048]{1,0:T(8,128)(2,1)}, bf16[512,2048]{1,0:T(8,128)(2,1)}, u32[]{:S(2)}, u32[]{:S(2)}) collective-permute-start(bf16[512,2048]{1,0:T(8,128)(2,1)} %get-tuple-element.187), channel_id=1, source_target_pairs={{0,2},{2,0},{4,6},{6,4},{8,10},{10,8},{12,14},{14,12},{16,18},{18,... | collective-permute-start | bytes 6291464 | tf_op jit(solution)/shard_map/ppermute | solution.py:831
  121.8 49.9 %collective-permute-start.25 = (bf16[512,1024]{1,0:T(8,128)(2,1)}, bf16[512,1024]{1,0:T(8,128)(2,1)}, u32[]{:S(2)}, u32[]{:S(2)}) collective-permute-start(bf16[512,1024]{1,0:T(8,128)(2,1)} %get-tuple-element.198), channel_id=1, source_target_pairs={{0,1},{1,0},{2,3},{3,2},{4,5},{5,4},{6,7},{7,6},{8,9},{9,8},{10,11... | collective-permute-start | bytes 3145736 | tf_op jit(solution)/shard_map/ppermute | solution.py:882
  138.0 30.6 %collective-permute-start.27 = (bf16[2,64,1024]{2,1,0:T(8,128)(2,1)}, bf16[2,64,1024]{2,1,0:T(8,128)(2,1)S(1)}, u32[]{:S(2)}, u32[]{:S(2)}) collective-permute-start(bf16[2,64,1024]{2,1,0:T(8,128)(2,1)} %get-tuple-element.292), channel_id=1, source_target_pairs={{0,8},{2,10},{4,12},{6,14},{8,0},{10,2},{12,4},{14,6},{16,24},{18,... | collective-permute-start | bytes 786440 | tf_op jit(solution)/shard_map/ppermute | solution.py:831
  138.1 30.4 %collective-permute-start.28 = (bf16[2,64,1024]{2,1,0:T(8,128)(2,1)}, bf16[2,64,1024]{2,1,0:T(8,128)(2,1)}, u32[]{:S(2)}, u32[]{:S(2)}) collective-permute-start(bf16[2,64,1024]{2,1,0:T(8,128)(2,1)} %get-tuple-element.294), channel_id=1, source_target_pairs={{0,16},{2,18},{4,20},{6,22},{8,24},{10,26},{12,28},{14,30},{16,0},... | collective-permute-start | bytes 786440 | tf_op jit(solution)/shard_map/ppermute | solution.py:831
  140.7 28.6 %collective-permute-start.29 = (bf16[2,64,1024]{2,1,0:T(8,128)(2,1)}, bf16[2,64,1024]{2,1,0:T(8,128)(2,1)}, u32[]{:S(2)}, u32[]{:S(2)}) collective-permute-start(bf16[2,64,1024]{2,1,0:T(8,128)(2,1)} %get-tuple-element.293), channel_id=1, source_target_pairs={{0,24},{2,26},{4,28},{6,30},{8,16},{10,18},{12,20},{14,22},{16,8},... | collective-permute-start | bytes 786440 | tf_op jit(solution)/shard_map/ppermute | solution.py:831
  143.2 27.3 %collective-permute-start.26 = (bf16[4,64,1024]{2,1,0:T(8,128)(2,1)}, bf16[4,64,1024]{2,1,0:T(8,128)(2,1)}, u32[]{:S(2)}, u32[]{:S(2)}) collective-permute-start(bf16[4,64,1024]{2,1,0:T(8,128)(2,1)} %dynamic-slice_bitcast_fusion), channel_id=1, source_target_pairs={{0,4},{2,6},{4,0},{6,2},{8,12},{10,14},{12,8},{14,10},{16,20},{18,... | collective-permute-start | bytes 1572872 | tf_op jit(solution)/shard_map/ppermute | solution.py:831
  172.4 19.9 %collective-permute-start.33 = (bf16[64,1024]{1,0:T(8,128)(2,1)}, bf16[64,1024]{1,0:T(8,128)(2,1)}, u32[]{:S(2)}, u32[]{:S(2)}) collective-permute-start(bf16[64,1024]{1,0:T(8,128)(2,1)} %dynamic-slice_bitcast_fusion.8), channel_id=1, source_target_pairs={{0,4},{2,6},{4,0},{6,2},{8,12},{10,14},{12,8},{14,10},{16,20},{18,... | collective-permute-start | bytes 393224 | tf_op jit(solution)/shard_map/ppermute | solution.py:831
  173.6 21.5 %collective-permute-start.34 = (bf16[256,1024]{1,0:T(8,128)(2,1)}, bf16[256,1024]{1,0:T(8,128)(2,1)}, u32[]{:S(2)}, u32[]{:S(2)}) collective-permute-start(bf16[256,1024]{1,0:T(8,128)(2,1)} %get-tuple-element.208), channel_id=1, source_target_pairs={{0,1},{1,0},{2,3},{3,2},{4,5},{5,4},{6,7},{7,6},{8,9},{9,8},{10,11... | collective-permute-start | bytes 1572872 | tf_op jit(solution)/shard_map/ppermute | solution.py:882
  175.9 18.1 %collective-permute-start.30 = (bf16[64,1024]{1,0:T(8,128)(2,1)}, bf16[64,1024]{1,0:T(8,128)(2,1)S(1)}, u32[]{:S(2)}, u32[]{:S(2)}) collective-permute-start(bf16[64,1024]{1,0:T(8,128)(2,1)} %get-tuple-element.300), channel_id=1, source_target_pairs={{0,8},{2,10},{4,12},{6,14},{8,0},{10,2},{12,4},{14,6},{16,24},{18,... | collective-permute-start | bytes 393224 | tf_op jit(solution)/shard_map/ppermute | solution.py:831
  175.9 18.1 %collective-permute-start.31 = (bf16[64,1024]{1,0:T(8,128)(2,1)}, bf16[64,1024]{1,0:T(8,128)(2,1)}, u32[]{:S(2)}, u32[]{:S(2)}) collective-permute-start(bf16[64,1024]{1,0:T(8,128)(2,1)} %get-tuple-element.302), channel_id=1, source_target_pairs={{0,16},{2,18},{4,20},{6,22},{8,24},{10,26},{12,28},{14,30},{16,0},... | collective-permute-start | bytes 393224 | tf_op jit(solution)/shard_map/ppermute | solution.py:831
  178.6 15.4 %collective-permute-start.32 = (bf16[64,1024]{1,0:T(8,128)(2,1)}, bf16[64,1024]{1,0:T(8,128)(2,1)}, u32[]{:S(2)}, u32[]{:S(2)}) collective-permute-start(bf16[64,1024]{1,0:T(8,128)(2,1)} %get-tuple-element.301), channel_id=1, source_target_pairs={{0,24},{2,26},{4,28},{6,30},{8,16},{10,18},{12,20},{14,22},{16,8},... | collective-permute-start | bytes 393224 | tf_op jit(solution)/shard_map/ppermute | solution.py:831
  196.2 13.0 %collective-permute-start.39 = (bf16[256,1024]{1,0:T(8,128)(2,1)S(1)}, bf16[256,1024]{1,0:T(8,128)(2,1)S(1)}, u32[]{:S(2)}, u32[]{:S(2)}) collective-permute-start(bf16[256,1024]{1,0:T(8,128)(2,1)S(1)} %broadcast_select_fusion), channel_id=1, source_target_pairs={{0,1},{1,0},{2,3},{3,2},{4,5},{5,4},{6,7},{7,6},{8,9},{9,8},{10,11... | collective-permute-start | bytes 1572872 | tf_op jit(solution)/shard_map/ppermute | solution.py:882
  213.0 14.1 %collective-permute-start.40 = (bf16[4,64,896]{2,1,0:T(8,128)(2,1)S(1)}, bf16[4,64,896]{2,1,0:T(8,128)(2,1)S(1)}, u32[]{:S(2)}, u32[]{:S(2)}) collective-permute-start(bf16[4,64,896]{2,1,0:T(8,128)(2,1)S(1)} %dynamic-slice_bitcast_fusion.1), channel_id=1, source_target_pairs={{0,4},{2,6},{4,0},{6,2},{8,12},{10,14},{12,8},{14,10},{16,20},{18,... | collective-permute-start | bytes 1376264 | tf_op jit(solution)/shard_map/ppermute | solution.py:831
  213.7 13.4 %collective-permute-start.41 = (bf16[2,64,512]{2,1,0:T(8,128)(2,1)S(1)}, bf16[2,64,512]{2,1,0:T(8,128)(2,1)S(1)}, u32[]{:S(2)}, u32[]{:S(2)}) collective-permute-start(bf16[2,64,512]{2,1,0:T(8,128)(2,1)S(1)} %get-tuple-element.299), channel_id=1, source_target_pairs={{0,8},{2,10},{4,12},{6,14},{8,0},{10,2},{12,4},{14,6},{16,24},{18,... | collective-permute-start | bytes 393224 | tf_op jit(solution)/shard_map/ppermute | solution.py:831
  213.7 13.3 %collective-permute-start.42 = (bf16[2,64,512]{2,1,0:T(8,128)(2,1)S(1)}, bf16[2,64,512]{2,1,0:T(8,128)(2,1)S(1)}, u32[]{:S(2)}, u32[]{:S(2)}) collective-permute-start(bf16[2,64,512]{2,1,0:T(8,128)(2,1)S(1)} %get-tuple-element.298), channel_id=1, source_target_pairs={{0,16},{2,18},{4,20},{6,22},{8,24},{10,26},{12,28},{14,30},{16,0},... | collective-permute-start | bytes 393224 | tf_op jit(solution)/shard_map/ppermute | solution.py:831
  216.4 10.6 %collective-permute-start.43 = (bf16[2,64,512]{2,1,0:T(8,128)(2,1)S(1)}, bf16[2,64,512]{2,1,0:T(8,128)(2,1)S(1)}, u32[]{:S(2)}, u32[]{:S(2)}) collective-permute-start(bf16[2,64,512]{2,1,0:T(8,128)(2,1)S(1)} %get-tuple-element.297), channel_id=1, source_target_pairs={{0,24},{2,26},{4,28},{6,30},{8,16},{10,18},{12,20},{14,22},{16,8},... | collective-permute-start | bytes 393224 | tf_op jit(solution)/shard_map/ppermute | solution.py:831
  227.2 9.8 %collective-permute-start.52 = (bf16[64,512]{1,0:T(8,128)(2,1)S(1)}, bf16[64,512]{1,0:T(8,128)(2,1)S(1)}, u32[]{:S(2)}, u32[]{:S(2)}) collective-permute-start(bf16[64,512]{1,0:T(8,128)(2,1)S(1)} %dynamic-slice_bitcast_fusion.15), channel_id=1, source_target_pairs={{0,4},{2,6},{4,0},{6,2},{8,12},{10,14},{12,8},{14,10},{16,20},{18,... | collective-permute-start | bytes 196616 | tf_op jit(solution)/shard_map/ppermute | solution.py:831
  228.5 13.2 %collective-permute-start.49 = (bf16[64,896]{1,0:T(8,128)(2,1)S(1)}, bf16[64,896]{1,0:T(8,128)(2,1)S(1)}, u32[]{:S(2)}, u32[]{:S(2)}) collective-permute-start(bf16[64,896]{1,0:T(8,128)(2,1)S(1)} %get-tuple-element.303), channel_id=1, source_target_pairs={{0,8},{2,10},{4,12},{6,14},{8,0},{10,2},{12,4},{14,6},{16,24},{18,... | collective-permute-start | bytes 344072 | tf_op jit(solution)/shard_map/ppermute | solution.py:831
  230.6 11.0 %collective-permute-start.50 = (bf16[64,896]{1,0:T(8,128)(2,1)S(1)}, bf16[64,896]{1,0:T(8,128)(2,1)S(1)}, u32[]{:S(2)}, u32[]{:S(2)}) collective-permute-start(bf16[64,896]{1,0:T(8,128)(2,1)S(1)} %get-tuple-element.305), channel_id=1, source_target_pairs={{0,16},{2,18},{4,20},{6,22},{8,24},{10,26},{12,28},{14,30},{16,0},... | collective-permute-start | bytes 344072 | tf_op jit(solution)/shard_map/ppermute | solution.py:831
  231.4 10.3 %collective-permute-start.51 = (bf16[64,896]{1,0:T(8,128)(2,1)S(1)}, bf16[64,896]{1,0:T(8,128)(2,1)S(1)}, u32[]{:S(2)}, u32[]{:S(2)}) collective-permute-start(bf16[64,896]{1,0:T(8,128)(2,1)S(1)} %get-tuple-element.304), channel_id=1, source_target_pairs={{0,24},{2,26},{4,28},{6,30},{8,16},{10,18},{12,20},{14,22},{16,8},... | collective-permute-start | bytes 344072 | tf_op jit(solution)/shard_map/ppermute | solution.py:831
  (60 other events, 377.1 us)

commit v7 on v6

--- a/solution.py
+++ b/solution.py
@@ -315,11 +315,15 @@
 
 
 def backward_kernel(
-    first_block, total_rows, lengths_ref, upstream_ref, ssm_ref, inner_ref, pre_inner_ref,
+    first_block, total_rows, first_call, sending, lengths_ref, upstream_ref, ssm_ref, inner_ref, pre_inner_ref,
     shared_ref, pre_shared_ref, step_ref, entering_ref, conv_inner_ref, conv_shared_ref, rate_ref, skip_ref, spread_ref,
     grad_gate_ref, gate_w_ref, weight_ref, sums_in_ref, *refs,
 ):
-    carried_in, refs = refs[:-11], refs[-11:]
+    inputs = 5 if sending else 0 if first_call else 3
+    carried_in, refs = refs[:inputs], refs[inputs:]
+    if sending:
+        send_ref = refs[6]
+        refs = refs[:6] + refs[7:]
     (
         grads_ref, terms_ref, sums_ref, inner_out_ref, shared_out_ref, adjoint, inner_head,
         shared_head, gate_w, weight, done,
@@ -486,6 +490,13 @@
 
     terms = mm(grad_gate_ref[...], gate_w[...], NT) + mm(grads_ref[...], weight[...], NT)
     terms_ref[...] = terms.astype(bf16)
+    if sending:
+        spot_ref, earlier_ref = carried_in[3:]
+
+        @pl.when(turn == pl.num_programs(0) - 1)
+        def _():
+            send_ref[...] = jnp.where(spot_ref[0, 0] == 0, earlier_ref[...], terms.astype(bf16))
+
     sums_ref[:, channels + width :] += jnp.concatenate(
         [
             jnp.sum(grad_step, axis=0, keepdims=True),
@@ -504,7 +515,7 @@
 
 def mixer_backward(
     lengths, upstream, saved, conv_inner, conv_shared, rate, skip, spread, grad_gate, weight_late,
-    weight, carry, blocks, span
+    weight, carry, blocks, span, spot=None, earlier=None
 ):
     ssm, inner, pre_inner, shared, pre_shared, step_raw, entering = saved
     rows, channels = upstream.shape
@@ -514,9 +525,16 @@
     known = channels + width + LANES
     model = weight.shape[0]
     by_row = lambda cols: pl.BlockSpec((span, cols), lambda i: (end - 1 - i, 0))
+    extra, extra_specs = (), ()
+    if earlier is not None:
+        last = earlier.shape[0] // span - 1
+        extra = (spot, earlier)
+        extra_specs = (
+            pl.BlockSpec(memory_space=pltpu.SMEM), pl.BlockSpec((span, model), lambda i: (last, 0)),
+        )
     small = ((TAIL, known), (TAIL, channels), (TAIL, width), (states, channels))
     results = pl.pallas_call(
-        partial(backward_kernel, begin, rows),
+        partial(backward_kernel, begin, rows, len(carry) == 1, earlier is not None),
         grid=(end - begin,),
         in_specs=[
             pl.BlockSpec(memory_space=pltpu.SMEM),
@@ -532,16 +550,19 @@
             pl.BlockSpec(memory_space=pl.ANY),
             pl.BlockSpec(memory_space=pl.ANY),
             *[full(x.shape) for x in carry],
+            *extra_specs,
         ],
         out_specs=[
             pl.BlockSpec((span, known), lambda i: (end - begin - 1 - i, 0)),
             pl.BlockSpec((span, model), lambda i: (end - begin - 1 - i, 0)),
             *[full(shape) for shape in small],
+            *([full((span, model))] if extra else []),
         ],
         out_shape=[
             jax.ShapeDtypeStruct(((end - begin) * span, known), bf16),
             jax.ShapeDtypeStruct(((end - begin) * span, model), bf16),
             *[jax.ShapeDtypeStruct(shape, f32) for shape in small],
+            *([jax.ShapeDtypeStruct((span, model), bf16)] if extra else []),
         ],
         scratch_shapes=[
             pltpu.VMEM((TAIL + span, channels), f32),
@@ -557,8 +578,9 @@
     )(
         lengths, upstream, ssm, inner, pre_inner, shared, pre_shared, step_raw, entering,
         conv_inner, conv_shared, rate, skip, spread, grad_gate, weight_late, weight, *carry,
-    )
-    return results[0], results[1], tuple(results[2:])
+        *extra,
+    )
+    return results[0], results[1], tuple(results[2:6]), *results[6:]
 
 
 def gain_row(weight_ref, total_ref, columns):
@@ -994,10 +1016,13 @@
     quarter = grad_ssm.shape[0] // SPAN // 4
     carry = (gain_sum,)
 
-    def back(begin, end, carry):
+    fused = split and quarter == 1
+
+    def back(begin, end, carry, earlier=None):
         return mixer_backward(
             lengths, grad_ssm, saved, conv_inner, conv_shared, rate, skip, spread, grad_gate,
-            weight_late, weight, carry, (begin * quarter, end * quarter), SPAN,
+            weight_late, weight, carry, (begin * quarter, end * quarter), SPAN, spot,
+            earlier if fused else None,
         )
 
     first = dp_send(send, 1)
@@ -1006,22 +1031,22 @@
     first = first.reshape(count, 2, -1, first.shape[1])
     carry, first = lax.optimization_barrier((carry, first))
     first_gate, first_out = first[..., :channels], first[..., channels:]
-    grads1, terms1, carry = back(1, 3, carry)
+    grads1, terms1, carry, *ready = back(1, 3, carry, terms3)
     first_gate = fold(first_gate, 2, 1)
     first_out = fold_chips(first_out).astype(bf16)
     each = terms3.shape[0]
-    send1 = pick_half(terms3, terms1[:each], size)
+    send1 = ready[0] if fused else pick_half(terms3, terms1[:each], size)
     carry, send1, branch_other, first_gate, first_out = lax.optimization_barrier(
         (carry, send1, branch_other, first_gate, first_out)
     )
     other1 = gather_other(send1, size) if split else send1
     part_gate = fold_chips(first_gate)
     part_out = fold(first_out, 2, 0)
-    grads0, terms0, carry = back(0, 1, carry)
+    grads0, terms0, carry, *ready = back(0, 1, carry, terms1)
     sums, part_gate, part_out, grads0, other1, terms0 = lax.optimization_barrier(
         (carry[0], part_gate, part_out, grads0, other1, terms0)
     )
-    send0 = pick_half(terms1[each:], terms0, size)
+    send0 = ready[0] if fused else pick_half(terms1[each:], terms0, size)
     send0, grads0 = lax.optimization_barrier((send0, grads0))
     other0 = gather_other(send0, size) if split else send0
     keep, *send, sums, shared_sums = weight_products(

time: 251 us -> 247 us (0.984)
  other arithmetic: 27.5 us -> 23.1 us
    unnamed x85 -> x83, local copies, waits for them, and re-layouts: 10.6 us -> 9.89 us
  transfers between devices with their start and end apart: 54 -> 54, of which waited for: 15 -> 16; matrix products, arithmetic and copies ran while one was open for 14% -> 13% of each run, Pallas kernels for 31% -> 32%
where the time goes in v7:
time: 247 us; the launch traced here: 243 us
  Pallas kernels  113 us (46%)
  starting transfers between devices  60.2 us (24%)
  waiting for transfers between devices  25 us (10%)
  other arithmetic  23.1 us (9%)
  local copies, waits for them, and re-layouts  19.5 us (8%)
    ppermute x45, starting transfers between devices, dp_send(): return lax.ppermute(value, 'dp', [(i, i ^ bit) for i in range(size)])  50.8 us
    pallas_call x3, Pallas kernels, mixer_backward(): pl.pallas_call(partial(backward_kernel, begin, rows, len(carry) == 1, ear...  47.1 us
    pallas_call x1, Pallas kernels, mixer_forward(): pl.pallas_call(partial(forward_kernel, 1 + len(others), count), grid=(blo...  22.7 us
    pallas_call x1, Pallas kernels, gate_norm(): pl.pallas_call(partial(norm_kernel, float(full_inner), chips, split), gri...  20.1 us
    ppermute x45, waiting for transfers between devices, dp_send(): return lax.ppermute(value, 'dp', [(i, i ^ bit) for i in range(size)])  20.1 us
    pallas_call x1, Pallas kernels, gate_forward(): pl.pallas_call(partial(gate_kernel, 1 + len(others), count), grid=(rows /...  13.1 us
    unnamed x83, local copies, waits for them, and re-layouts  9.89 us
    ppermute x9, starting transfers between devices, tensor_swap(): return lax.ppermute(value, 'tensor', [(0, 1), (1, 0)])  9.4 us
  transfers between devices with their start and end apart: 54, of which 16 were waited for; matrix products, arithmetic and copies ran while one was open for 13% of the time, Pallas kernels for 32%

profile of v7, /device:TPU:0, one launch (start us, length us, event | category | flops | bytes accessed | tf_op | source)
XLA Modules:
  0.0 242.8 jit_solution(7517676154203576814)
XLA Ops:
  4.5 3.0 %collective-permute-start = (bf16[64,1408]{1,0:T(8,128)(2,1)}, bf16[64,1408]{1,0:T(8,128)(2,1)}, u32[]{:S(2)}, u32[]{:S(2)}) collective-permute-start(bf16[64,1408]{1,0:T(8,128)(2,1)} %pad_maximum_fusion.4), channel_id=1, source_target_pairs={{0,8},{2,10},{4,12},{6,14},{8,0},{10,2},{12,4},{14,6},{16,24},{18,... | collective-permute-start | bytes 540680 | tf_op jit(solution)/shard_map/ppermute | solution.py:853
  7.6 2.6 %collective-permute-start.1 = (bf16[64,1408]{1,0:T(8,128)(2,1)}, bf16[64,1408]{1,0:T(8,128)(2,1)}, u32[]{:S(2)}, u32[]{:S(2)}) collective-permute-start(bf16[64,1408]{1,0:T(8,128)(2,1)} %pad_maximum_fusion.4), channel_id=1, source_target_pairs={{0,16},{2,18},{4,20},{6,22},{8,24},{10,26},{12,28},{14,30},{16,0},... | collective-permute-start | bytes 540680 | tf_op jit(solution)/shard_map/ppermute | solution.py:853
  13.0 1.7 collective-permute-start.4
  22.1 1.9 collective-permute-done.1
  29.5 1.9 collective-permute-start.7
  31.4 2.3 collective-permute-start.8
  35.4 7.1 %collective-permute-done.8 = bf16[64,1024]{1,0:T(8,128)(2,1)S(1)} collective-permute-done((bf16[64,1024]{1,0:T(8,128)(2,1)S(1)}, bf16[64,1024]{1,0:T(8,128)(2,1)S(1)}, u32[]{:S(2)}, u32[]{:S(2)}) %collective-permute-start.8) | collective-permute-done | bytes 131104 | tf_op jit(solution)/shard_map/ppermute | solution.py:853
  48.8 2.4 collective-permute-start.14
  51.2 1.6 collective-permute-start.15
  53.7 1.7 collective-permute-start.16
  55.4 22.7 %mixer_forward.1 = (bf16[1024,1024]{1,0:T(8,128)(2,1)}, bf16[1024,1408]{1,0:T(8,128)(2,1)}, f32[1024,1024]{1,0:T(8,128)}, f32[1024,1024]{1,0:T(8,128)}, f32[1024...) custom-call(s32[1,4]{1,0:T(1,128)} %add_bitcast_fusion.spot_ref.refs, ...), custom_call_target="tpu_custom_call" | custom-call | tf_op jit(solution)/shard_map/mixer_forward/pallas_call | solution.py:286
  83.6 13.1 %gate_forward.1 = (bf16[1024,1024]{1,0:T(8,128)(2,1)}, bf16[1024,2048]{1,0:T(8,128)(2,1)}, f32[1024,1024]{1,0:T(8,128)}, f32[1024,1024]{1,0:T(8,128)}, f32[8,1024]{1,0:T(8,128)}) custom-call(s32[1,4]{1,0:T(1,128)} %add_bitcast_fusion.spot_ref.refs_3_, bf16[1024,1024]{1,0:T(8,128)(2,1)} %get-tuple-element.152.normed_ref, bf16[512,1024]{1,0:T(8,128)(2,1)} %refs_0_.1, ...), custom_call_target="tpu_custom_call" | custom-call | tf_op jit(solution)/shard_map/gate_forward/pallas_call | solution.py:678
  97.3 3.6 %collective-permute-done.23.more_ref = f32[8,1024]{1,0:T(8,128)S(1)} collective-permute-done((f32[8,1024]{1,0:T(8,128)}, f32[8,1024]{1,0:T(8,128)S(1)}, u32[]{:S(2)}, u32[]{:S(2)}) %collective-permute-start.23) | collective-permute-done | bytes 32800 | tf_op jit(solution)/shard_map/ppermute | solution.py:904
  101.5 20.1 %gate_norm.1 = (bf16[1024,1024]{1,0:T(8,128)(2,1)}, f32[1024,1024]{1,0:T(8,128)}, f32[8,1408]{1,0:T(8,128)}, bf16[512,2048]{1,0:T(8,128)(2,1)}, bf16[512,2048]{1...) custom-call(s32[1,4]{1,0:T(1,128)} %add_bitcast_fusion.spot_ref.refs_3_, ...), custom_call_target="tpu_custom_call" | custom-call | tf_op jit(solution)/shard_map/gate_norm/pallas_call | solution.py:775
  122.4 11.9 %mixer_backward.3 = (bf16[256,1408]{1,0:T(8,128)(2,1)}, bf16[256,1024]{1,0:T(8,128)(2,1)}, f32[8,1408]{1,0:T(8,128)}, f32[8,1024]{1,0:T(8,128)}, f32[8,256]{1,0:T(8,128)}, /*index=5*/f32[128,1024]{1,0:T(8,128)}) custom-call(s32[1,4]{1,0:T(1,128)} %lengths_ref.7, f32[1024,1024]{1,0:T(8,128)} %get-tuple-element.175.upstream_ref, ...), custom_call_target="tpu_custom_call" | custom-call | tf_op jit(solution)/shard_map/mixer_backward/pallas_call | solution.py:536
  134.3 2.4 add_convert_fusion
  139.8 2.1 collective-permute-start.28
  142.0 2.1 collective-permute-start.29
  144.1 22.6 %mixer_backward.4 = (bf16[512,1408]{1,0:T(8,128)(2,1)}, bf16[512,1024]{1,0:T(8,128)(2,1)}, f32[8,1408]{1,0:T(8,128)}, f32[8,1024]{1,0:T(8,128)}, f32[8,256]{1,0:...) custom-call(s32[1,4]{1,0:T(1,128)} %lengths_ref.7, f32[1024,1024]{1,0:T(8,128)} %get-tuple-element.175.upstream_ref, ...), custom_call_target="tpu_custom_call" | custom-call | tf_op jit(solution)/shard_map/mixer_backward/pallas_call | solution.py:536
  172.1 2.7 %collective-permute-start.31 = (bf16[64,1024]{1,0:T(8,128)(2,1)S(1)}, bf16[64,1024]{1,0:T(8,128)(2,1)S(1)}, u32[]{:S(2)}, u32[]{:S(2)}) collective-permute-start(bf16[64,1024]{1,0:T(8,128)(2,1)S(1)} %get-tuple-element.305), channel_id=1, source_target_pairs={{0,16},{2,18},{4,20},{6,22},{8,24},{10,26},{12,28},{14,30},{16,0},... | collective-permute-start | bytes 393224 | tf_op jit(solution)/shard_map/ppermute | solution.py:853
  174.8 1.7 collective-permute-start.32
  176.5 12.5 %mixer_backward.5 = (bf16[256,1408]{1,0:T(8,128)(2,1)}, bf16[256,1024]{1,0:T(8,128)(2,1)}, f32[8,1408]{1,0:T(8,128)}, f32[8,1024]{1,0:T(8,128)}, f32[8,256]{1,0:...) custom-call(s32[1,4]{1,0:T(1,128)} %lengths_ref.7, f32[1024,1024]{1,0:T(8,128)} %get-tuple-element.175.upstream_ref, ...), custom_call_target="tpu_custom_call" | custom-call | tf_op jit(solution)/shard_map/mixer_backward/pallas_call | solution.py:536
  190.4 8.9 %weight_products.1 = (bf16[512,1408]{1,0:T(8,128)(2,1)}, bf16[128,1408]{1,0:T(8,128)(2,1)}, bf16[128,1408]{1,0:T(8,128)(2,1)}, bf16[128,1408]{1,0:T(8,128)(2,1)}...) custom-call(s32[1,4]{1,0:T(1,128)} %add_bitcast_fusion.spot_ref.refs_3_, ...), custom_call_target="tpu_custom_call" | custom-call | tf_op jit(solution)/shard_map/weight_products/pallas_call | solution.py:623
  202.9 1.7 add_convert_fusion.1
  207.7 2.7 %collective-permute-start.42 = (bf16[2,64,512]{2,1,0:T(8,128)(2,1)S(1)}, bf16[2,64,512]{2,1,0:T(8,128)(2,1)S(1)}, u32[]{:S(2)}, u32[]{:S(2)}) collective-permute-start(bf16[2,64,512]{2,1,0:T(8,128)(2,1)S(1)} %get-tuple-element.301), channel_id=1, source_target_pairs={{0,16},{2,18},{4,20},{6,22},{8,24},{10,26},{12,28},{14,30},{16,0},... | collective-permute-start | bytes 393224 | tf_op jit(solution)/shard_map/ppermute | solution.py:853
  210.3 1.7 collective-permute-start.43
  214.9 2.9 %fusion.6 = bf16[512,1024]{1,0:T(8,128)(2,1)} fusion(bf16[512,1024]{1,0:T(8,128)(2,1)S(1)} %copy-done, bf16[512,1024]{1,0:T(8,128)(2,1)S(1)} %copy-done.5, f32[512]{0:T(512)S(1)} %broadcast_multiply_fusion, f32[512]{0:T(512)S(1)} %copy-done.34, f32[1024]{0:T(1024)S(1)} %copy-done.28, f32[512]{0:T(512)S(1)} %copy-done.33, ...), kind=kLoop, calls=%fused_computation.13 | loop fusion | flops 12582912 | bytes 6301697 | tf_op jit(solution)/shard_map/convert_element_type | solution.py:1076
  217.9 3.1 %collective-permute-done.46 = f32[8,2432]{1,0:T(8,128)S(1)} collective-permute-done((f32[8,2432]{1,0:T(8,128)S(1)}, f32[8,2432]{1,0:T(8,128)S(1)}, u32[]{:S(2)}, u32[]{:S(2)}) %collective-permute-start.46) | collective-permute-done | bytes 77856 | tf_op jit(solution)/shard_map/ppermute | solution.py:853
  223.0 2.1 collective-permute-start.49
  225.8 1.7 collective-permute-start.51
  228.6 2.8 %fusion.8 = bf16[512,1024]{1,0:T(8,128)(2,1)} fusion(bf16[512,1024]{1,0:T(8,128)(2,1)S(1)} %copy-done, bf16[512,1024]{1,0:T(8,128)(2,1)} %collective-permute-done.25, bf16[512,1024]{1,0:T(8,128)(2,1)S(1)} %copy-done.12), kind=kLoop, calls=%fused_computation.15 | loop fusion | flops 3145728 | bytes 4194304 | tf_op jit(solution)/shard_map/convert_element_type | solution.py:1080
  234.0 3.3 %collective-permute-start.48 = (f32[8,2432]{1,0:T(8,128)S(1)}, f32[8,2432]{1,0:T(8,128)S(1)}, u32[]{:S(2)}, u32[]{:S(2)}) collective-permute-start(f32[8,2432]{1,0:T(8,128)S(1)} %add.202.sums_ref), channel_id=1, source_target_pairs={{0,16},{2,18},{4,20},{6,22},{8,24},{10,26},{12,28},{14,30},{16,0},... | collective-permute-start | bytes 233480 | tf_op jit(solution)/shard_map/ppermute | solution.py:853
  (225 shorter events, 66.4 us)
Async XLA Ops:
  4.5 17.6 %collective-permute-start = (bf16[64,1408]{1,0:T(8,128)(2,1)}, bf16[64,1408]{1,0:T(8,128)(2,1)}, u32[]{:S(2)}, u32[]{:S(2)}) collective-permute-start(bf16[64,1408]{1,0:T(8,128)(2,1)} %pad_maximum_fusion.4), channel_id=1, source_target_pairs={{0,8},{2,10},{4,12},{6,14},{8,0},{10,2},{12,4},{14,6},{16,24},{18,... | collective-permute-start | bytes 540680 | tf_op jit(solution)/shard_map/ppermute | solution.py:853
  7.6 16.4 %collective-permute-start.1 = (bf16[64,1408]{1,0:T(8,128)(2,1)}, bf16[64,1408]{1,0:T(8,128)(2,1)}, u32[]{:S(2)}, u32[]{:S(2)}) collective-permute-start(bf16[64,1408]{1,0:T(8,128)(2,1)} %pad_maximum_fusion.4), channel_id=1, source_target_pairs={{0,16},{2,18},{4,20},{6,22},{8,24},{10,26},{12,28},{14,30},{16,0},... | collective-permute-start | bytes 540680 | tf_op jit(solution)/shard_map/ppermute | solution.py:853
  10.1 13.8 %collective-permute-start.2 = (bf16[64,1408]{1,0:T(8,128)(2,1)}, bf16[64,1408]{1,0:T(8,128)(2,1)}, u32[]{:S(2)}, u32[]{:S(2)}) collective-permute-start(bf16[64,1408]{1,0:T(8,128)(2,1)} %pad_maximum_fusion.4), channel_id=1, source_target_pairs={{0,24},{2,26},{4,28},{6,30},{8,16},{10,18},{12,20},{14,22},{16,8},... | collective-permute-start | bytes 540680 | tf_op jit(solution)/shard_map/ppermute | solution.py:853
  13.0 13.4 %collective-permute-start.4 = (bf16[256,1024]{1,0:T(8,128)(2,1)}, bf16[256,1024]{1,0:T(8,128)(2,1)}, u32[]{:S(2)}, u32[]{:S(2)}) collective-permute-start(bf16[256,1024]{1,0:T(8,128)(2,1)} %get-tuple-element.299), channel_id=1, source_target_pairs={{0,1},{1,0},{2,3},{3,2},{4,5},{5,4},{6,7},{7,6},{8,9},{9,8},{10,11... | collective-permute-start | bytes 1572872 | tf_op jit(solution)/shard_map/ppermute | solution.py:904
  26.4 17.0 %collective-permute-start.5 = (bf16[256,1408]{1,0:T(8,128)(2,1)S(1)}, bf16[256,1408]{1,0:T(8,128)(2,1)S(1)}, u32[]{:S(2)}, u32[]{:S(2)}) collective-permute-start(bf16[256,1408]{1,0:T(8,128)(2,1)S(1)} %pad_maximum_fusion.1.refs_3_), channel_id=1, source_target_pairs={{0,4},{2,6},{4,0},{6,2},{8,12},{10,14},{12,8},{14,10},{16,20},{18,... | collective-permute-start | bytes 2162696 | tf_op jit(solution)/shard_map/ppermute | solution.py:853
  27.9 14.7 %collective-permute-start.6 = (bf16[256,1024]{1,0:T(8,128)(2,1)}, bf16[256,1024]{1,0:T(8,128)(2,1)S(1)}, u32[]{:S(2)}, u32[]{:S(2)}) collective-permute-start(bf16[256,1024]{1,0:T(8,128)(2,1)} %get-tuple-element.298), channel_id=1, source_target_pairs={{0,1},{1,0},{2,3},{3,2},{4,5},{5,4},{6,7},{7,6},{8,9},{9,8},{10,11... | collective-permute-start | bytes 1572872 | tf_op jit(solution)/shard_map/ppermute | solution.py:904
  31.4 11.2 %collective-permute-start.8 = (bf16[64,1024]{1,0:T(8,128)(2,1)S(1)}, bf16[64,1024]{1,0:T(8,128)(2,1)S(1)}, u32[]{:S(2)}, u32[]{:S(2)}) collective-permute-start(bf16[64,1024]{1,0:T(8,128)(2,1)S(1)} %bitcast.102), channel_id=1, source_target_pairs={{0,16},{2,18},{4,20},{6,22},{8,24},{10,26},{12,28},{14,30},{16,0},... | collective-permute-start | bytes 393224 | tf_op jit(solution)/shard_map/ppermute | solution.py:853
  43.4 34.7 %collective-permute-start.12 = (bf16[512,1024]{1,0:T(8,128)(2,1)S(1)}, bf16[512,1024]{1,0:T(8,128)(2,1)S(1)}, u32[]{:S(2)}, u32[]{:S(2)}) collective-permute-start(bf16[512,1024]{1,0:T(8,128)(2,1)S(1)} %copy-done.4), channel_id=1, source_target_pairs={{0,1},{1,0},{2,3},{3,2},{4,5},{5,4},{6,7},{7,6},{8,9},{9,8},{10,11... | collective-permute-start | bytes 3145736 | tf_op jit(solution)/shard_map/ppermute | solution.py:904
  47.3 30.8 %collective-permute-start.13 = (bf16[256,1024]{1,0:T(8,128)(2,1)}, bf16[256,1024]{1,0:T(8,128)(2,1)}, u32[]{:S(2)}, u32[]{:S(2)}) collective-permute-start(bf16[256,1024]{1,0:T(8,128)(2,1)} %constant_dynamic-update-slice_fusion.refs_2_), channel_id=1, source_target_pairs={{0,4},{2,6},{4,0},{6,2},{8,12},{10,14},{12,8},{14,10},{16,20},{18,... | collective-permute-start | bytes 1572872 | tf_op jit(solution)/shard_map/ppermute | solution.py:853
  48.8 29.3 %collective-permute-start.14 = (bf16[128,1024]{1,0:T(8,128)(2,1)S(1)}, bf16[128,1024]{1,0:T(8,128)(2,1)S(1)}, u32[]{:S(2)}, u32[]{:S(2)}) collective-permute-start(bf16[128,1024]{1,0:T(8,128)(2,1)S(1)} %pad_maximum_fusion.3.refs_6_), channel_id=1, source_target_pairs={{0,8},{2,10},{4,12},{6,14},{8,0},{10,2},{12,4},{14,6},{16,24},{18,... | collective-permute-start | bytes 786440 | tf_op jit(solution)/shard_map/ppermute | solution.py:853
  51.2 26.9 %collective-permute-start.15 = (bf16[128,1024]{1,0:T(8,128)(2,1)S(1)}, bf16[128,1024]{1,0:T(8,128)(2,1)S(1)}, u32[]{:S(2)}, u32[]{:S(2)}) collective-permute-start(bf16[128,1024]{1,0:T(8,128)(2,1)S(1)} %pad_maximum_fusion.3.refs_6_), channel_id=1, source_target_pairs={{0,16},{2,18},{4,20},{6,22},{8,24},{10,26},{12,28},{14,30},{16,0},... | collective-permute-start | bytes 786440 | tf_op jit(solution)/shard_map/ppermute | solution.py:853
  53.7 24.4 %collective-permute-start.16 = (bf16[128,1024]{1,0:T(8,128)(2,1)S(1)}, bf16[128,1024]{1,0:T(8,128)(2,1)}, u32[]{:S(2)}, u32[]{:S(2)}) collective-permute-start(bf16[128,1024]{1,0:T(8,128)(2,1)S(1)} %pad_maximum_fusion.3.refs_6_), channel_id=1, source_target_pairs={{0,24},{2,26},{4,28},{6,30},{8,16},{10,18},{12,20},{14,22},{16,8},... | collective-permute-start | bytes 786440 | tf_op jit(solution)/shard_map/ppermute | solution.py:853
  121.7 12.6 %collective-permute-start.24 = (bf16[512,2048]{1,0:T(8,128)(2,1)}, bf16[512,2048]{1,0:T(8,128)(2,1)}, u32[]{:S(2)}, u32[]{:S(2)}) collective-permute-start(bf16[512,2048]{1,0:T(8,128)(2,1)} %get-tuple-element.189), channel_id=1, source_target_pairs={{0,2},{2,0},{4,6},{6,4},{8,10},{10,8},{12,14},{14,12},{16,18},{18,... | collective-permute-start | bytes 6291464 | tf_op jit(solution)/shard_map/ppermute | solution.py:853
  121.8 47.4 %collective-permute-start.25 = (bf16[512,1024]{1,0:T(8,128)(2,1)}, bf16[512,1024]{1,0:T(8,128)(2,1)}, u32[]{:S(2)}, u32[]{:S(2)}) collective-permute-start(bf16[512,1024]{1,0:T(8,128)(2,1)} %get-tuple-element.200), channel_id=1, source_target_pairs={{0,1},{1,0},{2,3},{3,2},{4,5},{5,4},{6,7},{7,6},{8,9},{9,8},{10,11... | collective-permute-start | bytes 3145736 | tf_op jit(solution)/shard_map/ppermute | solution.py:904
  137.8 30.1 %collective-permute-start.26 = (bf16[4,64,1024]{2,1,0:T(8,128)(2,1)}, bf16[4,64,1024]{2,1,0:T(8,128)(2,1)}, u32[]{:S(2)}, u32[]{:S(2)}) collective-permute-start(bf16[4,64,1024]{2,1,0:T(8,128)(2,1)} %dynamic-slice_bitcast_fusion), channel_id=1, source_target_pairs={{0,4},{2,6},{4,0},{6,2},{8,12},{10,14},{12,8},{14,10},{16,20},{18,... | collective-permute-start | bytes 1572872 | tf_op jit(solution)/shard_map/ppermute | solution.py:853
  139.7 27.0 %collective-permute-start.27 = (bf16[2,64,1024]{2,1,0:T(8,128)(2,1)}, bf16[2,64,1024]{2,1,0:T(8,128)(2,1)S(1)}, u32[]{:S(2)}, u32[]{:S(2)}) collective-permute-start(bf16[2,64,1024]{2,1,0:T(8,128)(2,1)} %get-tuple-element.295), channel_id=1, source_target_pairs={{0,8},{2,10},{4,12},{6,14},{8,0},{10,2},{12,4},{14,6},{16,24},{18,... | collective-permute-start | bytes 786440 | tf_op jit(solution)/shard_map/ppermute | solution.py:853
  139.8 26.9 %collective-permute-start.28 = (bf16[2,64,1024]{2,1,0:T(8,128)(2,1)}, bf16[2,64,1024]{2,1,0:T(8,128)(2,1)}, u32[]{:S(2)}, u32[]{:S(2)}) collective-permute-start(bf16[2,64,1024]{2,1,0:T(8,128)(2,1)} %get-tuple-element.297), channel_id=1, source_target_pairs={{0,16},{2,18},{4,20},{6,22},{8,24},{10,26},{12,28},{14,30},{16,0},... | collective-permute-start | bytes 786440 | tf_op jit(solution)/shard_map/ppermute | solution.py:853
  142.0 24.8 %collective-permute-start.29 = (bf16[2,64,1024]{2,1,0:T(8,128)(2,1)}, bf16[2,64,1024]{2,1,0:T(8,128)(2,1)}, u32[]{:S(2)}, u32[]{:S(2)}) collective-permute-start(bf16[2,64,1024]{2,1,0:T(8,128)(2,1)} %get-tuple-element.296), channel_id=1, source_target_pairs={{0,24},{2,26},{4,28},{6,30},{8,16},{10,18},{12,20},{14,22},{16,8},... | collective-permute-start | bytes 786440 | tf_op jit(solution)/shard_map/ppermute | solution.py:853
  169.2 19.8 %collective-permute-start.33 = (bf16[64,1024]{1,0:T(8,128)(2,1)S(1)}, bf16[64,1024]{1,0:T(8,128)(2,1)S(1)}, u32[]{:S(2)}, u32[]{:S(2)}) collective-permute-start(bf16[64,1024]{1,0:T(8,128)(2,1)S(1)} %dynamic-slice_bitcast_fusion.8), channel_id=1, source_target_pairs={{0,4},{2,6},{4,0},{6,2},{8,12},{10,14},{12,8},{14,10},{16,20},{18,... | collective-permute-start | bytes 393224 | tf_op jit(solution)/shard_map/ppermute | solution.py:853
  170.4 19.4 %collective-permute-start.34 = (bf16[256,1024]{1,0:T(8,128)(2,1)}, bf16[256,1024]{1,0:T(8,128)(2,1)S(1)}, u32[]{:S(2)}, u32[]{:S(2)}) collective-permute-start(bf16[256,1024]{1,0:T(8,128)(2,1)} %get-tuple-element.211), channel_id=1, source_target_pairs={{0,1},{1,0},{2,3},{3,2},{4,5},{5,4},{6,7},{7,6},{8,9},{9,8},{10,11... | collective-permute-start | bytes 1572872 | tf_op jit(solution)/shard_map/ppermute | solution.py:904
  172.0 17.7 %collective-permute-start.30 = (bf16[64,1024]{1,0:T(8,128)(2,1)S(1)}, bf16[64,1024]{1,0:T(8,128)(2,1)S(1)}, u32[]{:S(2)}, u32[]{:S(2)}) collective-permute-start(bf16[64,1024]{1,0:T(8,128)(2,1)S(1)} %get-tuple-element.303), channel_id=1, source_target_pairs={{0,8},{2,10},{4,12},{6,14},{8,0},{10,2},{12,4},{14,6},{16,24},{18,... | collective-permute-start | bytes 393224 | tf_op jit(solution)/shard_map/ppermute | solution.py:853
  172.1 17.7 %collective-permute-start.31 = (bf16[64,1024]{1,0:T(8,128)(2,1)S(1)}, bf16[64,1024]{1,0:T(8,128)(2,1)S(1)}, u32[]{:S(2)}, u32[]{:S(2)}) collective-permute-start(bf16[64,1024]{1,0:T(8,128)(2,1)S(1)} %get-tuple-element.305), channel_id=1, source_target_pairs={{0,16},{2,18},{4,20},{6,22},{8,24},{10,26},{12,28},{14,30},{16,0},... | collective-permute-start | bytes 393224 | tf_op jit(solution)/shard_map/ppermute | solution.py:853
  174.8 15.0 %collective-permute-start.32 = (bf16[64,1024]{1,0:T(8,128)(2,1)S(1)}, bf16[64,1024]{1,0:T(8,128)(2,1)S(1)}, u32[]{:S(2)}, u32[]{:S(2)}) collective-permute-start(bf16[64,1024]{1,0:T(8,128)(2,1)S(1)} %get-tuple-element.304), channel_id=1, source_target_pairs={{0,24},{2,26},{4,28},{6,30},{8,16},{10,18},{12,20},{14,22},{16,8},... | collective-permute-start | bytes 393224 | tf_op jit(solution)/shard_map/ppermute | solution.py:853
  189.8 13.0 %collective-permute-start.39 = (bf16[256,1024]{1,0:T(8,128)(2,1)}, bf16[256,1024]{1,0:T(8,128)(2,1)S(1)}, u32[]{:S(2)}, u32[]{:S(2)}) collective-permute-start(bf16[256,1024]{1,0:T(8,128)(2,1)} %get-tuple-element.224), channel_id=1, source_target_pairs={{0,1},{1,0},{2,3},{3,2},{4,5},{5,4},{6,7},{7,6},{8,9},{9,8},{10,11... | collective-permute-start | bytes 1572872 | tf_op jit(solution)/shard_map/ppermute | solution.py:904
  206.9 14.1 %collective-permute-start.40 = (bf16[4,64,896]{2,1,0:T(8,128)(2,1)S(1)}, bf16[4,64,896]{2,1,0:T(8,128)(2,1)S(1)}, u32[]{:S(2)}, u32[]{:S(2)}) collective-permute-start(bf16[4,64,896]{2,1,0:T(8,128)(2,1)S(1)} %dynamic-slice_bitcast_fusion.1), channel_id=1, source_target_pairs={{0,4},{2,6},{4,0},{6,2},{8,12},{10,14},{12,8},{14,10},{16,20},{18,... | collective-permute-start | bytes 1376264 | tf_op jit(solution)/shard_map/ppermute | solution.py:853
  207.6 13.4 %collective-permute-start.41 = (bf16[2,64,512]{2,1,0:T(8,128)(2,1)S(1)}, bf16[2,64,512]{2,1,0:T(8,128)(2,1)S(1)}, u32[]{:S(2)}, u32[]{:S(2)}) collective-permute-start(bf16[2,64,512]{2,1,0:T(8,128)(2,1)S(1)} %get-tuple-element.302), channel_id=1, source_target_pairs={{0,8},{2,10},{4,12},{6,14},{8,0},{10,2},{12,4},{14,6},{16,24},{18,... | collective-permute-start | bytes 393224 | tf_op jit(solution)/shard_map/ppermute | solution.py:853
  207.7 13.3 %collective-permute-start.42 = (bf16[2,64,512]{2,1,0:T(8,128)(2,1)S(1)}, bf16[2,64,512]{2,1,0:T(8,128)(2,1)S(1)}, u32[]{:S(2)}, u32[]{:S(2)}) collective-permute-start(bf16[2,64,512]{2,1,0:T(8,128)(2,1)S(1)} %get-tuple-element.301), channel_id=1, source_target_pairs={{0,16},{2,18},{4,20},{6,22},{8,24},{10,26},{12,28},{14,30},{16,0},... | collective-permute-start | bytes 393224 | tf_op jit(solution)/shard_map/ppermute | solution.py:853
  210.3 10.6 %collective-permute-start.43 = (bf16[2,64,512]{2,1,0:T(8,128)(2,1)S(1)}, bf16[2,64,512]{2,1,0:T(8,128)(2,1)S(1)}, u32[]{:S(2)}, u32[]{:S(2)}) collective-permute-start(bf16[2,64,512]{2,1,0:T(8,128)(2,1)S(1)} %get-tuple-element.300), channel_id=1, source_target_pairs={{0,24},{2,26},{4,28},{6,30},{8,16},{10,18},{12,20},{14,22},{16,8},... | collective-permute-start | bytes 393224 | tf_op jit(solution)/shard_map/ppermute | solution.py:853
  221.1 10.4 %collective-permute-start.52 = (bf16[64,512]{1,0:T(8,128)(2,1)S(1)}, bf16[64,512]{1,0:T(8,128)(2,1)S(1)}, u32[]{:S(2)}, u32[]{:S(2)}) collective-permute-start(bf16[64,512]{1,0:T(8,128)(2,1)S(1)} %dynamic-slice_bitcast_fusion.15), channel_id=1, source_target_pairs={{0,4},{2,6},{4,0},{6,2},{8,12},{10,14},{12,8},{14,10},{16,20},{18,... | collective-permute-start | bytes 196616 | tf_op jit(solution)/shard_map/ppermute | solution.py:853
  223.0 14.3 %collective-permute-start.49 = (bf16[64,896]{1,0:T(8,128)(2,1)}, bf16[64,896]{1,0:T(8,128)(2,1)}, u32[]{:S(2)}, u32[]{:S(2)}) collective-permute-start(bf16[64,896]{1,0:T(8,128)(2,1)} %get-tuple-element.306), channel_id=1, source_target_pairs={{0,8},{2,10},{4,12},{6,14},{8,0},{10,2},{12,4},{14,6},{16,24},{18,... | collective-permute-start | bytes 344072 | tf_op jit(solution)/shard_map/ppermute | solution.py:853
  225.1 12.2 %collective-permute-start.50 = (bf16[64,896]{1,0:T(8,128)(2,1)}, bf16[64,896]{1,0:T(8,128)(2,1)}, u32[]{:S(2)}, u32[]{:S(2)}) collective-permute-start(bf16[64,896]{1,0:T(8,128)(2,1)} %get-tuple-element.308), channel_id=1, source_target_pairs={{0,16},{2,18},{4,20},{6,22},{8,24},{10,26},{12,28},{14,30},{16,0},... | collective-permute-start | bytes 344072 | tf_op jit(solution)/shard_map/ppermute | solution.py:853
  225.8 11.6 %collective-permute-start.51 = (bf16[64,896]{1,0:T(8,128)(2,1)S(1)}, bf16[64,896]{1,0:T(8,128)(2,1)}, u32[]{:S(2)}, u32[]{:S(2)}) collective-permute-start(bf16[64,896]{1,0:T(8,128)(2,1)S(1)} %get-tuple-element.307), channel_id=1, source_target_pairs={{0,24},{2,26},{4,28},{6,30},{8,16},{10,18},{12,20},{14,22},{16,8},... | collective-permute-start | bytes 344072 | tf_op jit(solution)/shard_map/ppermute | solution.py:853
  (59 other events, 366.6 us)
